TPU v7x, 32 devices: a whole 2x2x4 slice. The times are simulated.
32 devices in a mesh: fsdp: 8 (over y, x, core), sp: 4 (over z).
Axes of the slice: x: 2, y: 2, z: 4, core: 2. Of those that a mesh axis runs over, the one named last changes fastest.
Arguments:
- tokens: bfloat16 [4096, 5120], P(('fsdp', 'sp')), may hold values from -6 to 6
- norm_gain: float32 [5120], replicated, may hold values from 0.1 to 1.9
- q_weight: bfloat16 [5120, 5120], P('fsdp', 'sp'), may hold values from -0.078125 to 0.078125
- key_matrix: bfloat16 [5120, 1024], P('fsdp', 'sp'), may hold values from -0.078125 to 0.078125
- value_matrix: bfloat16 [5120, 1024], P('fsdp', 'sp'), may hold values from -0.078125 to 0.078125
- q_bias: float32 [5120], P('sp'), may hold values from -8 to 8
- k_bias: float32 [1024], P('sp'), may hold values from -8 to 8
- value_offset_bias: float32 [1024], P('sp'), may hold values from -3 to 3
- out_weight: bfloat16 [5120, 5120], P('fsdp', 'sp'), may hold values from -0.078125 to 0.078125
Outputs:
- mixed: bfloat16 [4096, 5120], P(('fsdp', 'sp'))
All inputs are finite; a program needn't handle non-finite values.
Results may differ from a plain program's by a relative error of at most 0.014.
Values may be sent and summed in bfloat16 or wider, within the bound.
No kernel may reach another device: no remote copies, remote signals or barrier semaphores. Data moves between devices by JAX's collectives and lax.ppermute only.
A program may use at most 128 MiB of HBM per device.

v0:
```python
import jax
import jax.numpy as jnp
from jax import lax
from jax.sharding import PartitionSpec as P

HEAD_SIZE = 128


ROPE_BASE = 1000000.0


def rms_normed(tokens, norm_gain):
    rows = tokens.astype(jnp.float32)
    meansq = jnp.mean(rows * rows, axis=-1, keepdims=True)
    return (rows * lax.rsqrt(meansq + 1e-06) * norm_gain).astype(jnp.bfloat16)


def rotary(projected, positions):
    count = projected.shape[0]
    heads_grid = projected.reshape(count, -1, HEAD_SIZE)
    half_dim = HEAD_SIZE // 2
    frequency = ROPE_BASE ** (-(jnp.arange(half_dim, dtype=jnp.float32) * 2.0 / HEAD_SIZE))
    angle = positions[:, None] * frequency[None, :]
    cosine = jnp.cos(angle)[:, None, :]
    sine = jnp.sin(angle)[:, None, :]
    first = heads_grid[..., :half_dim]
    second = heads_grid[..., half_dim:]
    rotated = jnp.concatenate(
        [first * cosine - second * sine, second * cosine + first * sine], axis=-1
    )
    return rotated.reshape(count, -1)


def attend(queries, keys, values):
    length = queries.shape[0]
    kv_heads = keys.shape[1] // HEAD_SIZE
    group_size = queries.shape[1] // keys.shape[1]
    query_grid = queries.reshape(length, kv_heads, group_size, HEAD_SIZE)
    key_grid = keys.reshape(length, kv_heads, HEAD_SIZE)
    value_grid = values.reshape(length, kv_heads, HEAD_SIZE)
    scores = jnp.einsum(
        "qkgd,skd->kgqs", query_grid, key_grid, preferred_element_type=jnp.float32
    ) / jnp.sqrt(jnp.float32(HEAD_SIZE))
    causal = lax.iota(jnp.int32, length)[:, None] >= lax.iota(jnp.int32, length)[None, :]
    scores = jnp.where(causal, scores, jnp.float32(-1e30))
    largest = jnp.max(scores, axis=-1, keepdims=True)
    weights = jnp.exp(scores - largest)
    totals = jnp.sum(weights, axis=-1, keepdims=True)
    probs = (weights / totals).astype(jnp.bfloat16)
    result = jnp.einsum("kgqs,skd->qkgd", probs, value_grid, preferred_element_type=jnp.float32)
    return result.reshape(length, -1).astype(jnp.bfloat16)


def project_heads(normed, q_full, k_full, v_full, q_bias, k_bias, value_offset_bias):
    q_cols = q_full.shape[1]
    k_cols = k_full.shape[1]
    piece = lax.all_gather(normed, "sp", axis=0, tiled=True)
    count = piece.shape[0]
    positions = lax.iota(jnp.int32, count).astype(jnp.float32)
    queries = rotary(jnp.dot(piece, q_full, preferred_element_type=jnp.float32) + q_bias, positions)
    keys = rotary(jnp.dot(piece, k_full, preferred_element_type=jnp.float32) + k_bias, positions)
    values = jnp.dot(piece, v_full, preferred_element_type=jnp.float32) + value_offset_bias
    stacked = jnp.concatenate([queries, keys, values], axis=1).astype(jnp.bfloat16)
    queries = stacked[:, :q_cols]
    keys = stacked[:, q_cols : q_cols + k_cols]
    values = stacked[:, q_cols + k_cols :]
    return attend(queries, keys, values)


def body(
    tokens,
    norm_gain,
    q_weight,
    key_matrix,
    value_matrix,
    q_bias,
    k_bias,
    value_offset_bias,
    out_weight,
):
    normed = rms_normed(tokens, norm_gain)
    q_full, k_full, v_full = (
        lax.all_gather(q_weight, "fsdp", axis=0, tiled=True),
        lax.all_gather(key_matrix, "fsdp", axis=0, tiled=True),
        lax.all_gather(value_matrix, "fsdp", axis=0, tiled=True),
    )
    heads = project_heads(normed, q_full, k_full, v_full, q_bias, k_bias, value_offset_bias)
    partial_value = lax.dot_general(
        heads,
        lax.all_gather(out_weight, "fsdp", axis=0, tiled=True),
        (((1,), (1,)), ((), ())),
        preferred_element_type=jnp.float32,
    )
    mixed = lax.psum_scatter(
        partial_value.astype(jnp.bfloat16), "sp", scatter_dimension=0, tiled=True
    )
    return mixed


def solution(mesh):
    placed = (
        P(("fsdp", "sp"), None),
        P(),
        P("fsdp", "sp"),
        P("fsdp", "sp"),
        P("fsdp", "sp"),
        P("sp"),
        P("sp"),
        P("sp"),
        P("fsdp", "sp"),
    )
    return jax.shard_map(
        body, mesh=mesh, in_specs=placed, out_specs=P(("fsdp", "sp"), None), check_vma=False
    )
```

profile of v0, /device:TPU:0, one launch (start us, length us, event | category | flops | bytes accessed | tf_op | source)
XLA Modules:
  0.0 438.7 jit_solution(18211921042575762517)
XLA Ops:
  6.5 0.7 all-gather.10.cloned.1.call-update
  7.3 0.0 all-gather.6.cloned.1.call-start
  7.3 1.7 fusion.6
  9.0 2.8 fusion.8
  11.8 0.0 all-gather.8.cloned.1.call-start
  11.8 0.7 all-gather.8.cloned.1.call-update
  12.6 0.5 all-gather.12.cloned.1.call-update
  13.1 0.5 all-gather.14.cloned.1.call-update
  13.7 0.0 reduce-scatter.2.cloned.1.call-start
  13.7 0.5 multiply_cosine_fusion
  14.3 0.1 copy.22
  14.4 0.1 copy.24
  14.6 0.1 iota_compare_fusion
  14.6 27.4 %all-gather.10.cloned.1.call-done = bf16[5120,256]{1,0:T(8,128)(2,1)} async-done(((bf16[640,256]{1,0:T(8,128)(2,1)}), bf16[5120,256]{1,0:T(8,128)(2,1)}) %all-gather.10.cloned.1.call-update) | async-done | bytes 2621456 | tf_op jit(solution)/shard_map/all_gather | solution.py:84
  42.1 99.7 %all-gather.6.cloned.1.call-done = bf16[512,5120]{1,0:T(8,128)(2,1)} async-done(((bf16[128,5120]{1,0:T(8,128)(2,1)}), bf16[512,5120]{1,0:T(8,128)(2,1)}) %all-gather.6.cloned.1.call-update) | async-done | bytes 5242896 | tf_op jit(solution)/shard_map/all_gather | solution.py:57
  141.8 4.9 %convolution_add_fusion.1 = f32[512,256]{0,1:T(8,128)S(1)} fusion(bf16[512,5120]{1,0:T(8,128)(2,1)} %all-gather.6.cloned.1.call-done, bf16[5120,256]{1,0:T(8,128)(2,1)} %all-gather.10.cloned.1.call-done, f32[256]{0:T(256)S(1)} %copy-done.2), kind=kOutput, calls=%fused_computation.20 | convolution fusion | flops 1342308352 | bytes 8389632 | tf_op jit(solution)/shard_map/dot_general | solution.py:61
  146.7 0.2 copy.31
  146.9 0.2 copy.32
  147.1 0.9 subtract_convert_fusion.1
  148.0 24.2 %all-gather.8.cloned.1.call-done = bf16[5120,256]{1,0:T(8,128)(2,1)} async-done(((bf16[640,256]{1,0:T(8,128)(2,1)}), bf16[5120,256]{1,0:T(8,128)(2,1)}) %all-gather.8.cloned.1.call-update) | async-done | bytes 2621456 | tf_op jit(solution)/shard_map/all_gather | solution.py:85
  172.2 5.6 %fusion.10 = bf16[512,256]{0,1:T(8,128)(2,1)} fusion(bf16[512,5120]{1,0:T(8,128)(2,1)} %all-gather.6.cloned.1.call-done, bf16[5120,256]{1,0:T(8,128)(2,1)} %all-gather.8.cloned.1.call-done, f32[256]{0:T(256)S(1)} %copy-done.3), kind=kOutput, calls=%fused_computation.22 | convolution fusion | flops 1342439424 | bytes 8127488 | tf_op jit(solution)/shard_map/dot_general | solution.py:62
  177.8 70.5 %all-gather.12.cloned.1.call-done = bf16[5120,1280]{1,0:T(8,128)(2,1)} async-done(((bf16[640,1280]{1,0:T(8,128)(2,1)}), bf16[5120,1280]{1,0:T(8,128)(2,1)}) %all-gather.12.cloned.1.call-update) | async-done | bytes 13107216 | tf_op jit(solution)/shard_map/all_gather | solution.py:83
  248.3 13.7 %convolution_add_fusion = f32[512,1280]{1,0:T(8,128)} fusion(bf16[512,5120]{1,0:T(8,128)(2,1)} %all-gather.6.cloned.1.call-done, bf16[5120,1280]{1,0:T(8,128)(2,1)} %all-gather.12.cloned.1.call-done, f32[1280]{0:T(1024)S(1)} %copy-done.1), kind=kOutput, calls=%fused_computation.10 | convolution fusion | flops 6711541760 | bytes 20976640 | tf_op jit(solution)/shard_map/dot_general | solution.py:60
  262.0 2.1 copy.25
  264.2 0.4 subtract_convert_fusion
  264.6 0.1 pad_maximum_fusion
  264.8 0.8 copy-done
  265.6 6.6 %fusion.21 = (f32[2,5,512]{2,1,0:T(8,128)S(1)}, f32[2,5,512,512]{2,3,1,0:T(8,128)}) fusion(pred[512,512]{0,1:T(8,128)(4,1)S(1)} %iota_compare_fusion, bf16[512,2,5,128]{0,3,2,1:T(8,128)(2,1)S(1)} %bitcast.49, bf16[512,2,64]{2,0,1:T(8,128)(2,1)S(1)} %copy-done, bf16[512,2,64]{2,0,1:T(8,128)(2,1)S(1)} %get-tuple-element.7), kind=kOutput, calls=%fused_computation.39 | convolution fusion | flops 682099200 | bytes 12341248 | tf_op jit(solution)/shard_map/sub | solution.py:47
  272.1 4.8 %fusion.9 = bf16[2,128,5,512]{3,1,2,0:T(8,128)(2,1)S(1)} fusion(bf16[512,2,128,1]{0,2,3,1:T(8,128)(2,1)S(1)} %bitcast.52, f32[2,5,512,512]{2,3,1,0:T(8,128)} %get-tuple-element.14, f32[2,5,512]{2,1,0:T(8,128)S(1)} %get-tuple-element.13), kind=kOutput, calls=%fused_computation.16 | convolution fusion | flops 676986880 | bytes 12079104 | tf_op jit(solution)/shard_map/kgqs,skd->qkgd/dot_general | solution.py:50
  277.0 47.4 %all-gather.14.cloned.1.call-done = bf16[5120,1280]{1,0:T(8,128)(2,1)} async-done(((bf16[640,1280]{1,0:T(8,128)(2,1)}), bf16[5120,1280]{1,0:T(8,128)(2,1)}) %all-gather.14.cloned.1.call-update) | async-done | bytes 13107216 | tf_op jit(solution)/shard_map/all_gather | solution.py:90
  324.4 13.5 %convolution_convert_fusion = bf16[512,5120]{1,0:T(8,128)(2,1)} fusion(bf16[512,1280]{0,1:T(8,128)(2,1)S(1)} %bitcast.51, bf16[5120,1280]{1,0:T(8,128)(2,1)} %all-gather.14.cloned.1.call-done), kind=kOutput, calls=%fused_computation.5 | convolution fusion | flops 6713507840 | bytes 19660800 | tf_op jit(solution)/shard_map/dot_general | solution.py:88
  337.9 93.9 %reduce-scatter.2.cloned.1.call-done = bf16[128,5120]{1,0:T(8,128)(2,1)} async-done(((bf16[512,5120]{1,0:T(8,128)(2,1)}), bf16[128,5120]{1,0:T(8,128)(2,1)}) %reduce-scatter.2.cloned.1.call-update) | async-done | bytes 1310736 | tf_op jit(solution)/shard_map/reduce_scatter | solution.py:94
  (18 shorter events, 0.2 us)
Async XLA Ops:
  6.5 35.6 %all-gather.10.cloned.1.call-start = ((), (), s32[]{:S(2)}) async-start(), calls=%async_computation.3 | async-start | bytes 2949120 | tf_op jit(solution)/shard_map/all_gather | solution.py:84
  7.3 134.5 %all-gather.6.cloned.1.call-start = ((), (), s32[]{:S(2)}) async-start(), calls=%async_computation.1 | async-start | bytes 6553600 | tf_op jit(solution)/shard_map/all_gather | solution.py:57
  11.8 130.0 %copy-start.2 = (f32[256]{0:T(256)S(1)}, f32[256]{0:T(256)}, u32[]{:S(2)}) copy-start(f32[256]{0:T(256)} %param.15) | copy-start | bytes 3076
  11.8 160.4 %all-gather.8.cloned.1.call-start = ((), (), s32[]{:S(2)}) async-start(), calls=%async_computation.2 | async-start | bytes 2949120 | tf_op jit(solution)/shard_map/all_gather | solution.py:85
  12.5 235.8 %all-gather.12.cloned.1.call-start = ((), (), s32[]{:S(2)}) async-start(), calls=%async_computation.4 | async-start | bytes 14745600 | tf_op jit(solution)/shard_map/all_gather | solution.py:83
  13.1 311.3 %all-gather.14.cloned.1.call-start = ((), (), s32[]{:S(2)}) async-start(), calls=%async_computation.5 | async-start | bytes 14745600 | tf_op jit(solution)/shard_map/all_gather | solution.py:90
  13.7 418.2 %reduce-scatter.2.cloned.1.call-start = ((), (), s32[]{:S(2)}) async-start(), calls=%async_computation.6 | async-start | bytes 6553600 | tf_op jit(solution)/shard_map/reduce_scatter | solution.py:94
  146.6 25.5 %copy-start.3 = (f32[256]{0:T(256)S(1)}, f32[256]{0:T(256)}, u32[]{:S(2)}) copy-start(f32[256]{0:T(256)} %param.16) | copy-start | bytes 3076
  148.0 100.3 %copy-start.1 = (f32[1280]{0:T(1024)S(1)}, f32[1280]{0:T(1024)}, u32[]{:S(2)}) copy-start(f32[1280]{0:T(1024)} %param.14) | copy-start | bytes 15364
  264.6 1.0 copy-start
  265.6 6.6 %copy-start.4 = (bf16[512,256]{0,1:T(8,128)(2,1)S(1)}, bf16[512,256]{0,1:T(8,128)(2,1)}, u32[]{:S(2)}) copy-start(bf16[512,256]{0,1:T(8,128)(2,1)} %fusion.10) | copy-start | bytes 786436
Sparse Core Ops, SparseCore 0:
  9.2 32.8 all-gather.9
  43.7 98.0 all-gather.5
  143.6 28.4 all-gather.7
  173.9 74.3 all-gather.11
  250.0 74.3 all-gather.13
  338.1 93.7 reduce-scatter.1
where the time goes:
time: 439 us
  waiting for transfers between devices  366 us (83%)
  matrix products  49.1 us (11%)
  between operations  13.6 us (3%)
  other arithmetic  6.49 us (1%)
    all_gather x1, waiting for transfers between devices, project_heads(): piece = lax.all_gather(normed, 'sp', axis=0, tiled=True)  99.7 us
    reduce_scatter x1, waiting for transfers between devices, body(): lax.psum_scatter(partial_value.astype(jnp.bfloat16), 'sp', scatter_dimens...  93.9 us
    all_gather x1, waiting for transfers between devices, body(): lax.all_gather(q_weight, 'fsdp', axis=0, tiled=True)  70.5 us
    all_gather x1, waiting for transfers between devices, body(): lax.all_gather(out_weight, 'fsdp', axis=0, tiled=True)  47.4 us
    all_gather x1, waiting for transfers between devices, body(): lax.all_gather(key_matrix, 'fsdp', axis=0, tiled=True)  27.4 us
    all_gather x1, waiting for transfers between devices, body(): lax.all_gather(value_matrix, 'fsdp', axis=0, tiled=True)  24.2 us
    dot_general x1, matrix products, project_heads(): jnp.dot(piece, q_full, preferred_element_type=jnp.float32) + q_bias  13.7 us
    dot_general x1, matrix products, body(): lax.dot_general(heads, lax.all_gather(out_weight, 'fsdp', axis=0, tiled=T...  13.5 us
  transfers between devices with their start and end apart: 6, of which 6 were waited for; matrix products, arithmetic and copies ran while one was open for 10% of the time, Pallas kernels for 0%

commit v1 on v0

v1 whole, which is shorter than its diff:
```python
import functools

import jax
import jax.numpy as jnp
from jax import lax
from jax.experimental import pallas as pl
from jax.experimental.pallas import tpu as pltpu
from jax.sharding import PartitionSpec as P

HEAD_SIZE = 128
HALF = HEAD_SIZE // 2
ROPE_BASE = 1000000.0
LOG2E = 1.4426950408889634
VMEM_LIMIT = 50 * 1024 * 1024
Z_CHUNKS = 2
NT = (((1,), (1,)), ((), ()))


def params():
    return pltpu.CompilerParams(vmem_limit_bytes=VMEM_LIMIT)


def normed_kernel(n_f, me_ref, tokens_ref, gain_ref, *out_refs):
    rows = tokens_ref[...].astype(jnp.float32)
    scale = lax.rsqrt(jnp.mean(rows * rows, axis=-1, keepdims=True) + 1e-06)
    shard = tokens_ref.shape[1] // n_f
    per_chunk = n_f // len(out_refs)
    for j in range(n_f):
        start = pl.multiple_of(jnp.bitwise_xor(me_ref[0], j) * shard, 128)
        columns = pl.ds(start, shard)
        piece = tokens_ref[:, columns].astype(jnp.float32) * scale * gain_ref[:, columns]
        at = (j % per_chunk) * shard
        out_refs[j // per_chunk][:, at : at + shard] = piece.astype(jnp.bfloat16)


def normed_pieces(me, tokens, gain, n_f, chunks):
    count, width = tokens.shape
    shard = width // n_f
    if shard % 128 == 0:
        return pl.pallas_call(
            functools.partial(normed_kernel, n_f),
            out_shape=[jax.ShapeDtypeStruct((count, width // chunks), jnp.bfloat16)] * chunks,
            in_specs=[
                pl.BlockSpec(memory_space=pltpu.SMEM),
                pl.BlockSpec(memory_space=pltpu.VMEM),
                pl.BlockSpec(memory_space=pltpu.VMEM),
            ],
            out_specs=[pl.BlockSpec(memory_space=pltpu.VMEM)] * chunks,
            compiler_params=params(),
            name="norm",
        )(me[None], tokens, gain[None, :])
    rows = tokens.astype(jnp.float32)
    meansq = jnp.mean(rows * rows, axis=-1, keepdims=True)
    normed = (rows * lax.rsqrt(meansq + 1e-06) * gain).astype(jnp.bfloat16)
    pieces = [
        lax.dynamic_slice_in_dim(normed, jnp.bitwise_xor(me, j) * shard, shard, axis=1)
        for j in range(n_f)
    ]
    per_chunk = n_f // chunks
    return [
        jnp.concatenate(pieces[c * per_chunk : (c + 1) * per_chunk], axis=1) for c in range(chunks)
    ]


def rope_tile(tile, cos, sin):
    parts = []
    for at in range(0, tile.shape[1], HEAD_SIZE):
        head = tile[:, at : at + HEAD_SIZE]
        parts.append(head * cos + pltpu.roll(head, HALF, axis=1) * sin)
    return parts[0] if len(parts) == 1 else jnp.concatenate(parts, axis=1)


def project_kernel(n_f, chunks, q_tiles, k_tiles, *refs):
    x_refs = refs[:chunks]
    q_refs = refs[chunks : chunks + n_f]
    kv_refs = refs[chunks + n_f : chunks + 2 * n_f]
    q_bias, kv_bias, cos_ref, sin_ref, q_out, kv_out = refs[chunks + 2 * n_f :]
    shard = q_refs[0].shape[0]
    per_chunk = n_f // chunks
    step = pl.program_id(0)

    def product(w_refs, bias):
        total = None
        for j in range(n_f):
            at = (j % per_chunk) * shard
            term = jnp.dot(
                x_refs[j // per_chunk][:, at : at + shard],
                w_refs[j][...],
                preferred_element_type=jnp.float32,
            )
            total = term if total is None else total + term
        return total + bias[...]

    @pl.when(step < q_tiles)
    def _():
        tile = product(q_refs, q_bias)
        q_out[...] = rope_tile(tile, cos_ref[...], sin_ref[...]).astype(jnp.bfloat16)

    @pl.when(jnp.logical_and(step >= q_tiles, step < q_tiles + k_tiles))
    def _():
        tile = product(kv_refs, kv_bias)
        kv_out[...] = rope_tile(tile, cos_ref[...], sin_ref[...]).astype(jnp.bfloat16)

    @pl.when(step >= q_tiles + k_tiles)
    def _():
        kv_out[...] = product(kv_refs, kv_bias).astype(jnp.bfloat16)


def project(x_chunks, q_pieces, kv_pieces, q_bias, kv_bias, cos, sin):
    n_f, chunks = len(q_pieces), len(x_chunks)
    count = x_chunks[0].shape[0]
    shard, q_cols = q_pieces[0].shape
    kv_cols = kv_pieces[0].shape[1]
    wide = 256 if q_cols % 256 == 0 and (kv_cols // 2) % 256 == 0 else 128
    q_tiles, kv_tiles = q_cols // wide, kv_cols // wide

    def q_at(i):
        return (0, jnp.minimum(i, q_tiles - 1))

    def kv_at(i):
        return (0, jnp.maximum(i - q_tiles, 0))

    def whole(i):
        return (0, 0)

    return pl.pallas_call(
        functools.partial(project_kernel, n_f, chunks, q_tiles, kv_tiles // 2),
        grid=(q_tiles + kv_tiles,),
        in_specs=[pl.BlockSpec(x.shape, whole, pipeline_mode=pl.Buffered(1)) for x in x_chunks]
        + [pl.BlockSpec((shard, wide), q_at)] * n_f
        + [pl.BlockSpec((shard, wide), kv_at)] * n_f
        + [
            pl.BlockSpec((1, wide), q_at),
            pl.BlockSpec((1, wide), kv_at),
            pl.BlockSpec(cos.shape, whole, pipeline_mode=pl.Buffered(1)),
            pl.BlockSpec(sin.shape, whole, pipeline_mode=pl.Buffered(1)),
        ],
        out_specs=[pl.BlockSpec((count, wide), q_at), pl.BlockSpec((count, wide), kv_at)],
        out_shape=[
            jax.ShapeDtypeStruct((count, q_cols), jnp.bfloat16),
            jax.ShapeDtypeStruct((count, kv_cols), jnp.bfloat16),
        ],
        compiler_params=params(),
        cost_estimate=pl.CostEstimate(
            flops=2 * count * shard * n_f * (q_cols + kv_cols),
            bytes_accessed=2 * shard * n_f * (count + q_cols + kv_cols),
            transcendentals=0,
        ),
        name="project",
    )(*x_chunks, *q_pieces, *kv_pieces, q_bias[None, :], kv_bias[None, :], cos, sin)


def attend_kernel(blocks, group, s_ref, q_ref, k_ref, v_ref, out_ref, keys, values):
    length = q_ref.shape[0]
    rows = length // blocks
    factor = LOG2E / (HEAD_SIZE**0.5)

    def held(b):
        return pl.ds(pl.multiple_of(lax.rem(s_ref[0] - b + blocks, blocks) * rows, rows), rows)

    for b in range(blocks):
        keys[b * rows : (b + 1) * rows, :] = k_ref[held(b), :]
        values[b * rows : (b + 1) * rows, :] = v_ref[held(b), :]
    row = lax.broadcasted_iota(jnp.int32, (rows, rows), 0)
    column = lax.broadcasted_iota(jnp.int32, (rows, rows), 1)
    causal = row >= column
    causal = jnp.concatenate([causal.astype(jnp.float32)] * group, axis=0) > 0.5
    for b in range(blocks):
        q_block = q_ref[held(b), :]
        queries = jnp.concatenate(
            [q_block[:, h * HEAD_SIZE : (h + 1) * HEAD_SIZE] for h in range(group)], axis=0
        )
        at = b * rows
        near = lax.dot_general(
            queries, keys[at : at + rows, :], NT, preferred_element_type=jnp.float32
        )
        near = jnp.where(causal, near, jnp.float32(-1e30))
        largest = jnp.max(near, axis=-1, keepdims=True)
        if b > 0:
            far = lax.dot_general(queries, keys[:at, :], NT, preferred_element_type=jnp.float32)
            largest = jnp.maximum(largest, jnp.max(far, axis=-1, keepdims=True))
        near = jnp.exp2((near - largest) * factor)
        total = jnp.sum(near, axis=-1, keepdims=True)
        result = jnp.dot(
            near.astype(jnp.bfloat16), values[at : at + rows, :], preferred_element_type=jnp.float32
        )
        if b > 0:
            far = jnp.exp2((far - largest) * factor)
            total = total + jnp.sum(far, axis=-1, keepdims=True)
            result = result + jnp.dot(
                far.astype(jnp.bfloat16), values[:at, :], preferred_element_type=jnp.float32
            )
        result = (result / total).astype(jnp.bfloat16)
        for h in range(group):
            out_ref[held(b), h * HEAD_SIZE : (h + 1) * HEAD_SIZE] = result[
                h * rows : (h + 1) * rows, :
            ]


def attend(s, queries, kv, blocks):
    length, q_cols = queries.shape
    kv_heads = kv.shape[1] // (2 * HEAD_SIZE)
    group = q_cols // HEAD_SIZE // kv_heads
    return pl.pallas_call(
        functools.partial(attend_kernel, blocks, group),
        grid=(kv_heads,),
        in_specs=[
            pl.BlockSpec(memory_space=pltpu.SMEM),
            pl.BlockSpec((length, group * HEAD_SIZE), lambda g: (0, g)),
            pl.BlockSpec((length, HEAD_SIZE), lambda g: (0, g)),
            pl.BlockSpec((length, HEAD_SIZE), lambda g: (0, kv_heads + g)),
        ],
        out_specs=pl.BlockSpec((length, group * HEAD_SIZE), lambda g: (0, g)),
        out_shape=jax.ShapeDtypeStruct((length, q_cols), jnp.bfloat16),
        scratch_shapes=[
            pltpu.VMEM((length, HEAD_SIZE), jnp.bfloat16),
            pltpu.VMEM((length, HEAD_SIZE), jnp.bfloat16),
        ],
        compiler_params=params(),
        cost_estimate=pl.CostEstimate(
            flops=4 * length * length * q_cols,
            bytes_accessed=6 * length * q_cols,
            transcendentals=length * length * q_cols // HEAD_SIZE,
        ),
        name="attend",
    )(s[None], queries, kv, kv)


def mix_kernel(core_ref, heads_ref, mine_ref, sibling_ref, *out_refs):
    shard = mine_ref.shape[0]
    rows = out_refs[0].shape[0]

    def write(first_ref, second_ref):
        for at, w_ref in ((0, first_ref), (shard, second_ref)):
            term = lax.dot_general(
                heads_ref[...], w_ref[...], NT, preferred_element_type=jnp.float32
            ).astype(jnp.bfloat16)
            for k, out_ref in enumerate(out_refs):
                out_ref[:, at : at + shard] = term[k * rows : (k + 1) * rows, :]

    @pl.when(core_ref[0] == 0)
    def _():
        write(mine_ref, sibling_ref)

    @pl.when(core_ref[0] != 0)
    def _():
        write(sibling_ref, mine_ref)


def mix(core, heads, mine, sibling, blocks):
    length = heads.shape[0]
    shard, features = mine.shape
    vmem = pl.BlockSpec(memory_space=pltpu.VMEM)
    return pl.pallas_call(
        mix_kernel,
        in_specs=[pl.BlockSpec(memory_space=pltpu.SMEM), vmem, vmem, vmem],
        out_specs=[vmem] * blocks,
        out_shape=[jax.ShapeDtypeStruct((length // blocks, 2 * shard), jnp.bfloat16)] * blocks,
        compiler_params=params(),
        cost_estimate=pl.CostEstimate(
            flops=4 * length * shard * features,
            bytes_accessed=2 * (length * features + 2 * shard * (features + length)),
            transcendentals=0,
        ),
        name="mix",
    )(core[None], heads, mine, sibling)


def swapped(array, n_f, mask):
    return lax.ppermute(array, "fsdp", [(i, i ^ mask) for i in range(n_f)])


def chip_pieces(array, n_f, first_bit):
    chips = n_f // 2
    bits = [b for b in (1, 2, 4, 8, 16, 32) if b < chips]
    if first_bit:
        bits = bits[::-1]
    pieces = {0: array}
    for r in sorted(range(1, chips), key=lambda r: (bin(r).count("1"), r)):
        bit = next(b for b in bits if r & b)
        pieces[r] = swapped(pieces[r ^ bit], n_f, 2 * bit)
    return [pieces[r] for r in range(chips)]


def with_siblings(pieces, n_f):
    both = []
    for piece in pieces:
        both += [piece, swapped(piece, n_f, 1)]
    return both


def after(array, *others):
    return lax.optimization_barrier((array, *others))[0]


def body(
    n_f,
    n_s,
    tokens,
    norm_gain,
    q_weight,
    key_matrix,
    value_matrix,
    q_bias,
    k_bias,
    value_offset_bias,
    out_weight,
):
    me = lax.axis_index("fsdp")
    s = lax.axis_index("sp")
    core = lax.rem(me, 2)
    count = tokens.shape[0]
    ring = [(i, (i + 1) % n_s) for i in range(n_s)]

    blocks = [normed_pieces(me, tokens, norm_gain, n_f, Z_CHUNKS)]
    for _ in range(n_s - 1):
        blocks.append([lax.ppermute(x, "sp", ring) for x in blocks[-1]])

    kv_weight = jnp.concatenate([key_matrix, value_matrix], axis=1)
    q_chips = chip_pieces(q_weight, n_f, True)
    kv_chips = chip_pieces(kv_weight, n_f, False)
    o_chips = chip_pieces(after(out_weight, *q_chips[1:2], *kv_chips[1:2]), n_f, False)
    q_pieces = with_siblings(q_chips, n_f)
    kv_pieces = with_siblings(kv_chips, n_f)
    o_pieces = with_siblings(o_chips, n_f)

    order = lax.rem(s - lax.iota(jnp.int32, n_s) + n_s, n_s)
    positions = (order[:, None] * count + lax.iota(jnp.int32, count)[None, :]).reshape(-1)
    frequency = ROPE_BASE ** (-(jnp.arange(HALF, dtype=jnp.float32) * 2.0 / HEAD_SIZE))
    angle = positions.astype(jnp.float32)[:, None] * frequency[None, :]
    cos, sin = jnp.cos(angle), jnp.sin(angle)
    cos = jnp.concatenate([cos, cos], axis=1)
    sin = jnp.concatenate([-sin, sin], axis=1)

    x_chunks = [jnp.concatenate(parts, axis=0) for parts in zip(*blocks)]
    kv_bias = jnp.concatenate([k_bias, value_offset_bias])
    queries, kv = project(x_chunks, q_pieces, kv_pieces, q_bias, kv_bias, cos, sin)
    heads = attend(s, queries, kv, n_s)

    width = out_weight.shape[0] * n_f
    mixed = jnp.zeros((count, width), jnp.bfloat16)
    chips = n_f // 2
    for r in range(chips):
        terms = mix(core, heads, o_pieces[2 * r], o_pieces[2 * r + 1], n_s)
        total = terms[1 % n_s]
        for k in range(2, n_s + 1):
            arrived = lax.ppermute(total, "sp", ring).astype(jnp.float32)
            total = (arrived + terms[k % n_s].astype(jnp.float32)).astype(jnp.bfloat16)
        at = jnp.bitwise_xor(me // 2, r) * (width // chips)
        mixed = lax.dynamic_update_slice(mixed, total, (0, at))
    return mixed


def solution(mesh):
    n_f, n_s = mesh.shape["fsdp"], mesh.shape["sp"]
    placed = (
        P(("fsdp", "sp"), None),
        P(),
        P("fsdp", "sp"),
        P("fsdp", "sp"),
        P("fsdp", "sp"),
        P("sp"),
        P("sp"),
        P("sp"),
        P("fsdp", "sp"),
    )
    return jax.shard_map(
        functools.partial(body, n_f, n_s),
        mesh=mesh,
        in_specs=placed,
        out_specs=P(("fsdp", "sp"), None),
        check_vma=False,
    )
```

time: 439 us -> 280 us (0.64)
  waiting for transfers between devices: 366 us -> 196 us
  matrix products: 49.1 us -> 0 us
  Pallas kernels: 0 us -> 39.5 us
  starting transfers between devices: 0.2 us -> 26.9 us
  between operations: 13.6 us -> 0.45 us
  local copies, waits for them, and re-layouts: 3.68 us -> 10.7 us
    all_gather x5 -> x0, waiting for transfers between devices: 269 us -> none  [the longest x1 99.7 us: project_heads(): piece = lax.all_gather(normed, 'sp', axis=0, tiled=True)]
    ppermute x0 -> x39, waiting for transfers between devices: none -> 196 us  [the longest x6 79.5 us: body(): blocks.append([lax.ppermute(x, 'sp', ring) for x in blocks[-1]])]
    reduce_scatter x1 -> x0, waiting for transfers between devices: 93.9 us -> none  [body(): lax.psum_scatter(partial_value.astype(jnp.bfloat16), 'sp', scatter_dimens...]
    dot_general x5 -> x0, matrix products: 42.5 us -> none  [the longest x1 13.7 us: project_heads(): jnp.dot(piece, q_full, preferred_element_type=jnp.float32) + q_bias]
    pallas_call x0 -> x7, Pallas kernels: none -> 39.5 us  [the longest x1 18.3 us: project(): pl.pallas_call(functools.partial(project_kernel, n_f, chunks, q_tiles, kv...]
    ppermute x0 -> x39, starting transfers between devices: none -> 26.9 us  [the longest x21 12.1 us: swapped(): return lax.ppermute(array, 'fsdp', [(i, i ^ mask) for i in range(n_f)])]
    unnamed x12 -> x63, local copies, waits for them, and re-layouts: 1.24 us -> 10.5 us
    sub x1 -> x0, matrix products: 6.56 us -> none  [attend(): weights = jnp.exp(scores - largest)]
  transfers between devices with their start and end apart: 6 -> 39, of which waited for: 6 -> 18; matrix products, arithmetic and copies ran while one was open for 10% -> 2% of each run, Pallas kernels for 0% -> 14%
where the time goes in v1:
time: 280 us
  waiting for transfers between devices  196 us (70%)
  Pallas kernels  39.5 us (14%)
  starting transfers between devices  26.9 us (10%)
  local copies, waits for them, and re-layouts  10.7 us (4%)
  other arithmetic  6.31 us (2%)
    ppermute x6, waiting for transfers between devices, body(): blocks.append([lax.ppermute(x, 'sp', ring) for x in blocks[-1]])  79.5 us
    ppermute x12, waiting for transfers between devices, body(): arrived = lax.ppermute(total, 'sp', ring).astype(jnp.float32)  73.5 us
    ppermute x21, waiting for transfers between devices, swapped(): return lax.ppermute(array, 'fsdp', [(i, i ^ mask) for i in range(n_f)])  42.9 us
    pallas_call x1, Pallas kernels, project(): pl.pallas_call(functools.partial(project_kernel, n_f, chunks, q_tiles, kv...  18.3 us
    pallas_call x4, Pallas kernels, mix(): pl.pallas_call(mix_kernel, in_specs=[pl.BlockSpec(memory_space=pltpu.SMEM...  16.8 us
    ppermute x21, starting transfers between devices, swapped(): return lax.ppermute(array, 'fsdp', [(i, i ^ mask) for i in range(n_f)])  12.1 us
    unnamed x63, local copies, waits for them, and re-layouts  10.5 us
    ppermute x6, starting transfers between devices, body(): blocks.append([lax.ppermute(x, 'sp', ring) for x in blocks[-1]])  8.17 us
  transfers between devices with their start and end apart: 39, of which 18 were waited for; matrix products, arithmetic and copies ran while one was open for 2% of the time, Pallas kernels for 14%

profile of v1, /device:TPU:0, one launch (start us, length us, event | category | flops | bytes accessed | tf_op | source)
XLA Modules:
  0.0 279.8 jit_solution(15558163309893772418)
XLA Ops:
  2.8 3.1 %collective-permute-start.3 = (bf16[128,2560]{1,0:T(8,128)(2,1)S(1)}, bf16[128,2560]{1,0:T(8,128)(2,1)S(1)}, u32[]{:S(2)}, u32[]{:S(2)}) collective-permute-start(bf16[128,2560]{1,0:T(8,128)(2,1)S(1)} %get-tuple-element.27), channel_id=1, source_target_pairs={{0,1},{1,2},{2,3},{3,0},{4,5},{5,6},{6,7},{7,4},{8,9},{9,10},{10,1... | collective-permute-start | bytes 1966088 | tf_op jit(solution)/shard_map/ppermute | solution.py:317
  5.9 1.6 collective-permute-start
  8.5 1.6 collective-permute-start.16
  12.1 11.4 %collective-permute-done.3 = bf16[128,2560]{1,0:T(8,128)(2,1)S(1)} collective-permute-done((bf16[128,2560]{1,0:T(8,128)(2,1)S(1)}, bf16[128,2560]{1,0:T(8,128)(2,1)S(1)}, u32[]{:S(2)}, u32[]{:S(2)}) %collective-permute-start.3) | collective-permute-done | bytes 655392 | tf_op jit(solution)/shard_map/ppermute | solution.py:317
  23.5 13.2 %collective-permute-done = bf16[128,2560]{1,0:T(8,128)(2,1)S(1)} collective-permute-done((bf16[128,2560]{1,0:T(8,128)(2,1)S(1)}, bf16[128,2560]{1,0:T(8,128)(2,1)S(1)}, u32[]{:S(2)}, u32[]{:S(2)}) %collective-permute-start) | collective-permute-done | bytes 655392 | tf_op jit(solution)/shard_map/ppermute | solution.py:317
  38.0 1.5 collective-permute-start.9
  39.5 16.6 %collective-permute-done.4 = bf16[128,2560]{1,0:T(8,128)(2,1)S(1)} collective-permute-done((bf16[128,2560]{1,0:T(8,128)(2,1)S(1)}, bf16[128,2560]{1,0:T(8,128)(2,1)S(1)}, u32[]{:S(2)}, u32[]{:S(2)}) %collective-permute-start.4) | collective-permute-done | bytes 655392 | tf_op jit(solution)/shard_map/ppermute | solution.py:317
  57.7 10.8 %collective-permute-done.1 = bf16[128,2560]{1,0:T(8,128)(2,1)S(1)} collective-permute-done((bf16[128,2560]{1,0:T(8,128)(2,1)S(1)}, bf16[128,2560]{1,0:T(8,128)(2,1)S(1)}, u32[]{:S(2)}, u32[]{:S(2)}) %collective-permute-start.1) | collective-permute-done | bytes 655392 | tf_op jit(solution)/shard_map/ppermute | solution.py:317
  68.5 6.4 %collective-permute-done.18.refs_16_ = bf16[640,512]{1,0:T(8,128)(2,1)S(1)} collective-permute-done((bf16[640,512]{1,0:T(8,128)(2,1)S(1)}, bf16[640,512]{1,0:T(8,128)(2,1)S(1)}, u32[]{:S(2)}, u32[]{:S(2)}) %collective-permute-start.18) | collective-permute-done | bytes 655392 | tf_op jit(solution)/shard_map/ppermute | solution.py:270
  76.3 1.6 collective-permute-start.5
  79.9 15.8 %collective-permute-done.5 = bf16[128,2560]{1,0:T(8,128)(2,1)S(1)} collective-permute-done((bf16[128,2560]{1,0:T(8,128)(2,1)S(1)}, bf16[128,2560]{1,0:T(8,128)(2,1)S(1)}, u32[]{:S(2)}, u32[]{:S(2)}) %collective-permute-start.5) | collective-permute-done | bytes 655392 | tf_op jit(solution)/shard_map/ppermute | solution.py:317
  97.2 11.8 %collective-permute-done.2 = bf16[128,2560]{1,0:T(8,128)(2,1)S(1)} collective-permute-done((bf16[128,2560]{1,0:T(8,128)(2,1)S(1)}, bf16[128,2560]{1,0:T(8,128)(2,1)S(1)}, u32[]{:S(2)}, u32[]{:S(2)}) %collective-permute-start.2) | collective-permute-done | bytes 655392 | tf_op jit(solution)/shard_map/ppermute | solution.py:317
  110.7 3.1 %collective-permute-done.11.refs_8_ = bf16[640,1280]{1,0:T(8,128)(2,1)} collective-permute-done((bf16[640,1280]{1,0:T(8,128)(2,1)}, bf16[640,1280]{1,0:T(8,128)(2,1)}, u32[]{:S(2)}, u32[]{:S(2)}) %collective-permute-start.11) | collective-permute-done | bytes 1638432 | tf_op jit(solution)/shard_map/ppermute | solution.py:270
  115.2 33.3 %collective-permute-done.29.mine_ref = bf16[640,1280]{1,0:T(8,128)(2,1)} collective-permute-done((bf16[640,1280]{1,0:T(8,128)(2,1)}, bf16[640,1280]{1,0:T(8,128)(2,1)}, u32[]{:S(2)}, u32[]{:S(2)}) %collective-permute-start.29) | collective-permute-done | bytes 1638432 | tf_op jit(solution)/shard_map/ppermute | solution.py:270
  149.0 1.6 pad_maximum_fusion.1.refs_1_
  150.7 1.5 collective-permute-start.34
  152.2 1.6 pad_maximum_fusion.refs_0_
  155.1 18.3 %project.1 = (bf16[512,1280]{1,0:T(8,128)(2,1)}, bf16[512,512]{1,0:T(8,128)(2,1)S(1)}) custom-call(bf16[512,2560]{1,0:T(8,128)(2,1)} %pad_maximum_fusion.refs_0_, bf16[512,2560]{1,0:T(8,128)(2,1)} %pad_maximum_fusion.1.refs_1_, bf16[640,1280]{1,0:T(8,128)(2,1)} %refs_2_.1, bf16[640,1280]{1,0:T(8,128)(2,1)} %copy-done.23, ...), custom_call_target="tpu_custom_call" | custom-call | flops 9395240960 | bytes 23592960 | tf_op jit(solution)/shard_map/project/pallas_call | solution.py:126
  174.7 3.7 %attend.1.heads_ref = bf16[512,1280]{1,0:T(8,128)(2,1)S(1)} custom-call(s32[1]{0:T(128)} %bitcast.1.s_ref, bf16[512,1280]{1,0:T(8,128)(2,1)S(1)} %copy-done.4, bf16[512,512]{1,0:T(8,128)(2,1)S(1)} %get-tuple-element.29.k_ref.v_ref, bf16[512,512]{1,0:T(8,128)(2,1)S(1)} %get-tuple-element.29.k_ref.v_ref), custom_call_target="tpu_custom_call" | custom-call | flops 1342177280 | bytes 3932160 | tf_op jit(solution)/shard_map/attend/pallas_call | solution.py:204
  179.6 4.3 %mix.6 = (bf16[128,1280]{1,0:T(8,128)(2,1)S(1)}, bf16[128,1280]{1,0:T(8,128)(2,1)S(1)}, bf16[128,1280]{1,0:T(8,128)(2,1)S(1)}, bf16[128,1280]{1,0:T(8,128)(2,1)S(1)}) custom-call(s32[1]{0:T(128)} %bitcast.core_ref, bf16[512,1280]{1,0:T(8,128)(2,1)S(1)} %attend.1.heads_ref, bf16[640,1280]{1,0:T(8,128)(2,1)} %collective-permute-done.29.mine_ref, ...), custom_call_target="tpu_custom_call" | custom-call | flops 1677721600 | bytes 5898240 | tf_op jit(solution)/shard_map/mix/pallas_call | solution.py:254
  183.9 1.6 collective-permute-start.31
  185.6 4.2 %mix.5 = (bf16[128,1280]{1,0:T(8,128)(2,1)S(1)}, bf16[128,1280]{1,0:T(8,128)(2,1)S(1)}, bf16[128,1280]{1,0:T(8,128)(2,1)S(1)}, bf16[128,1280]{1,0:T(8,128)(2,1)S(1)}) custom-call(s32[1]{0:T(128)} %bitcast.core_ref, bf16[512,1280]{1,0:T(8,128)(2,1)S(1)} %attend.1.heads_ref, bf16[640,1280]{1,0:T(8,128)(2,1)} %collective-permute-done.24.mine_ref, ...), custom_call_target="tpu_custom_call" | custom-call | flops 1677721600 | bytes 5898240 | tf_op jit(solution)/shard_map/mix/pallas_call | solution.py:254
  190.1 4.2 %mix.4 = (bf16[128,1280]{1,0:T(8,128)(2,1)S(1)}, bf16[128,1280]{1,0:T(8,128)(2,1)S(1)}, bf16[128,1280]{1,0:T(8,128)(2,1)S(1)}, bf16[128,1280]{1,0:T(8,128)(2,1)S(1)}) custom-call(s32[1]{0:T(128)} %bitcast.core_ref, bf16[512,1280]{1,0:T(8,128)(2,1)S(1)} %attend.1.heads_ref, bf16[640,1280]{1,0:T(8,128)(2,1)} %mine_ref, ...), custom_call_target="tpu_custom_call" | custom-call | flops 1677721600 | bytes 5898240 | tf_op jit(solution)/shard_map/mix/pallas_call | solution.py:254
  197.5 5.9 %collective-permute-done.26 = bf16[128,1280]{1,0:T(8,128)(2,1)S(1)} collective-permute-done((bf16[128,1280]{1,0:T(8,128)(2,1)S(1)}, bf16[128,1280]{1,0:T(8,128)(2,1)S(1)}, u32[]{:S(2)}, u32[]{:S(2)}) %collective-permute-start.26) | collective-permute-done | bytes 327712 | tf_op jit(solution)/shard_map/ppermute | solution.py:347
  203.6 6.9 %collective-permute-done.21 = bf16[128,1280]{1,0:T(8,128)(2,1)S(1)} collective-permute-done((bf16[128,1280]{1,0:T(8,128)(2,1)S(1)}, bf16[128,1280]{1,0:T(8,128)(2,1)S(1)}, u32[]{:S(2)}, u32[]{:S(2)}) %collective-permute-start.21) | collective-permute-done | bytes 327712 | tf_op jit(solution)/shard_map/ppermute | solution.py:347
  210.6 6.9 %collective-permute-done.32 = bf16[128,1280]{1,0:T(8,128)(2,1)S(1)} collective-permute-done((bf16[128,1280]{1,0:T(8,128)(2,1)S(1)}, bf16[128,1280]{1,0:T(8,128)(2,1)S(1)}, u32[]{:S(2)}, u32[]{:S(2)}) %collective-permute-start.32) | collective-permute-done | bytes 327712 | tf_op jit(solution)/shard_map/ppermute | solution.py:347
  217.6 13.9 %collective-permute-done.22 = bf16[128,1280]{1,0:T(8,128)(2,1)S(1)} collective-permute-done((bf16[128,1280]{1,0:T(8,128)(2,1)S(1)}, bf16[128,1280]{1,0:T(8,128)(2,1)S(1)}, u32[]{:S(2)}, u32[]{:S(2)}) %collective-permute-start.22) | collective-permute-done | bytes 327712 | tf_op jit(solution)/shard_map/ppermute | solution.py:347
  233.1 4.2 %mix.7 = (bf16[128,1280]{1,0:T(8,128)(2,1)S(1)}, bf16[128,1280]{1,0:T(8,128)(2,1)S(1)}, bf16[128,1280]{1,0:T(8,128)(2,1)S(1)}, bf16[128,1280]{1,0:T(8,128)(2,1)S(1)}) custom-call(s32[1]{0:T(128)} %bitcast.core_ref, bf16[512,1280]{1,0:T(8,128)(2,1)S(1)} %attend.1.heads_ref, bf16[640,1280]{1,0:T(8,128)(2,1)} %collective-permute-done.34.mine_ref, ...), custom_call_target="tpu_custom_call" | custom-call | flops 1677721600 | bytes 5898240 | tf_op jit(solution)/shard_map/mix/pallas_call | solution.py:254
  238.8 6.8 %collective-permute-done.23 = bf16[128,1280]{1,0:T(8,128)(2,1)S(1)} collective-permute-done((bf16[128,1280]{1,0:T(8,128)(2,1)S(1)}, bf16[128,1280]{1,0:T(8,128)(2,1)S(1)}, u32[]{:S(2)}, u32[]{:S(2)}) %collective-permute-start.23) | collective-permute-done | bytes 327712 | tf_op jit(solution)/shard_map/ppermute | solution.py:347
  245.8 12.8 %collective-permute-done.36 = bf16[128,1280]{1,0:T(8,128)(2,1)S(1)} collective-permute-done((bf16[128,1280]{1,0:T(8,128)(2,1)S(1)}, bf16[128,1280]{1,0:T(8,128)(2,1)S(1)}, u32[]{:S(2)}, u32[]{:S(2)}) %collective-permute-start.36) | collective-permute-done | bytes 327712 | tf_op jit(solution)/shard_map/ppermute | solution.py:347
  258.9 10.4 %collective-permute-done.37 = bf16[128,1280]{1,0:T(8,128)(2,1)S(1)} collective-permute-done((bf16[128,1280]{1,0:T(8,128)(2,1)S(1)}, bf16[128,1280]{1,0:T(8,128)(2,1)S(1)}, u32[]{:S(2)}, u32[]{:S(2)}) %collective-permute-start.37) | collective-permute-done | bytes 327712 | tf_op jit(solution)/shard_map/ppermute | solution.py:347
  269.5 9.5 %collective-permute-done.38 = bf16[128,1280]{1,0:T(8,128)(2,1)S(1)} collective-permute-done((bf16[128,1280]{1,0:T(8,128)(2,1)S(1)}, bf16[128,1280]{1,0:T(8,128)(2,1)S(1)}, u32[]{:S(2)}, u32[]{:S(2)}) %collective-permute-start.38) | collective-permute-done | bytes 327712 | tf_op jit(solution)/shard_map/ppermute | solution.py:347
  (139 shorter events, 29.5 us)
Async XLA Ops:
  2.8 20.7 %collective-permute-start.3 = (bf16[128,2560]{1,0:T(8,128)(2,1)S(1)}, bf16[128,2560]{1,0:T(8,128)(2,1)S(1)}, u32[]{:S(2)}, u32[]{:S(2)}) collective-permute-start(bf16[128,2560]{1,0:T(8,128)(2,1)S(1)} %get-tuple-element.27), channel_id=1, source_target_pairs={{0,1},{1,2},{2,3},{3,0},{4,5},{5,6},{6,7},{7,4},{8,9},{9,10},{10,1... | collective-permute-start | bytes 1966088 | tf_op jit(solution)/shard_map/ppermute | solution.py:317
  5.9 30.8 %collective-permute-start = (bf16[128,2560]{1,0:T(8,128)(2,1)S(1)}, bf16[128,2560]{1,0:T(8,128)(2,1)S(1)}, u32[]{:S(2)}, u32[]{:S(2)}) collective-permute-start(bf16[128,2560]{1,0:T(8,128)(2,1)S(1)} %get-tuple-element.26), channel_id=1, source_target_pairs={{0,1},{1,2},{2,3},{3,0},{4,5},{5,6},{6,7},{7,4},{8,9},{9,10},{10,1... | collective-permute-start | bytes 1966088 | tf_op jit(solution)/shard_map/ppermute | solution.py:317
  8.5 28.2 %collective-permute-start.16 = (bf16[640,512]{1,0:T(8,128)(2,1)S(1)}, bf16[640,512]{1,0:T(8,128)(2,1)S(1)}, u32[]{:S(2)}, u32[]{:S(2)}) collective-permute-start(bf16[640,512]{1,0:T(8,128)(2,1)S(1)} %constant_dynamic-update-slice_fusion.refs_10_), channel_id=1, source_target_pairs={{0,16},{4,20},{8,24},{12,28},{16,0},{20,4},{24,8},{28,12},{1,17},{... | collective-permute-start | bytes 1966088 | tf_op jit(solution)/shard_map/ppermute | solution.py:270
  10.1 27.9 %collective-permute-start.14 = (bf16[640,512]{1,0:T(8,128)(2,1)S(1)}, bf16[640,512]{1,0:T(8,128)(2,1)S(1)}, u32[]{:S(2)}, u32[]{:S(2)}) collective-permute-start(bf16[640,512]{1,0:T(8,128)(2,1)S(1)} %constant_dynamic-update-slice_fusion.refs_10_), channel_id=1, source_target_pairs={{0,8},{4,12},{8,0},{12,4},{16,24},{20,28},{24,16},{28,20},{1,9},{5... | collective-permute-start | bytes 1966088 | tf_op jit(solution)/shard_map/ppermute | solution.py:270
  11.6 63.3 %collective-permute-start.7 = (bf16[640,1280]{1,0:T(8,128)(2,1)S(1)}, bf16[640,1280]{1,0:T(8,128)(2,1)}, u32[]{:S(2)}, u32[]{:S(2)}) collective-permute-start(bf16[640,1280]{1,0:T(8,128)(2,1)S(1)} %copy-done.22), channel_id=1, source_target_pairs={{0,8},{4,12},{8,0},{12,4},{16,24},{20,28},{24,16},{28,20},{1,9},{5... | collective-permute-start | bytes 4915208 | tf_op jit(solution)/shard_map/ppermute | solution.py:270
  23.5 16.1 %collective-permute-start.13 = (bf16[640,512]{1,0:T(8,128)(2,1)S(1)}, bf16[640,512]{1,0:T(8,128)(2,1)S(1)}, u32[]{:S(2)}, u32[]{:S(2)}) collective-permute-start(bf16[640,512]{1,0:T(8,128)(2,1)S(1)} %constant_dynamic-update-slice_fusion.refs_10_), channel_id=1, source_target_pairs={{0,4},{4,0},{8,12},{12,8},{16,20},{20,16},{24,28},{28,24},{1,5},{5... | collective-permute-start | bytes 1966088 | tf_op jit(solution)/shard_map/ppermute | solution.py:270
  36.7 19.5 %collective-permute-start.4 = (bf16[128,2560]{1,0:T(8,128)(2,1)S(1)}, bf16[128,2560]{1,0:T(8,128)(2,1)S(1)}, u32[]{:S(2)}, u32[]{:S(2)}) collective-permute-start(bf16[128,2560]{1,0:T(8,128)(2,1)S(1)} %collective-permute-done.3), channel_id=1, source_target_pairs={{0,1},{1,2},{2,3},{3,0},{4,5},{5,6},{6,7},{7,4},{8,9},{9,10},{10,1... | collective-permute-start | bytes 1966088 | tf_op jit(solution)/shard_map/ppermute | solution.py:317
  36.7 31.7 %collective-permute-start.1 = (bf16[128,2560]{1,0:T(8,128)(2,1)S(1)}, bf16[128,2560]{1,0:T(8,128)(2,1)S(1)}, u32[]{:S(2)}, u32[]{:S(2)}) collective-permute-start(bf16[128,2560]{1,0:T(8,128)(2,1)S(1)} %collective-permute-done), channel_id=1, source_target_pairs={{0,1},{1,2},{2,3},{3,0},{4,5},{5,6},{6,7},{7,4},{8,9},{9,10},{10,1... | collective-permute-start | bytes 1966088 | tf_op jit(solution)/shard_map/ppermute | solution.py:317
  38.0 40.6 %collective-permute-start.9 = (bf16[640,1280]{1,0:T(8,128)(2,1)S(1)}, bf16[640,1280]{1,0:T(8,128)(2,1)}, u32[]{:S(2)}, u32[]{:S(2)}) collective-permute-start(bf16[640,1280]{1,0:T(8,128)(2,1)S(1)} %copy-done.22), channel_id=1, source_target_pairs={{0,16},{4,20},{8,24},{12,28},{16,0},{20,4},{24,8},{28,12},{1,17},{... | collective-permute-start | bytes 4915208 | tf_op jit(solution)/shard_map/ppermute | solution.py:270
  39.5 39.0 %collective-permute-start.6 = (bf16[640,1280]{1,0:T(8,128)(2,1)S(1)}, bf16[640,1280]{1,0:T(8,128)(2,1)S(1)}, u32[]{:S(2)}, u32[]{:S(2)}) collective-permute-start(bf16[640,1280]{1,0:T(8,128)(2,1)S(1)} %copy-done.22), channel_id=1, source_target_pairs={{0,4},{4,0},{8,12},{12,8},{16,20},{20,16},{24,28},{28,24},{1,5},{5... | collective-permute-start | bytes 4915208 | tf_op jit(solution)/shard_map/ppermute | solution.py:270
  56.2 18.7 %collective-permute-start.18 = (bf16[640,512]{1,0:T(8,128)(2,1)S(1)}, bf16[640,512]{1,0:T(8,128)(2,1)S(1)}, u32[]{:S(2)}, u32[]{:S(2)}) collective-permute-start(bf16[640,512]{1,0:T(8,128)(2,1)S(1)} %collective-permute-done.16.refs_14_), channel_id=1, source_target_pairs={{0,8},{4,12},{8,0},{12,4},{16,24},{20,28},{24,16},{28,20},{1,9},{5... | collective-permute-start | bytes 1966088 | tf_op jit(solution)/shard_map/ppermute | solution.py:270
  74.9 39.0 %collective-permute-start.11 = (bf16[640,1280]{1,0:T(8,128)(2,1)}, bf16[640,1280]{1,0:T(8,128)(2,1)}, u32[]{:S(2)}, u32[]{:S(2)}) collective-permute-start(bf16[640,1280]{1,0:T(8,128)(2,1)} %collective-permute-done.7.refs_4_), channel_id=1, source_target_pairs={{0,16},{4,20},{8,24},{12,28},{16,0},{20,4},{24,8},{28,12},{1,17},{... | collective-permute-start | bytes 4915208 | tf_op jit(solution)/shard_map/ppermute | solution.py:270
  76.3 19.4 %collective-permute-start.5 = (bf16[128,2560]{1,0:T(8,128)(2,1)S(1)}, bf16[128,2560]{1,0:T(8,128)(2,1)S(1)}, u32[]{:S(2)}, u32[]{:S(2)}) collective-permute-start(bf16[128,2560]{1,0:T(8,128)(2,1)S(1)} %collective-permute-done.4), channel_id=1, source_target_pairs={{0,1},{1,2},{2,3},{3,0},{4,5},{5,6},{6,7},{7,4},{8,9},{9,10},{10,1... | collective-permute-start | bytes 1966088 | tf_op jit(solution)/shard_map/ppermute | solution.py:317
  77.9 31.0 %collective-permute-start.2 = (bf16[128,2560]{1,0:T(8,128)(2,1)S(1)}, bf16[128,2560]{1,0:T(8,128)(2,1)S(1)}, u32[]{:S(2)}, u32[]{:S(2)}) collective-permute-start(bf16[128,2560]{1,0:T(8,128)(2,1)S(1)} %collective-permute-done.1), channel_id=1, source_target_pairs={{0,1},{1,2},{2,3},{3,0},{4,5},{5,6},{6,7},{7,4},{8,9},{9,10},{10,1... | collective-permute-start | bytes 1966088 | tf_op jit(solution)/shard_map/ppermute | solution.py:317
  78.6 31.2 %collective-permute-start.19 = (bf16[640,512]{1,0:T(8,128)(2,1)S(1)}, bf16[640,512]{1,0:T(8,128)(2,1)S(1)}, u32[]{:S(2)}, u32[]{:S(2)}) collective-permute-start(bf16[640,512]{1,0:T(8,128)(2,1)S(1)} %collective-permute-done.18.refs_16_), channel_id=1, source_target_pairs={{0,4},{4,0},{8,12},{12,8},{16,20},{20,16},{24,28},{28,24},{1,5},{5... | collective-permute-start | bytes 1966088 | tf_op jit(solution)/shard_map/ppermute | solution.py:270
  78.6 69.9 %collective-permute-start.29 = (bf16[640,1280]{1,0:T(8,128)(2,1)}, bf16[640,1280]{1,0:T(8,128)(2,1)}, u32[]{:S(2)}, u32[]{:S(2)}) collective-permute-start(bf16[640,1280]{1,0:T(8,128)(2,1)} %mine_ref), channel_id=1, source_target_pairs={{0,16},{4,20},{8,24},{12,28},{16,0},{20,4},{24,8},{28,12},{1,17},{... | collective-permute-start | bytes 4915208 | tf_op jit(solution)/shard_map/ppermute | solution.py:270
  95.7 52.8 %collective-permute-start.24 = (bf16[640,1280]{1,0:T(8,128)(2,1)}, bf16[640,1280]{1,0:T(8,128)(2,1)}, u32[]{:S(2)}, u32[]{:S(2)}) collective-permute-start(bf16[640,1280]{1,0:T(8,128)(2,1)} %mine_ref), channel_id=1, source_target_pairs={{0,8},{4,12},{8,0},{12,4},{16,24},{20,28},{24,16},{28,20},{1,9},{5... | collective-permute-start | bytes 4915208 | tf_op jit(solution)/shard_map/ppermute | solution.py:270
  109.0 41.7 %collective-permute-start.8 = (bf16[640,1280]{1,0:T(8,128)(2,1)}, bf16[640,1280]{1,0:T(8,128)(2,1)}, u32[]{:S(2)}, u32[]{:S(2)}) collective-permute-start(bf16[640,1280]{1,0:T(8,128)(2,1)} %collective-permute-done.7.refs_4_), channel_id=1, source_target_pairs={{0,4},{4,0},{8,12},{12,8},{16,20},{20,16},{24,28},{28,24},{1,5},{5... | collective-permute-start | bytes 4915208 | tf_op jit(solution)/shard_map/ppermute | solution.py:270
  110.7 40.0 %collective-permute-start.10 = (bf16[640,1280]{1,0:T(8,128)(2,1)}, bf16[640,1280]{1,0:T(8,128)(2,1)}, u32[]{:S(2)}, u32[]{:S(2)}) collective-permute-start(bf16[640,1280]{1,0:T(8,128)(2,1)} %collective-permute-done.9.refs_6_), channel_id=1, source_target_pairs={{0,4},{4,0},{8,12},{12,8},{16,20},{20,16},{24,28},{28,24},{1,5},{5... | collective-permute-start | bytes 4915208 | tf_op jit(solution)/shard_map/ppermute | solution.py:270
  113.9 40.0 %collective-permute-start.12 = (bf16[640,1280]{1,0:T(8,128)(2,1)}, bf16[640,1280]{1,0:T(8,128)(2,1)S(1)}, u32[]{:S(2)}, u32[]{:S(2)}) collective-permute-start(bf16[640,1280]{1,0:T(8,128)(2,1)} %collective-permute-done.11.refs_8_), channel_id=1, source_target_pairs={{0,4},{4,0},{8,12},{12,8},{16,20},{20,16},{24,28},{28,24},{1,5},{5... | collective-permute-start | bytes 4915208 | tf_op jit(solution)/shard_map/ppermute | solution.py:270
  148.5 29.9 %collective-permute-start.30 = (bf16[640,1280]{1,0:T(8,128)(2,1)}, bf16[640,1280]{1,0:T(8,128)(2,1)S(1)}, u32[]{:S(2)}, u32[]{:S(2)}) collective-permute-start(bf16[640,1280]{1,0:T(8,128)(2,1)} %collective-permute-done.29.mine_ref), channel_id=1, source_target_pairs={{0,4},{4,0},{8,12},{12,8},{16,20},{20,16},{24,28},{28,24},{1,5},{5... | collective-permute-start | bytes 4915208 | tf_op jit(solution)/shard_map/ppermute | solution.py:270
  148.5 37.0 %collective-permute-start.25 = (bf16[640,1280]{1,0:T(8,128)(2,1)}, bf16[640,1280]{1,0:T(8,128)(2,1)}, u32[]{:S(2)}, u32[]{:S(2)}) collective-permute-start(bf16[640,1280]{1,0:T(8,128)(2,1)} %collective-permute-done.24.mine_ref), channel_id=1, source_target_pairs={{0,4},{4,0},{8,12},{12,8},{16,20},{20,16},{24,28},{28,24},{1,5},{5... | collective-permute-start | bytes 4915208 | tf_op jit(solution)/shard_map/ppermute | solution.py:270
  150.6 39.5 %collective-permute-start.20 = (bf16[640,1280]{1,0:T(8,128)(2,1)}, bf16[640,1280]{1,0:T(8,128)(2,1)}, u32[]{:S(2)}, u32[]{:S(2)}) collective-permute-start(bf16[640,1280]{1,0:T(8,128)(2,1)} %mine_ref), channel_id=1, source_target_pairs={{0,4},{4,0},{8,12},{12,8},{16,20},{20,16},{24,28},{28,24},{1,5},{5... | collective-permute-start | bytes 4915208 | tf_op jit(solution)/shard_map/ppermute | solution.py:270
  150.7 45.1 %collective-permute-start.34 = (bf16[640,1280]{1,0:T(8,128)(2,1)}, bf16[640,1280]{1,0:T(8,128)(2,1)}, u32[]{:S(2)}, u32[]{:S(2)}) collective-permute-start(bf16[640,1280]{1,0:T(8,128)(2,1)} %collective-permute-done.29.mine_ref), channel_id=1, source_target_pairs={{0,8},{4,12},{8,0},{12,4},{16,24},{20,28},{24,16},{28,20},{1,9},{5... | collective-permute-start | bytes 4915208 | tf_op jit(solution)/shard_map/ppermute | solution.py:270
  194.3 16.1 %collective-permute-start.21 = (bf16[128,1280]{1,0:T(8,128)(2,1)S(1)}, bf16[128,1280]{1,0:T(8,128)(2,1)S(1)}, u32[]{:S(2)}, u32[]{:S(2)}) collective-permute-start(bf16[128,1280]{1,0:T(8,128)(2,1)S(1)} %get-tuple-element.31), channel_id=1, source_target_pairs={{0,1},{1,2},{2,3},{3,0},{4,5},{5,6},{6,7},{7,4},{8,9},{9,10},{10,1... | collective-permute-start | bytes 983048 | tf_op jit(solution)/shard_map/ppermute | solution.py:347
  195.8 36.1 %collective-permute-start.35 = (bf16[640,1280]{1,0:T(8,128)(2,1)}, bf16[640,1280]{1,0:T(8,128)(2,1)S(1)}, u32[]{:S(2)}, u32[]{:S(2)}) collective-permute-start(bf16[640,1280]{1,0:T(8,128)(2,1)} %collective-permute-done.34.mine_ref), channel_id=1, source_target_pairs={{0,4},{4,0},{8,12},{12,8},{16,20},{20,16},{24,28},{28,24},{1,5},{5... | collective-permute-start | bytes 4915208 | tf_op jit(solution)/shard_map/ppermute | solution.py:270
  196.4 21.0 %collective-permute-start.32 = (bf16[128,1280]{1,0:T(8,128)(2,1)S(1)}, bf16[128,1280]{1,0:T(8,128)(2,1)S(1)}, u32[]{:S(2)}, u32[]{:S(2)}) collective-permute-start(bf16[128,1280]{1,0:T(8,128)(2,1)S(1)} %add_convert_fusion.5), channel_id=1, source_target_pairs={{0,1},{1,2},{2,3},{3,0},{4,5},{5,6},{6,7},{7,4},{8,9},{9,10},{10,1... | collective-permute-start | bytes 983048 | tf_op jit(solution)/shard_map/ppermute | solution.py:347
  203.5 28.2 %collective-permute-start.27 = (bf16[128,1280]{1,0:T(8,128)(2,1)S(1)}, bf16[128,1280]{1,0:T(8,128)(2,1)S(1)}, u32[]{:S(2)}, u32[]{:S(2)}) collective-permute-start(bf16[128,1280]{1,0:T(8,128)(2,1)S(1)} %add_convert_fusion.8), channel_id=1, source_target_pairs={{0,1},{1,2},{2,3},{3,0},{4,5},{5,6},{6,7},{7,4},{8,9},{9,10},{10,1... | collective-permute-start | bytes 983048 | tf_op jit(solution)/shard_map/ppermute | solution.py:347
  210.5 21.0 %collective-permute-start.22 = (bf16[128,1280]{1,0:T(8,128)(2,1)S(1)}, bf16[128,1280]{1,0:T(8,128)(2,1)S(1)}, u32[]{:S(2)}, u32[]{:S(2)}) collective-permute-start(bf16[128,1280]{1,0:T(8,128)(2,1)S(1)} %add_convert_fusion.11), channel_id=1, source_target_pairs={{0,1},{1,2},{2,3},{3,0},{4,5},{5,6},{6,7},{7,4},{8,9},{9,10},{10,1... | collective-permute-start | bytes 983048 | tf_op jit(solution)/shard_map/ppermute | solution.py:347
  217.5 51.9 %collective-permute-start.33 = (bf16[128,1280]{1,0:T(8,128)(2,1)S(1)}, bf16[128,1280]{1,0:T(8,128)(2,1)S(1)}, u32[]{:S(2)}, u32[]{:S(2)}) collective-permute-start(bf16[128,1280]{1,0:T(8,128)(2,1)S(1)} %add_convert_fusion.4), channel_id=1, source_target_pairs={{0,1},{1,2},{2,3},{3,0},{4,5},{5,6},{6,7},{7,4},{8,9},{9,10},{10,1... | collective-permute-start | bytes 983048 | tf_op jit(solution)/shard_map/ppermute | solution.py:347
  231.8 27.0 %collective-permute-start.28 = (bf16[128,1280]{1,0:T(8,128)(2,1)S(1)}, bf16[128,1280]{1,0:T(8,128)(2,1)S(1)}, u32[]{:S(2)}, u32[]{:S(2)}) collective-permute-start(bf16[128,1280]{1,0:T(8,128)(2,1)S(1)} %add_convert_fusion.7), channel_id=1, source_target_pairs={{0,1},{1,2},{2,3},{3,0},{4,5},{5,6},{6,7},{7,4},{8,9},{9,10},{10,1... | collective-permute-start | bytes 983048 | tf_op jit(solution)/shard_map/ppermute | solution.py:347
  237.2 21.3 %collective-permute-start.36 = (bf16[128,1280]{1,0:T(8,128)(2,1)S(1)}, bf16[128,1280]{1,0:T(8,128)(2,1)S(1)}, u32[]{:S(2)}, u32[]{:S(2)}) collective-permute-start(bf16[128,1280]{1,0:T(8,128)(2,1)S(1)} %get-tuple-element.43), channel_id=1, source_target_pairs={{0,1},{1,2},{2,3},{3,0},{4,5},{5,6},{6,7},{7,4},{8,9},{9,10},{10,1... | collective-permute-start | bytes 983048 | tf_op jit(solution)/shard_map/ppermute | solution.py:347
  (38 other events, 1014.9 us)

commit v2 on v1

--- a/solution.py
+++ b/solution.py
@@ -70,84 +70,88 @@
     return parts[0] if len(parts) == 1 else jnp.concatenate(parts, axis=1)
 
 
-def project_kernel(n_f, chunks, q_tiles, k_tiles, *refs):
-    x_refs = refs[:chunks]
-    q_refs = refs[chunks : chunks + n_f]
-    kv_refs = refs[chunks + n_f : chunks + 2 * n_f]
-    q_bias, kv_bias, cos_ref, sin_ref, q_out, kv_out = refs[chunks + 2 * n_f :]
-    shard = q_refs[0].shape[0]
-    per_chunk = n_f // chunks
-    step = pl.program_id(0)
-
-    def product(w_refs, bias):
-        total = None
-        for j in range(n_f):
-            at = (j % per_chunk) * shard
-            term = jnp.dot(
-                x_refs[j // per_chunk][:, at : at + shard],
-                w_refs[j][...],
-                preferred_element_type=jnp.float32,
-            )
-            total = term if total is None else total + term
-        return total + bias[...]
-
-    @pl.when(step < q_tiles)
-    def _():
-        tile = product(q_refs, q_bias)
-        q_out[...] = rope_tile(tile, cos_ref[...], sin_ref[...]).astype(jnp.bfloat16)
-
-    @pl.when(jnp.logical_and(step >= q_tiles, step < q_tiles + k_tiles))
-    def _():
-        tile = product(kv_refs, kv_bias)
-        kv_out[...] = rope_tile(tile, cos_ref[...], sin_ref[...]).astype(jnp.bfloat16)
-
-    @pl.when(step >= q_tiles + k_tiles)
-    def _():
-        kv_out[...] = product(kv_refs, kv_bias).astype(jnp.bfloat16)
-
-
-def project(x_chunks, q_pieces, kv_pieces, q_bias, kv_bias, cos, sin):
-    n_f, chunks = len(q_pieces), len(x_chunks)
-    count = x_chunks[0].shape[0]
-    shard, q_cols = q_pieces[0].shape
-    kv_cols = kv_pieces[0].shape[1]
+def project_kernel(at_rows, n_x, n_w, wide, roped, *refs):
+    x_refs, w_refs = refs[:n_x], refs[n_x : n_x + n_w]
+    bias_ref, cos_ref, sin_ref, q_out, kv_out, rows, weights, x_sem, w_sem = refs[n_x + n_w :]
+    count, part = x_refs[0].shape
+    per_block = rows.shape[1] // part
+    q_cols = q_out.shape[1]
+    tiles = (q_cols + kv_out.shape[1]) // wide
+
+    def fetch_rows(i):
+        place = rows.at[
+            pl.ds(i // per_block * count, count), pl.ds(i % per_block * part, part)
+        ]
+        return pltpu.make_async_copy(x_refs[i], place, x_sem.at[i])
+
+    def fetch_weights(tile, i):
+        depth = w_refs[i].shape[0]
+        return pltpu.make_async_copy(
+            w_refs[i].at[:, pl.ds(tile * wide, wide)],
+            weights.at[tile % 2, pl.ds(at_rows[i], depth), :],
+            w_sem.at[tile % 2, i],
+        )
+
+    for i in range(n_w):
+        fetch_weights(0, i).start()
+    for i in range(n_x):
+        fetch_rows(i).start()
+    for i in range(n_x):
+        fetch_rows(i).wait()
+    for tile in range(tiles):
+        for i in range(n_w):
+            fetch_weights(tile, i).wait()
+        if tile + 1 < tiles:
+            for i in range(n_w):
+                fetch_weights(tile + 1, i).start()
+        at = tile * wide
+        total = jnp.dot(rows[...], weights[tile % 2], preferred_element_type=jnp.float32)
+        total = total + bias_ref[:, at : at + wide]
+        if at < roped:
+            total = rope_tile(total, cos_ref[...], sin_ref[...])
+        total = total.astype(jnp.bfloat16)
+        if at < q_cols:
+            q_out[:, at : at + wide] = total
+        else:
+            kv_out[:, at - q_cols : at - q_cols + wide] = total
+
+
+def project(blocks, pieces, bias, cos, sin, q_cols):
+    x_parts = [chunk for block in blocks for chunk in block]
+    w_parts, at_rows, at = [], [], 0
+    for piece in pieces:
+        for part in piece:
+            w_parts.append(part)
+            at_rows.append(at)
+            at += part.shape[0]
+    width, columns = at, w_parts[0].shape[1]
+    kv_cols = columns - q_cols
+    length = len(blocks) * blocks[0][0].shape[0]
     wide = 256 if q_cols % 256 == 0 and (kv_cols // 2) % 256 == 0 else 128
-    q_tiles, kv_tiles = q_cols // wide, kv_cols // wide
-
-    def q_at(i):
-        return (0, jnp.minimum(i, q_tiles - 1))
-
-    def kv_at(i):
-        return (0, jnp.maximum(i - q_tiles, 0))
-
-    def whole(i):
-        return (0, 0)
-
+    vmem = pl.BlockSpec(memory_space=pltpu.VMEM)
+    n_x, n_w = len(x_parts), len(w_parts)
     return pl.pallas_call(
-        functools.partial(project_kernel, n_f, chunks, q_tiles, kv_tiles // 2),
-        grid=(q_tiles + kv_tiles,),
-        in_specs=[pl.BlockSpec(x.shape, whole, pipeline_mode=pl.Buffered(1)) for x in x_chunks]
-        + [pl.BlockSpec((shard, wide), q_at)] * n_f
-        + [pl.BlockSpec((shard, wide), kv_at)] * n_f
-        + [
-            pl.BlockSpec((1, wide), q_at),
-            pl.BlockSpec((1, wide), kv_at),
-            pl.BlockSpec(cos.shape, whole, pipeline_mode=pl.Buffered(1)),
-            pl.BlockSpec(sin.shape, whole, pipeline_mode=pl.Buffered(1)),
+        functools.partial(project_kernel, at_rows, n_x, n_w, wide, q_cols + kv_cols // 2),
+        in_specs=[pl.BlockSpec(memory_space=pl.ANY)] * (n_x + n_w) + [vmem] * 3,
+        out_specs=[vmem, vmem],
+        out_shape=[
+            jax.ShapeDtypeStruct((length, q_cols), jnp.bfloat16),
+            jax.ShapeDtypeStruct((length, kv_cols), jnp.bfloat16),
         ],
-        out_specs=[pl.BlockSpec((count, wide), q_at), pl.BlockSpec((count, wide), kv_at)],
-        out_shape=[
-            jax.ShapeDtypeStruct((count, q_cols), jnp.bfloat16),
-            jax.ShapeDtypeStruct((count, kv_cols), jnp.bfloat16),
+        scratch_shapes=[
+            pltpu.VMEM((length, width), jnp.bfloat16),
+            pltpu.VMEM((2, width, wide), jnp.bfloat16),
+            pltpu.SemaphoreType.DMA((n_x,)),
+            pltpu.SemaphoreType.DMA((2, n_w)),
         ],
         compiler_params=params(),
         cost_estimate=pl.CostEstimate(
-            flops=2 * count * shard * n_f * (q_cols + kv_cols),
-            bytes_accessed=2 * shard * n_f * (count + q_cols + kv_cols),
+            flops=2 * length * width * columns,
+            bytes_accessed=2 * (length * width + columns * (length + width)),
             transcendentals=0,
         ),
         name="project",
-    )(*x_chunks, *q_pieces, *kv_pieces, q_bias[None, :], kv_bias[None, :], cos, sin)
+    )(*x_parts, *w_parts, bias[None, :], cos, sin)
 
 
 def attend_kernel(blocks, group, s_ref, q_ref, k_ref, v_ref, out_ref, keys, values):
@@ -226,71 +230,79 @@
     )(s[None], queries, kv, kv)
 
 
-def mix_kernel(core_ref, heads_ref, mine_ref, sibling_ref, *out_refs):
-    shard = mine_ref.shape[0]
+def mix_kernel(n_w, heads_ref, *refs):
+    w_refs, out_refs = refs[:n_w], refs[n_w:]
     rows = out_refs[0].shape[0]
-
-    def write(first_ref, second_ref):
-        for at, w_ref in ((0, first_ref), (shard, second_ref)):
-            term = lax.dot_general(
-                heads_ref[...], w_ref[...], NT, preferred_element_type=jnp.float32
-            ).astype(jnp.bfloat16)
-            for k, out_ref in enumerate(out_refs):
-                out_ref[:, at : at + shard] = term[k * rows : (k + 1) * rows, :]
-
-    @pl.when(core_ref[0] == 0)
-    def _():
-        write(mine_ref, sibling_ref)
-
-    @pl.when(core_ref[0] != 0)
-    def _():
-        write(sibling_ref, mine_ref)
-
-
-def mix(core, heads, mine, sibling, blocks):
-    length = heads.shape[0]
-    shard, features = mine.shape
+    at = 0
+    for w_ref in w_refs:
+        columns = w_ref.shape[0]
+        term = lax.dot_general(
+            heads_ref[...], w_ref[...], NT, preferred_element_type=jnp.float32
+        ).astype(jnp.bfloat16)
+        for k, out_ref in enumerate(out_refs):
+            out_ref[:, at : at + columns] = term[k * rows : (k + 1) * rows, :]
+        at += columns
+
+
+def mix(heads, pieces, blocks):
+    parts = [part for piece in pieces for part in piece]
+    length, features = heads.shape
+    columns = sum(part.shape[0] for part in parts)
     vmem = pl.BlockSpec(memory_space=pltpu.VMEM)
     return pl.pallas_call(
-        mix_kernel,
-        in_specs=[pl.BlockSpec(memory_space=pltpu.SMEM), vmem, vmem, vmem],
+        functools.partial(mix_kernel, len(parts)),
+        in_specs=[vmem] * (1 + len(parts)),
         out_specs=[vmem] * blocks,
-        out_shape=[jax.ShapeDtypeStruct((length // blocks, 2 * shard), jnp.bfloat16)] * blocks,
+        out_shape=[jax.ShapeDtypeStruct((length // blocks, columns), jnp.bfloat16)] * blocks,
         compiler_params=params(),
         cost_estimate=pl.CostEstimate(
-            flops=4 * length * shard * features,
-            bytes_accessed=2 * (length * features + 2 * shard * (features + length)),
+            flops=2 * length * columns * features,
+            bytes_accessed=2 * (length * features + columns * (features + length)),
             transcendentals=0,
         ),
         name="mix",
-    )(core[None], heads, mine, sibling)
+    )(heads, *parts)
 
 
 def swapped(array, n_f, mask):
     return lax.ppermute(array, "fsdp", [(i, i ^ mask) for i in range(n_f)])
 
 
-def chip_pieces(array, n_f, first_bit):
-    chips = n_f // 2
-    bits = [b for b in (1, 2, 4, 8, 16, 32) if b < chips]
-    if first_bit:
-        bits = bits[::-1]
-    pieces = {0: array}
-    for r in sorted(range(1, chips), key=lambda r: (bin(r).count("1"), r)):
-        bit = next(b for b in bits if r & b)
-        pieces[r] = swapped(pieces[r ^ bit], n_f, 2 * bit)
-    return [pieces[r] for r in range(chips)]
-
-
-def with_siblings(pieces, n_f):
-    both = []
-    for piece in pieces:
-        both += [piece, swapped(piece, n_f, 1)]
-    return both
+def half_of(parts, half):
+    if len(parts) == 2:
+        return parts[half]
+    rows = parts[0].shape[0]
+    cut = rows // 2
+    return parts[0][:cut] if half == 0 else parts[0][cut:]
+
+
+def of_level(chips, level):
+    return [r for r in range(chips) if bin(r).count("1") == level]
+
+
+def send_level(held, n_f, level, *before):
+    for r in of_level(n_f // 2, level):
+        if level == 1:
+            held[r] = [swapped(after(held[0][0], *before), n_f, 2 * r)]
+        else:
+            low, high = r & -r, 1 << (r.bit_length() - 1)
+            held[r] = [
+                swapped(after(half_of(held[r ^ low], 0), *before), n_f, 2 * low),
+                swapped(after(half_of(held[r ^ high], 1), *before), n_f, 2 * high),
+            ]
+
+
+def send_siblings(held, sibling, n_f, level, *before):
+    for r in of_level(n_f // 2, level):
+        sibling[r] = [swapped(after(part, *before), n_f, 1) for part in held[r]]
+
+
+def in_order(held, sibling):
+    return [side[r] for r in range(len(held)) for side in (held, sibling)]
 
 
 def after(array, *others):
-    return lax.optimization_barrier((array, *others))[0]
+    return lax.optimization_barrier((array, *others))[0] if others else array
 
 
 def body(
@@ -308,21 +320,32 @@
 ):
     me = lax.axis_index("fsdp")
     s = lax.axis_index("sp")
-    core = lax.rem(me, 2)
     count = tokens.shape[0]
     ring = [(i, (i + 1) % n_s) for i in range(n_s)]
 
-    blocks = [normed_pieces(me, tokens, norm_gain, n_f, Z_CHUNKS)]
-    for _ in range(n_s - 1):
-        blocks.append([lax.ppermute(x, "sp", ring) for x in blocks[-1]])
-
-    kv_weight = jnp.concatenate([key_matrix, value_matrix], axis=1)
-    q_chips = chip_pieces(q_weight, n_f, True)
-    kv_chips = chip_pieces(kv_weight, n_f, False)
-    o_chips = chip_pieces(after(out_weight, *q_chips[1:2], *kv_chips[1:2]), n_f, False)
-    q_pieces = with_siblings(q_chips, n_f)
-    kv_pieces = with_siblings(kv_chips, n_f)
-    o_pieces = with_siblings(o_chips, n_f)
+    chips = n_f // 2
+    levels = chips.bit_length() - 1
+
+    own = normed_pieces(me, tokens, norm_gain, n_f, Z_CHUNKS)
+    blocks = [own] + [[None] * Z_CHUNKS for _ in range(n_s - 1)]
+    events = (n_s - 1) * Z_CHUNKS
+    turns = {events * level // levels: level for level in range(1, levels)}
+
+    held = {0: [jnp.concatenate([q_weight, key_matrix, value_matrix], axis=1)]}
+    o_held, sibling, o_sibling = {0: [out_weight]}, {}, {}
+    send_level(held, n_f, 1)
+    send_siblings(held, sibling, n_f, 0)
+    for event in range(events):
+        k, c = event // Z_CHUNKS + 1, event % Z_CHUNKS
+        blocks[k][c] = arrived = lax.ppermute(blocks[k - 1][c], "sp", ring)
+        if event == 0:
+            send_siblings(o_held, o_sibling, n_f, 0, arrived)
+        if event + 1 in turns:
+            level = turns[event + 1]
+            send_level(held, n_f, level + 1, arrived)
+            send_siblings(held, sibling, n_f, level, arrived)
+    send_siblings(held, sibling, n_f, levels, blocks[-1][0])
+    send_level(o_held, n_f, 1, *held[chips - 1])
 
     order = lax.rem(s - lax.iota(jnp.int32, n_s) + n_s, n_s)
     positions = (order[:, None] * count + lax.iota(jnp.int32, count)[None, :]).reshape(-1)
@@ -332,22 +355,31 @@
     cos = jnp.concatenate([cos, cos], axis=1)
     sin = jnp.concatenate([-sin, sin], axis=1)
 
-    x_chunks = [jnp.concatenate(parts, axis=0) for parts in zip(*blocks)]
-    kv_bias = jnp.concatenate([k_bias, value_offset_bias])
-    queries, kv = project(x_chunks, q_pieces, kv_pieces, q_bias, kv_bias, cos, sin)
+    bias = jnp.concatenate([q_bias, k_bias, value_offset_bias])
+    pieces = in_order(held, sibling)
+    queries, kv = project(blocks, pieces, bias, cos, sin, q_weight.shape[1])
     heads = attend(s, queries, kv, n_s)
 
-    width = out_weight.shape[0] * n_f
-    mixed = jnp.zeros((count, width), jnp.bfloat16)
-    chips = n_f // 2
-    for r in range(chips):
-        terms = mix(core, heads, o_pieces[2 * r], o_pieces[2 * r + 1], n_s)
-        total = terms[1 % n_s]
-        for k in range(2, n_s + 1):
-            arrived = lax.ppermute(total, "sp", ring).astype(jnp.float32)
-            total = (arrived + terms[k % n_s].astype(jnp.float32)).astype(jnp.bfloat16)
-        at = jnp.bitwise_xor(me // 2, r) * (width // chips)
-        mixed = lax.dynamic_update_slice(mixed, total, (0, at))
+    shard = out_weight.shape[0]
+    mixed = jnp.zeros((count, shard * n_f), jnp.bfloat16)
+    for level in range(levels + 1):
+        for r in of_level(chips, level):
+            pair = (o_held[r], o_sibling[r])
+            alone = level in (0, levels)
+            for group in ((2 * r,), (2 * r + 1,)) if alone else ((2 * r, 2 * r + 1),):
+                terms = mix(heads, [pair[j % 2] for j in group], n_s)
+                if level < levels and group[0] == 2 * of_level(chips, level)[-1]:
+                    send_siblings(o_held, o_sibling, n_f, level + 1, terms[0])
+                    send_level(o_held, n_f, level + 2, terms[0])
+                total = terms[1 % n_s]
+                for k in range(2, n_s + 1):
+                    arrived = lax.ppermute(total, "sp", ring).astype(jnp.float32)
+                    total = (arrived + terms[k % n_s].astype(jnp.float32)).astype(jnp.bfloat16)
+                for i, j in enumerate(group):
+                    at = jnp.bitwise_xor(me, j) * shard
+                    mixed = lax.dynamic_update_slice(
+                        mixed, total[:, i * shard : (i + 1) * shard], (0, at)
+                    )
     return mixed
 
 

time: 280 us -> 252 us (0.900)
  waiting for transfers between devices: 196 us -> 158 us
  starting transfers between devices: 26.9 us -> 32.7 us
  local copies, waits for them, and re-layouts: 10.7 us -> 15.6 us
  other arithmetic: 6.31 us -> 2.96 us
    ppermute x6, waiting for transfers between devices: 79.5 us -> 59.7 us  [body(): blocks[k][c] = arrived = lax.ppermute(blocks[k - 1][c], 'sp', ring)]
    ppermute x12 -> x18, waiting for transfers between devices: 73.5 us -> 61.2 us  [body(): arrived = lax.ppermute(total, 'sp', ring).astype(jnp.float32)]
    ppermute x12 -> x18, starting transfers between devices: 6.63 us -> 13 us  [body(): arrived = lax.ppermute(total, 'sp', ring).astype(jnp.float32)]
    ppermute x21 -> x18, waiting for transfers between devices: 42.9 us -> 36.9 us  [swapped(): return lax.ppermute(array, 'fsdp', [(i, i ^ mask) for i in range(n_f)])]
    slice x0 -> x4, local copies, waits for them, and re-layouts: none -> 5.06 us  [half_of(): return parts[0][:cut] if half == 0 else parts[0][cut:]]
    concatenate x3 -> x1, other arithmetic: 3.2 us -> 0.01 us  [body(): bias = jnp.concatenate([q_bias, k_bias, value_offset_bias])]
    pallas_call x5 -> x7, Pallas kernels: 35.1 us -> 37.5 us  [the longest x1 22.2 us: project(): pl.pallas_call(functools.partial(project_kernel, at_rows, n_x, n_w, wide,...]
    ppermute x21 -> x18, starting transfers between devices: 12.1 us -> 13.5 us  [swapped(): return lax.ppermute(array, 'fsdp', [(i, i ^ mask) for i in range(n_f)])]
  transfers between devices with their start and end apart: 39 -> 42, of which waited for: 18 -> 20; matrix products, arithmetic and copies ran while one was open for 2% -> 3% of each run, Pallas kernels for 14% -> 17%
where the time goes in v2:
time: 252 us; the launch traced here: 251 us
  waiting for transfers between devices  158 us (63%)
  Pallas kernels  41.9 us (17%)
  starting transfers between devices  32.7 us (13%)
  local copies, waits for them, and re-layouts  15.6 us (6%)
  other arithmetic  2.96 us (1%)
    ppermute x18, waiting for transfers between devices, body(): arrived = lax.ppermute(total, 'sp', ring).astype(jnp.float32)  61.2 us
    ppermute x6, waiting for transfers between devices, body(): blocks[k][c] = arrived = lax.ppermute(blocks[k - 1][c], 'sp', ring)  59.7 us
    ppermute x18, waiting for transfers between devices, swapped(): return lax.ppermute(array, 'fsdp', [(i, i ^ mask) for i in range(n_f)])  36.9 us
    pallas_call x1, Pallas kernels, project(): pl.pallas_call(functools.partial(project_kernel, at_rows, n_x, n_w, wide,...  22.2 us
    pallas_call x6, Pallas kernels, mix(): pl.pallas_call(functools.partial(mix_kernel, len(parts)), in_specs=[vmem]...  15.3 us
    ppermute x18, starting transfers between devices, swapped(): return lax.ppermute(array, 'fsdp', [(i, i ^ mask) for i in range(n_f)])  13.5 us
    ppermute x18, starting transfers between devices, body(): arrived = lax.ppermute(total, 'sp', ring).astype(jnp.float32)  13 us
    unnamed x46, local copies, waits for them, and re-layouts  9.53 us
  transfers between devices with their start and end apart: 42, of which 20 were waited for; matrix products, arithmetic and copies ran while one was open for 3% of the time, Pallas kernels for 17%

profile of v2, /device:TPU:0, one launch (start us, length us, event | category | flops | bytes accessed | tf_op | source)
XLA Modules:
  0.0 251.4 jit_solution(6490646380318067356)
XLA Ops:
  0.0 2.8 %constant_dynamic-update-slice_fusion.2 = bf16[640,1792]{1,0:T(8,128)(2,1)} fusion(bf16[640,1280]{1,0:T(8,128)(2,1)} %param.11), kind=kLoop, calls=%fused_computation.33 | loop fusion | bytes 3276800
  4.4 3.0 %collective-permute-start.9 = (bf16[640,1792]{1,0:T(8,128)(2,1)}, bf16[640,1792]{1,0:T(8,128)(2,1)}, u32[]{:S(2)}, u32[]{:S(2)}) collective-permute-start(bf16[640,1792]{1,0:T(8,128)(2,1)} %constant_dynamic-update-slice_fusion.refs_8_), channel_id=1, source_target_pairs={{0,16},{4,20},{8,24},{12,28},{16,0},{20,4},{24,8},{28,12},{1,17},{... | collective-permute-start | bytes 6881288 | tf_op jit(solution)/shard_map/ppermute | solution.py:268
  9.6 1.6 collective-permute-start
  11.2 16.2 %collective-permute-done.refs_2_ = bf16[128,2560]{1,0:T(8,128)(2,1)S(1)} collective-permute-done((bf16[128,2560]{1,0:T(8,128)(2,1)S(1)}, bf16[128,2560]{1,0:T(8,128)(2,1)S(1)}, u32[]{:S(2)}, u32[]{:S(2)}) %collective-permute-start) | collective-permute-done | bytes 655392 | tf_op jit(solution)/shard_map/ppermute | solution.py:340
  28.7 28.8 %collective-permute-done.9.refs_12_ = bf16[640,1792]{1,0:T(8,128)(2,1)} collective-permute-done((bf16[640,1792]{1,0:T(8,128)(2,1)}, bf16[640,1792]{1,0:T(8,128)(2,1)}, u32[]{:S(2)}, u32[]{:S(2)}) %collective-permute-start.9) | collective-permute-done | bytes 2293792 | tf_op jit(solution)/shard_map/ppermute | solution.py:268
  59.0 1.8 collective-permute-start.11
  65.2 1.6 collective-permute-start.12
  66.8 13.4 %collective-permute-done.3.refs_5_ = bf16[128,2560]{1,0:T(8,128)(2,1)S(1)} collective-permute-done((bf16[128,2560]{1,0:T(8,128)(2,1)S(1)}, bf16[128,2560]{1,0:T(8,128)(2,1)S(1)}, u32[]{:S(2)}, u32[]{:S(2)}) %collective-permute-start.3) | collective-permute-done | bytes 655392 | tf_op jit(solution)/shard_map/ppermute | solution.py:340
  80.2 11.8 %collective-permute-done.4.refs_6_ = bf16[128,2560]{1,0:T(8,128)(2,1)S(1)} collective-permute-done((bf16[128,2560]{1,0:T(8,128)(2,1)S(1)}, bf16[128,2560]{1,0:T(8,128)(2,1)S(1)}, u32[]{:S(2)}, u32[]{:S(2)}) %collective-permute-start.4) | collective-permute-done | bytes 655392 | tf_op jit(solution)/shard_map/ppermute | solution.py:340
  92.6 18.3 %collective-permute-done.5.refs_7_ = bf16[128,2560]{1,0:T(8,128)(2,1)S(1)} collective-permute-done((bf16[128,2560]{1,0:T(8,128)(2,1)S(1)}, bf16[128,2560]{1,0:T(8,128)(2,1)S(1)}, u32[]{:S(2)}, u32[]{:S(2)}) %collective-permute-start.5) | collective-permute-done | bytes 655392 | tf_op jit(solution)/shard_map/ppermute | solution.py:340
  113.0 1.9 collective-permute-done.14.refs_17_
  117.7 22.2 %project.1 = (bf16[512,1280]{1,0:T(8,128)(2,1)}, bf16[512,512]{1,0:T(8,128)(2,1)S(1)}) custom-call(bf16[128,2560]{1,0:T(8,128)(2,1)S(1)} %get-tuple-element.47.refs_0_, bf16[128,2560]{1,0:T(8,128)(2,1)S(1)} %get-tuple-element.48.refs_1_, bf16[128,2560]{1,0:T(8,128)(2,1)S(1)} %copy-done.4, bf16[128,2560]{1,0:T(8,128)(2,1)S(1)} %copy-done.6, ...), custom_call_target="tpu_custom_call" | custom-call | flops 9395240960 | bytes 25427968 | tf_op jit(solution)/shard_map/project/pallas_call | solution.py:133
  141.2 3.7 %attend.1.heads_ref = bf16[512,1280]{1,0:T(8,128)(2,1)S(1)} custom-call(s32[1]{0:T(128)} %bitcast.s_ref, bf16[512,1280]{1,0:T(8,128)(2,1)S(1)} %copy-done.9, bf16[512,512]{1,0:T(8,128)(2,1)S(1)} %get-tuple-element.56.k_ref.v_ref, bf16[512,512]{1,0:T(8,128)(2,1)S(1)} %get-tuple-element.56.k_ref.v_ref), custom_call_target="tpu_custom_call" | custom-call | flops 1342177280 | bytes 3932160 | tf_op jit(solution)/shard_map/attend/pallas_call | solution.py:208
  147.8 2.6 %mix.7 = (bf16[128,640]{1,0:T(8,128)(2,1)S(1)}, bf16[128,640]{1,0:T(8,128)(2,1)S(1)}, bf16[128,640]{1,0:T(8,128)(2,1)S(1)}, bf16[128,640]{1,0:T(8,128)(2,1)S(1)}) custom-call(bf16[512,1280]{1,0:T(8,128)(2,1)S(1)} %copy-done.8, bf16[640,1280]{1,0:T(8,128)(2,1)} %collective-permute-done.18.refs_0_), custom_call_target="tpu_custom_call" | custom-call | flops 838860800 | bytes 3604480 | tf_op jit(solution)/shard_map/mix/pallas_call | solution.py:252
  155.2 3.1 %collective-permute-done.19 = bf16[128,640]{1,0:T(8,128)(2,1)S(1)} collective-permute-done((bf16[128,640]{1,0:T(8,128)(2,1)S(1)}, bf16[128,640]{1,0:T(8,128)(2,1)S(1)}, u32[]{:S(2)}, u32[]{:S(2)}) %collective-permute-start.19) | collective-permute-done | bytes 163872 | tf_op jit(solution)/shard_map/ppermute | solution.py:376
  159.2 4.6 %collective-permute-done.16 = bf16[128,640]{1,0:T(8,128)(2,1)S(1)} collective-permute-done((bf16[128,640]{1,0:T(8,128)(2,1)S(1)}, bf16[128,640]{1,0:T(8,128)(2,1)S(1)}, u32[]{:S(2)}, u32[]{:S(2)}) %collective-permute-start.16) | collective-permute-done | bytes 163872 | tf_op jit(solution)/shard_map/ppermute | solution.py:376
  163.9 3.1 %collective-permute-done.20 = bf16[128,640]{1,0:T(8,128)(2,1)S(1)} collective-permute-done((bf16[128,640]{1,0:T(8,128)(2,1)S(1)}, bf16[128,640]{1,0:T(8,128)(2,1)S(1)}, u32[]{:S(2)}, u32[]{:S(2)}) %collective-permute-start.20) | collective-permute-done | bytes 163872 | tf_op jit(solution)/shard_map/ppermute | solution.py:376
  167.0 4.8 %collective-permute-done.33.refs_1_ = bf16[320,1280]{1,0:T(8,128)(2,1)S(1)} collective-permute-done((bf16[320,1280]{1,0:T(8,128)(2,1)S(1)}, bf16[320,1280]{1,0:T(8,128)(2,1)S(1)}, u32[]{:S(2)}, u32[]{:S(2)}) %collective-permute-start.33) | collective-permute-done | bytes 819232 | tf_op jit(solution)/shard_map/ppermute | solution.py:268
  175.1 2.6 %collective-permute-start.34 = (bf16[128,640]{1,0:T(8,128)(2,1)S(1)}, bf16[128,640]{1,0:T(8,128)(2,1)S(1)}, u32[]{:S(2)}, u32[]{:S(2)}) collective-permute-start(bf16[128,640]{1,0:T(8,128)(2,1)S(1)} %get-tuple-element.79), channel_id=1, source_target_pairs={{0,1},{1,2},{2,3},{3,0},{4,5},{5,6},{6,7},{7,4},{8,9},{9,10},{10,1... | collective-permute-start | bytes 491528 | tf_op jit(solution)/shard_map/ppermute | solution.py:376
  177.9 4.5 %collective-permute-done.34 = bf16[128,640]{1,0:T(8,128)(2,1)S(1)} collective-permute-done((bf16[128,640]{1,0:T(8,128)(2,1)S(1)}, bf16[128,640]{1,0:T(8,128)(2,1)S(1)}, u32[]{:S(2)}, u32[]{:S(2)}) %collective-permute-start.34) | collective-permute-done | bytes 163872 | tf_op jit(solution)/shard_map/ppermute | solution.py:376
  184.4 4.1 %mix.8 = (bf16[128,1280]{1,0:T(8,128)(2,1)S(1)}, bf16[128,1280]{1,0:T(8,128)(2,1)S(1)}, bf16[128,1280]{1,0:T(8,128)(2,1)S(1)}, bf16[128,1280]{1,0:T(8,128)(2,1)S(1)}) custom-call(bf16[512,1280]{1,0:T(8,128)(2,1)S(1)} %copy-done.8, bf16[640,1280]{1,0:T(8,128)(2,1)} %collective-permute-done.22.refs_0_, bf16[640,1280]{1,0:T(8,128)(2,1)} %copy-done.16), custom_call_target="tpu_custom_call" | custom-call | flops 1677721600 | bytes 5898240 | tf_op jit(solution)/shard_map/mix/pallas_call | solution.py:252
  188.6 1.9 collective-permute-start.24
  192.1 4.1 %mix.9 = (bf16[128,1280]{1,0:T(8,128)(2,1)S(1)}, bf16[128,1280]{1,0:T(8,128)(2,1)S(1)}, bf16[128,1280]{1,0:T(8,128)(2,1)S(1)}, bf16[128,1280]{1,0:T(8,128)(2,1)S(1)}) custom-call(bf16[512,1280]{1,0:T(8,128)(2,1)S(1)} %copy-done.8, bf16[640,1280]{1,0:T(8,128)(2,1)} %collective-permute-done.27.refs_0_, bf16[640,1280]{1,0:T(8,128)(2,1)} %copy-done.17), custom_call_target="tpu_custom_call" | custom-call | flops 1677721600 | bytes 5898240 | tf_op jit(solution)/shard_map/mix/pallas_call | solution.py:252
  196.9 2.1 collective-permute-start.29
  200.3 8.9 %collective-permute-done.29 = bf16[128,1280]{1,0:T(8,128)(2,1)S(1)} collective-permute-done((bf16[128,1280]{1,0:T(8,128)(2,1)S(1)}, bf16[128,1280]{1,0:T(8,128)(2,1)S(1)}, u32[]{:S(2)}, u32[]{:S(2)}) %collective-permute-start.29) | collective-permute-done | bytes 327712 | tf_op jit(solution)/shard_map/ppermute | solution.py:376
  209.7 6.6 %collective-permute-done.25 = bf16[128,1280]{1,0:T(8,128)(2,1)S(1)} collective-permute-done((bf16[128,1280]{1,0:T(8,128)(2,1)S(1)}, bf16[128,1280]{1,0:T(8,128)(2,1)S(1)}, u32[]{:S(2)}, u32[]{:S(2)}) %collective-permute-start.25) | collective-permute-done | bytes 327712 | tf_op jit(solution)/shard_map/ppermute | solution.py:376
  216.7 1.6 mix.11
  219.0 4.3 %collective-permute-done.30 = bf16[128,1280]{1,0:T(8,128)(2,1)S(1)} collective-permute-done((bf16[128,1280]{1,0:T(8,128)(2,1)S(1)}, bf16[128,1280]{1,0:T(8,128)(2,1)S(1)}, u32[]{:S(2)}, u32[]{:S(2)}) %collective-permute-start.30) | collective-permute-done | bytes 327712 | tf_op jit(solution)/shard_map/ppermute | solution.py:376
  223.7 10.1 %collective-permute-done.39 = bf16[128,640]{1,0:T(8,128)(2,1)S(1)} collective-permute-done((bf16[128,640]{1,0:T(8,128)(2,1)S(1)}, bf16[128,640]{1,0:T(8,128)(2,1)S(1)}, u32[]{:S(2)}, u32[]{:S(2)}) %collective-permute-start.39) | collective-permute-done | bytes 163872 | tf_op jit(solution)/shard_map/ppermute | solution.py:376
  234.4 6.5 %collective-permute-done.31 = bf16[128,1280]{1,0:T(8,128)(2,1)S(1)} collective-permute-done((bf16[128,1280]{1,0:T(8,128)(2,1)S(1)}, bf16[128,1280]{1,0:T(8,128)(2,1)S(1)}, u32[]{:S(2)}, u32[]{:S(2)}) %collective-permute-start.31) | collective-permute-done | bytes 327712 | tf_op jit(solution)/shard_map/ppermute | solution.py:376
  241.0 2.5 collective-permute-done.40
  244.3 6.5 %collective-permute-done.41 = bf16[128,640]{1,0:T(8,128)(2,1)S(1)} collective-permute-done((bf16[128,640]{1,0:T(8,128)(2,1)S(1)}, bf16[128,640]{1,0:T(8,128)(2,1)S(1)}, u32[]{:S(2)}, u32[]{:S(2)}) %collective-permute-start.41) | collective-permute-done | bytes 163872 | tf_op jit(solution)/shard_map/ppermute | solution.py:376
  (142 shorter events, 39.4 us)
Async XLA Ops:
  4.4 53.1 %collective-permute-start.9 = (bf16[640,1792]{1,0:T(8,128)(2,1)}, bf16[640,1792]{1,0:T(8,128)(2,1)}, u32[]{:S(2)}, u32[]{:S(2)}) collective-permute-start(bf16[640,1792]{1,0:T(8,128)(2,1)} %constant_dynamic-update-slice_fusion.refs_8_), channel_id=1, source_target_pairs={{0,16},{4,20},{8,24},{12,28},{16,0},{20,4},{24,8},{28,12},{1,17},{... | collective-permute-start | bytes 6881288 | tf_op jit(solution)/shard_map/ppermute | solution.py:268
  7.4 56.5 %collective-permute-start.7 = (bf16[640,1792]{1,0:T(8,128)(2,1)}, bf16[640,1792]{1,0:T(8,128)(2,1)}, u32[]{:S(2)}, u32[]{:S(2)}) collective-permute-start(bf16[640,1792]{1,0:T(8,128)(2,1)} %constant_dynamic-update-slice_fusion.refs_8_), channel_id=1, source_target_pairs={{0,8},{4,12},{8,0},{12,4},{16,24},{20,28},{24,16},{28,20},{1,9},{5... | collective-permute-start | bytes 6881288 | tf_op jit(solution)/shard_map/ppermute | solution.py:268
  9.6 17.8 %collective-permute-start = (bf16[128,2560]{1,0:T(8,128)(2,1)S(1)}, bf16[128,2560]{1,0:T(8,128)(2,1)S(1)}, u32[]{:S(2)}, u32[]{:S(2)}) collective-permute-start(bf16[128,2560]{1,0:T(8,128)(2,1)S(1)} %get-tuple-element.47.refs_0_), channel_id=1, source_target_pairs={{0,1},{1,2},{2,3},{3,0},{4,5},{5,6},{6,7},{7,4},{8,9},{9,10},{10,1... | collective-permute-start | bytes 1966088 | tf_op jit(solution)/shard_map/ppermute | solution.py:340
  27.4 31.5 %collective-permute-start.2 = (bf16[128,2560]{1,0:T(8,128)(2,1)S(1)}, bf16[128,2560]{1,0:T(8,128)(2,1)S(1)}, u32[]{:S(2)}, u32[]{:S(2)}) collective-permute-start(bf16[128,2560]{1,0:T(8,128)(2,1)S(1)} %collective-permute-done.refs_2_), channel_id=1, source_target_pairs={{0,1},{1,2},{2,3},{3,0},{4,5},{5,6},{6,7},{7,4},{8,9},{9,10},{10,1... | collective-permute-start | bytes 1966088 | tf_op jit(solution)/shard_map/ppermute | solution.py:340
  27.4 33.3 %collective-permute-start.1 = (bf16[128,2560]{1,0:T(8,128)(2,1)S(1)}, bf16[128,2560]{1,0:T(8,128)(2,1)S(1)}, u32[]{:S(2)}, u32[]{:S(2)}) collective-permute-start(bf16[128,2560]{1,0:T(8,128)(2,1)S(1)} %get-tuple-element.48.refs_1_), channel_id=1, source_target_pairs={{0,1},{1,2},{2,3},{3,0},{4,5},{5,6},{6,7},{7,4},{8,9},{9,10},{10,1... | collective-permute-start | bytes 1966088 | tf_op jit(solution)/shard_map/ppermute | solution.py:340
  59.0 33.0 %collective-permute-start.11 = (bf16[320,1792]{1,0:T(8,128)(2,1)S(1)}, bf16[320,1792]{1,0:T(8,128)(2,1)}, u32[]{:S(2)}, u32[]{:S(2)}) collective-permute-start(bf16[320,1792]{1,0:T(8,128)(2,1)S(1)} %slice.32), channel_id=1, source_target_pairs={{0,8},{4,12},{8,0},{12,4},{16,24},{20,28},{24,16},{28,20},{1,9},{5... | collective-permute-start | bytes 3440648 | tf_op jit(solution)/shard_map/ppermute | solution.py:268
  60.7 19.5 %collective-permute-start.3 = (bf16[128,2560]{1,0:T(8,128)(2,1)S(1)}, bf16[128,2560]{1,0:T(8,128)(2,1)S(1)}, u32[]{:S(2)}, u32[]{:S(2)}) collective-permute-start(bf16[128,2560]{1,0:T(8,128)(2,1)S(1)} %collective-permute-done.1.refs_3_), channel_id=1, source_target_pairs={{0,1},{1,2},{2,3},{3,0},{4,5},{5,6},{6,7},{7,4},{8,9},{9,10},{10,1... | collective-permute-start | bytes 1966088 | tf_op jit(solution)/shard_map/ppermute | solution.py:340
  62.3 29.6 %collective-permute-start.4 = (bf16[128,2560]{1,0:T(8,128)(2,1)S(1)}, bf16[128,2560]{1,0:T(8,128)(2,1)S(1)}, u32[]{:S(2)}, u32[]{:S(2)}) collective-permute-start(bf16[128,2560]{1,0:T(8,128)(2,1)S(1)} %collective-permute-done.2.refs_4_), channel_id=1, source_target_pairs={{0,1},{1,2},{2,3},{3,0},{4,5},{5,6},{6,7},{7,4},{8,9},{9,10},{10,1... | collective-permute-start | bytes 1966088 | tf_op jit(solution)/shard_map/ppermute | solution.py:340
  65.2 26.8 %collective-permute-start.12 = (bf16[320,1792]{1,0:T(8,128)(2,1)S(1)}, bf16[320,1792]{1,0:T(8,128)(2,1)}, u32[]{:S(2)}, u32[]{:S(2)}) collective-permute-start(bf16[320,1792]{1,0:T(8,128)(2,1)S(1)} %slice.33), channel_id=1, source_target_pairs={{0,16},{4,20},{8,24},{12,28},{16,0},{20,4},{24,8},{28,12},{1,17},{... | collective-permute-start | bytes 3440648 | tf_op jit(solution)/shard_map/ppermute | solution.py:268
  66.8 45.1 %collective-permute-start.6 = (bf16[640,1792]{1,0:T(8,128)(2,1)}, bf16[640,1792]{1,0:T(8,128)(2,1)}, u32[]{:S(2)}, u32[]{:S(2)}) collective-permute-start(bf16[640,1792]{1,0:T(8,128)(2,1)} %constant_dynamic-update-slice_fusion.refs_8_), channel_id=1, source_target_pairs={{0,4},{4,0},{8,12},{12,8},{16,20},{20,16},{24,28},{28,24},{1,5},{5... | collective-permute-start | bytes 6881288 | tf_op jit(solution)/shard_map/ppermute | solution.py:268
  80.2 37.4 %collective-permute-start.10 = (bf16[640,1792]{1,0:T(8,128)(2,1)}, bf16[640,1792]{1,0:T(8,128)(2,1)}, u32[]{:S(2)}, u32[]{:S(2)}) collective-permute-start(bf16[640,1792]{1,0:T(8,128)(2,1)} %collective-permute-done.9.refs_12_), channel_id=1, source_target_pairs={{0,4},{4,0},{8,12},{12,8},{16,20},{20,16},{24,28},{28,24},{1,5},{5... | collective-permute-start | bytes 6881288 | tf_op jit(solution)/shard_map/ppermute | solution.py:268
  92.0 25.7 %collective-permute-start.8 = (bf16[640,1792]{1,0:T(8,128)(2,1)}, bf16[640,1792]{1,0:T(8,128)(2,1)}, u32[]{:S(2)}, u32[]{:S(2)}) collective-permute-start(bf16[640,1792]{1,0:T(8,128)(2,1)} %collective-permute-done.7.refs_10_), channel_id=1, source_target_pairs={{0,4},{4,0},{8,12},{12,8},{16,20},{20,16},{24,28},{28,24},{1,5},{5... | collective-permute-start | bytes 6881288 | tf_op jit(solution)/shard_map/ppermute | solution.py:268
  92.0 18.9 %collective-permute-start.5 = (bf16[128,2560]{1,0:T(8,128)(2,1)S(1)}, bf16[128,2560]{1,0:T(8,128)(2,1)S(1)}, u32[]{:S(2)}, u32[]{:S(2)}) collective-permute-start(bf16[128,2560]{1,0:T(8,128)(2,1)S(1)} %collective-permute-done.3.refs_5_), channel_id=1, source_target_pairs={{0,1},{1,2},{2,3},{3,0},{4,5},{5,6},{6,7},{7,4},{8,9},{9,10},{10,1... | collective-permute-start | bytes 1966088 | tf_op jit(solution)/shard_map/ppermute | solution.py:340
  92.1 20.4 %collective-permute-start.13 = (bf16[320,1792]{1,0:T(8,128)(2,1)}, bf16[320,1792]{1,0:T(8,128)(2,1)}, u32[]{:S(2)}, u32[]{:S(2)}) collective-permute-start(bf16[320,1792]{1,0:T(8,128)(2,1)} %collective-permute-done.11.refs_14_), channel_id=1, source_target_pairs={{0,4},{4,0},{8,12},{12,8},{16,20},{20,16},{24,28},{28,24},{1,5},{5... | collective-permute-start | bytes 3440648 | tf_op jit(solution)/shard_map/ppermute | solution.py:268
  111.9 34.6 %collective-permute-start.18 = (bf16[640,1280]{1,0:T(8,128)(2,1)S(1)}, bf16[640,1280]{1,0:T(8,128)(2,1)}, u32[]{:S(2)}, u32[]{:S(2)}) collective-permute-start(bf16[640,1280]{1,0:T(8,128)(2,1)S(1)} %copy-done.2), channel_id=1, source_target_pairs={{0,4},{4,0},{8,12},{12,8},{16,20},{20,16},{24,28},{28,24},{1,5},{5... | collective-permute-start | bytes 4915208 | tf_op jit(solution)/shard_map/ppermute | solution.py:268
  112.4 38.1 %collective-permute-start.22 = (bf16[640,1280]{1,0:T(8,128)(2,1)S(1)}, bf16[640,1280]{1,0:T(8,128)(2,1)}, u32[]{:S(2)}, u32[]{:S(2)}) collective-permute-start(bf16[640,1280]{1,0:T(8,128)(2,1)S(1)} %copy-done.2), channel_id=1, source_target_pairs={{0,8},{4,12},{8,0},{12,4},{16,24},{20,28},{24,16},{28,20},{1,9},{5... | collective-permute-start | bytes 4915208 | tf_op jit(solution)/shard_map/ppermute | solution.py:268
  114.9 38.2 %collective-permute-start.27 = (bf16[640,1280]{1,0:T(8,128)(2,1)S(1)}, bf16[640,1280]{1,0:T(8,128)(2,1)}, u32[]{:S(2)}, u32[]{:S(2)}) collective-permute-start(bf16[640,1280]{1,0:T(8,128)(2,1)S(1)} %copy-done.2), channel_id=1, source_target_pairs={{0,16},{4,20},{8,24},{12,28},{16,0},{20,4},{24,8},{28,12},{1,17},{... | collective-permute-start | bytes 4915208 | tf_op jit(solution)/shard_map/ppermute | solution.py:268
  151.7 20.1 %collective-permute-start.33 = (bf16[320,1280]{1,0:T(8,128)(2,1)S(1)}, bf16[320,1280]{1,0:T(8,128)(2,1)S(1)}, u32[]{:S(2)}, u32[]{:S(2)}) collective-permute-start(bf16[320,1280]{1,0:T(8,128)(2,1)S(1)} %slice.39), channel_id=1, source_target_pairs={{0,16},{4,20},{8,24},{12,28},{16,0},{20,4},{24,8},{28,12},{1,17},{... | collective-permute-start | bytes 2457608 | tf_op jit(solution)/shard_map/ppermute | solution.py:268
  154.3 19.2 %collective-permute-start.32 = (bf16[320,1280]{1,0:T(8,128)(2,1)S(1)}, bf16[320,1280]{1,0:T(8,128)(2,1)S(1)}, u32[]{:S(2)}, u32[]{:S(2)}) collective-permute-start(bf16[320,1280]{1,0:T(8,128)(2,1)S(1)} %slice.38), channel_id=1, source_target_pairs={{0,8},{4,12},{8,0},{12,4},{16,24},{20,28},{24,16},{28,20},{1,9},{5... | collective-permute-start | bytes 2457608 | tf_op jit(solution)/shard_map/ppermute | solution.py:268
  154.9 28.3 %collective-permute-start.23 = (bf16[640,1280]{1,0:T(8,128)(2,1)}, bf16[640,1280]{1,0:T(8,128)(2,1)S(1)}, u32[]{:S(2)}, u32[]{:S(2)}) collective-permute-start(bf16[640,1280]{1,0:T(8,128)(2,1)} %collective-permute-done.22.refs_0_), channel_id=1, source_target_pairs={{0,4},{4,0},{8,12},{12,8},{16,20},{20,16},{24,28},{28,24},{1,5},{5... | collective-permute-start | bytes 4915208 | tf_op jit(solution)/shard_map/ppermute | solution.py:268
  163.8 27.1 %collective-permute-start.28 = (bf16[640,1280]{1,0:T(8,128)(2,1)}, bf16[640,1280]{1,0:T(8,128)(2,1)S(1)}, u32[]{:S(2)}, u32[]{:S(2)}) collective-permute-start(bf16[640,1280]{1,0:T(8,128)(2,1)} %collective-permute-done.27.refs_0_), channel_id=1, source_target_pairs={{0,4},{4,0},{8,12},{12,8},{16,20},{20,16},{24,28},{28,24},{1,5},{5... | collective-permute-start | bytes 4915208 | tf_op jit(solution)/shard_map/ppermute | solution.py:268
  171.8 11.4 %collective-permute-start.21 = (bf16[128,640]{1,0:T(8,128)(2,1)S(1)}, bf16[128,640]{1,0:T(8,128)(2,1)S(1)}, u32[]{:S(2)}, u32[]{:S(2)}) collective-permute-start(bf16[128,640]{1,0:T(8,128)(2,1)S(1)} %add_convert_fusion.13), channel_id=1, source_target_pairs={{0,1},{1,2},{2,3},{3,0},{4,5},{5,6},{6,7},{7,4},{8,9},{9,10},{10,1... | collective-permute-start | bytes 491528 | tf_op jit(solution)/shard_map/ppermute | solution.py:376
  188.6 11.0 %collective-permute-start.24 = (bf16[128,1280]{1,0:T(8,128)(2,1)S(1)}, bf16[128,1280]{1,0:T(8,128)(2,1)S(1)}, u32[]{:S(2)}, u32[]{:S(2)}) collective-permute-start(bf16[128,1280]{1,0:T(8,128)(2,1)S(1)} %get-tuple-element.68), channel_id=1, source_target_pairs={{0,1},{1,2},{2,3},{3,0},{4,5},{5,6},{6,7},{7,4},{8,9},{9,10},{10,1... | collective-permute-start | bytes 983048 | tf_op jit(solution)/shard_map/ppermute | solution.py:376
  190.5 53.7 %collective-permute-start.36 = (bf16[128,640]{1,0:T(8,128)(2,1)S(1)}, bf16[128,640]{1,0:T(8,128)(2,1)S(1)}, u32[]{:S(2)}, u32[]{:S(2)}) collective-permute-start(bf16[128,640]{1,0:T(8,128)(2,1)S(1)} %add_convert_fusion.10), channel_id=1, source_target_pairs={{0,1},{1,2},{2,3},{3,0},{4,5},{5,6},{6,7},{7,4},{8,9},{9,10},{10,1... | collective-permute-start | bytes 491528 | tf_op jit(solution)/shard_map/ppermute | solution.py:376
  196.3 20.4 %collective-permute-start.38 = (bf16[320,1280]{1,0:T(8,128)(2,1)S(1)}, bf16[320,1280]{1,0:T(8,128)(2,1)S(1)}, u32[]{:S(2)}, u32[]{:S(2)}) collective-permute-start(bf16[320,1280]{1,0:T(8,128)(2,1)S(1)} %collective-permute-done.33.refs_1_), channel_id=1, source_target_pairs={{0,4},{4,0},{8,12},{12,8},{16,20},{20,16},{24,28},{28,24},{1,5},{5... | collective-permute-start | bytes 2457608 | tf_op jit(solution)/shard_map/ppermute | solution.py:268
  196.4 20.3 %collective-permute-start.37 = (bf16[320,1280]{1,0:T(8,128)(2,1)S(1)}, bf16[320,1280]{1,0:T(8,128)(2,1)S(1)}, u32[]{:S(2)}, u32[]{:S(2)}) collective-permute-start(bf16[320,1280]{1,0:T(8,128)(2,1)S(1)} %collective-permute-done.32.refs_0_), channel_id=1, source_target_pairs={{0,4},{4,0},{8,12},{12,8},{16,20},{20,16},{24,28},{28,24},{1,5},{5... | collective-permute-start | bytes 2457608 | tf_op jit(solution)/shard_map/ppermute | solution.py:268
  196.9 12.4 %collective-permute-start.29 = (bf16[128,1280]{1,0:T(8,128)(2,1)S(1)}, bf16[128,1280]{1,0:T(8,128)(2,1)S(1)}, u32[]{:S(2)}, u32[]{:S(2)}) collective-permute-start(bf16[128,1280]{1,0:T(8,128)(2,1)S(1)} %get-tuple-element.73), channel_id=1, source_target_pairs={{0,1},{1,2},{2,3},{3,0},{4,5},{5,6},{6,7},{7,4},{8,9},{9,10},{10,1... | collective-permute-start | bytes 983048 | tf_op jit(solution)/shard_map/ppermute | solution.py:376
  199.7 16.6 %collective-permute-start.25 = (bf16[128,1280]{1,0:T(8,128)(2,1)S(1)}, bf16[128,1280]{1,0:T(8,128)(2,1)S(1)}, u32[]{:S(2)}, u32[]{:S(2)}) collective-permute-start(bf16[128,1280]{1,0:T(8,128)(2,1)S(1)} %add_convert_fusion.5), channel_id=1, source_target_pairs={{0,1},{1,2},{2,3},{3,0},{4,5},{5,6},{6,7},{7,4},{8,9},{9,10},{10,1... | collective-permute-start | bytes 983048 | tf_op jit(solution)/shard_map/ppermute | solution.py:376
  209.3 14.0 %collective-permute-start.30 = (bf16[128,1280]{1,0:T(8,128)(2,1)S(1)}, bf16[128,1280]{1,0:T(8,128)(2,1)S(1)}, u32[]{:S(2)}, u32[]{:S(2)}) collective-permute-start(bf16[128,1280]{1,0:T(8,128)(2,1)S(1)} %add_convert_fusion.2), channel_id=1, source_target_pairs={{0,1},{1,2},{2,3},{3,0},{4,5},{5,6},{6,7},{7,4},{8,9},{9,10},{10,1... | collective-permute-start | bytes 983048 | tf_op jit(solution)/shard_map/ppermute | solution.py:376
  216.3 17.9 %collective-permute-start.26 = (bf16[128,1280]{1,0:T(8,128)(2,1)S(1)}, bf16[128,1280]{1,0:T(8,128)(2,1)S(1)}, u32[]{:S(2)}, u32[]{:S(2)}) collective-permute-start(bf16[128,1280]{1,0:T(8,128)(2,1)S(1)} %add_convert_fusion.4), channel_id=1, source_target_pairs={{0,1},{1,2},{2,3},{3,0},{4,5},{5,6},{6,7},{7,4},{8,9},{9,10},{10,1... | collective-permute-start | bytes 983048 | tf_op jit(solution)/shard_map/ppermute | solution.py:376
  218.3 15.5 %collective-permute-start.39 = (bf16[128,640]{1,0:T(8,128)(2,1)S(1)}, bf16[128,640]{1,0:T(8,128)(2,1)S(1)}, u32[]{:S(2)}, u32[]{:S(2)}) collective-permute-start(bf16[128,640]{1,0:T(8,128)(2,1)S(1)} %get-tuple-element.85), channel_id=1, source_target_pairs={{0,1},{1,2},{2,3},{3,0},{4,5},{5,6},{6,7},{7,4},{8,9},{9,10},{10,1... | collective-permute-start | bytes 491528 | tf_op jit(solution)/shard_map/ppermute | solution.py:376
  223.4 17.5 %collective-permute-start.31 = (bf16[128,1280]{1,0:T(8,128)(2,1)S(1)}, bf16[128,1280]{1,0:T(8,128)(2,1)S(1)}, u32[]{:S(2)}, u32[]{:S(2)}) collective-permute-start(bf16[128,1280]{1,0:T(8,128)(2,1)S(1)} %add_convert_fusion.1), channel_id=1, source_target_pairs={{0,1},{1,2},{2,3},{3,0},{4,5},{5,6},{6,7},{7,4},{8,9},{9,10},{10,1... | collective-permute-start | bytes 983048 | tf_op jit(solution)/shard_map/ppermute | solution.py:376
  (32 other events, 446.9 us)

commit v3 on v2

--- a/solution.py
+++ b/solution.py
@@ -16,8 +16,8 @@
 NT = (((1,), (1,)), ((), ()))
 
 
-def params():
-    return pltpu.CompilerParams(vmem_limit_bytes=VMEM_LIMIT)
+def params(mib=16):
+    return pltpu.CompilerParams(vmem_limit_bytes=mib * 1024 * 1024)
 
 
 def normed_kernel(n_f, me_ref, tokens_ref, gain_ref, *out_refs):
@@ -144,7 +144,7 @@
             pltpu.SemaphoreType.DMA((n_x,)),
             pltpu.SemaphoreType.DMA((2, n_w)),
         ],
-        compiler_params=params(),
+        compiler_params=params(20),
         cost_estimate=pl.CostEstimate(
             flops=2 * length * width * columns,
             bytes_accessed=2 * (length * width + columns * (length + width)),

time: 252 us -> 259 us (1.028)
  local copies, waits for them, and re-layouts: 15.6 us -> 27 us
  Pallas kernels: 41.9 us -> 37.9 us
    unnamed x46 -> x74, local copies, waits for them, and re-layouts: 9.53 us -> 23.1 us
    ppermute x18, waiting for transfers between devices: 61.2 us -> 68 us  [body(): arrived = lax.ppermute(total, 'sp', ring).astype(jnp.float32)]
    ppermute x18, waiting for transfers between devices: 36.9 us -> 32.1 us  [swapped(): return lax.ppermute(array, 'fsdp', [(i, i ^ mask) for i in range(n_f)])]
    pallas_call x6, Pallas kernels: 15.3 us -> 12.1 us  [mix(): pl.pallas_call(functools.partial(mix_kernel, len(parts)), in_specs=[vmem]...]
    ppermute x6, waiting for transfers between devices: 59.7 us -> 57.1 us  [body(): blocks[k][c] = arrived = lax.ppermute(blocks[k - 1][c], 'sp', ring)]
  transfers between devices with their start and end apart: 42 -> 42, of which waited for: 20 -> 21; matrix products, arithmetic and copies ran while one was open for 3% -> 2% of each run, Pallas kernels for 17% -> 15%
where the time goes in v3:
time: 259 us; the launch traced here: 258 us
  waiting for transfers between devices  157 us (61%)
  Pallas kernels  37.9 us (15%)
  starting transfers between devices  31.9 us (12%)
  local copies, waits for them, and re-layouts  27 us (10%)
  other arithmetic  3.88 us (1%)
    ppermute x18, waiting for transfers between devices, body(): arrived = lax.ppermute(total, 'sp', ring).astype(jnp.float32)  68 us
    ppermute x6, waiting for transfers between devices, body(): blocks[k][c] = arrived = lax.ppermute(blocks[k - 1][c], 'sp', ring)  57.1 us
    ppermute x18, waiting for transfers between devices, swapped(): return lax.ppermute(array, 'fsdp', [(i, i ^ mask) for i in range(n_f)])  32.1 us
    unnamed x74, local copies, waits for them, and re-layouts  23.1 us
    pallas_call x1, Pallas kernels, project(): pl.pallas_call(functools.partial(project_kernel, at_rows, n_x, n_w, wide,...  21.2 us
    ppermute x18, starting transfers between devices, swapped(): return lax.ppermute(array, 'fsdp', [(i, i ^ mask) for i in range(n_f)])  13.1 us
    ppermute x18, starting transfers between devices, body(): arrived = lax.ppermute(total, 'sp', ring).astype(jnp.float32)  12.7 us
    pallas_call x6, Pallas kernels, mix(): pl.pallas_call(functools.partial(mix_kernel, len(parts)), in_specs=[vmem]...  12.1 us
  transfers between devices with their start and end apart: 42, of which 21 were waited for; matrix products, arithmetic and copies ran while one was open for 2% of the time, Pallas kernels for 15%

profile of v3, /device:TPU:0, one launch (start us, length us, event | category | flops | bytes accessed | tf_op | source)
XLA Modules:
  0.0 258.4 jit_solution(8621385824567795643)
XLA Ops:
  0.0 2.8 %constant_dynamic-update-slice_fusion.2 = bf16[640,1792]{1,0:T(8,128)(2,1)} fusion(bf16[640,1280]{1,0:T(8,128)(2,1)} %param.11), kind=kLoop, calls=%fused_computation.33 | loop fusion | bytes 3276800
  4.5 3.0 %collective-permute-start.9 = (bf16[640,1792]{1,0:T(8,128)(2,1)}, bf16[640,1792]{1,0:T(8,128)(2,1)}, u32[]{:S(2)}, u32[]{:S(2)}) collective-permute-start(bf16[640,1792]{1,0:T(8,128)(2,1)} %constant_dynamic-update-slice_fusion.refs_8_), channel_id=1, source_target_pairs={{0,16},{4,20},{8,24},{12,28},{16,0},{20,4},{24,8},{28,12},{1,17},{... | collective-permute-start | bytes 6881288 | tf_op jit(solution)/shard_map/ppermute | solution.py:268
  9.6 1.6 collective-permute-start
  12.1 15.3 %collective-permute-done.refs_2_ = bf16[128,2560]{1,0:T(8,128)(2,1)S(1)} collective-permute-done((bf16[128,2560]{1,0:T(8,128)(2,1)S(1)}, bf16[128,2560]{1,0:T(8,128)(2,1)S(1)}, u32[]{:S(2)}, u32[]{:S(2)}) %collective-permute-start) | collective-permute-done | bytes 655392 | tf_op jit(solution)/shard_map/ppermute | solution.py:340
  30.5 27.1 %collective-permute-done.9.refs_12_ = bf16[640,1792]{1,0:T(8,128)(2,1)} collective-permute-done((bf16[640,1792]{1,0:T(8,128)(2,1)}, bf16[640,1792]{1,0:T(8,128)(2,1)}, u32[]{:S(2)}, u32[]{:S(2)}) %collective-permute-start.9) | collective-permute-done | bytes 2293792 | tf_op jit(solution)/shard_map/ppermute | solution.py:268
  59.0 1.8 collective-permute-start.11
  66.8 13.4 %collective-permute-done.3.refs_5_ = bf16[128,2560]{1,0:T(8,128)(2,1)S(1)} collective-permute-done((bf16[128,2560]{1,0:T(8,128)(2,1)S(1)}, bf16[128,2560]{1,0:T(8,128)(2,1)S(1)}, u32[]{:S(2)}, u32[]{:S(2)}) %collective-permute-start.3) | collective-permute-done | bytes 655392 | tf_op jit(solution)/shard_map/ppermute | solution.py:340
  80.2 11.8 %collective-permute-done.4.refs_6_ = bf16[128,2560]{1,0:T(8,128)(2,1)S(1)} collective-permute-done((bf16[128,2560]{1,0:T(8,128)(2,1)S(1)}, bf16[128,2560]{1,0:T(8,128)(2,1)S(1)}, u32[]{:S(2)}, u32[]{:S(2)}) %collective-permute-start.4) | collective-permute-done | bytes 655392 | tf_op jit(solution)/shard_map/ppermute | solution.py:340
  95.2 16.6 %collective-permute-done.5.refs_7_ = bf16[128,2560]{1,0:T(8,128)(2,1)S(1)} collective-permute-done((bf16[128,2560]{1,0:T(8,128)(2,1)S(1)}, bf16[128,2560]{1,0:T(8,128)(2,1)S(1)}, u32[]{:S(2)}, u32[]{:S(2)}) %collective-permute-start.5) | collective-permute-done | bytes 655392 | tf_op jit(solution)/shard_map/ppermute | solution.py:340
  118.6 1.6 copy-done.7
  127.9 21.2 %project.1 = (bf16[512,1280]{1,0:T(8,128)(2,1)S(1)}, bf16[512,512]{1,0:T(8,128)(2,1)S(1)}) custom-call(bf16[128,2560]{1,0:T(8,128)(2,1)S(1)} %copy-done.12, bf16[128,2560]{1,0:T(8,128)(2,1)S(1)} %copy-done.14, bf16[128,2560]{1,0:T(8,128)(2,1)S(1)} %copy-done.16, bf16[128,2560]{1,0:T(8,128)(2,1)S(1)} %copy-done.20, bf16[128,2560]{1,0:T(8,128)(2,1)S(1)} %copy-done.18, ...), custom_call_target="tpu_custom_call" | custom-call | flops 9395240960 | bytes 25427968 | tf_op jit(solution)/shard_map/project/pallas_call | solution.py:133
  149.1 3.9 %attend.1.heads_ref = bf16[512,1280]{1,0:T(8,128)(2,1)S(1)} custom-call(s32[1]{0:T(128)} %bitcast.s_ref, bf16[512,1280]{1,0:T(8,128)(2,1)S(1)} %get-tuple-element.55.q_ref, bf16[512,512]{1,0:T(8,128)(2,1)S(1)} %get-tuple-element.56.k_ref.v_ref, bf16[512,512]{1,0:T(8,128)(2,1)S(1)} %get-tuple-element.56.k_ref.v_ref), custom_call_target="tpu_custom_call" | custom-call | flops 1342177280 | bytes 3932160 | tf_op jit(solution)/shard_map/attend/pallas_call | solution.py:208
  153.1 1.8 mix.6
  157.5 2.6 %mix.7 = (bf16[128,640]{1,0:T(8,128)(2,1)S(1)}, bf16[128,640]{1,0:T(8,128)(2,1)S(1)}, bf16[128,640]{1,0:T(8,128)(2,1)S(1)}, bf16[128,640]{1,0:T(8,128)(2,1)S(1)}) custom-call(bf16[512,1280]{1,0:T(8,128)(2,1)S(1)} %copy-done.28, bf16[640,1280]{1,0:T(8,128)(2,1)} %collective-permute-done.18.refs_0_), custom_call_target="tpu_custom_call" | custom-call | flops 838860800 | bytes 3604480 | tf_op jit(solution)/shard_map/mix/pallas_call | solution.py:252
  162.0 2.3 collective-permute-done.15
  165.3 2.7 %collective-permute-done.19 = bf16[128,640]{1,0:T(8,128)(2,1)S(1)} collective-permute-done((bf16[128,640]{1,0:T(8,128)(2,1)S(1)}, bf16[128,640]{1,0:T(8,128)(2,1)S(1)}, u32[]{:S(2)}, u32[]{:S(2)}) %collective-permute-start.19) | collective-permute-done | bytes 163872 | tf_op jit(solution)/shard_map/ppermute | solution.py:376
  168.1 5.3 %collective-permute-done.16 = bf16[128,640]{1,0:T(8,128)(2,1)S(1)} collective-permute-done((bf16[128,640]{1,0:T(8,128)(2,1)S(1)}, bf16[128,640]{1,0:T(8,128)(2,1)S(1)}, u32[]{:S(2)}, u32[]{:S(2)}) %collective-permute-start.16) | collective-permute-done | bytes 163872 | tf_op jit(solution)/shard_map/ppermute | solution.py:376
  173.4 2.5 collective-permute-done.20
  176.0 4.4 %collective-permute-done.33.refs_1_ = bf16[320,1280]{1,0:T(8,128)(2,1)S(1)} collective-permute-done((bf16[320,1280]{1,0:T(8,128)(2,1)S(1)}, bf16[320,1280]{1,0:T(8,128)(2,1)S(1)}, u32[]{:S(2)}, u32[]{:S(2)}) %collective-permute-start.33) | collective-permute-done | bytes 819232 | tf_op jit(solution)/shard_map/ppermute | solution.py:268
  182.5 3.9 %collective-permute-start.34 = (bf16[128,640]{1,0:T(8,128)(2,1)S(1)}, bf16[128,640]{1,0:T(8,128)(2,1)S(1)}, u32[]{:S(2)}, u32[]{:S(2)}) collective-permute-start(bf16[128,640]{1,0:T(8,128)(2,1)S(1)} %get-tuple-element.79), channel_id=1, source_target_pairs={{0,1},{1,2},{2,3},{3,0},{4,5},{5,6},{6,7},{7,4},{8,9},{9,10},{10,1... | collective-permute-start | bytes 491528 | tf_op jit(solution)/shard_map/ppermute | solution.py:376
  186.6 4.2 %collective-permute-done.34 = bf16[128,640]{1,0:T(8,128)(2,1)S(1)} collective-permute-done((bf16[128,640]{1,0:T(8,128)(2,1)S(1)}, bf16[128,640]{1,0:T(8,128)(2,1)S(1)}, u32[]{:S(2)}, u32[]{:S(2)}) %collective-permute-start.34) | collective-permute-done | bytes 163872 | tf_op jit(solution)/shard_map/ppermute | solution.py:376
  191.9 2.2 mix.8
  195.4 4.3 %collective-permute-done.35 = bf16[128,640]{1,0:T(8,128)(2,1)S(1)} collective-permute-done((bf16[128,640]{1,0:T(8,128)(2,1)S(1)}, bf16[128,640]{1,0:T(8,128)(2,1)S(1)}, u32[]{:S(2)}, u32[]{:S(2)}) %collective-permute-start.35) | collective-permute-done | bytes 163872 | tf_op jit(solution)/shard_map/ppermute | solution.py:376
  199.8 2.2 mix.9
  203.0 3.2 %collective-permute-done.24 = bf16[128,1280]{1,0:T(8,128)(2,1)S(1)} collective-permute-done((bf16[128,1280]{1,0:T(8,128)(2,1)S(1)}, bf16[128,1280]{1,0:T(8,128)(2,1)S(1)}, u32[]{:S(2)}, u32[]{:S(2)}) %collective-permute-start.24) | collective-permute-done | bytes 327712 | tf_op jit(solution)/shard_map/ppermute | solution.py:376
  206.4 9.2 %collective-permute-done.29 = bf16[128,1280]{1,0:T(8,128)(2,1)S(1)} collective-permute-done((bf16[128,1280]{1,0:T(8,128)(2,1)S(1)}, bf16[128,1280]{1,0:T(8,128)(2,1)S(1)}, u32[]{:S(2)}, u32[]{:S(2)}) %collective-permute-start.29) | collective-permute-done | bytes 327712 | tf_op jit(solution)/shard_map/ppermute | solution.py:376
  216.7 5.9 %collective-permute-done.25 = bf16[128,1280]{1,0:T(8,128)(2,1)S(1)} collective-permute-done((bf16[128,1280]{1,0:T(8,128)(2,1)S(1)}, bf16[128,1280]{1,0:T(8,128)(2,1)S(1)}, u32[]{:S(2)}, u32[]{:S(2)}) %collective-permute-start.25) | collective-permute-done | bytes 327712 | tf_op jit(solution)/shard_map/ppermute | solution.py:376
  226.5 3.2 %collective-permute-done.30 = bf16[128,1280]{1,0:T(8,128)(2,1)S(1)} collective-permute-done((bf16[128,1280]{1,0:T(8,128)(2,1)S(1)}, bf16[128,1280]{1,0:T(8,128)(2,1)S(1)}, u32[]{:S(2)}, u32[]{:S(2)}) %collective-permute-start.30) | collective-permute-done | bytes 327712 | tf_op jit(solution)/shard_map/ppermute | solution.py:376
  230.8 9.4 %collective-permute-done.39 = bf16[128,640]{1,0:T(8,128)(2,1)S(1)} collective-permute-done((bf16[128,640]{1,0:T(8,128)(2,1)S(1)}, bf16[128,640]{1,0:T(8,128)(2,1)S(1)}, u32[]{:S(2)}, u32[]{:S(2)}) %collective-permute-start.39) | collective-permute-done | bytes 163872 | tf_op jit(solution)/shard_map/ppermute | solution.py:376
  241.4 5.8 %collective-permute-done.31 = bf16[128,1280]{1,0:T(8,128)(2,1)S(1)} collective-permute-done((bf16[128,1280]{1,0:T(8,128)(2,1)S(1)}, bf16[128,1280]{1,0:T(8,128)(2,1)S(1)}, u32[]{:S(2)}, u32[]{:S(2)}) %collective-permute-start.31) | collective-permute-done | bytes 327712 | tf_op jit(solution)/shard_map/ppermute | solution.py:376
  247.4 2.8 %collective-permute-done.40 = bf16[128,640]{1,0:T(8,128)(2,1)S(1)} collective-permute-done((bf16[128,640]{1,0:T(8,128)(2,1)S(1)}, bf16[128,640]{1,0:T(8,128)(2,1)S(1)}, u32[]{:S(2)}, u32[]{:S(2)}) %collective-permute-start.40) | collective-permute-done | bytes 163872 | tf_op jit(solution)/shard_map/ppermute | solution.py:376
  250.3 7.3 %collective-permute-done.41 = bf16[128,640]{1,0:T(8,128)(2,1)S(1)} collective-permute-done((bf16[128,640]{1,0:T(8,128)(2,1)S(1)}, bf16[128,640]{1,0:T(8,128)(2,1)S(1)}, u32[]{:S(2)}, u32[]{:S(2)}) %collective-permute-start.41) | collective-permute-done | bytes 163872 | tf_op jit(solution)/shard_map/ppermute | solution.py:376
  (170 shorter events, 52.5 us)
Async XLA Ops:
  4.5 53.1 %collective-permute-start.9 = (bf16[640,1792]{1,0:T(8,128)(2,1)}, bf16[640,1792]{1,0:T(8,128)(2,1)}, u32[]{:S(2)}, u32[]{:S(2)}) collective-permute-start(bf16[640,1792]{1,0:T(8,128)(2,1)} %constant_dynamic-update-slice_fusion.refs_8_), channel_id=1, source_target_pairs={{0,16},{4,20},{8,24},{12,28},{16,0},{20,4},{24,8},{28,12},{1,17},{... | collective-permute-start | bytes 6881288 | tf_op jit(solution)/shard_map/ppermute | solution.py:268
  7.4 56.5 %collective-permute-start.7 = (bf16[640,1792]{1,0:T(8,128)(2,1)}, bf16[640,1792]{1,0:T(8,128)(2,1)}, u32[]{:S(2)}, u32[]{:S(2)}) collective-permute-start(bf16[640,1792]{1,0:T(8,128)(2,1)} %constant_dynamic-update-slice_fusion.refs_8_), channel_id=1, source_target_pairs={{0,8},{4,12},{8,0},{12,4},{16,24},{20,28},{24,16},{28,20},{1,9},{5... | collective-permute-start | bytes 6881288 | tf_op jit(solution)/shard_map/ppermute | solution.py:268
  9.6 17.8 %collective-permute-start = (bf16[128,2560]{1,0:T(8,128)(2,1)S(1)}, bf16[128,2560]{1,0:T(8,128)(2,1)S(1)}, u32[]{:S(2)}, u32[]{:S(2)}) collective-permute-start(bf16[128,2560]{1,0:T(8,128)(2,1)S(1)} %get-tuple-element.47.refs_0_), channel_id=1, source_target_pairs={{0,1},{1,2},{2,3},{3,0},{4,5},{5,6},{6,7},{7,4},{8,9},{9,10},{10,1... | collective-permute-start | bytes 1966088 | tf_op jit(solution)/shard_map/ppermute | solution.py:340
  27.5 31.5 %collective-permute-start.2 = (bf16[128,2560]{1,0:T(8,128)(2,1)S(1)}, bf16[128,2560]{1,0:T(8,128)(2,1)S(1)}, u32[]{:S(2)}, u32[]{:S(2)}) collective-permute-start(bf16[128,2560]{1,0:T(8,128)(2,1)S(1)} %collective-permute-done.refs_2_), channel_id=1, source_target_pairs={{0,1},{1,2},{2,3},{3,0},{4,5},{5,6},{6,7},{7,4},{8,9},{9,10},{10,1... | collective-permute-start | bytes 1966088 | tf_op jit(solution)/shard_map/ppermute | solution.py:340
  28.3 32.4 %collective-permute-start.1 = (bf16[128,2560]{1,0:T(8,128)(2,1)S(1)}, bf16[128,2560]{1,0:T(8,128)(2,1)S(1)}, u32[]{:S(2)}, u32[]{:S(2)}) collective-permute-start(bf16[128,2560]{1,0:T(8,128)(2,1)S(1)} %get-tuple-element.48.refs_1_), channel_id=1, source_target_pairs={{0,1},{1,2},{2,3},{3,0},{4,5},{5,6},{6,7},{7,4},{8,9},{9,10},{10,1... | collective-permute-start | bytes 1966088 | tf_op jit(solution)/shard_map/ppermute | solution.py:340
  59.0 33.9 %collective-permute-start.11 = (bf16[320,1792]{1,0:T(8,128)(2,1)S(1)}, bf16[320,1792]{1,0:T(8,128)(2,1)S(1)}, u32[]{:S(2)}, u32[]{:S(2)}) collective-permute-start(bf16[320,1792]{1,0:T(8,128)(2,1)S(1)} %slice.32), channel_id=1, source_target_pairs={{0,8},{4,12},{8,0},{12,4},{16,24},{20,28},{24,16},{28,20},{1,9},{5... | collective-permute-start | bytes 3440648 | tf_op jit(solution)/shard_map/ppermute | solution.py:268
  60.8 19.5 %collective-permute-start.3 = (bf16[128,2560]{1,0:T(8,128)(2,1)S(1)}, bf16[128,2560]{1,0:T(8,128)(2,1)S(1)}, u32[]{:S(2)}, u32[]{:S(2)}) collective-permute-start(bf16[128,2560]{1,0:T(8,128)(2,1)S(1)} %collective-permute-done.1.refs_3_), channel_id=1, source_target_pairs={{0,1},{1,2},{2,3},{3,0},{4,5},{5,6},{6,7},{7,4},{8,9},{9,10},{10,1... | collective-permute-start | bytes 1966088 | tf_op jit(solution)/shard_map/ppermute | solution.py:340
  62.3 29.6 %collective-permute-start.4 = (bf16[128,2560]{1,0:T(8,128)(2,1)S(1)}, bf16[128,2560]{1,0:T(8,128)(2,1)S(1)}, u32[]{:S(2)}, u32[]{:S(2)}) collective-permute-start(bf16[128,2560]{1,0:T(8,128)(2,1)S(1)} %collective-permute-done.2.refs_4_), channel_id=1, source_target_pairs={{0,1},{1,2},{2,3},{3,0},{4,5},{5,6},{6,7},{7,4},{8,9},{9,10},{10,1... | collective-permute-start | bytes 1966088 | tf_op jit(solution)/shard_map/ppermute | solution.py:340
  65.3 28.4 %collective-permute-start.12 = (bf16[320,1792]{1,0:T(8,128)(2,1)S(1)}, bf16[320,1792]{1,0:T(8,128)(2,1)}, u32[]{:S(2)}, u32[]{:S(2)}) collective-permute-start(bf16[320,1792]{1,0:T(8,128)(2,1)S(1)} %slice.33), channel_id=1, source_target_pairs={{0,16},{4,20},{8,24},{12,28},{16,0},{20,4},{24,8},{28,12},{1,17},{... | collective-permute-start | bytes 3440648 | tf_op jit(solution)/shard_map/ppermute | solution.py:268
  66.8 46.0 %collective-permute-start.6 = (bf16[640,1792]{1,0:T(8,128)(2,1)}, bf16[640,1792]{1,0:T(8,128)(2,1)S(1)}, u32[]{:S(2)}, u32[]{:S(2)}) collective-permute-start(bf16[640,1792]{1,0:T(8,128)(2,1)} %constant_dynamic-update-slice_fusion.refs_8_), channel_id=1, source_target_pairs={{0,4},{4,0},{8,12},{12,8},{16,20},{20,16},{24,28},{28,24},{1,5},{5... | collective-permute-start | bytes 6881288 | tf_op jit(solution)/shard_map/ppermute | solution.py:268
  80.2 38.4 %collective-permute-start.10 = (bf16[640,1792]{1,0:T(8,128)(2,1)}, bf16[640,1792]{1,0:T(8,128)(2,1)}, u32[]{:S(2)}, u32[]{:S(2)}) collective-permute-start(bf16[640,1792]{1,0:T(8,128)(2,1)} %collective-permute-done.9.refs_12_), channel_id=1, source_target_pairs={{0,4},{4,0},{8,12},{12,8},{16,20},{20,16},{24,28},{28,24},{1,5},{5... | collective-permute-start | bytes 6881288 | tf_op jit(solution)/shard_map/ppermute | solution.py:268
  92.8 25.8 %collective-permute-start.8 = (bf16[640,1792]{1,0:T(8,128)(2,1)}, bf16[640,1792]{1,0:T(8,128)(2,1)}, u32[]{:S(2)}, u32[]{:S(2)}) collective-permute-start(bf16[640,1792]{1,0:T(8,128)(2,1)} %collective-permute-done.7.refs_10_), channel_id=1, source_target_pairs={{0,4},{4,0},{8,12},{12,8},{16,20},{20,16},{24,28},{28,24},{1,5},{5... | collective-permute-start | bytes 6881288 | tf_op jit(solution)/shard_map/ppermute | solution.py:268
  92.8 18.9 %collective-permute-start.5 = (bf16[128,2560]{1,0:T(8,128)(2,1)S(1)}, bf16[128,2560]{1,0:T(8,128)(2,1)S(1)}, u32[]{:S(2)}, u32[]{:S(2)}) collective-permute-start(bf16[128,2560]{1,0:T(8,128)(2,1)S(1)} %collective-permute-done.3.refs_5_), channel_id=1, source_target_pairs={{0,1},{1,2},{2,3},{3,0},{4,5},{5,6},{6,7},{7,4},{8,9},{9,10},{10,1... | collective-permute-start | bytes 1966088 | tf_op jit(solution)/shard_map/ppermute | solution.py:340
  93.7 21.1 %collective-permute-start.13 = (bf16[320,1792]{1,0:T(8,128)(2,1)S(1)}, bf16[320,1792]{1,0:T(8,128)(2,1)}, u32[]{:S(2)}, u32[]{:S(2)}) collective-permute-start(bf16[320,1792]{1,0:T(8,128)(2,1)S(1)} %collective-permute-done.11.refs_14_), channel_id=1, source_target_pairs={{0,4},{4,0},{8,12},{12,8},{16,20},{20,16},{24,28},{28,24},{1,5},{5... | collective-permute-start | bytes 3440648 | tf_op jit(solution)/shard_map/ppermute | solution.py:268
  114.2 42.0 %collective-permute-start.18 = (bf16[640,1280]{1,0:T(8,128)(2,1)}, bf16[640,1280]{1,0:T(8,128)(2,1)}, u32[]{:S(2)}, u32[]{:S(2)}) collective-permute-start(bf16[640,1280]{1,0:T(8,128)(2,1)} %refs_0_.1), channel_id=1, source_target_pairs={{0,4},{4,0},{8,12},{12,8},{16,20},{20,16},{24,28},{28,24},{1,5},{5... | collective-permute-start | bytes 4915208 | tf_op jit(solution)/shard_map/ppermute | solution.py:268
  114.8 45.5 %collective-permute-start.22 = (bf16[640,1280]{1,0:T(8,128)(2,1)}, bf16[640,1280]{1,0:T(8,128)(2,1)S(1)}, u32[]{:S(2)}, u32[]{:S(2)}) collective-permute-start(bf16[640,1280]{1,0:T(8,128)(2,1)} %refs_0_.1), channel_id=1, source_target_pairs={{0,8},{4,12},{8,0},{12,4},{16,24},{20,28},{24,16},{28,20},{1,9},{5... | collective-permute-start | bytes 4915208 | tf_op jit(solution)/shard_map/ppermute | solution.py:268
  115.8 45.1 %collective-permute-start.27 = (bf16[640,1280]{1,0:T(8,128)(2,1)}, bf16[640,1280]{1,0:T(8,128)(2,1)S(1)}, u32[]{:S(2)}, u32[]{:S(2)}) collective-permute-start(bf16[640,1280]{1,0:T(8,128)(2,1)} %refs_0_.1), channel_id=1, source_target_pairs={{0,16},{4,20},{8,24},{12,28},{16,0},{20,4},{24,8},{28,12},{1,17},{... | collective-permute-start | bytes 4915208 | tf_op jit(solution)/shard_map/ppermute | solution.py:268
  160.3 20.1 %collective-permute-start.33 = (bf16[320,1280]{1,0:T(8,128)(2,1)S(1)}, bf16[320,1280]{1,0:T(8,128)(2,1)S(1)}, u32[]{:S(2)}, u32[]{:S(2)}) collective-permute-start(bf16[320,1280]{1,0:T(8,128)(2,1)S(1)} %slice.39), channel_id=1, source_target_pairs={{0,16},{4,20},{8,24},{12,28},{16,0},{20,4},{24,8},{28,12},{1,17},{... | collective-permute-start | bytes 2457608 | tf_op jit(solution)/shard_map/ppermute | solution.py:268
  161.0 19.9 %collective-permute-start.32 = (bf16[320,1280]{1,0:T(8,128)(2,1)S(1)}, bf16[320,1280]{1,0:T(8,128)(2,1)S(1)}, u32[]{:S(2)}, u32[]{:S(2)}) collective-permute-start(bf16[320,1280]{1,0:T(8,128)(2,1)S(1)} %slice.38), channel_id=1, source_target_pairs={{0,8},{4,12},{8,0},{12,4},{16,24},{20,28},{24,16},{28,20},{1,9},{5... | collective-permute-start | bytes 2457608 | tf_op jit(solution)/shard_map/ppermute | solution.py:268
  162.0 29.9 %collective-permute-start.23 = (bf16[640,1280]{1,0:T(8,128)(2,1)S(1)}, bf16[640,1280]{1,0:T(8,128)(2,1)S(1)}, u32[]{:S(2)}, u32[]{:S(2)}) collective-permute-start(bf16[640,1280]{1,0:T(8,128)(2,1)S(1)} %collective-permute-done.22.refs_0_), channel_id=1, source_target_pairs={{0,4},{4,0},{8,12},{12,8},{16,20},{20,16},{24,28},{28,24},{1,5},{5... | collective-permute-start | bytes 4915208 | tf_op jit(solution)/shard_map/ppermute | solution.py:268
  173.4 26.4 %collective-permute-start.28 = (bf16[640,1280]{1,0:T(8,128)(2,1)S(1)}, bf16[640,1280]{1,0:T(8,128)(2,1)S(1)}, u32[]{:S(2)}, u32[]{:S(2)}) collective-permute-start(bf16[640,1280]{1,0:T(8,128)(2,1)S(1)} %collective-permute-done.27.refs_0_), channel_id=1, source_target_pairs={{0,4},{4,0},{8,12},{12,8},{16,20},{20,16},{24,28},{28,24},{1,5},{5... | collective-permute-start | bytes 4915208 | tf_op jit(solution)/shard_map/ppermute | solution.py:268
  180.4 11.4 %collective-permute-start.21 = (bf16[128,640]{1,0:T(8,128)(2,1)S(1)}, bf16[128,640]{1,0:T(8,128)(2,1)S(1)}, u32[]{:S(2)}, u32[]{:S(2)}) collective-permute-start(bf16[128,640]{1,0:T(8,128)(2,1)S(1)} %add_convert_fusion.13), channel_id=1, source_target_pairs={{0,1},{1,2},{2,3},{3,0},{4,5},{5,6},{6,7},{7,4},{8,9},{9,10},{10,1... | collective-permute-start | bytes 491528 | tf_op jit(solution)/shard_map/ppermute | solution.py:376
  194.1 12.1 %collective-permute-start.24 = (bf16[128,1280]{1,0:T(8,128)(2,1)S(1)}, bf16[128,1280]{1,0:T(8,128)(2,1)S(1)}, u32[]{:S(2)}, u32[]{:S(2)}) collective-permute-start(bf16[128,1280]{1,0:T(8,128)(2,1)S(1)} %get-tuple-element.68), channel_id=1, source_target_pairs={{0,1},{1,2},{2,3},{3,0},{4,5},{5,6},{6,7},{7,4},{8,9},{9,10},{10,1... | collective-permute-start | bytes 983048 | tf_op jit(solution)/shard_map/ppermute | solution.py:376
  199.7 50.5 %collective-permute-start.36 = (bf16[128,640]{1,0:T(8,128)(2,1)S(1)}, bf16[128,640]{1,0:T(8,128)(2,1)S(1)}, u32[]{:S(2)}, u32[]{:S(2)}) collective-permute-start(bf16[128,640]{1,0:T(8,128)(2,1)S(1)} %add_convert_fusion.10), channel_id=1, source_target_pairs={{0,1},{1,2},{2,3},{3,0},{4,5},{5,6},{6,7},{7,4},{8,9},{9,10},{10,1... | collective-permute-start | bytes 491528 | tf_op jit(solution)/shard_map/ppermute | solution.py:376
  202.0 21.7 %collective-permute-start.38 = (bf16[320,1280]{1,0:T(8,128)(2,1)S(1)}, bf16[320,1280]{1,0:T(8,128)(2,1)S(1)}, u32[]{:S(2)}, u32[]{:S(2)}) collective-permute-start(bf16[320,1280]{1,0:T(8,128)(2,1)S(1)} %collective-permute-done.33.refs_1_), channel_id=1, source_target_pairs={{0,4},{4,0},{8,12},{12,8},{16,20},{20,16},{24,28},{28,24},{1,5},{5... | collective-permute-start | bytes 2457608 | tf_op jit(solution)/shard_map/ppermute | solution.py:268
  202.1 21.6 %collective-permute-start.37 = (bf16[320,1280]{1,0:T(8,128)(2,1)S(1)}, bf16[320,1280]{1,0:T(8,128)(2,1)S(1)}, u32[]{:S(2)}, u32[]{:S(2)}) collective-permute-start(bf16[320,1280]{1,0:T(8,128)(2,1)S(1)} %collective-permute-done.32.refs_0_), channel_id=1, source_target_pairs={{0,4},{4,0},{8,12},{12,8},{16,20},{20,16},{24,28},{28,24},{1,5},{5... | collective-permute-start | bytes 2457608 | tf_op jit(solution)/shard_map/ppermute | solution.py:268
  202.6 13.0 %collective-permute-start.29 = (bf16[128,1280]{1,0:T(8,128)(2,1)S(1)}, bf16[128,1280]{1,0:T(8,128)(2,1)S(1)}, u32[]{:S(2)}, u32[]{:S(2)}) collective-permute-start(bf16[128,1280]{1,0:T(8,128)(2,1)S(1)} %get-tuple-element.73), channel_id=1, source_target_pairs={{0,1},{1,2},{2,3},{3,0},{4,5},{5,6},{6,7},{7,4},{8,9},{9,10},{10,1... | collective-permute-start | bytes 983048 | tf_op jit(solution)/shard_map/ppermute | solution.py:376
  206.3 16.3 %collective-permute-start.25 = (bf16[128,1280]{1,0:T(8,128)(2,1)S(1)}, bf16[128,1280]{1,0:T(8,128)(2,1)S(1)}, u32[]{:S(2)}, u32[]{:S(2)}) collective-permute-start(bf16[128,1280]{1,0:T(8,128)(2,1)S(1)} %add_convert_fusion.5), channel_id=1, source_target_pairs={{0,1},{1,2},{2,3},{3,0},{4,5},{5,6},{6,7},{7,4},{8,9},{9,10},{10,1... | collective-permute-start | bytes 983048 | tf_op jit(solution)/shard_map/ppermute | solution.py:376
  215.7 14.0 %collective-permute-start.30 = (bf16[128,1280]{1,0:T(8,128)(2,1)S(1)}, bf16[128,1280]{1,0:T(8,128)(2,1)S(1)}, u32[]{:S(2)}, u32[]{:S(2)}) collective-permute-start(bf16[128,1280]{1,0:T(8,128)(2,1)S(1)} %add_convert_fusion.2), channel_id=1, source_target_pairs={{0,1},{1,2},{2,3},{3,0},{4,5},{5,6},{6,7},{7,4},{8,9},{9,10},{10,1... | collective-permute-start | bytes 983048 | tf_op jit(solution)/shard_map/ppermute | solution.py:376
  222.7 18.5 %collective-permute-start.26 = (bf16[128,1280]{1,0:T(8,128)(2,1)S(1)}, bf16[128,1280]{1,0:T(8,128)(2,1)S(1)}, u32[]{:S(2)}, u32[]{:S(2)}) collective-permute-start(bf16[128,1280]{1,0:T(8,128)(2,1)S(1)} %add_convert_fusion.4), channel_id=1, source_target_pairs={{0,1},{1,2},{2,3},{3,0},{4,5},{5,6},{6,7},{7,4},{8,9},{9,10},{10,1... | collective-permute-start | bytes 983048 | tf_op jit(solution)/shard_map/ppermute | solution.py:376
  225.3 14.9 %collective-permute-start.39 = (bf16[128,640]{1,0:T(8,128)(2,1)S(1)}, bf16[128,640]{1,0:T(8,128)(2,1)S(1)}, u32[]{:S(2)}, u32[]{:S(2)}) collective-permute-start(bf16[128,640]{1,0:T(8,128)(2,1)S(1)} %get-tuple-element.85), channel_id=1, source_target_pairs={{0,1},{1,2},{2,3},{3,0},{4,5},{5,6},{6,7},{7,4},{8,9},{9,10},{10,1... | collective-permute-start | bytes 491528 | tf_op jit(solution)/shard_map/ppermute | solution.py:376
  229.7 17.5 %collective-permute-start.31 = (bf16[128,1280]{1,0:T(8,128)(2,1)S(1)}, bf16[128,1280]{1,0:T(8,128)(2,1)S(1)}, u32[]{:S(2)}, u32[]{:S(2)}) collective-permute-start(bf16[128,1280]{1,0:T(8,128)(2,1)S(1)} %add_convert_fusion.1), channel_id=1, source_target_pairs={{0,1},{1,2},{2,3},{3,0},{4,5},{5,6},{6,7},{7,4},{8,9},{9,10},{10,1... | collective-permute-start | bytes 983048 | tf_op jit(solution)/shard_map/ppermute | solution.py:376
  (46 other events, 430.6 us)

commit v4 on v0

v4 whole, which is shorter than its diff:
```python
import functools

import jax
import jax.numpy as jnp
import numpy as np
from jax import lax
from jax.experimental import pallas as pl
from jax.experimental.pallas import tpu as pltpu
from jax.sharding import PartitionSpec as P

HEAD_SIZE = 128
HALF = HEAD_SIZE // 2
ROPE_BASE = 1000000.0
LOG2E = 1.4426950408889634
NT = (((1,), (1,)), ((), ()))
VMEM = pl.BlockSpec(memory_space=pltpu.VMEM)
SMEM = pl.BlockSpec(memory_space=pltpu.SMEM)
ANY = pl.BlockSpec(memory_space=pl.ANY)


def params(mib):
    return pltpu.CompilerParams(vmem_limit_bytes=mib * 1024 * 1024)


def bf16(*shape):
    return jax.ShapeDtypeStruct(shape, jnp.bfloat16)


def work(flops, *arrays):
    size = sum(int(np.prod(x.shape)) * x.dtype.itemsize for x in arrays)
    return pl.CostEstimate(flops=flops, bytes_accessed=size, transcendentals=0)


def normed_kernel(n_f, me_ref, tokens_ref, gain_ref, out_ref):
    rows = tokens_ref[...].astype(jnp.float32)
    scale = lax.rsqrt(jnp.mean(rows * rows, axis=-1, keepdims=True) + 1e-06)
    shard = tokens_ref.shape[1] // n_f
    for j in range(n_f):
        start = pl.multiple_of(jnp.bitwise_xor(me_ref[0], j) * shard, 128)
        columns = pl.ds(start, shard)
        piece = tokens_ref[:, columns].astype(jnp.float32) * scale * gain_ref[:, columns]
        out_ref[:, j * shard : (j + 1) * shard] = piece.astype(jnp.bfloat16)


def normed_pieces(me, tokens, gain, n_f):
    count, width = tokens.shape
    shard = width // n_f
    if shard % 128 == 0:
        return pl.pallas_call(
            functools.partial(normed_kernel, n_f),
            out_shape=bf16(count, width),
            in_specs=[SMEM, VMEM, VMEM],
            out_specs=VMEM,
            compiler_params=params(16),
            cost_estimate=work(6 * count * width, tokens, tokens),
            name="norm",
        )(me[None], tokens, gain[None, :])
    rows = tokens.astype(jnp.float32)
    meansq = jnp.mean(rows * rows, axis=-1, keepdims=True)
    normed = (rows * lax.rsqrt(meansq + 1e-06) * gain).astype(jnp.bfloat16)
    pieces = [
        lax.dynamic_slice_in_dim(normed, jnp.bitwise_xor(me, j) * shard, shard, axis=1)
        for j in range(n_f)
    ]
    return jnp.concatenate(pieces, axis=1)


def pack_kernel(q_ref, k_ref, v_ref, first_ref, second_ref):
    q_cols, kv_cols, cut = q_ref.shape[1], k_ref.shape[1], first_ref.shape[1]
    first_ref[...] = q_ref[:, :cut]
    second_ref[:, : q_cols - cut] = q_ref[:, cut:]
    second_ref[:, q_cols - cut : q_cols - cut + kv_cols] = k_ref[...]
    second_ref[:, q_cols - cut + kv_cols :] = v_ref[...]


def pack(q, k, v, cut):
    rows = q.shape[0]
    total = q.shape[1] + 2 * k.shape[1]
    return pl.pallas_call(
        pack_kernel,
        in_specs=[VMEM] * 3,
        out_specs=[VMEM] * 2,
        out_shape=[bf16(rows, cut), bf16(rows, total - cut)],
        compiler_params=params(16),
        cost_estimate=work(0, q, k, v, q, k, v),
        name="pack",
    )(q, k, v)


def cut_kernel(w_ref, first_ref, second_ref):
    cut = first_ref.shape[0]
    first_ref[...] = w_ref[:cut, :]
    second_ref[...] = w_ref[cut:, :]


def cut_rows(w, cut):
    rows, columns = w.shape
    return pl.pallas_call(
        cut_kernel,
        in_specs=[VMEM],
        out_specs=[VMEM] * 2,
        out_shape=[bf16(cut, columns), bf16(rows - cut, columns)],
        compiler_params=params(16),
        cost_estimate=work(0, w, w),
        name="cut",
    )(w)


def partial_kernel(n_x, n_r, wide, *refs):
    x_refs, w_refs, (out_ref, rows) = refs[:n_x], refs[n_x:-2], refs[-2:]
    count = x_refs[0].shape[0]
    shard = w_refs[0].shape[0]
    for i, x_ref in enumerate(x_refs):
        rows[i * count : (i + 1) * count, :] = x_ref[:, : rows.shape[1]]
    base = 0
    for h in range(2):
        half = w_refs[2 * n_r * h : 2 * n_r * (h + 1)]
        for at in range(0, half[0].shape[1], wide):
            total = None
            for j, w_ref in enumerate(half):
                term = jnp.dot(
                    rows[:, j * shard : (j + 1) * shard],
                    w_ref[:, at : at + wide],
                    preferred_element_type=jnp.float32,
                )
                total = term if total is None else total + term
            out_ref[:, base + at : base + at + wide] = total
        base += half[0].shape[1]


def partial(blocks, first, second, wide):
    n_x, n_r = len(blocks), len(first) // 2
    count = blocks[0].shape[0]
    depth = 2 * n_r * first[0].shape[0]
    columns = first[0].shape[1] + second[0].shape[1]
    out = jax.ShapeDtypeStruct((n_x * count, columns), jnp.float32)
    return pl.pallas_call(
        functools.partial(partial_kernel, n_x, n_r, wide),
        in_specs=[VMEM] * (n_x + 4 * n_r),
        out_specs=VMEM,
        out_shape=out,
        scratch_shapes=[pltpu.VMEM((n_x * count, depth), jnp.bfloat16)],
        compiler_params=params(16),
        cost_estimate=work(
            2 * n_x * count * depth * columns, *blocks, *first, *second, out
        ),
        name="partial",
    )(*blocks, *first, *second)


def rope_tile(tile, cos, sin):
    parts = []
    for at in range(0, tile.shape[1], HEAD_SIZE):
        head = tile[:, at : at + HEAD_SIZE]
        parts.append(head * cos + pltpu.roll(head, HALF, axis=1) * sin)
    return parts[0] if len(parts) == 1 else jnp.concatenate(parts, axis=1)


def finish_kernel(n_x, wide, roped, first_col, s_ref, *refs):
    x_refs = refs[:n_x]
    w_refs = refs[n_x : n_x + 4]
    early_ref, late_ref = refs[n_x + 4 : n_x + 6]
    bias_refs, (cos_ref, sin_ref) = refs[n_x + 6 : n_x + 9], refs[n_x + 9 : n_x + 11]
    q_out, kv_out, rows, cos, sin = refs[n_x + 11 :]
    count = x_refs[0].shape[0]
    shard = w_refs[0].shape[0]
    cut = early_ref.shape[0]
    for i, x_ref in enumerate(x_refs):
        here = slice(i * count, (i + 1) * count)
        rows[here, :] = x_ref[:, first_col : first_col + 2 * shard]
        place = pl.ds(pl.multiple_of(lax.rem(s_ref[0] - i + n_x, n_x) * count, count), count)
        cos[here, :] = cos_ref[place, :]
        sin[here, :] = sin_ref[place, :]
    q_cols = q_out.shape[1]

    def bias_tile(col):
        for bias_ref in bias_refs:
            if col < bias_ref.shape[0]:
                return bias_ref[pl.ds(col, wide)][None, :]
            col -= bias_ref.shape[0]

    base = 0
    for mine, sibling in (w_refs[:2], w_refs[2:]):
        for at in range(0, mine.shape[1], wide):
            total = jnp.dot(
                rows[:, :shard], mine[:, at : at + wide], preferred_element_type=jnp.float32
            )
            total = total + jnp.dot(
                rows[:, shard:], sibling[:, at : at + wide], preferred_element_type=jnp.float32
            )
            col = base + at
            total = total + jnp.concatenate(
                [early_ref[:, col : col + wide], late_ref[:, col : col + wide]], axis=0
            )
            total = total + bias_tile(col)
            if col < roped:
                total = rope_tile(total, cos[...], sin[...])
            total = total.astype(jnp.bfloat16)
            if col < q_cols:
                q_out[:, col : col + wide] = total
            else:
                kv_out[:, col - q_cols : col - q_cols + wide] = total
        base += mine.shape[1]


def finish(s, blocks, weights, early, late, biases, cos, sin, q_cols, first_col, wide):
    n_x, count = len(blocks), blocks[0].shape[0]
    shard = weights[0].shape[0]
    columns = early.shape[1]
    kv_cols = columns - q_cols
    length = n_x * count
    return pl.pallas_call(
        functools.partial(finish_kernel, n_x, wide, q_cols + kv_cols // 2, first_col),
        in_specs=[SMEM] + [VMEM] * (n_x + 11),
        out_specs=[VMEM, VMEM],
        out_shape=[bf16(length, q_cols), bf16(length, kv_cols)],
        scratch_shapes=[
            pltpu.VMEM((length, 2 * shard), jnp.bfloat16),
            pltpu.VMEM((length, HEAD_SIZE), jnp.float32),
            pltpu.VMEM((length, HEAD_SIZE), jnp.float32),
        ],
        compiler_params=params(16),
        cost_estimate=work(4 * length * shard * columns, *weights, early, late),
        name="finish",
    )(s[None], *blocks, *weights, early, late, *biases, cos, sin)


def attend_kernel(blocks, group, s_ref, q_ref, kv_ref, out_ref, keys, values):
    length = q_ref.shape[0]
    rows = length // blocks
    factor = LOG2E / (HEAD_SIZE**0.5)

    def held(b):
        return pl.ds(pl.multiple_of(lax.rem(s_ref[0] - b + blocks, blocks) * rows, rows), rows)

    kv_half = kv_ref.shape[1] // 2
    for b in range(blocks):
        keys[b * rows : (b + 1) * rows, :] = kv_ref[held(b), :kv_half]
        values[b * rows : (b + 1) * rows, :] = kv_ref[held(b), kv_half:]
    row = lax.broadcasted_iota(jnp.int32, (rows, rows), 0)
    column = lax.broadcasted_iota(jnp.int32, (rows, rows), 1)
    causal = row >= column
    causal = jnp.concatenate([causal.astype(jnp.float32)] * group, axis=0) > 0.5
    for g, b in [(g, b) for g in range(kv_half // HEAD_SIZE) for b in range(blocks)]:
        left = g * group * HEAD_SIZE
        head = slice(g * HEAD_SIZE, (g + 1) * HEAD_SIZE)
        q_block = q_ref[held(b), left : left + group * HEAD_SIZE]
        queries = jnp.concatenate(
            [q_block[:, h * HEAD_SIZE : (h + 1) * HEAD_SIZE] for h in range(group)], axis=0
        )
        at = b * rows
        near = lax.dot_general(
            queries, keys[at : at + rows, head], NT, preferred_element_type=jnp.float32
        )
        near = jnp.where(causal, near, jnp.float32(-1e30))
        largest = jnp.max(near, axis=-1, keepdims=True)
        if b > 0:
            far = lax.dot_general(queries, keys[:at, head], NT, preferred_element_type=jnp.float32)
            largest = jnp.maximum(largest, jnp.max(far, axis=-1, keepdims=True))
        near = jnp.exp2((near - largest) * factor)
        total = jnp.sum(near, axis=-1, keepdims=True)
        result = jnp.dot(
            near.astype(jnp.bfloat16), values[at : at + rows, head], preferred_element_type=jnp.float32
        )
        if b > 0:
            far = jnp.exp2((far - largest) * factor)
            total = total + jnp.sum(far, axis=-1, keepdims=True)
            result = result + jnp.dot(
                far.astype(jnp.bfloat16), values[:at, head], preferred_element_type=jnp.float32
            )
        result = (result / total).astype(jnp.bfloat16)
        for h in range(group):
            out_ref[held(b), left + h * HEAD_SIZE : left + (h + 1) * HEAD_SIZE] = result[
                h * rows : (h + 1) * rows, :
            ]


def attend(s, queries, kv, blocks):
    length, q_cols = queries.shape
    kv_half = kv.shape[1] // 2
    return pl.pallas_call(
        functools.partial(attend_kernel, blocks, q_cols // kv_half),
        in_specs=[SMEM, VMEM, VMEM],
        out_specs=VMEM,
        out_shape=bf16(length, q_cols),
        scratch_shapes=[
            pltpu.VMEM((length, kv_half), jnp.bfloat16),
            pltpu.VMEM((length, kv_half), jnp.bfloat16),
        ],
        compiler_params=params(16),
        cost_estimate=work(4 * length * length * q_cols, queries, queries, kv),
        name="attend",
    )(s[None], queries, kv)


def mix_kernel(n_w, heads_ref, *refs):
    w_refs, out_refs = refs[:n_w], refs[n_w:]
    rows = out_refs[0].shape[0]
    weights = [w_ref[...] for w_ref in w_refs]
    weights = weights[0] if n_w == 1 else jnp.concatenate(weights, axis=0)
    term = lax.dot_general(
        heads_ref[...], weights, NT, preferred_element_type=jnp.float32
    ).astype(jnp.bfloat16)
    for k, out_ref in enumerate(out_refs):
        out_ref[...] = term[k * rows : (k + 1) * rows, :]


def mix(heads, parts, blocks):
    length, features = heads.shape
    columns = sum(part.shape[0] for part in parts)
    return pl.pallas_call(
        functools.partial(mix_kernel, len(parts)),
        in_specs=[VMEM] * (1 + len(parts)),
        out_specs=[VMEM] * blocks,
        out_shape=[bf16(length // blocks, columns)] * blocks,
        compiler_params=params(16),
        cost_estimate=work(2 * length * columns * features, heads, *parts),
        name="mix",
    )(heads, *parts)


def add_kernel(a_ref, b_ref, out_ref):
    total = a_ref[...].astype(jnp.float32) + b_ref[...].astype(jnp.float32)
    out_ref[...] = total.astype(jnp.bfloat16)


def add(a, b):
    return pl.pallas_call(
        add_kernel,
        in_specs=[VMEM, VMEM],
        out_specs=VMEM,
        out_shape=bf16(*a.shape),
        compiler_params=params(8),
        cost_estimate=work(0, a, a, a),
        name="add",
    )(a, b)


def place_kernel(parts, me_ref, a_ref, b_ref, *refs):
    out_ref, total, sem = refs[-3:]
    add_kernel(a_ref, b_ref, total)
    copies, left = [], 0
    for i, (j, shard, offset, width) in enumerate(parts):
        start = pl.multiple_of(jnp.bitwise_xor(me_ref[0], j) * shard + offset, 128)
        copies.append(
            pltpu.make_async_copy(
                total.at[:, pl.ds(left, width)], out_ref.at[:, pl.ds(start, width)], sem.at[i]
            )
        )
        left += width
    for copy in copies:
        copy.start()
    for copy in copies:
        copy.wait()


def place(mixed, me, a, b, parts, columns):
    if any(offset % 128 or width % 128 or shard % 128 for _, shard, offset, width in parts):
        total, left = add(a, b), 0
        if mixed is None:
            mixed = jnp.zeros((a.shape[0], columns), jnp.bfloat16)
        for j, shard, offset, width in parts:
            start = jnp.bitwise_xor(me, j) * shard + offset
            mixed = lax.dynamic_update_slice(mixed, total[:, left : left + width], (0, start))
            left += width
        return mixed
    held = [] if mixed is None else [mixed]
    return pl.pallas_call(
        functools.partial(place_kernel, parts),
        in_specs=[SMEM, VMEM, VMEM] + [ANY] * len(held),
        out_specs=ANY,
        out_shape=bf16(a.shape[0], columns),
        scratch_shapes=[
            pltpu.VMEM(a.shape, jnp.bfloat16),
            pltpu.SemaphoreType.DMA((len(parts),)),
        ],
        input_output_aliases={3: 0} if held else {},
        compiler_params=params(8),
        cost_estimate=work(0, a, a, a),
        name="place",
    )(me[None], a, b, *held)


def swapped(array, n_f, mask):
    return lax.ppermute(array, "fsdp", [(i, i ^ mask) for i in range(n_f)])


def after(array, *others):
    return lax.optimization_barrier((array, *others))[0] if others else array


def phase_of(piece):
    r, half = piece
    bits = bin(r).count("1")
    if bits <= 1:
        return bits if half == (1 if r == 1 else 0) else 2 * bits
    return bits + 1


def send_phase(held, n_f, phase, *before):
    sent = [(r, h) for r in range(1, n_f // 2) for h in range(2) if phase_of((r, h)) == phase]
    for r, half in sent:
        bit = r & -r if half == 0 else 1 << (r.bit_length() - 1)
        held[r, half] = swapped(after(held[r ^ bit, half], *before), n_f, 2 * bit)
    return [held[piece] for piece in sent]


def send_siblings(held, sibling, n_f, phase, *before):
    for piece in [piece for piece in held if phase_of(piece) == phase]:
        sibling[piece] = swapped(after(held[piece], *before), n_f, 1)


def rope_tables(length):
    frequency = np.float32(ROPE_BASE) ** (
        -(np.arange(HALF, dtype=np.float32) * np.float32(2.0) / np.float32(HEAD_SIZE))
    )
    angle = np.arange(length, dtype=np.float32)[:, None] * frequency[None, :].astype(np.float32)
    angle = angle.astype(np.float64)
    cos, sin = np.cos(angle).astype(np.float32), np.sin(angle).astype(np.float32)
    return np.concatenate([cos, cos], axis=1), np.concatenate([-sin, sin], axis=1)


def body(
    n_f,
    n_s,
    tokens,
    norm_gain,
    q_weight,
    key_matrix,
    value_matrix,
    q_bias,
    k_bias,
    value_offset_bias,
    out_weight,
):
    me = lax.axis_index("fsdp")
    s = lax.axis_index("sp")
    count = tokens.shape[0]
    chips = n_f // 2
    phases = chips.bit_length()
    shard, q_cols = q_weight.shape
    kv_cols = key_matrix.shape[1]
    wide = 256 if q_cols % 256 == 0 and kv_cols % 256 == 0 else 128
    cut = (q_cols + 2 * kv_cols) // wide // 2 * wide
    cut += wide if cut + wide <= q_cols else 0
    ring = [(i, (i + 1) % n_s) for i in range(n_s)]
    cos, sin = rope_tables(n_s * count)

    blocks = [normed_pieces(me, tokens, norm_gain, n_f)]
    first, second = pack(after(q_weight, blocks[0]), key_matrix, value_matrix, cut)
    held, sibling = {(0, 0): first, (0, 1): second}, {}
    send_siblings(held, sibling, n_f, 0)
    o_cut = shard * 3 // 5 // 128 * 128 or shard // 2 // 16 * 16
    o_first, o_second = cut_rows(after(out_weight, first), o_cut)
    o_held, o_sibling = {(0, 0): o_first, (0, 1): o_second}, {}

    gates, sent = [], []
    for k in range(1, n_s):
        if k <= phases:
            sent = send_phase(held, n_f, k, *gates[-1:], *sent)
            if k > 1:
                send_siblings(held, sibling, n_f, k - 1, *gates[-1:])
        blocks.append(lax.ppermute(blocks[-1], "sp", ring))
        gates.append(blocks[-1])
    send_siblings(o_held, o_sibling, n_f, 0, gates[0])

    def parts(half, chosen):
        return [side[r, half] for r in chosen for side in (held, sibling)]

    most = range(chips - 1)
    early = partial(blocks[:-1], parts(0, most), parts(1, most), wide)
    send_siblings(held, sibling, n_f, phases, gates[-1], early)
    send_phase(o_held, n_f, 1, gates[-1], early)
    late = partial(blocks[-1:], parts(0, most), parts(1, most), wide)
    last = parts(0, [chips - 1]) + parts(1, [chips - 1])
    queries, kv = finish(
        s,
        blocks,
        last,
        early,
        late,
        (q_bias, k_bias, value_offset_bias),
        cos,
        sin,
        q_cols,
        2 * shard * (chips - 1),
        wide,
    )
    heads = attend(s, queries, kv, n_s)

    mixed, rings, previous = None, [], []

    def mix_group(group):
        nonlocal mixed
        weights = [(o_sibling if core else o_held)[r, half] for r, half, core in group]
        t = len(rings) - 2
        behind = [rings[t - d][d] for d in range(n_s - 1) if t - d >= 0]
        terms = mix(after(heads, *behind, *previous), weights, n_s)
        previous[:] = terms[:1]
        total, arrivals = terms[1], []
        for k in range(2, n_s + 1):
            arrivals.append(lax.ppermute(total, "sp", ring))
            if k < n_s:
                total = add(arrivals[-1], terms[k])
        where = [
            (2 * r + core, shard, half * o_cut, w.shape[0])
            for (r, half, core), w in zip(group, weights)
        ]
        mixed = place(mixed, me, arrivals[-1], terms[0], where, shard * n_f)
        rings.append(arrivals)

    mix_group([(0, 0, 0), (0, 1, 0)])
    mix_group([(0, 0, 1), (0, 1, 1)])
    for phase in range(1, phases + 1):
        gate = rings[-2][0]
        send_siblings(o_held, o_sibling, n_f, phase, gate)
        send_phase(o_held, n_f, phase + 1, gate)
        for piece in [piece for piece in o_held if phase_of(piece) == phase]:
            mix_group([(*piece, 0), (*piece, 1)])
    return mixed


def solution(mesh):
    n_f, n_s = mesh.shape["fsdp"], mesh.shape["sp"]
    placed = (
        P(("fsdp", "sp"), None),
        P(),
        P("fsdp", "sp"),
        P("fsdp", "sp"),
        P("fsdp", "sp"),
        P("sp"),
        P("sp"),
        P("sp"),
        P("fsdp", "sp"),
    )
    return jax.shard_map(
        functools.partial(body, n_f, n_s),
        mesh=mesh,
        in_specs=placed,
        out_specs=P(("fsdp", "sp"), None),
        check_vma=False,
    )
```

time: 439 us -> 277 us (0.63)
  waiting for transfers between devices: 366 us -> 196 us
  matrix products: 49.1 us -> 0 us
  Pallas kernels: 0 us -> 33.6 us
  starting transfers between devices: 0.2 us -> 22.7 us
  local copies, waits for them, and re-layouts: 3.68 us -> 22.9 us
  between operations: 13.6 us -> 0.85 us
  other arithmetic: 6.49 us -> 0 us
    all_gather x5 -> x0, waiting for transfers between devices: 269 us -> none  [the longest x1 99.7 us: project_heads(): piece = lax.all_gather(normed, 'sp', axis=0, tiled=True)]
    ppermute x0 -> x55, waiting for transfers between devices: none -> 196 us  [the longest x28 91.4 us: swapped(): return lax.ppermute(array, 'fsdp', [(i, i ^ mask) for i in range(n_f)])]
    reduce_scatter x1 -> x0, waiting for transfers between devices: 93.9 us -> none  [body(): lax.psum_scatter(partial_value.astype(jnp.bfloat16), 'sp', scatter_dimens...]
    dot_general x5 -> x0, matrix products: 42.5 us -> none  [the longest x1 13.7 us: project_heads(): jnp.dot(piece, q_full, preferred_element_type=jnp.float32) + q_bias]
    pallas_call x0 -> x39, Pallas kernels: none -> 33.6 us  [the longest x2 8.84 us: partial(): pl.pallas_call(functools.partial(partial_kernel, n_x, n_r, wide), in_spec...]
    ppermute x0 -> x55, starting transfers between devices: none -> 22.7 us  [the longest x28 14.4 us: swapped(): return lax.ppermute(array, 'fsdp', [(i, i ^ mask) for i in range(n_f)])]
    unnamed x12 -> x84, local copies, waits for them, and re-layouts: 1.24 us -> 22.9 us
    sub x1 -> x0, matrix products: 6.56 us -> none  [attend(): weights = jnp.exp(scores - largest)]
  transfers between devices with their start and end apart: 6 -> 55, of which waited for: 6 -> 32; matrix products, arithmetic and copies ran while one was open for 10% -> 0% of each run, Pallas kernels for 0% -> 12%
where the time goes in v4:
time: 277 us; the launch traced here: 276 us
  waiting for transfers between devices  196 us (71%)
  Pallas kernels  33.6 us (12%)
  local copies, waits for them, and re-layouts  22.9 us (8%)
  starting transfers between devices  22.7 us (8%)
    ppermute x28, waiting for transfers between devices, swapped(): return lax.ppermute(array, 'fsdp', [(i, i ^ mask) for i in range(n_f)])  91.4 us
    ppermute x24, waiting for transfers between devices, mix_group(): arrivals.append(lax.ppermute(total, 'sp', ring))  79.6 us
    ppermute x3, waiting for transfers between devices, body(): blocks.append(lax.ppermute(blocks[-1], 'sp', ring))  25.3 us
    unnamed x84, local copies, waits for them, and re-layouts  22.9 us
    ppermute x28, starting transfers between devices, swapped(): return lax.ppermute(array, 'fsdp', [(i, i ^ mask) for i in range(n_f)])  14.4 us
    pallas_call x2, Pallas kernels, partial(): pl.pallas_call(functools.partial(partial_kernel, n_x, n_r, wide), in_spec...  8.84 us
    pallas_call x8, Pallas kernels, mix(): pl.pallas_call(functools.partial(mix_kernel, len(parts)), in_specs=[VMEM]...  8.69 us
    ppermute x24, starting transfers between devices, mix_group(): arrivals.append(lax.ppermute(total, 'sp', ring))  6.77 us
  transfers between devices with their start and end apart: 55, of which 32 were waited for; matrix products, arithmetic and copies ran while one was open for 0% of the time, Pallas kernels for 12%

profile of v4, /device:TPU:0, one launch (start us, length us, event | category | flops | bytes accessed | tf_op | source)
XLA Modules:
  0.0 276.4 jit_solution(11270590210756431146)
XLA Ops:
  3.8 3.0 %collective-permute-start.3 = (bf16[640,1024]{1,0:T(8,128)(2,1)S(1)}, bf16[640,1024]{1,0:T(8,128)(2,1)S(1)}, u32[]{:S(2)}, u32[]{:S(2)}) collective-permute-start(bf16[640,1024]{1,0:T(8,128)(2,1)S(1)} %get-tuple-element.79.refs_3_.refs_1_), channel_id=1, source_target_pairs={{0,16},{4,20},{8,24},{12,28},{16,0},{20,4},{24,8},{28,12},{1,17},{... | collective-permute-start | bytes 3932168 | tf_op jit(solution)/shard_map/ppermute | solution.py:385
  9.9 21.4 %collective-permute-done.4.refs_11_.refs_9_ = bf16[640,768]{1,0:T(8,128)(2,1)S(1)} collective-permute-done((bf16[640,768]{1,0:T(8,128)(2,1)S(1)}, bf16[640,768]{1,0:T(8,128)(2,1)S(1)}, u32[]{:S(2)}, u32[]{:S(2)}) %collective-permute-start.4) | collective-permute-done | bytes 983072 | tf_op jit(solution)/shard_map/ppermute | solution.py:385
  31.3 4.3 %collective-permute-done.3.refs_7_.refs_5_ = bf16[640,1024]{1,0:T(8,128)(2,1)S(1)} collective-permute-done((bf16[640,1024]{1,0:T(8,128)(2,1)S(1)}, bf16[640,1024]{1,0:T(8,128)(2,1)S(1)}, u32[]{:S(2)}, u32[]{:S(2)}) %collective-permute-start.3) | collective-permute-done | bytes 1310752 | tf_op jit(solution)/shard_map/ppermute | solution.py:385
  35.6 3.3 %collective-permute-done.refs_1_ = bf16[128,5120]{1,0:T(8,128)(2,1)S(1)} collective-permute-done((bf16[128,5120]{1,0:T(8,128)(2,1)S(1)}, bf16[128,5120]{1,0:T(8,128)(2,1)S(1)}, u32[]{:S(2)}, u32[]{:S(2)}) %collective-permute-start) | collective-permute-done | bytes 1310752 | tf_op jit(solution)/shard_map/ppermute | solution.py:463
  41.4 26.9 %collective-permute-done.5.refs_5_.refs_3_ = bf16[640,1024]{1,0:T(8,128)(2,1)S(1)} collective-permute-done((bf16[640,1024]{1,0:T(8,128)(2,1)S(1)}, bf16[640,1024]{1,0:T(8,128)(2,1)S(1)}, u32[]{:S(2)}, u32[]{:S(2)}) %collective-permute-start.5) | collective-permute-done | bytes 1310752 | tf_op jit(solution)/shard_map/ppermute | solution.py:385
  68.3 3.0 %collective-permute-done.1.refs_2_ = bf16[128,5120]{1,0:T(8,128)(2,1)S(1)} collective-permute-done((bf16[128,5120]{1,0:T(8,128)(2,1)S(1)}, bf16[128,5120]{1,0:T(8,128)(2,1)S(1)}, u32[]{:S(2)}, u32[]{:S(2)}) %collective-permute-start.1) | collective-permute-done | bytes 1310752 | tf_op jit(solution)/shard_map/ppermute | solution.py:463
  74.9 2.8 %collective-permute-done.13.refs_14_.refs_12_ = bf16[640,768]{1,0:T(8,128)(2,1)S(1)} collective-permute-done((bf16[640,768]{1,0:T(8,128)(2,1)S(1)}, bf16[640,768]{1,0:T(8,128)(2,1)S(1)}, u32[]{:S(2)}, u32[]{:S(2)}) %collective-permute-start.13) | collective-permute-done | bytes 983072 | tf_op jit(solution)/shard_map/ppermute | solution.py:385
  77.6 6.5 %partial.2.refs_8_ = f32[384,1792]{1,0:T(8,128)S(1)} custom-call(bf16[128,5120]{1,0:T(8,128)(2,1)S(1)} %norm.1.refs_0_, bf16[128,5120]{1,0:T(8,128)(2,1)S(1)} %collective-permute-done.refs_1_, bf16[128,5120]{1,0:T(8,128)(2,1)S(1)} %collective-permute-done.1.refs_2_, bf16[640,1024]{1,0:T(8,128)(2,1)S(1)} %get-tuple-element.79.refs_3_.refs_1_, ...), custom_call_target="tpu_custom_call" | custom-call | flops 5284823040 | bytes 20447232 | tf_op jit(solution)/shard_map/partial/pallas_call | solution.py:137
  85.8 19.0 %collective-permute-done.2.refs_0_.refs_3_ = bf16[128,5120]{1,0:T(8,128)(2,1)S(1)} collective-permute-done((bf16[128,5120]{1,0:T(8,128)(2,1)S(1)}, bf16[128,5120]{1,0:T(8,128)(2,1)S(1)}, u32[]{:S(2)}, u32[]{:S(2)}) %collective-permute-start.2) | collective-permute-done | bytes 1310752 | tf_op jit(solution)/shard_map/ppermute | solution.py:463
  124.4 2.3 partial.3.refs_9_
  127.0 5.3 %finish.1 = (bf16[512,1280]{1,0:T(8,128)(2,1)S(1)}, bf16[512,512]{1,0:T(8,128)(2,1)S(1)}) custom-call(s32[1]{0:T(128)} %bitcast.1.s_ref, bf16[128,5120]{1,0:T(8,128)(2,1)S(1)} %norm.1.refs_0_, bf16[128,5120]{1,0:T(8,128)(2,1)S(1)} %collective-permute-done.refs_1_, bf16[128,5120]{1,0:T(8,128)(2,1)S(1)} %copy-done.7, bf16[128,5120]{1,0:T(8,128)(2,1)S(1)} %copy-done.18, ...), custom_call_target="tpu_custom_call" | custom-call | flops 2348810240 | bytes 8257536 | tf_op jit(solution)/shard_map/finish/pallas_call | solution.py:212
  132.3 3.4 %attend.1.heads_ref = bf16[512,1280]{1,0:T(8,128)(2,1)S(1)} custom-call(s32[1]{0:T(128)} %bitcast.1.s_ref, bf16[512,1280]{1,0:T(8,128)(2,1)S(1)} %get-tuple-element.89.q_ref, bf16[512,512]{1,0:T(8,128)(2,1)S(1)} %get-tuple-element.90.kv_ref), custom_call_target="tpu_custom_call" | custom-call | flops 1342177280 | bytes 3145728 | tf_op jit(solution)/shard_map/attend/pallas_call | solution.py:281
  137.6 7.4 %collective-permute-done.20.a_ref = bf16[128,640]{1,0:T(8,128)(2,1)S(1)} collective-permute-done((bf16[128,640]{1,0:T(8,128)(2,1)S(1)}, bf16[128,640]{1,0:T(8,128)(2,1)S(1)}, u32[]{:S(2)}, u32[]{:S(2)}) %collective-permute-start.20) | collective-permute-done | bytes 163872 | tf_op jit(solution)/shard_map/ppermute | solution.py:502
  150.3 10.5 %collective-permute-done.24.refs_0_ = bf16[384,1280]{1,0:T(8,128)(2,1)S(1)} collective-permute-done((bf16[384,1280]{1,0:T(8,128)(2,1)S(1)}, bf16[384,1280]{1,0:T(8,128)(2,1)S(1)}, u32[]{:S(2)}, u32[]{:S(2)}) %collective-permute-start.24) | collective-permute-done | bytes 983072 | tf_op jit(solution)/shard_map/ppermute | solution.py:385
  160.8 7.0 %collective-permute-done.32.refs_0_ = bf16[384,1280]{1,0:T(8,128)(2,1)S(1)} collective-permute-done((bf16[384,1280]{1,0:T(8,128)(2,1)S(1)}, bf16[384,1280]{1,0:T(8,128)(2,1)S(1)}, u32[]{:S(2)}, u32[]{:S(2)}) %collective-permute-start.32) | collective-permute-done | bytes 983072 | tf_op jit(solution)/shard_map/ppermute | solution.py:385
  169.2 8.7 %collective-permute-done.19.a_ref = bf16[128,640]{1,0:T(8,128)(2,1)S(1)} collective-permute-done((bf16[128,640]{1,0:T(8,128)(2,1)S(1)}, bf16[128,640]{1,0:T(8,128)(2,1)S(1)}, u32[]{:S(2)}, u32[]{:S(2)}) %collective-permute-start.19) | collective-permute-done | bytes 163872 | tf_op jit(solution)/shard_map/ppermute | solution.py:502
  178.0 2.7 collective-permute-done.21.a_ref
  182.6 3.0 %collective-permute-done.29.a_ref = bf16[128,640]{1,0:T(8,128)(2,1)S(1)} collective-permute-done((bf16[128,640]{1,0:T(8,128)(2,1)S(1)}, bf16[128,640]{1,0:T(8,128)(2,1)S(1)}, u32[]{:S(2)}, u32[]{:S(2)}) %collective-permute-start.29) | collective-permute-done | bytes 163872 | tf_op jit(solution)/shard_map/ppermute | solution.py:502
  185.6 3.0 %collective-permute-done.31.a_ref = bf16[128,640]{1,0:T(8,128)(2,1)S(1)} collective-permute-done((bf16[128,640]{1,0:T(8,128)(2,1)S(1)}, bf16[128,640]{1,0:T(8,128)(2,1)S(1)}, u32[]{:S(2)}, u32[]{:S(2)}) %collective-permute-start.31) | collective-permute-done | bytes 163872 | tf_op jit(solution)/shard_map/ppermute | solution.py:502
  192.0 5.4 %collective-permute-done.37.a_ref = bf16[128,768]{1,0:T(8,128)(2,1)S(1)} collective-permute-done((bf16[128,768]{1,0:T(8,128)(2,1)S(1)}, bf16[128,768]{1,0:T(8,128)(2,1)S(1)}, u32[]{:S(2)}, u32[]{:S(2)}) %collective-permute-start.37) | collective-permute-done | bytes 196640 | tf_op jit(solution)/shard_map/ppermute | solution.py:502
  198.5 12.4 %collective-permute-done.44.refs_0_ = bf16[256,1280]{1,0:T(8,128)(2,1)S(1)} collective-permute-done((bf16[256,1280]{1,0:T(8,128)(2,1)S(1)}, bf16[256,1280]{1,0:T(8,128)(2,1)S(1)}, u32[]{:S(2)}, u32[]{:S(2)}) %collective-permute-start.44) | collective-permute-done | bytes 655392 | tf_op jit(solution)/shard_map/ppermute | solution.py:385
  212.1 7.0 %collective-permute-done.28.a_ref = bf16[128,512]{1,0:T(8,128)(2,1)S(1)} collective-permute-done((bf16[128,512]{1,0:T(8,128)(2,1)S(1)}, bf16[128,512]{1,0:T(8,128)(2,1)S(1)}, u32[]{:S(2)}, u32[]{:S(2)}) %collective-permute-start.28) | collective-permute-done | bytes 131104 | tf_op jit(solution)/shard_map/ppermute | solution.py:502
  219.2 3.8 %collective-permute-done.39.a_ref = bf16[128,768]{1,0:T(8,128)(2,1)S(1)} collective-permute-done((bf16[128,768]{1,0:T(8,128)(2,1)S(1)}, bf16[128,768]{1,0:T(8,128)(2,1)S(1)}, u32[]{:S(2)}, u32[]{:S(2)}) %collective-permute-start.39) | collective-permute-done | bytes 196640 | tf_op jit(solution)/shard_map/ppermute | solution.py:502
  223.1 3.4 %collective-permute-done.30.a_ref = bf16[128,640]{1,0:T(8,128)(2,1)S(1)} collective-permute-done((bf16[128,640]{1,0:T(8,128)(2,1)S(1)}, bf16[128,640]{1,0:T(8,128)(2,1)S(1)}, u32[]{:S(2)}, u32[]{:S(2)}) %collective-permute-start.30) | collective-permute-done | bytes 163872 | tf_op jit(solution)/shard_map/ppermute | solution.py:502
  228.2 2.2 collective-permute-done.41.a_ref
  233.7 2.4 collective-permute-done.40.a_ref
  236.1 9.2 %collective-permute-done.36.a_ref = bf16[128,512]{1,0:T(8,128)(2,1)S(1)} collective-permute-done((bf16[128,512]{1,0:T(8,128)(2,1)S(1)}, bf16[128,512]{1,0:T(8,128)(2,1)S(1)}, u32[]{:S(2)}, u32[]{:S(2)}) %collective-permute-start.36) | collective-permute-done | bytes 131104 | tf_op jit(solution)/shard_map/ppermute | solution.py:502
  248.7 5.9 %collective-permute-done.46.a_ref = bf16[128,512]{1,0:T(8,128)(2,1)S(1)} collective-permute-done((bf16[128,512]{1,0:T(8,128)(2,1)S(1)}, bf16[128,512]{1,0:T(8,128)(2,1)S(1)}, u32[]{:S(2)}, u32[]{:S(2)}) %collective-permute-start.46) | collective-permute-done | bytes 131104 | tf_op jit(solution)/shard_map/ppermute | solution.py:502
  254.7 4.0 %collective-permute-done.50.a_ref = bf16[128,768]{1,0:T(8,128)(2,1)S(1)} collective-permute-done((bf16[128,768]{1,0:T(8,128)(2,1)S(1)}, bf16[128,768]{1,0:T(8,128)(2,1)S(1)}, u32[]{:S(2)}, u32[]{:S(2)}) %collective-permute-start.50) | collective-permute-done | bytes 196640 | tf_op jit(solution)/shard_map/ppermute | solution.py:502
  258.8 2.7 collective-permute-done.52.a_ref
  261.6 2.7 collective-permute-done.47.a_ref
  269.3 4.8 %collective-permute-done.53.a_ref = bf16[128,512]{1,0:T(8,128)(2,1)S(1)} collective-permute-done((bf16[128,512]{1,0:T(8,128)(2,1)S(1)}, bf16[128,512]{1,0:T(8,128)(2,1)S(1)}, u32[]{:S(2)}, u32[]{:S(2)}) %collective-permute-start.53) | collective-permute-done | bytes 131104 | tf_op jit(solution)/shard_map/ppermute | solution.py:502
  (201 shorter events, 65.9 us)
Async XLA Ops:
  3.8 31.8 %collective-permute-start.3 = (bf16[640,1024]{1,0:T(8,128)(2,1)S(1)}, bf16[640,1024]{1,0:T(8,128)(2,1)S(1)}, u32[]{:S(2)}, u32[]{:S(2)}) collective-permute-start(bf16[640,1024]{1,0:T(8,128)(2,1)S(1)} %get-tuple-element.79.refs_3_.refs_1_), channel_id=1, source_target_pairs={{0,16},{4,20},{8,24},{12,28},{16,0},{20,4},{24,8},{28,12},{1,17},{... | collective-permute-start | bytes 3932168 | tf_op jit(solution)/shard_map/ppermute | solution.py:385
  6.8 32.1 %collective-permute-start = (bf16[128,5120]{1,0:T(8,128)(2,1)S(1)}, bf16[128,5120]{1,0:T(8,128)(2,1)S(1)}, u32[]{:S(2)}, u32[]{:S(2)}) collective-permute-start(bf16[128,5120]{1,0:T(8,128)(2,1)S(1)} %norm.1.refs_0_), channel_id=1, source_target_pairs={{0,1},{1,2},{2,3},{3,0},{4,5},{5,6},{6,7},{7,4},{8,9},{9,10},{10,1... | collective-permute-start | bytes 3932168 | tf_op jit(solution)/shard_map/ppermute | solution.py:463
  8.4 22.9 %collective-permute-start.4 = (bf16[640,768]{1,0:T(8,128)(2,1)S(1)}, bf16[640,768]{1,0:T(8,128)(2,1)S(1)}, u32[]{:S(2)}, u32[]{:S(2)}) collective-permute-start(bf16[640,768]{1,0:T(8,128)(2,1)S(1)} %get-tuple-element.80.refs_9_.refs_7_), channel_id=1, source_target_pairs={{0,8},{4,12},{8,0},{12,4},{16,24},{20,28},{24,16},{28,20},{1,9},{5... | collective-permute-start | bytes 2949128 | tf_op jit(solution)/shard_map/ppermute | solution.py:385
  38.9 29.4 %collective-permute-start.5 = (bf16[640,1024]{1,0:T(8,128)(2,1)S(1)}, bf16[640,1024]{1,0:T(8,128)(2,1)S(1)}, u32[]{:S(2)}, u32[]{:S(2)}) collective-permute-start(bf16[640,1024]{1,0:T(8,128)(2,1)S(1)} %get-tuple-element.79.refs_3_.refs_1_), channel_id=1, source_target_pairs={{0,8},{4,12},{8,0},{12,4},{16,24},{20,28},{24,16},{28,20},{1,9},{5... | collective-permute-start | bytes 3932168 | tf_op jit(solution)/shard_map/ppermute | solution.py:385
  40.4 30.9 %collective-permute-start.1 = (bf16[128,5120]{1,0:T(8,128)(2,1)S(1)}, bf16[128,5120]{1,0:T(8,128)(2,1)S(1)}, u32[]{:S(2)}, u32[]{:S(2)}) collective-permute-start(bf16[128,5120]{1,0:T(8,128)(2,1)S(1)} %collective-permute-done.refs_1_), channel_id=1, source_target_pairs={{0,1},{1,2},{2,3},{3,0},{4,5},{5,6},{6,7},{7,4},{8,9},{9,10},{10,1... | collective-permute-start | bytes 3932168 | tf_op jit(solution)/shard_map/ppermute | solution.py:463
  40.4 30.9 %collective-permute-start.6 = (bf16[640,768]{1,0:T(8,128)(2,1)S(1)}, bf16[640,768]{1,0:T(8,128)(2,1)S(1)}, u32[]{:S(2)}, u32[]{:S(2)}) collective-permute-start(bf16[640,768]{1,0:T(8,128)(2,1)S(1)} %get-tuple-element.80.refs_9_.refs_7_), channel_id=1, source_target_pairs={{0,16},{4,20},{8,24},{12,28},{16,0},{20,4},{24,8},{28,12},{1,17},{... | collective-permute-start | bytes 2949128 | tf_op jit(solution)/shard_map/ppermute | solution.py:385
  40.9 31.0 %collective-permute-start.8 = (bf16[640,1024]{1,0:T(8,128)(2,1)S(1)}, bf16[640,1024]{1,0:T(8,128)(2,1)S(1)}, u32[]{:S(2)}, u32[]{:S(2)}) collective-permute-start(bf16[640,1024]{1,0:T(8,128)(2,1)S(1)} %get-tuple-element.79.refs_3_.refs_1_), channel_id=1, source_target_pairs={{0,4},{4,0},{8,12},{12,8},{16,20},{20,16},{24,28},{28,24},{1,5},{5... | collective-permute-start | bytes 3932168 | tf_op jit(solution)/shard_map/ppermute | solution.py:385
  40.9 30.9 %collective-permute-start.11 = (bf16[640,768]{1,0:T(8,128)(2,1)S(1)}, bf16[640,768]{1,0:T(8,128)(2,1)S(1)}, u32[]{:S(2)}, u32[]{:S(2)}) collective-permute-start(bf16[640,768]{1,0:T(8,128)(2,1)S(1)} %get-tuple-element.80.refs_9_.refs_7_), channel_id=1, source_target_pairs={{0,4},{4,0},{8,12},{12,8},{16,20},{20,16},{24,28},{28,24},{1,5},{5... | collective-permute-start | bytes 2949128 | tf_op jit(solution)/shard_map/ppermute | solution.py:385
  71.9 32.9 %collective-permute-start.2 = (bf16[128,5120]{1,0:T(8,128)(2,1)S(1)}, bf16[128,5120]{1,0:T(8,128)(2,1)S(1)}, u32[]{:S(2)}, u32[]{:S(2)}) collective-permute-start(bf16[128,5120]{1,0:T(8,128)(2,1)S(1)} %collective-permute-done.1.refs_2_), channel_id=1, source_target_pairs={{0,1},{1,2},{2,3},{3,0},{4,5},{5,6},{6,7},{7,4},{8,9},{9,10},{10,1... | collective-permute-start | bytes 3932168 | tf_op jit(solution)/shard_map/ppermute | solution.py:463
  72.0 34.0 %collective-permute-start.7 = (bf16[640,1024]{1,0:T(8,128)(2,1)S(1)}, bf16[640,1024]{1,0:T(8,128)(2,1)}, u32[]{:S(2)}, u32[]{:S(2)}) collective-permute-start(bf16[640,1024]{1,0:T(8,128)(2,1)S(1)} %collective-permute-done.3.refs_7_.refs_5_), channel_id=1, source_target_pairs={{0,8},{4,12},{8,0},{12,4},{16,24},{20,28},{24,16},{28,20},{1,9},{5... | collective-permute-start | bytes 3932168 | tf_op jit(solution)/shard_map/ppermute | solution.py:385
  74.4 31.6 %collective-permute-start.15 = (bf16[640,768]{1,0:T(8,128)(2,1)S(1)}, bf16[640,768]{1,0:T(8,128)(2,1)}, u32[]{:S(2)}, u32[]{:S(2)}) collective-permute-start(bf16[640,768]{1,0:T(8,128)(2,1)S(1)} %collective-permute-done.4.refs_11_.refs_9_), channel_id=1, source_target_pairs={{0,16},{4,20},{8,24},{12,28},{16,0},{20,4},{24,8},{28,12},{1,17},{... | collective-permute-start | bytes 2949128 | tf_op jit(solution)/shard_map/ppermute | solution.py:385
  106.0 20.8 %collective-permute-start.14 = (bf16[640,1024]{1,0:T(8,128)(2,1)}, bf16[640,1024]{1,0:T(8,128)(2,1)}, u32[]{:S(2)}, u32[]{:S(2)}) collective-permute-start(bf16[640,1024]{1,0:T(8,128)(2,1)} %collective-permute-done.7.refs_4_), channel_id=1, source_target_pairs={{0,4},{4,0},{8,12},{12,8},{16,20},{20,16},{24,28},{28,24},{1,5},{5... | collective-permute-start | bytes 3932168 | tf_op jit(solution)/shard_map/ppermute | solution.py:385
  106.0 20.7 %collective-permute-start.16 = (bf16[640,768]{1,0:T(8,128)(2,1)}, bf16[640,768]{1,0:T(8,128)(2,1)}, u32[]{:S(2)}, u32[]{:S(2)}) collective-permute-start(bf16[640,768]{1,0:T(8,128)(2,1)} %collective-permute-done.15.refs_6_), channel_id=1, source_target_pairs={{0,4},{4,0},{8,12},{12,8},{16,20},{20,16},{24,28},{28,24},{1,5},{5... | collective-permute-start | bytes 2949128 | tf_op jit(solution)/shard_map/ppermute | solution.py:385
  108.1 40.1 %collective-permute-start.17 = (bf16[384,1280]{1,0:T(8,128)(2,1)S(1)}, bf16[384,1280]{1,0:T(8,128)(2,1)S(1)}, u32[]{:S(2)}, u32[]{:S(2)}) collective-permute-start(bf16[384,1280]{1,0:T(8,128)(2,1)S(1)} %get-tuple-element.117.refs_0_), channel_id=1, source_target_pairs={{0,4},{4,0},{8,12},{12,8},{16,20},{20,16},{24,28},{28,24},{1,5},{5... | collective-permute-start | bytes 2949128 | tf_op jit(solution)/shard_map/ppermute | solution.py:385
  108.2 37.8 %collective-permute-start.22 = (bf16[256,1280]{1,0:T(8,128)(2,1)S(1)}, bf16[256,1280]{1,0:T(8,128)(2,1)S(1)}, u32[]{:S(2)}, u32[]{:S(2)}) collective-permute-start(bf16[256,1280]{1,0:T(8,128)(2,1)S(1)} %get-tuple-element.121.refs_1_), channel_id=1, source_target_pairs={{0,8},{4,12},{8,0},{12,4},{16,24},{20,28},{24,16},{28,20},{1,9},{5... | collective-permute-start | bytes 1966088 | tf_op jit(solution)/shard_map/ppermute | solution.py:385
  137.0 23.8 %collective-permute-start.24 = (bf16[384,1280]{1,0:T(8,128)(2,1)S(1)}, bf16[384,1280]{1,0:T(8,128)(2,1)S(1)}, u32[]{:S(2)}, u32[]{:S(2)}) collective-permute-start(bf16[384,1280]{1,0:T(8,128)(2,1)S(1)} %get-tuple-element.117.refs_0_), channel_id=1, source_target_pairs={{0,16},{4,20},{8,24},{12,28},{16,0},{20,4},{24,8},{28,12},{1,17},{... | collective-permute-start | bytes 2949128 | tf_op jit(solution)/shard_map/ppermute | solution.py:385
  145.0 22.9 %collective-permute-start.32 = (bf16[384,1280]{1,0:T(8,128)(2,1)S(1)}, bf16[384,1280]{1,0:T(8,128)(2,1)S(1)}, u32[]{:S(2)}, u32[]{:S(2)}) collective-permute-start(bf16[384,1280]{1,0:T(8,128)(2,1)S(1)} %get-tuple-element.117.refs_0_), channel_id=1, source_target_pairs={{0,8},{4,12},{8,0},{12,4},{16,24},{20,28},{24,16},{28,20},{1,9},{5... | collective-permute-start | bytes 2949128 | tf_op jit(solution)/shard_map/ppermute | solution.py:385
  160.8 20.0 %collective-permute-start.25 = (bf16[384,1280]{1,0:T(8,128)(2,1)S(1)}, bf16[384,1280]{1,0:T(8,128)(2,1)S(1)}, u32[]{:S(2)}, u32[]{:S(2)}) collective-permute-start(bf16[384,1280]{1,0:T(8,128)(2,1)S(1)} %collective-permute-done.24.refs_0_), channel_id=1, source_target_pairs={{0,4},{4,0},{8,12},{12,8},{16,20},{20,16},{24,28},{28,24},{1,5},{5... | collective-permute-start | bytes 2949128 | tf_op jit(solution)/shard_map/ppermute | solution.py:385
  167.9 20.7 %collective-permute-start.33 = (bf16[384,1280]{1,0:T(8,128)(2,1)S(1)}, bf16[384,1280]{1,0:T(8,128)(2,1)S(1)}, u32[]{:S(2)}, u32[]{:S(2)}) collective-permute-start(bf16[384,1280]{1,0:T(8,128)(2,1)S(1)} %collective-permute-done.32.refs_0_), channel_id=1, source_target_pairs={{0,4},{4,0},{8,12},{12,8},{16,20},{20,16},{24,28},{28,24},{1,5},{5... | collective-permute-start | bytes 2949128 | tf_op jit(solution)/shard_map/ppermute | solution.py:385
  167.9 24.2 %collective-permute-start.42 = (bf16[384,1280]{1,0:T(8,128)(2,1)S(1)}, bf16[384,1280]{1,0:T(8,128)(2,1)S(1)}, u32[]{:S(2)}, u32[]{:S(2)}) collective-permute-start(bf16[384,1280]{1,0:T(8,128)(2,1)S(1)} %collective-permute-done.24.refs_0_), channel_id=1, source_target_pairs={{0,8},{4,12},{8,0},{12,4},{16,24},{20,28},{24,16},{28,20},{1,9},{5... | collective-permute-start | bytes 2949128 | tf_op jit(solution)/shard_map/ppermute | solution.py:385
  180.8 17.7 %collective-permute-start.34 = (bf16[256,1280]{1,0:T(8,128)(2,1)S(1)}, bf16[256,1280]{1,0:T(8,128)(2,1)S(1)}, u32[]{:S(2)}, u32[]{:S(2)}) collective-permute-start(bf16[256,1280]{1,0:T(8,128)(2,1)S(1)} %get-tuple-element.121.refs_1_), channel_id=1, source_target_pairs={{0,16},{4,20},{8,24},{12,28},{16,0},{20,4},{24,8},{28,12},{1,17},{... | collective-permute-start | bytes 1966088 | tf_op jit(solution)/shard_map/ppermute | solution.py:385
  189.9 21.1 %collective-permute-start.44 = (bf16[256,1280]{1,0:T(8,128)(2,1)S(1)}, bf16[256,1280]{1,0:T(8,128)(2,1)S(1)}, u32[]{:S(2)}, u32[]{:S(2)}) collective-permute-start(bf16[256,1280]{1,0:T(8,128)(2,1)S(1)} %collective-permute-done.22.refs_0_), channel_id=1, source_target_pairs={{0,16},{4,20},{8,24},{12,28},{16,0},{20,4},{24,8},{28,12},{1,17},{... | collective-permute-start | bytes 1966088 | tf_op jit(solution)/shard_map/ppermute | solution.py:385
  197.5 32.9 %collective-permute-start.43 = (bf16[384,1280]{1,0:T(8,128)(2,1)S(1)}, bf16[384,1280]{1,0:T(8,128)(2,1)S(1)}, u32[]{:S(2)}, u32[]{:S(2)}) collective-permute-start(bf16[384,1280]{1,0:T(8,128)(2,1)S(1)} %collective-permute-done.42.refs_0_), channel_id=1, source_target_pairs={{0,4},{4,0},{8,12},{12,8},{16,20},{20,16},{24,28},{28,24},{1,5},{5... | collective-permute-start | bytes 2949128 | tf_op jit(solution)/shard_map/ppermute | solution.py:385
  198.5 27.9 %collective-permute-start.35 = (bf16[256,1280]{1,0:T(8,128)(2,1)S(1)}, bf16[256,1280]{1,0:T(8,128)(2,1)S(1)}, u32[]{:S(2)}, u32[]{:S(2)}) collective-permute-start(bf16[256,1280]{1,0:T(8,128)(2,1)S(1)} %collective-permute-done.34.refs_0_), channel_id=1, source_target_pairs={{0,4},{4,0},{8,12},{12,8},{16,20},{20,16},{24,28},{28,24},{1,5},{5... | collective-permute-start | bytes 1966088 | tf_op jit(solution)/shard_map/ppermute | solution.py:385
  198.5 12.5 %collective-permute-start.26 = (bf16[128,768]{1,0:T(8,128)(2,1)S(1)}, bf16[128,768]{1,0:T(8,128)(2,1)S(1)}, u32[]{:S(2)}, u32[]{:S(2)}) collective-permute-start(bf16[128,768]{1,0:T(8,128)(2,1)S(1)} %get-tuple-element.109), channel_id=1, source_target_pairs={{0,1},{1,2},{2,3},{3,0},{4,5},{5,6},{6,7},{7,4},{8,9},{9,10},{10,1... | collective-permute-start | bytes 589832 | tf_op jit(solution)/shard_map/ppermute | solution.py:502
  211.0 34.4 %collective-permute-start.45 = (bf16[256,1280]{1,0:T(8,128)(2,1)S(1)}, bf16[256,1280]{1,0:T(8,128)(2,1)S(1)}, u32[]{:S(2)}, u32[]{:S(2)}) collective-permute-start(bf16[256,1280]{1,0:T(8,128)(2,1)S(1)} %collective-permute-done.44.refs_0_), channel_id=1, source_target_pairs={{0,4},{4,0},{8,12},{12,8},{16,20},{20,16},{24,28},{28,24},{1,5},{5... | collective-permute-start | bytes 1966088 | tf_op jit(solution)/shard_map/ppermute | solution.py:385
  227.4 17.9 %collective-permute-start.38 = (bf16[128,768]{1,0:T(8,128)(2,1)S(1)}, bf16[128,768]{1,0:T(8,128)(2,1)S(1)}, u32[]{:S(2)}, u32[]{:S(2)}) collective-permute-start(bf16[128,768]{1,0:T(8,128)(2,1)S(1)} %add.21), channel_id=1, source_target_pairs={{0,1},{1,2},{2,3},{3,0},{4,5},{5,6},{6,7},{7,4},{8,9},{9,10},{10,1... | collective-permute-start | bytes 589832 | tf_op jit(solution)/shard_map/ppermute | solution.py:502
  231.6 14.7 %collective-permute-start.49 = (bf16[128,768]{1,0:T(8,128)(2,1)S(1)}, bf16[128,768]{1,0:T(8,128)(2,1)S(1)}, u32[]{:S(2)}, u32[]{:S(2)}) collective-permute-start(bf16[128,768]{1,0:T(8,128)(2,1)S(1)} %get-tuple-element.141), channel_id=1, source_target_pairs={{0,1},{1,2},{2,3},{3,0},{4,5},{5,6},{6,7},{7,4},{8,9},{9,10},{10,1... | collective-permute-start | bytes 589832 | tf_op jit(solution)/shard_map/ppermute | solution.py:502
  231.9 13.4 %collective-permute-start.36 = (bf16[128,512]{1,0:T(8,128)(2,1)S(1)}, bf16[128,512]{1,0:T(8,128)(2,1)S(1)}, u32[]{:S(2)}, u32[]{:S(2)}) collective-permute-start(bf16[128,512]{1,0:T(8,128)(2,1)S(1)} %get-tuple-element.123), channel_id=1, source_target_pairs={{0,1},{1,2},{2,3},{3,0},{4,5},{5,6},{6,7},{7,4},{8,9},{9,10},{10,1... | collective-permute-start | bytes 393224 | tf_op jit(solution)/shard_map/ppermute | solution.py:502
  246.5 15.1 %collective-permute-start.52 = (bf16[128,512]{1,0:T(8,128)(2,1)S(1)}, bf16[128,512]{1,0:T(8,128)(2,1)S(1)}, u32[]{:S(2)}, u32[]{:S(2)}) collective-permute-start(bf16[128,512]{1,0:T(8,128)(2,1)S(1)} %add.29), channel_id=1, source_target_pairs={{0,1},{1,2},{2,3},{3,0},{4,5},{5,6},{6,7},{7,4},{8,9},{9,10},{10,1... | collective-permute-start | bytes 393224 | tf_op jit(solution)/shard_map/ppermute | solution.py:502
  254.7 13.9 %collective-permute-start.54 = (bf16[128,768]{1,0:T(8,128)(2,1)S(1)}, bf16[128,768]{1,0:T(8,128)(2,1)S(1)}, u32[]{:S(2)}, u32[]{:S(2)}) collective-permute-start(bf16[128,768]{1,0:T(8,128)(2,1)S(1)} %add.31), channel_id=1, source_target_pairs={{0,1},{1,2},{2,3},{3,0},{4,5},{5,6},{6,7},{7,4},{8,9},{9,10},{10,1... | collective-permute-start | bytes 589832 | tf_op jit(solution)/shard_map/ppermute | solution.py:502
  258.8 16.0 %collective-permute-start.51 = (bf16[128,768]{1,0:T(8,128)(2,1)S(1)}, bf16[128,768]{1,0:T(8,128)(2,1)S(1)}, u32[]{:S(2)}, u32[]{:S(2)}) collective-permute-start(bf16[128,768]{1,0:T(8,128)(2,1)S(1)} %add.28), channel_id=1, source_target_pairs={{0,1},{1,2},{2,3},{3,0},{4,5},{5,6},{6,7},{7,4},{8,9},{9,10},{10,1... | collective-permute-start | bytes 589832 | tf_op jit(solution)/shard_map/ppermute | solution.py:502
  (65 other events, 596.6 us)

commit v5 on v4

--- a/solution.py
+++ b/solution.py
@@ -31,18 +31,18 @@
     return pl.CostEstimate(flops=flops, bytes_accessed=size, transcendentals=0)
 
 
-def normed_kernel(n_f, me_ref, tokens_ref, gain_ref, out_ref):
+def normed_kernel(n_f, index_ref, tokens_ref, gain_ref, out_ref):
     rows = tokens_ref[...].astype(jnp.float32)
     scale = lax.rsqrt(jnp.mean(rows * rows, axis=-1, keepdims=True) + 1e-06)
     shard = tokens_ref.shape[1] // n_f
     for j in range(n_f):
-        start = pl.multiple_of(jnp.bitwise_xor(me_ref[0], j) * shard, 128)
+        start = pl.multiple_of(jnp.bitwise_xor(index_ref[0], j) * shard, 128)
         columns = pl.ds(start, shard)
         piece = tokens_ref[:, columns].astype(jnp.float32) * scale * gain_ref[:, columns]
         out_ref[:, j * shard : (j + 1) * shard] = piece.astype(jnp.bfloat16)
 
 
-def normed_pieces(me, tokens, gain, n_f):
+def normed_pieces(index, tokens, gain, n_f):
     count, width = tokens.shape
     shard = width // n_f
     if shard % 128 == 0:
@@ -54,12 +54,12 @@
             compiler_params=params(16),
             cost_estimate=work(6 * count * width, tokens, tokens),
             name="norm",
-        )(me[None], tokens, gain[None, :])
+        )(index, tokens, gain[None, :])
     rows = tokens.astype(jnp.float32)
     meansq = jnp.mean(rows * rows, axis=-1, keepdims=True)
     normed = (rows * lax.rsqrt(meansq + 1e-06) * gain).astype(jnp.bfloat16)
     pieces = [
-        lax.dynamic_slice_in_dim(normed, jnp.bitwise_xor(me, j) * shard, shard, axis=1)
+        lax.dynamic_slice_in_dim(normed, jnp.bitwise_xor(index[0], j) * shard, shard, axis=1)
         for j in range(n_f)
     ]
     return jnp.concatenate(pieces, axis=1)
@@ -87,21 +87,19 @@
     )(q, k, v)
 
 
-def cut_kernel(w_ref, first_ref, second_ref):
-    cut = first_ref.shape[0]
-    first_ref[...] = w_ref[:cut, :]
-    second_ref[...] = w_ref[cut:, :]
-
-
-def cut_rows(w, cut):
+def cut_kernel(start, w_ref, out_ref):
+    out_ref[...] = w_ref[start : start + out_ref.shape[0], :]
+
+
+def cut_rows(w, cut, half):
     rows, columns = w.shape
     return pl.pallas_call(
-        cut_kernel,
+        functools.partial(cut_kernel, cut if half else 0),
         in_specs=[VMEM],
-        out_specs=[VMEM] * 2,
-        out_shape=[bf16(cut, columns), bf16(rows - cut, columns)],
+        out_specs=VMEM,
+        out_shape=bf16(rows - cut if half else cut, columns),
         compiler_params=params(16),
-        cost_estimate=work(0, w, w),
+        cost_estimate=work(0, w),
         name="cut",
     )(w)
 
@@ -156,7 +154,7 @@
     return parts[0] if len(parts) == 1 else jnp.concatenate(parts, axis=1)
 
 
-def finish_kernel(n_x, wide, roped, first_col, s_ref, *refs):
+def finish_kernel(n_x, wide, roped, first_col, index_ref, *refs):
     x_refs = refs[:n_x]
     w_refs = refs[n_x : n_x + 4]
     early_ref, late_ref = refs[n_x + 4 : n_x + 6]
@@ -168,7 +166,7 @@
     for i, x_ref in enumerate(x_refs):
         here = slice(i * count, (i + 1) * count)
         rows[here, :] = x_ref[:, first_col : first_col + 2 * shard]
-        place = pl.ds(pl.multiple_of(lax.rem(s_ref[0] - i + n_x, n_x) * count, count), count)
+        place = pl.ds(pl.multiple_of(lax.rem(index_ref[1] - i + n_x, n_x) * count, count), count)
         cos[here, :] = cos_ref[place, :]
         sin[here, :] = sin_ref[place, :]
     q_cols = q_out.shape[1]
@@ -203,7 +201,7 @@
         base += mine.shape[1]
 
 
-def finish(s, blocks, weights, early, late, biases, cos, sin, q_cols, first_col, wide):
+def finish(index, blocks, weights, early, late, biases, cos, sin, q_cols, first_col, wide):
     n_x, count = len(blocks), blocks[0].shape[0]
     shard = weights[0].shape[0]
     columns = early.shape[1]
@@ -222,16 +220,16 @@
         compiler_params=params(16),
         cost_estimate=work(4 * length * shard * columns, *weights, early, late),
         name="finish",
-    )(s[None], *blocks, *weights, early, late, *biases, cos, sin)
-
-
-def attend_kernel(blocks, group, s_ref, q_ref, kv_ref, out_ref, keys, values):
+    )(index, *blocks, *weights, early, late, *biases, cos, sin)
+
+
+def attend_kernel(blocks, group, index_ref, q_ref, kv_ref, out_ref, keys, values):
     length = q_ref.shape[0]
     rows = length // blocks
     factor = LOG2E / (HEAD_SIZE**0.5)
 
     def held(b):
-        return pl.ds(pl.multiple_of(lax.rem(s_ref[0] - b + blocks, blocks) * rows, rows), rows)
+        return pl.ds(pl.multiple_of(lax.rem(index_ref[1] - b + blocks, blocks) * rows, rows), rows)
 
     kv_half = kv_ref.shape[1] // 2
     for b in range(blocks):
@@ -275,7 +273,7 @@
             ]
 
 
-def attend(s, queries, kv, blocks):
+def attend(index, queries, kv, blocks):
     length, q_cols = queries.shape
     kv_half = kv.shape[1] // 2
     return pl.pallas_call(
@@ -290,7 +288,7 @@
         compiler_params=params(16),
         cost_estimate=work(4 * length * length * q_cols, queries, queries, kv),
         name="attend",
-    )(s[None], queries, kv)
+    )(index, queries, kv)
 
 
 def mix_kernel(n_w, heads_ref, *refs):
@@ -336,12 +334,12 @@
     )(a, b)
 
 
-def place_kernel(parts, me_ref, a_ref, b_ref, *refs):
+def place_kernel(parts, index_ref, a_ref, b_ref, *refs):
     out_ref, total, sem = refs[-3:]
     add_kernel(a_ref, b_ref, total)
     copies, left = [], 0
     for i, (j, shard, offset, width) in enumerate(parts):
-        start = pl.multiple_of(jnp.bitwise_xor(me_ref[0], j) * shard + offset, 128)
+        start = pl.multiple_of(jnp.bitwise_xor(index_ref[0], j) * shard + offset, 128)
         copies.append(
             pltpu.make_async_copy(
                 total.at[:, pl.ds(left, width)], out_ref.at[:, pl.ds(start, width)], sem.at[i]
@@ -354,13 +352,13 @@
         copy.wait()
 
 
-def place(mixed, me, a, b, parts, columns):
+def place(mixed, index, a, b, parts, columns):
     if any(offset % 128 or width % 128 or shard % 128 for _, shard, offset, width in parts):
         total, left = add(a, b), 0
         if mixed is None:
             mixed = jnp.zeros((a.shape[0], columns), jnp.bfloat16)
         for j, shard, offset, width in parts:
-            start = jnp.bitwise_xor(me, j) * shard + offset
+            start = jnp.bitwise_xor(index[0], j) * shard + offset
             mixed = lax.dynamic_update_slice(mixed, total[:, left : left + width], (0, start))
             left += width
         return mixed
@@ -378,7 +376,7 @@
         compiler_params=params(8),
         cost_estimate=work(0, a, a, a),
         name="place",
-    )(me[None], a, b, *held)
+    )(index, a, b, *held)
 
 
 def swapped(array, n_f, mask):
@@ -405,9 +403,30 @@
     return [held[piece] for piece in sent]
 
 
-def send_siblings(held, sibling, n_f, phase, *before):
-    for piece in [piece for piece in held if phase_of(piece) == phase]:
+def send_level(held, n_f, cut, level, *before):
+    for r in [r for r in range(1, n_f // 2) if bin(r).count("1") == level]:
+        if level == 1:
+            held[r] = [swapped(after(held[0][0], *before), n_f, 2 * r)]
+            continue
+        held[r] = []
+        for half, bit in ((0, r & -r), (1, 1 << (r.bit_length() - 1))):
+            parts = held[r ^ bit]
+            part = parts[half] if len(parts) == 2 else cut_rows(parts[0], cut, half)
+            held[r].append(swapped(after(part, *before), n_f, 2 * bit))
+
+
+def send_o_siblings(held, sibling, n_f, level, *before):
+    for r in [r for r in held if bin(r).count("1") == level]:
+        sibling[r] = [swapped(after(part, *before), n_f, 1) for part in held[r]]
+
+
+def send_siblings(held, sibling, n_f, pieces, *before):
+    for piece in pieces:
         sibling[piece] = swapped(after(held[piece], *before), n_f, 1)
+
+
+def of_phase(held, phase):
+    return [piece for piece in held if phase_of(piece) == phase]
 
 
 def rope_tables(length):
@@ -433,8 +452,7 @@
     value_offset_bias,
     out_weight,
 ):
-    me = lax.axis_index("fsdp")
-    s = lax.axis_index("sp")
+    index = jnp.stack([lax.axis_index("fsdp"), lax.axis_index("sp")])
     count = tokens.shape[0]
     chips = n_f // 2
     phases = chips.bit_length()
@@ -446,35 +464,34 @@
     ring = [(i, (i + 1) % n_s) for i in range(n_s)]
     cos, sin = rope_tables(n_s * count)
 
-    blocks = [normed_pieces(me, tokens, norm_gain, n_f)]
+    blocks = [normed_pieces(index, tokens, norm_gain, n_f)]
     first, second = pack(after(q_weight, blocks[0]), key_matrix, value_matrix, cut)
     held, sibling = {(0, 0): first, (0, 1): second}, {}
-    send_siblings(held, sibling, n_f, 0)
+    send_siblings(held, sibling, n_f, list(held))
     o_cut = shard * 3 // 5 // 128 * 128 or shard // 2 // 16 * 16
-    o_first, o_second = cut_rows(after(out_weight, first), o_cut)
-    o_held, o_sibling = {(0, 0): o_first, (0, 1): o_second}, {}
+    o_held, o_sibling = {0: [after(out_weight, first)]}, {}
 
     gates, sent = [], []
     for k in range(1, n_s):
         if k <= phases:
             sent = send_phase(held, n_f, k, *gates[-1:], *sent)
             if k > 1:
-                send_siblings(held, sibling, n_f, k - 1, *gates[-1:])
+                send_siblings(held, sibling, n_f, of_phase(held, k - 1), *gates[-1:])
         blocks.append(lax.ppermute(blocks[-1], "sp", ring))
         gates.append(blocks[-1])
-    send_siblings(o_held, o_sibling, n_f, 0, gates[0])
+    send_o_siblings(o_held, o_sibling, n_f, 0, gates[0])
 
     def parts(half, chosen):
         return [side[r, half] for r in chosen for side in (held, sibling)]
 
     most = range(chips - 1)
     early = partial(blocks[:-1], parts(0, most), parts(1, most), wide)
-    send_siblings(held, sibling, n_f, phases, gates[-1], early)
-    send_phase(o_held, n_f, 1, gates[-1], early)
+    send_siblings(held, sibling, n_f, of_phase(held, phases), gates[-1], early)
+    send_level(o_held, n_f, o_cut, 1, gates[-1], early)
     late = partial(blocks[-1:], parts(0, most), parts(1, most), wide)
     last = parts(0, [chips - 1]) + parts(1, [chips - 1])
     queries, kv = finish(
-        s,
+        index,
         blocks,
         last,
         early,
@@ -486,37 +503,42 @@
         2 * shard * (chips - 1),
         wide,
     )
-    heads = attend(s, queries, kv, n_s)
-
-    mixed, rings, previous = None, [], []
-
-    def mix_group(group):
-        nonlocal mixed
-        weights = [(o_sibling if core else o_held)[r, half] for r, half, core in group]
-        t = len(rings) - 2
-        behind = [rings[t - d][d] for d in range(n_s - 1) if t - d >= 0]
-        terms = mix(after(heads, *behind, *previous), weights, n_s)
-        previous[:] = terms[:1]
-        total, arrivals = terms[1], []
+    heads = attend(index, queries, kv, n_s)
+
+    mixed = None
+    gate, behind = [], []
+    for level in range(phases):
+        if level:
+            send_o_siblings(o_held, o_sibling, n_f, level, *gate)
+            send_level(o_held, n_f, o_cut, level + 1, *gate)
+        groups = []
+        for r in [r for r in o_held if bin(r).count("1") == level]:
+            if len(o_held[r]) == 1:
+                groups += [((r, 0, 0),), ((r, 0, 1),)]
+            else:
+                groups += [((r, half, 0), (r, half, 1)) for half in (0, 1)]
+        rings = []
+        for group in groups:
+            weights = [(o_sibling if core else o_held)[r][half] for r, half, core in group]
+            rings.append(mix(after(heads, *gate), weights, n_s))
+        totals = [terms[1] for terms in rings]
+        arrivals = []
         for k in range(2, n_s + 1):
-            arrivals.append(lax.ppermute(total, "sp", ring))
+            arrived = [lax.ppermute(total, "sp", ring) for total in totals]
+            arrivals.append(arrived)
             if k < n_s:
-                total = add(arrivals[-1], terms[k])
-        where = [
-            (2 * r + core, shard, half * o_cut, w.shape[0])
-            for (r, half, core), w in zip(group, weights)
-        ]
-        mixed = place(mixed, me, arrivals[-1], terms[0], where, shard * n_f)
-        rings.append(arrivals)
-
-    mix_group([(0, 0, 0), (0, 1, 0)])
-    mix_group([(0, 0, 1), (0, 1, 1)])
-    for phase in range(1, phases + 1):
-        gate = rings[-2][0]
-        send_siblings(o_held, o_sibling, n_f, phase, gate)
-        send_phase(o_held, n_f, phase + 1, gate)
-        for piece in [piece for piece in o_held if phase_of(piece) == phase]:
-            mix_group([(*piece, 0), (*piece, 1)])
+                held_back = behind if k == n_s - 1 else []
+                totals = [
+                    add(after(a, *held_back), terms[k]) for a, terms in zip(arrived, rings)
+                ]
+        for group, a, terms in zip(groups, arrived, rings):
+            where = [
+                (2 * r + core, shard, half * o_cut, o_held[r][half].shape[0])
+                for r, half, core in group
+            ]
+            mixed = place(mixed, index, a, terms[0], where, shard * n_f)
+        gate = arrivals[-1] if level == 0 else arrivals[0]
+        behind = arrivals[-1]
     return mixed
 
 

time: 277 us -> 231 us (0.83)
  waiting for transfers between devices: 196 us -> 167 us
  local copies, waits for them, and re-layouts: 22.9 us -> 2.4 us
  Pallas kernels: 33.6 us -> 38.1 us
    unnamed x84 -> x22, local copies, waits for them, and re-layouts: 22.9 us -> 2.4 us
    ppermute x28 -> x23, waiting for transfers between devices: 91.4 us -> 73.4 us  [swapped(): return lax.ppermute(array, 'fsdp', [(i, i ^ mask) for i in range(n_f)])]
    ppermute x24, waiting for transfers between devices: 79.6 us -> 67 us  [body(): arrived = [lax.ppermute(total, 'sp', ring) for total in totals]]
    pallas_call x8, Pallas kernels: 5.77 us -> 10.1 us  [place(): pl.pallas_call(functools.partial(place_kernel, parts), in_specs=[SMEM, VM...]
    ppermute x28 -> x23, starting transfers between devices: 14.4 us -> 13 us  [swapped(): return lax.ppermute(array, 'fsdp', [(i, i ^ mask) for i in range(n_f)])]
  transfers between devices with their start and end apart: 55 -> 50, of which waited for: 32 -> 30; matrix products, arithmetic and copies ran while one was open for 0% -> 0% of each run, Pallas kernels for 12% -> 15%
where the time goes in v5:
time: 231 us; the launch traced here: 230 us
  waiting for transfers between devices  167 us (72%)
  Pallas kernels  38.1 us (16%)
  starting transfers between devices  21.8 us (9%)
  local copies, waits for them, and re-layouts  2.4 us (1%)
    ppermute x23, waiting for transfers between devices, swapped(): return lax.ppermute(array, 'fsdp', [(i, i ^ mask) for i in range(n_f)])  73.4 us
    ppermute x24, waiting for transfers between devices, body(): arrived = [lax.ppermute(total, 'sp', ring) for total in totals]  67 us
    ppermute x3, waiting for transfers between devices, body(): blocks.append(lax.ppermute(blocks[-1], 'sp', ring))  26.9 us
    ppermute x23, starting transfers between devices, swapped(): return lax.ppermute(array, 'fsdp', [(i, i ^ mask) for i in range(n_f)])  13 us
    pallas_call x8, Pallas kernels, place(): pl.pallas_call(functools.partial(place_kernel, parts), in_specs=[SMEM, VM...  10.1 us
    pallas_call x8, Pallas kernels, mix(): pl.pallas_call(functools.partial(mix_kernel, len(parts)), in_specs=[VMEM]...  9.37 us
    pallas_call x2, Pallas kernels, partial(): pl.pallas_call(functools.partial(partial_kernel, n_x, n_r, wide), in_spec...  8.84 us
    ppermute x24, starting transfers between devices, body(): arrived = [lax.ppermute(total, 'sp', ring) for total in totals]  7.16 us
  transfers between devices with their start and end apart: 50, of which 30 were waited for; matrix products, arithmetic and copies ran while one was open for 0% of the time, Pallas kernels for 15%

profile of v5, /device:TPU:0, one launch (start us, length us, event | category | flops | bytes accessed | tf_op | source)
XLA Modules:
  0.0 230.4 jit_solution(14369617052456115634)
XLA Ops:
  3.8 3.0 %collective-permute-start.3 = (bf16[640,1024]{1,0:T(8,128)(2,1)S(1)}, bf16[640,1024]{1,0:T(8,128)(2,1)S(1)}, u32[]{:S(2)}, u32[]{:S(2)}) collective-permute-start(bf16[640,1024]{1,0:T(8,128)(2,1)S(1)} %get-tuple-element.72.refs_3_.refs_1_), channel_id=1, source_target_pairs={{0,16},{4,20},{8,24},{12,28},{16,0},{20,4},{24,8},{28,12},{1,17},{... | collective-permute-start | bytes 3932168 | tf_op jit(solution)/shard_map/ppermute | solution.py:383
  9.9 21.4 %collective-permute-done.4.refs_11_.refs_9_ = bf16[640,768]{1,0:T(8,128)(2,1)S(1)} collective-permute-done((bf16[640,768]{1,0:T(8,128)(2,1)S(1)}, bf16[640,768]{1,0:T(8,128)(2,1)S(1)}, u32[]{:S(2)}, u32[]{:S(2)}) %collective-permute-start.4) | collective-permute-done | bytes 983072 | tf_op jit(solution)/shard_map/ppermute | solution.py:383
  31.4 4.3 %collective-permute-done.3.refs_7_.refs_5_ = bf16[640,1024]{1,0:T(8,128)(2,1)S(1)} collective-permute-done((bf16[640,1024]{1,0:T(8,128)(2,1)S(1)}, bf16[640,1024]{1,0:T(8,128)(2,1)S(1)}, u32[]{:S(2)}, u32[]{:S(2)}) %collective-permute-start.3) | collective-permute-done | bytes 1310752 | tf_op jit(solution)/shard_map/ppermute | solution.py:383
  35.6 3.3 %collective-permute-done.refs_1_ = bf16[128,5120]{1,0:T(8,128)(2,1)S(1)} collective-permute-done((bf16[128,5120]{1,0:T(8,128)(2,1)S(1)}, bf16[128,5120]{1,0:T(8,128)(2,1)S(1)}, u32[]{:S(2)}, u32[]{:S(2)}) %collective-permute-start) | collective-permute-done | bytes 1310752 | tf_op jit(solution)/shard_map/ppermute | solution.py:480
  41.5 26.9 %collective-permute-done.5.refs_5_.refs_3_ = bf16[640,1024]{1,0:T(8,128)(2,1)S(1)} collective-permute-done((bf16[640,1024]{1,0:T(8,128)(2,1)S(1)}, bf16[640,1024]{1,0:T(8,128)(2,1)S(1)}, u32[]{:S(2)}, u32[]{:S(2)}) %collective-permute-start.5) | collective-permute-done | bytes 1310752 | tf_op jit(solution)/shard_map/ppermute | solution.py:383
  68.4 3.0 %collective-permute-done.1.refs_2_ = bf16[128,5120]{1,0:T(8,128)(2,1)S(1)} collective-permute-done((bf16[128,5120]{1,0:T(8,128)(2,1)S(1)}, bf16[128,5120]{1,0:T(8,128)(2,1)S(1)}, u32[]{:S(2)}, u32[]{:S(2)}) %collective-permute-start.1) | collective-permute-done | bytes 1310752 | tf_op jit(solution)/shard_map/ppermute | solution.py:480
  74.9 2.8 %collective-permute-done.13.refs_14_.refs_12_ = bf16[640,768]{1,0:T(8,128)(2,1)S(1)} collective-permute-done((bf16[640,768]{1,0:T(8,128)(2,1)S(1)}, bf16[640,768]{1,0:T(8,128)(2,1)S(1)}, u32[]{:S(2)}, u32[]{:S(2)}) %collective-permute-start.13) | collective-permute-done | bytes 983072 | tf_op jit(solution)/shard_map/ppermute | solution.py:383
  77.7 6.5 %partial.2.refs_8_ = f32[384,1792]{1,0:T(8,128)S(1)} custom-call(bf16[128,5120]{1,0:T(8,128)(2,1)S(1)} %norm.1.refs_0_, bf16[128,5120]{1,0:T(8,128)(2,1)S(1)} %collective-permute-done.refs_1_, bf16[128,5120]{1,0:T(8,128)(2,1)S(1)} %collective-permute-done.1.refs_2_, bf16[640,1024]{1,0:T(8,128)(2,1)S(1)} %get-tuple-element.72.refs_3_.refs_1_, ...), custom_call_target="tpu_custom_call" | custom-call | flops 5284823040 | bytes 20447232 | tf_op jit(solution)/shard_map/partial/pallas_call | solution.py:135
  84.3 20.6 %collective-permute-done.2.refs_0_.refs_3_ = bf16[128,5120]{1,0:T(8,128)(2,1)S(1)} collective-permute-done((bf16[128,5120]{1,0:T(8,128)(2,1)S(1)}, bf16[128,5120]{1,0:T(8,128)(2,1)S(1)}, u32[]{:S(2)}, u32[]{:S(2)}) %collective-permute-start.2) | collective-permute-done | bytes 1310752 | tf_op jit(solution)/shard_map/ppermute | solution.py:480
  106.8 2.3 %partial.3.refs_9_ = f32[128,1792]{1,0:T(8,128)S(1)} custom-call(bf16[128,5120]{1,0:T(8,128)(2,1)S(1)} %collective-permute-done.2.refs_0_.refs_3_, bf16[640,1024]{1,0:T(8,128)(2,1)S(1)} %get-tuple-element.72.refs_3_.refs_1_, bf16[640,1024]{1,0:T(8,128)(2,1)S(1)} %collective-permute-done.8.refs_4_.refs_2_, ...), custom_call_target="tpu_custom_call" | custom-call | flops 1761607680 | bytes 15990784 | tf_op jit(solution)/shard_map/partial/pallas_call | solution.py:135
  109.1 2.6 %collective-permute-done.16.refs_7_ = bf16[640,768]{1,0:T(8,128)(2,1)S(1)} collective-permute-done((bf16[640,768]{1,0:T(8,128)(2,1)S(1)}, bf16[640,768]{1,0:T(8,128)(2,1)S(1)}, u32[]{:S(2)}, u32[]{:S(2)}) %collective-permute-start.16) | collective-permute-done | bytes 983072 | tf_op jit(solution)/shard_map/ppermute | solution.py:383
  111.7 3.7 %finish.1 = (bf16[512,1280]{1,0:T(8,128)(2,1)S(1)}, bf16[512,512]{1,0:T(8,128)(2,1)S(1)}) custom-call(s32[2]{0:T(128)S(1)} %pad_add_fusion.index_ref, bf16[128,5120]{1,0:T(8,128)(2,1)S(1)} %norm.1.refs_0_, bf16[128,5120]{1,0:T(8,128)(2,1)S(1)} %collective-permute-done.refs_1_, bf16[128,5120]{1,0:T(8,128)(2,1)S(1)} %collective-permute-done.1.refs_2_, ...), custom_call_target="tpu_custom_call" | custom-call | flops 2348810240 | bytes 8257536 | tf_op jit(solution)/shard_map/finish/pallas_call | solution.py:210
  115.4 4.0 %attend.1.heads_ref = bf16[512,1280]{1,0:T(8,128)(2,1)S(1)} custom-call(s32[2]{0:T(128)S(1)} %pad_add_fusion.index_ref, bf16[512,1280]{1,0:T(8,128)(2,1)S(1)} %get-tuple-element.82.q_ref, bf16[512,512]{1,0:T(8,128)(2,1)S(1)} %get-tuple-element.83.kv_ref), custom_call_target="tpu_custom_call" | custom-call | flops 1342177280 | bytes 3145728 | tf_op jit(solution)/shard_map/attend/pallas_call | solution.py:279
  121.9 7.5 %collective-permute-done.17.a_ref = bf16[128,640]{1,0:T(8,128)(2,1)S(1)} collective-permute-done((bf16[128,640]{1,0:T(8,128)(2,1)S(1)}, bf16[128,640]{1,0:T(8,128)(2,1)S(1)}, u32[]{:S(2)}, u32[]{:S(2)}) %collective-permute-start.17) | collective-permute-done | bytes 163872 | tf_op jit(solution)/shard_map/ppermute | solution.py:527
  129.6 2.6 %collective-permute-done.21.a_ref = bf16[128,640]{1,0:T(8,128)(2,1)S(1)} collective-permute-done((bf16[128,640]{1,0:T(8,128)(2,1)S(1)}, bf16[128,640]{1,0:T(8,128)(2,1)S(1)}, u32[]{:S(2)}, u32[]{:S(2)}) %collective-permute-start.21) | collective-permute-done | bytes 163872 | tf_op jit(solution)/shard_map/ppermute | solution.py:527
  132.3 5.1 %collective-permute-done.18.a_ref = bf16[128,640]{1,0:T(8,128)(2,1)S(1)} collective-permute-done((bf16[128,640]{1,0:T(8,128)(2,1)S(1)}, bf16[128,640]{1,0:T(8,128)(2,1)S(1)}, u32[]{:S(2)}, u32[]{:S(2)}) %collective-permute-start.18) | collective-permute-done | bytes 163872 | tf_op jit(solution)/shard_map/ppermute | solution.py:527
  137.5 3.7 %collective-permute-done.22.a_ref = bf16[128,640]{1,0:T(8,128)(2,1)S(1)} collective-permute-done((bf16[128,640]{1,0:T(8,128)(2,1)S(1)}, bf16[128,640]{1,0:T(8,128)(2,1)S(1)}, u32[]{:S(2)}, u32[]{:S(2)}) %collective-permute-start.22) | collective-permute-done | bytes 163872 | tf_op jit(solution)/shard_map/ppermute | solution.py:527
  141.3 2.3 collective-permute-done.24.refs_0_.w_ref
  145.4 3.0 %collective-permute-done.23.a_ref = bf16[128,640]{1,0:T(8,128)(2,1)S(1)} collective-permute-done((bf16[128,640]{1,0:T(8,128)(2,1)S(1)}, bf16[128,640]{1,0:T(8,128)(2,1)S(1)}, u32[]{:S(2)}, u32[]{:S(2)}) %collective-permute-start.23) | collective-permute-done | bytes 163872 | tf_op jit(solution)/shard_map/ppermute | solution.py:527
  156.1 3.7 %collective-permute-done.25.a_ref = bf16[128,640]{1,0:T(8,128)(2,1)S(1)} collective-permute-done((bf16[128,640]{1,0:T(8,128)(2,1)S(1)}, bf16[128,640]{1,0:T(8,128)(2,1)S(1)}, u32[]{:S(2)}, u32[]{:S(2)}) %collective-permute-start.25) | collective-permute-done | bytes 163872 | tf_op jit(solution)/shard_map/ppermute | solution.py:527
  160.5 2.9 %collective-permute-done.29.a_ref = bf16[128,640]{1,0:T(8,128)(2,1)S(1)} collective-permute-done((bf16[128,640]{1,0:T(8,128)(2,1)S(1)}, bf16[128,640]{1,0:T(8,128)(2,1)S(1)}, u32[]{:S(2)}, u32[]{:S(2)}) %collective-permute-start.29) | collective-permute-done | bytes 163872 | tf_op jit(solution)/shard_map/ppermute | solution.py:527
  163.3 9.4 %collective-permute-done.45.refs_0_ = bf16[384,1280]{1,0:T(8,128)(2,1)S(1)} collective-permute-done((bf16[384,1280]{1,0:T(8,128)(2,1)S(1)}, bf16[384,1280]{1,0:T(8,128)(2,1)S(1)}, u32[]{:S(2)}, u32[]{:S(2)}) %collective-permute-start.45) | collective-permute-done | bytes 983072 | tf_op jit(solution)/shard_map/ppermute | solution.py:383
  176.8 3.0 %collective-permute-start.38 = (bf16[128,640]{1,0:T(8,128)(2,1)S(1)}, bf16[128,640]{1,0:T(8,128)(2,1)S(1)}, u32[]{:S(2)}, u32[]{:S(2)}) collective-permute-start(bf16[128,640]{1,0:T(8,128)(2,1)S(1)} %add.25), channel_id=1, source_target_pairs={{0,1},{1,2},{2,3},{3,0},{4,5},{5,6},{6,7},{7,4},{8,9},{9,10},{10,1... | collective-permute-start | bytes 491528 | tf_op jit(solution)/shard_map/ppermute | solution.py:527
  182.9 3.3 %collective-permute-done.47.a_ref = bf16[128,768]{1,0:T(8,128)(2,1)S(1)} collective-permute-done((bf16[128,768]{1,0:T(8,128)(2,1)S(1)}, bf16[128,768]{1,0:T(8,128)(2,1)S(1)}, u32[]{:S(2)}, u32[]{:S(2)}) %collective-permute-start.47) | collective-permute-done | bytes 196640 | tf_op jit(solution)/shard_map/ppermute | solution.py:527
  186.2 3.5 %collective-permute-done.40.a_ref = bf16[128,640]{1,0:T(8,128)(2,1)S(1)} collective-permute-done((bf16[128,640]{1,0:T(8,128)(2,1)S(1)}, bf16[128,640]{1,0:T(8,128)(2,1)S(1)}, u32[]{:S(2)}, u32[]{:S(2)}) %collective-permute-start.40) | collective-permute-done | bytes 163872 | tf_op jit(solution)/shard_map/ppermute | solution.py:527
  189.7 3.5 %collective-permute-done.38.a_ref = bf16[128,640]{1,0:T(8,128)(2,1)S(1)} collective-permute-done((bf16[128,640]{1,0:T(8,128)(2,1)S(1)}, bf16[128,640]{1,0:T(8,128)(2,1)S(1)}, u32[]{:S(2)}, u32[]{:S(2)}) %collective-permute-start.38) | collective-permute-done | bytes 163872 | tf_op jit(solution)/shard_map/ppermute | solution.py:527
  193.2 3.5 %collective-permute-done.42.a_ref = bf16[128,640]{1,0:T(8,128)(2,1)S(1)} collective-permute-done((bf16[128,640]{1,0:T(8,128)(2,1)S(1)}, bf16[128,640]{1,0:T(8,128)(2,1)S(1)}, u32[]{:S(2)}, u32[]{:S(2)}) %collective-permute-start.42) | collective-permute-done | bytes 163872 | tf_op jit(solution)/shard_map/ppermute | solution.py:527
  196.7 2.8 %collective-permute-done.34.a_ref = bf16[128,512]{1,0:T(8,128)(2,1)S(1)} collective-permute-done((bf16[128,512]{1,0:T(8,128)(2,1)S(1)}, bf16[128,512]{1,0:T(8,128)(2,1)S(1)}, u32[]{:S(2)}, u32[]{:S(2)}) %collective-permute-start.34) | collective-permute-done | bytes 131104 | tf_op jit(solution)/shard_map/ppermute | solution.py:527
  199.5 3.5 %collective-permute-done.37.a_ref = bf16[128,640]{1,0:T(8,128)(2,1)S(1)} collective-permute-done((bf16[128,640]{1,0:T(8,128)(2,1)S(1)}, bf16[128,640]{1,0:T(8,128)(2,1)S(1)}, u32[]{:S(2)}, u32[]{:S(2)}) %collective-permute-start.37) | collective-permute-done | bytes 163872 | tf_op jit(solution)/shard_map/ppermute | solution.py:527
  203.0 7.7 %collective-permute-done.41.a_ref = bf16[128,640]{1,0:T(8,128)(2,1)S(1)} collective-permute-done((bf16[128,640]{1,0:T(8,128)(2,1)S(1)}, bf16[128,640]{1,0:T(8,128)(2,1)S(1)}, u32[]{:S(2)}, u32[]{:S(2)}) %collective-permute-start.41) | collective-permute-done | bytes 163872 | tf_op jit(solution)/shard_map/ppermute | solution.py:527
  210.7 3.5 %collective-permute-done.39.a_ref = bf16[128,640]{1,0:T(8,128)(2,1)S(1)} collective-permute-done((bf16[128,640]{1,0:T(8,128)(2,1)S(1)}, bf16[128,640]{1,0:T(8,128)(2,1)S(1)}, u32[]{:S(2)}, u32[]{:S(2)}) %collective-permute-start.39) | collective-permute-done | bytes 163872 | tf_op jit(solution)/shard_map/ppermute | solution.py:527
  214.2 3.5 %collective-permute-done.43.a_ref = bf16[128,640]{1,0:T(8,128)(2,1)S(1)} collective-permute-done((bf16[128,640]{1,0:T(8,128)(2,1)S(1)}, bf16[128,640]{1,0:T(8,128)(2,1)S(1)}, u32[]{:S(2)}, u32[]{:S(2)}) %collective-permute-start.43) | collective-permute-done | bytes 163872 | tf_op jit(solution)/shard_map/ppermute | solution.py:527
  (131 shorter events, 47.5 us)
Async XLA Ops:
  3.8 31.8 %collective-permute-start.3 = (bf16[640,1024]{1,0:T(8,128)(2,1)S(1)}, bf16[640,1024]{1,0:T(8,128)(2,1)S(1)}, u32[]{:S(2)}, u32[]{:S(2)}) collective-permute-start(bf16[640,1024]{1,0:T(8,128)(2,1)S(1)} %get-tuple-element.72.refs_3_.refs_1_), channel_id=1, source_target_pairs={{0,16},{4,20},{8,24},{12,28},{16,0},{20,4},{24,8},{28,12},{1,17},{... | collective-permute-start | bytes 3932168 | tf_op jit(solution)/shard_map/ppermute | solution.py:383
  6.9 32.1 %collective-permute-start = (bf16[128,5120]{1,0:T(8,128)(2,1)S(1)}, bf16[128,5120]{1,0:T(8,128)(2,1)S(1)}, u32[]{:S(2)}, u32[]{:S(2)}) collective-permute-start(bf16[128,5120]{1,0:T(8,128)(2,1)S(1)} %norm.1.refs_0_), channel_id=1, source_target_pairs={{0,1},{1,2},{2,3},{3,0},{4,5},{5,6},{6,7},{7,4},{8,9},{9,10},{10,1... | collective-permute-start | bytes 3932168 | tf_op jit(solution)/shard_map/ppermute | solution.py:480
  8.4 22.9 %collective-permute-start.4 = (bf16[640,768]{1,0:T(8,128)(2,1)S(1)}, bf16[640,768]{1,0:T(8,128)(2,1)S(1)}, u32[]{:S(2)}, u32[]{:S(2)}) collective-permute-start(bf16[640,768]{1,0:T(8,128)(2,1)S(1)} %get-tuple-element.73.refs_9_.refs_7_), channel_id=1, source_target_pairs={{0,8},{4,12},{8,0},{12,4},{16,24},{20,28},{24,16},{28,20},{1,9},{5... | collective-permute-start | bytes 2949128 | tf_op jit(solution)/shard_map/ppermute | solution.py:383
  39.0 29.4 %collective-permute-start.5 = (bf16[640,1024]{1,0:T(8,128)(2,1)S(1)}, bf16[640,1024]{1,0:T(8,128)(2,1)S(1)}, u32[]{:S(2)}, u32[]{:S(2)}) collective-permute-start(bf16[640,1024]{1,0:T(8,128)(2,1)S(1)} %get-tuple-element.72.refs_3_.refs_1_), channel_id=1, source_target_pairs={{0,8},{4,12},{8,0},{12,4},{16,24},{20,28},{24,16},{28,20},{1,9},{5... | collective-permute-start | bytes 3932168 | tf_op jit(solution)/shard_map/ppermute | solution.py:383
  40.5 30.9 %collective-permute-start.1 = (bf16[128,5120]{1,0:T(8,128)(2,1)S(1)}, bf16[128,5120]{1,0:T(8,128)(2,1)S(1)}, u32[]{:S(2)}, u32[]{:S(2)}) collective-permute-start(bf16[128,5120]{1,0:T(8,128)(2,1)S(1)} %collective-permute-done.refs_1_), channel_id=1, source_target_pairs={{0,1},{1,2},{2,3},{3,0},{4,5},{5,6},{6,7},{7,4},{8,9},{9,10},{10,1... | collective-permute-start | bytes 3932168 | tf_op jit(solution)/shard_map/ppermute | solution.py:480
  40.5 30.9 %collective-permute-start.6 = (bf16[640,768]{1,0:T(8,128)(2,1)S(1)}, bf16[640,768]{1,0:T(8,128)(2,1)S(1)}, u32[]{:S(2)}, u32[]{:S(2)}) collective-permute-start(bf16[640,768]{1,0:T(8,128)(2,1)S(1)} %get-tuple-element.73.refs_9_.refs_7_), channel_id=1, source_target_pairs={{0,16},{4,20},{8,24},{12,28},{16,0},{20,4},{24,8},{28,12},{1,17},{... | collective-permute-start | bytes 2949128 | tf_op jit(solution)/shard_map/ppermute | solution.py:383
  41.0 31.0 %collective-permute-start.8 = (bf16[640,1024]{1,0:T(8,128)(2,1)S(1)}, bf16[640,1024]{1,0:T(8,128)(2,1)S(1)}, u32[]{:S(2)}, u32[]{:S(2)}) collective-permute-start(bf16[640,1024]{1,0:T(8,128)(2,1)S(1)} %get-tuple-element.72.refs_3_.refs_1_), channel_id=1, source_target_pairs={{0,4},{4,0},{8,12},{12,8},{16,20},{20,16},{24,28},{28,24},{1,5},{5... | collective-permute-start | bytes 3932168 | tf_op jit(solution)/shard_map/ppermute | solution.py:383
  41.0 30.9 %collective-permute-start.11 = (bf16[640,768]{1,0:T(8,128)(2,1)S(1)}, bf16[640,768]{1,0:T(8,128)(2,1)S(1)}, u32[]{:S(2)}, u32[]{:S(2)}) collective-permute-start(bf16[640,768]{1,0:T(8,128)(2,1)S(1)} %get-tuple-element.73.refs_9_.refs_7_), channel_id=1, source_target_pairs={{0,4},{4,0},{8,12},{12,8},{16,20},{20,16},{24,28},{28,24},{1,5},{5... | collective-permute-start | bytes 2949128 | tf_op jit(solution)/shard_map/ppermute | solution.py:383
  72.0 32.9 %collective-permute-start.2 = (bf16[128,5120]{1,0:T(8,128)(2,1)S(1)}, bf16[128,5120]{1,0:T(8,128)(2,1)S(1)}, u32[]{:S(2)}, u32[]{:S(2)}) collective-permute-start(bf16[128,5120]{1,0:T(8,128)(2,1)S(1)} %collective-permute-done.1.refs_2_), channel_id=1, source_target_pairs={{0,1},{1,2},{2,3},{3,0},{4,5},{5,6},{6,7},{7,4},{8,9},{9,10},{10,1... | collective-permute-start | bytes 3932168 | tf_op jit(solution)/shard_map/ppermute | solution.py:480
  72.0 32.9 %collective-permute-start.7 = (bf16[640,1024]{1,0:T(8,128)(2,1)S(1)}, bf16[640,1024]{1,0:T(8,128)(2,1)S(1)}, u32[]{:S(2)}, u32[]{:S(2)}) collective-permute-start(bf16[640,1024]{1,0:T(8,128)(2,1)S(1)} %collective-permute-done.3.refs_7_.refs_5_), channel_id=1, source_target_pairs={{0,8},{4,12},{8,0},{12,4},{16,24},{20,28},{24,16},{28,20},{1,9},{5... | collective-permute-start | bytes 3932168 | tf_op jit(solution)/shard_map/ppermute | solution.py:383
  74.4 31.0 %collective-permute-start.15 = (bf16[640,768]{1,0:T(8,128)(2,1)S(1)}, bf16[640,768]{1,0:T(8,128)(2,1)S(1)}, u32[]{:S(2)}, u32[]{:S(2)}) collective-permute-start(bf16[640,768]{1,0:T(8,128)(2,1)S(1)} %collective-permute-done.4.refs_11_.refs_9_), channel_id=1, source_target_pairs={{0,16},{4,20},{8,24},{12,28},{16,0},{20,4},{24,8},{28,12},{1,17},{... | collective-permute-start | bytes 2949128 | tf_op jit(solution)/shard_map/ppermute | solution.py:383
  104.9 15.8 %collective-permute-start.20 = (bf16[640,1280]{1,0:T(8,128)(2,1)S(1)}, bf16[640,1280]{1,0:T(8,128)(2,1)S(1)}, u32[]{:S(2)}, u32[]{:S(2)}) collective-permute-start(bf16[640,1280]{1,0:T(8,128)(2,1)S(1)} %copy-done.10), channel_id=1, source_target_pairs={{0,4},{4,0},{8,12},{12,8},{16,20},{20,16},{24,28},{28,24},{1,5},{5... | collective-permute-start | bytes 4915208 | tf_op jit(solution)/shard_map/ppermute | solution.py:383
  105.5 38.1 %collective-permute-start.24 = (bf16[640,1280]{1,0:T(8,128)(2,1)S(1)}, bf16[640,1280]{1,0:T(8,128)(2,1)S(1)}, u32[]{:S(2)}, u32[]{:S(2)}) collective-permute-start(bf16[640,1280]{1,0:T(8,128)(2,1)S(1)} %copy-done.10), channel_id=1, source_target_pairs={{0,8},{4,12},{8,0},{12,4},{16,24},{20,28},{24,16},{28,20},{1,9},{5... | collective-permute-start | bytes 4915208 | tf_op jit(solution)/shard_map/ppermute | solution.py:383
  106.0 42.4 %collective-permute-start.28 = (bf16[640,1280]{1,0:T(8,128)(2,1)S(1)}, bf16[640,1280]{1,0:T(8,128)(2,1)S(1)}, u32[]{:S(2)}, u32[]{:S(2)}) collective-permute-start(bf16[640,1280]{1,0:T(8,128)(2,1)S(1)} %copy-done.10), channel_id=1, source_target_pairs={{0,16},{4,20},{8,24},{12,28},{16,0},{20,4},{24,8},{28,12},{1,17},{... | collective-permute-start | bytes 4915208 | tf_op jit(solution)/shard_map/ppermute | solution.py:383
  121.9 10.3 %collective-permute-start.21 = (bf16[128,640]{1,0:T(8,128)(2,1)S(1)}, bf16[128,640]{1,0:T(8,128)(2,1)S(1)}, u32[]{:S(2)}, u32[]{:S(2)}) collective-permute-start(bf16[128,640]{1,0:T(8,128)(2,1)S(1)} %get-tuple-element.89), channel_id=1, source_target_pairs={{0,1},{1,2},{2,3},{3,0},{4,5},{5,6},{6,7},{7,4},{8,9},{9,10},{10,1... | collective-permute-start | bytes 491528 | tf_op jit(solution)/shard_map/ppermute | solution.py:527
  149.0 23.7 %collective-permute-start.45 = (bf16[384,1280]{1,0:T(8,128)(2,1)S(1)}, bf16[384,1280]{1,0:T(8,128)(2,1)S(1)}, u32[]{:S(2)}, u32[]{:S(2)}) collective-permute-start(bf16[384,1280]{1,0:T(8,128)(2,1)S(1)} %cut.3), channel_id=1, source_target_pairs={{0,8},{4,12},{8,0},{12,4},{16,24},{20,28},{24,16},{28,20},{1,9},{5... | collective-permute-start | bytes 2949128 | tf_op jit(solution)/shard_map/ppermute | solution.py:383
  152.2 11.2 %collective-permute-start.29 = (bf16[128,640]{1,0:T(8,128)(2,1)S(1)}, bf16[128,640]{1,0:T(8,128)(2,1)S(1)}, u32[]{:S(2)}, u32[]{:S(2)}) collective-permute-start(bf16[128,640]{1,0:T(8,128)(2,1)S(1)} %get-tuple-element.97), channel_id=1, source_target_pairs={{0,1},{1,2},{2,3},{3,0},{4,5},{5,6},{6,7},{7,4},{8,9},{9,10},{10,1... | collective-permute-start | bytes 491528 | tf_op jit(solution)/shard_map/ppermute | solution.py:527
  152.2 20.5 %collective-permute-start.32 = (bf16[256,1280]{1,0:T(8,128)(2,1)S(1)}, bf16[256,1280]{1,0:T(8,128)(2,1)S(1)}, u32[]{:S(2)}, u32[]{:S(2)}) collective-permute-start(bf16[256,1280]{1,0:T(8,128)(2,1)S(1)} %cut.2), channel_id=1, source_target_pairs={{0,16},{4,20},{8,24},{12,28},{16,0},{20,4},{24,8},{28,12},{1,17},{... | collective-permute-start | bytes 1966088 | tf_op jit(solution)/shard_map/ppermute | solution.py:383
  154.3 18.4 %collective-permute-start.27 = (bf16[128,640]{1,0:T(8,128)(2,1)S(1)}, bf16[128,640]{1,0:T(8,128)(2,1)S(1)}, u32[]{:S(2)}, u32[]{:S(2)}) collective-permute-start(bf16[128,640]{1,0:T(8,128)(2,1)S(1)} %get-tuple-element.96), channel_id=1, source_target_pairs={{0,1},{1,2},{2,3},{3,0},{4,5},{5,6},{6,7},{7,4},{8,9},{9,10},{10,1... | collective-permute-start | bytes 491528 | tf_op jit(solution)/shard_map/ppermute | solution.py:527
  159.8 12.9 %collective-permute-start.31 = (bf16[128,640]{1,0:T(8,128)(2,1)S(1)}, bf16[128,640]{1,0:T(8,128)(2,1)S(1)}, u32[]{:S(2)}, u32[]{:S(2)}) collective-permute-start(bf16[128,640]{1,0:T(8,128)(2,1)S(1)} %get-tuple-element.99), channel_id=1, source_target_pairs={{0,1},{1,2},{2,3},{3,0},{4,5},{5,6},{6,7},{7,4},{8,9},{9,10},{10,1... | collective-permute-start | bytes 491528 | tf_op jit(solution)/shard_map/ppermute | solution.py:527
  176.5 9.6 %collective-permute-start.47 = (bf16[128,768]{1,0:T(8,128)(2,1)S(1)}, bf16[128,768]{1,0:T(8,128)(2,1)S(1)}, u32[]{:S(2)}, u32[]{:S(2)}) collective-permute-start(bf16[128,768]{1,0:T(8,128)(2,1)S(1)} %get-tuple-element.122), channel_id=1, source_target_pairs={{0,1},{1,2},{2,3},{3,0},{4,5},{5,6},{6,7},{7,4},{8,9},{9,10},{10,1... | collective-permute-start | bytes 589832 | tf_op jit(solution)/shard_map/ppermute | solution.py:527
  176.7 13.0 %collective-permute-start.40 = (bf16[128,640]{1,0:T(8,128)(2,1)S(1)}, bf16[128,640]{1,0:T(8,128)(2,1)S(1)}, u32[]{:S(2)}, u32[]{:S(2)}) collective-permute-start(bf16[128,640]{1,0:T(8,128)(2,1)S(1)} %add.27), channel_id=1, source_target_pairs={{0,1},{1,2},{2,3},{3,0},{4,5},{5,6},{6,7},{7,4},{8,9},{9,10},{10,1... | collective-permute-start | bytes 491528 | tf_op jit(solution)/shard_map/ppermute | solution.py:527
  176.8 16.4 %collective-permute-start.38 = (bf16[128,640]{1,0:T(8,128)(2,1)S(1)}, bf16[128,640]{1,0:T(8,128)(2,1)S(1)}, u32[]{:S(2)}, u32[]{:S(2)}) collective-permute-start(bf16[128,640]{1,0:T(8,128)(2,1)S(1)} %add.25), channel_id=1, source_target_pairs={{0,1},{1,2},{2,3},{3,0},{4,5},{5,6},{6,7},{7,4},{8,9},{9,10},{10,1... | collective-permute-start | bytes 491528 | tf_op jit(solution)/shard_map/ppermute | solution.py:527
  179.8 16.8 %collective-permute-start.42 = (bf16[128,640]{1,0:T(8,128)(2,1)S(1)}, bf16[128,640]{1,0:T(8,128)(2,1)S(1)}, u32[]{:S(2)}, u32[]{:S(2)}) collective-permute-start(bf16[128,640]{1,0:T(8,128)(2,1)S(1)} %add.29), channel_id=1, source_target_pairs={{0,1},{1,2},{2,3},{3,0},{4,5},{5,6},{6,7},{7,4},{8,9},{9,10},{10,1... | collective-permute-start | bytes 491528 | tf_op jit(solution)/shard_map/ppermute | solution.py:527
  182.7 16.7 %collective-permute-start.34 = (bf16[128,512]{1,0:T(8,128)(2,1)S(1)}, bf16[128,512]{1,0:T(8,128)(2,1)S(1)}, u32[]{:S(2)}, u32[]{:S(2)}) collective-permute-start(bf16[128,512]{1,0:T(8,128)(2,1)S(1)} %get-tuple-element.103), channel_id=1, source_target_pairs={{0,1},{1,2},{2,3},{3,0},{4,5},{5,6},{6,7},{7,4},{8,9},{9,10},{10,1... | collective-permute-start | bytes 393224 | tf_op jit(solution)/shard_map/ppermute | solution.py:527
  186.2 16.9 %collective-permute-start.37 = (bf16[128,640]{1,0:T(8,128)(2,1)S(1)}, bf16[128,640]{1,0:T(8,128)(2,1)S(1)}, u32[]{:S(2)}, u32[]{:S(2)}) collective-permute-start(bf16[128,640]{1,0:T(8,128)(2,1)S(1)} %add.24), channel_id=1, source_target_pairs={{0,1},{1,2},{2,3},{3,0},{4,5},{5,6},{6,7},{7,4},{8,9},{9,10},{10,1... | collective-permute-start | bytes 491528 | tf_op jit(solution)/shard_map/ppermute | solution.py:527
  189.7 28.1 %collective-permute-start.48 = (bf16[128,768]{1,0:T(8,128)(2,1)S(1)}, bf16[128,768]{1,0:T(8,128)(2,1)S(1)}, u32[]{:S(2)}, u32[]{:S(2)}) collective-permute-start(bf16[128,768]{1,0:T(8,128)(2,1)S(1)} %add.32), channel_id=1, source_target_pairs={{0,1},{1,2},{2,3},{3,0},{4,5},{5,6},{6,7},{7,4},{8,9},{9,10},{10,1... | collective-permute-start | bytes 589832 | tf_op jit(solution)/shard_map/ppermute | solution.py:527
  193.2 17.6 %collective-permute-start.41 = (bf16[128,640]{1,0:T(8,128)(2,1)S(1)}, bf16[128,640]{1,0:T(8,128)(2,1)S(1)}, u32[]{:S(2)}, u32[]{:S(2)}) collective-permute-start(bf16[128,640]{1,0:T(8,128)(2,1)S(1)} %add.28), channel_id=1, source_target_pairs={{0,1},{1,2},{2,3},{3,0},{4,5},{5,6},{6,7},{7,4},{8,9},{9,10},{10,1... | collective-permute-start | bytes 491528 | tf_op jit(solution)/shard_map/ppermute | solution.py:527
  196.7 17.6 %collective-permute-start.39 = (bf16[128,640]{1,0:T(8,128)(2,1)S(1)}, bf16[128,640]{1,0:T(8,128)(2,1)S(1)}, u32[]{:S(2)}, u32[]{:S(2)}) collective-permute-start(bf16[128,640]{1,0:T(8,128)(2,1)S(1)} %add.26), channel_id=1, source_target_pairs={{0,1},{1,2},{2,3},{3,0},{4,5},{5,6},{6,7},{7,4},{8,9},{9,10},{10,1... | collective-permute-start | bytes 491528 | tf_op jit(solution)/shard_map/ppermute | solution.py:527
  199.5 18.3 %collective-permute-start.43 = (bf16[128,640]{1,0:T(8,128)(2,1)S(1)}, bf16[128,640]{1,0:T(8,128)(2,1)S(1)}, u32[]{:S(2)}, u32[]{:S(2)}) collective-permute-start(bf16[128,640]{1,0:T(8,128)(2,1)S(1)} %add.30), channel_id=1, source_target_pairs={{0,1},{1,2},{2,3},{3,0},{4,5},{5,6},{6,7},{7,4},{8,9},{9,10},{10,1... | collective-permute-start | bytes 491528 | tf_op jit(solution)/shard_map/ppermute | solution.py:527
  203.0 17.0 %collective-permute-start.35 = (bf16[128,512]{1,0:T(8,128)(2,1)S(1)}, bf16[128,512]{1,0:T(8,128)(2,1)S(1)}, u32[]{:S(2)}, u32[]{:S(2)}) collective-permute-start(bf16[128,512]{1,0:T(8,128)(2,1)S(1)} %add.22), channel_id=1, source_target_pairs={{0,1},{1,2},{2,3},{3,0},{4,5},{5,6},{6,7},{7,4},{8,9},{9,10},{10,1... | collective-permute-start | bytes 393224 | tf_op jit(solution)/shard_map/ppermute | solution.py:527
  217.8 9.9 %collective-permute-start.49 = (bf16[128,768]{1,0:T(8,128)(2,1)S(1)}, bf16[128,768]{1,0:T(8,128)(2,1)S(1)}, u32[]{:S(2)}, u32[]{:S(2)}) collective-permute-start(bf16[128,768]{1,0:T(8,128)(2,1)S(1)} %add.33), channel_id=1, source_target_pairs={{0,1},{1,2},{2,3},{3,0},{4,5},{5,6},{6,7},{7,4},{8,9},{9,10},{10,1... | collective-permute-start | bytes 589832 | tf_op jit(solution)/shard_map/ppermute | solution.py:527
  (29 other events, 359.5 us)

commit v6 on v5

v6 whole, which is shorter than its diff:
```python
import functools

import jax
import jax.numpy as jnp
import numpy as np
from jax import lax
from jax.experimental import pallas as pl
from jax.experimental.pallas import tpu as pltpu
from jax.sharding import PartitionSpec as P

HEAD_SIZE = 128
HALF = HEAD_SIZE // 2
ROPE_BASE = 1000000.0
LOG2E = 1.4426950408889634
NT = (((1,), (1,)), ((), ()))
VMEM = pl.BlockSpec(memory_space=pltpu.VMEM)
SMEM = pl.BlockSpec(memory_space=pltpu.SMEM)
ANY = pl.BlockSpec(memory_space=pl.ANY)


def params(mib):
    return pltpu.CompilerParams(vmem_limit_bytes=mib * 1024 * 1024)


def bf16(*shape):
    return jax.ShapeDtypeStruct(shape, jnp.bfloat16)


def work(flops, *arrays):
    size = sum(int(np.prod(x.shape)) * x.dtype.itemsize for x in arrays)
    return pl.CostEstimate(flops=flops, bytes_accessed=size, transcendentals=0)


def normed_kernel(n_f, index_ref, tokens_ref, gain_ref, out_ref):
    rows = tokens_ref[...].astype(jnp.float32)
    scale = lax.rsqrt(jnp.mean(rows * rows, axis=-1, keepdims=True) + 1e-06)
    shard = tokens_ref.shape[1] // n_f
    for j in range(n_f):
        start = pl.multiple_of(jnp.bitwise_xor(index_ref[0], j) * shard, 128)
        columns = pl.ds(start, shard)
        piece = tokens_ref[:, columns].astype(jnp.float32) * scale * gain_ref[:, columns]
        out_ref[:, j * shard : (j + 1) * shard] = piece.astype(jnp.bfloat16)


def normed_pieces(index, tokens, gain, n_f):
    count, width = tokens.shape
    shard = width // n_f
    if shard % 128 == 0:
        return pl.pallas_call(
            functools.partial(normed_kernel, n_f),
            out_shape=bf16(count, width),
            in_specs=[SMEM, VMEM, VMEM],
            out_specs=VMEM,
            compiler_params=params(16),
            cost_estimate=work(6 * count * width, tokens, tokens),
            name="norm",
        )(index, tokens, gain[None, :])
    rows = tokens.astype(jnp.float32)
    meansq = jnp.mean(rows * rows, axis=-1, keepdims=True)
    normed = (rows * lax.rsqrt(meansq + 1e-06) * gain).astype(jnp.bfloat16)
    pieces = [
        lax.dynamic_slice_in_dim(normed, jnp.bitwise_xor(index[0], j) * shard, shard, axis=1)
        for j in range(n_f)
    ]
    return jnp.concatenate(pieces, axis=1)


def pack_kernel(*refs):
    out_ref, at = refs[-1], 0
    for ref in refs[:-1]:
        out_ref[:, at : at + ref.shape[1]] = ref[...]
        at += ref.shape[1]


def pack(*arrays):
    return pl.pallas_call(
        pack_kernel,
        in_specs=[VMEM] * len(arrays),
        out_specs=VMEM,
        out_shape=bf16(arrays[0].shape[0], sum(x.shape[1] for x in arrays)),
        compiler_params=params(16),
        cost_estimate=work(0, *arrays, *arrays),
        name="pack",
    )(*arrays)


def cut_kernel(rows, columns, ref, out_ref):
    out_ref[...] = ref[rows, columns]


def part_of(array, cut, half, axis):
    bounds = [slice(0, size) for size in array.shape]
    bounds[axis] = slice(cut, array.shape[axis]) if half else slice(0, cut)
    return pl.pallas_call(
        functools.partial(cut_kernel, *bounds),
        in_specs=[VMEM],
        out_specs=VMEM,
        out_shape=bf16(*[bound.stop - bound.start for bound in bounds]),
        compiler_params=params(16),
        cost_estimate=work(0, array),
        name="cut",
    )(array)


def partial_kernel(n_x, counts, wide, *refs):
    x_refs, w_refs, (out_ref, rows) = refs[:n_x], refs[n_x:-2], refs[-2:]
    at = 0
    for x_ref in x_refs:
        rows[at : at + x_ref.shape[0], :] = x_ref[:, : rows.shape[1]]
        at += x_ref.shape[0]
    shard = w_refs[0].shape[0]
    pieces, at = [], 0
    for count in counts:
        pieces.append(w_refs[at : at + count])
        at += count
    for col in range(0, out_ref.shape[1], wide):
        total = None
        for j, parts in enumerate(pieces):
            at = col
            for w_ref in parts:
                if at < w_ref.shape[1]:
                    break
                at -= w_ref.shape[1]
            term = jnp.dot(
                rows[:, j * shard : (j + 1) * shard],
                w_ref[:, at : at + wide],
                preferred_element_type=jnp.float32,
            )
            total = term if total is None else total + term
        out_ref[:, col : col + wide] = total


def partial(blocks, pieces, wide):
    weights = [part for piece in pieces for part in piece]
    length = sum(block.shape[0] for block in blocks)
    depth = len(pieces) * weights[0].shape[0]
    columns = sum(part.shape[1] for part in pieces[0])
    out = jax.ShapeDtypeStruct((length, columns), jnp.float32)
    counts = [len(piece) for piece in pieces]
    return pl.pallas_call(
        functools.partial(partial_kernel, len(blocks), counts, wide),
        in_specs=[VMEM] * (len(blocks) + len(weights)),
        out_specs=VMEM,
        out_shape=out,
        scratch_shapes=[pltpu.VMEM((length, depth), jnp.bfloat16)],
        compiler_params=params(16),
        cost_estimate=work(2 * length * depth * columns, *blocks, *weights, out),
        name="partial",
    )(*blocks, *weights)


def rope_tile(tile, cos, sin):
    parts = []
    for at in range(0, tile.shape[1], HEAD_SIZE):
        head = tile[:, at : at + HEAD_SIZE]
        parts.append(head * cos + pltpu.roll(head, HALF, axis=1) * sin)
    return parts[0] if len(parts) == 1 else jnp.concatenate(parts, axis=1)


def finish_kernel(n_x, offsets, wide, roped, first_col, index_ref, *refs):
    x_refs = refs[:n_x]
    w_refs = refs[n_x : n_x + 4]
    early_ref, late_ref = refs[n_x + 4 : n_x + 6]
    bias_refs, (cos_ref, sin_ref) = refs[n_x + 6 : n_x + 9], refs[n_x + 9 : n_x + 11]
    q_out, kv_out, rows, cos, sin = refs[n_x + 11 :]
    shard = w_refs[0].shape[0]
    at = 0
    for x_ref in x_refs:
        rows[at : at + x_ref.shape[0], :] = x_ref[:, first_col : first_col + 2 * shard]
        at += x_ref.shape[0]
    blocks = len(offsets)
    count = at // blocks
    for k, offset in enumerate(offsets):
        block = lax.rem(index_ref[1] - offset + blocks, blocks)
        place = pl.ds(pl.multiple_of(block * count, count), count)
        cos[k * count : (k + 1) * count, :] = cos_ref[place, :]
        sin[k * count : (k + 1) * count, :] = sin_ref[place, :]
    q_cols = q_out.shape[1]

    def bias_tile(col):
        for bias_ref in bias_refs:
            if col < bias_ref.shape[0]:
                return bias_ref[pl.ds(col, wide)][None, :]
            col -= bias_ref.shape[0]

    base = 0
    for mine, sibling in (w_refs[:2], w_refs[2:]):
        for at in range(0, mine.shape[1], wide):
            total = jnp.dot(
                rows[:, :shard], mine[:, at : at + wide], preferred_element_type=jnp.float32
            )
            total = total + jnp.dot(
                rows[:, shard:], sibling[:, at : at + wide], preferred_element_type=jnp.float32
            )
            col = base + at
            total = total + jnp.concatenate(
                [early_ref[:, col : col + wide], late_ref[:, col : col + wide]], axis=0
            )
            total = total + bias_tile(col)
            if col < roped:
                total = rope_tile(total, cos[...], sin[...])
            total = total.astype(jnp.bfloat16)
            if col < q_cols:
                q_out[:, col : col + wide] = total
            else:
                kv_out[:, col - q_cols : col - q_cols + wide] = total
        base += mine.shape[1]


def finish(index, blocks, offsets, weights, early, late, biases, cos, sin, q_cols, first_col, wide):
    n_x = len(blocks)
    length = sum(block.shape[0] for block in blocks)
    shard = weights[0].shape[0]
    columns = early.shape[1]
    kv_cols = columns - q_cols
    return pl.pallas_call(
        functools.partial(finish_kernel, n_x, offsets, wide, q_cols + kv_cols // 2, first_col),
        in_specs=[SMEM] + [VMEM] * (n_x + 11),
        out_specs=[VMEM, VMEM],
        out_shape=[bf16(length, q_cols), bf16(length, kv_cols)],
        scratch_shapes=[
            pltpu.VMEM((length, 2 * shard), jnp.bfloat16),
            pltpu.VMEM((length, HEAD_SIZE), jnp.float32),
            pltpu.VMEM((length, HEAD_SIZE), jnp.float32),
        ],
        compiler_params=params(16),
        cost_estimate=work(4 * length * shard * columns, *weights, early, late),
        name="finish",
    )(index, *blocks, *weights, early, late, *biases, cos, sin)


def attend_kernel(offsets, group, index_ref, q_ref, kv_ref, out_ref, keys, values):
    blocks = len(offsets)
    rows = q_ref.shape[0] // blocks
    factor = LOG2E / (HEAD_SIZE**0.5)

    def held(b):
        offset = lax.rem(index_ref[1] - b + blocks, blocks)
        k = sum(jnp.where(offset == value, i, 0) for i, value in enumerate(offsets))
        return pl.ds(pl.multiple_of(k * rows, rows), rows)

    kv_half = kv_ref.shape[1] // 2
    for b in range(blocks):
        keys[b * rows : (b + 1) * rows, :] = kv_ref[held(b), :kv_half]
        values[b * rows : (b + 1) * rows, :] = kv_ref[held(b), kv_half:]
    row = lax.broadcasted_iota(jnp.int32, (rows, rows), 0)
    column = lax.broadcasted_iota(jnp.int32, (rows, rows), 1)
    causal = row >= column
    causal = jnp.concatenate([causal.astype(jnp.float32)] * group, axis=0) > 0.5
    for g, b in [(g, b) for g in range(kv_half // HEAD_SIZE) for b in range(blocks)]:
        left = g * group * HEAD_SIZE
        head = slice(g * HEAD_SIZE, (g + 1) * HEAD_SIZE)
        q_block = q_ref[held(b), left : left + group * HEAD_SIZE]
        queries = jnp.concatenate(
            [q_block[:, h * HEAD_SIZE : (h + 1) * HEAD_SIZE] for h in range(group)], axis=0
        )
        at = b * rows
        near = lax.dot_general(
            queries, keys[at : at + rows, head], NT, preferred_element_type=jnp.float32
        )
        near = jnp.where(causal, near, jnp.float32(-1e30))
        largest = jnp.max(near, axis=-1, keepdims=True)
        if b > 0:
            far = lax.dot_general(queries, keys[:at, head], NT, preferred_element_type=jnp.float32)
            largest = jnp.maximum(largest, jnp.max(far, axis=-1, keepdims=True))
        near = jnp.exp2((near - largest) * factor)
        total = jnp.sum(near, axis=-1, keepdims=True)
        result = jnp.dot(
            near.astype(jnp.bfloat16), values[at : at + rows, head], preferred_element_type=jnp.float32
        )
        if b > 0:
            far = jnp.exp2((far - largest) * factor)
            total = total + jnp.sum(far, axis=-1, keepdims=True)
            result = result + jnp.dot(
                far.astype(jnp.bfloat16), values[:at, head], preferred_element_type=jnp.float32
            )
        result = (result / total).astype(jnp.bfloat16)
        for h in range(group):
            out_ref[held(b), left + h * HEAD_SIZE : left + (h + 1) * HEAD_SIZE] = result[
                h * rows : (h + 1) * rows, :
            ]


def attend(index, queries, kv, offsets):
    length, q_cols = queries.shape
    kv_half = kv.shape[1] // 2
    return pl.pallas_call(
        functools.partial(attend_kernel, offsets, q_cols // kv_half),
        in_specs=[SMEM, VMEM, VMEM],
        out_specs=VMEM,
        out_shape=bf16(length, q_cols),
        scratch_shapes=[
            pltpu.VMEM((length, kv_half), jnp.bfloat16),
            pltpu.VMEM((length, kv_half), jnp.bfloat16),
        ],
        compiler_params=params(16),
        cost_estimate=work(4 * length * length * q_cols, queries, queries, kv),
        name="attend",
    )(index, queries, kv)


def mix_kernel(n_w, heads_ref, *refs):
    w_refs, out_refs = refs[:n_w], refs[n_w:]
    rows = out_refs[0].shape[0]
    weights = [w_ref[...] for w_ref in w_refs]
    weights = weights[0] if n_w == 1 else jnp.concatenate(weights, axis=0)
    term = lax.dot_general(
        heads_ref[...], weights, NT, preferred_element_type=jnp.float32
    ).astype(jnp.bfloat16)
    for k, out_ref in enumerate(out_refs):
        out_ref[...] = term[k * rows : (k + 1) * rows, :]


def mix(heads, parts, blocks):
    length, features = heads.shape
    columns = sum(part.shape[0] for part in parts)
    return pl.pallas_call(
        functools.partial(mix_kernel, len(parts)),
        in_specs=[VMEM] * (1 + len(parts)),
        out_specs=[VMEM] * blocks,
        out_shape=[bf16(length // blocks, columns)] * blocks,
        compiler_params=params(16),
        cost_estimate=work(2 * length * columns * features, heads, *parts),
        name="mix",
    )(heads, *parts)


def add_kernel(a_ref, b_ref, out_ref):
    total = a_ref[...].astype(jnp.float32) + b_ref[...].astype(jnp.float32)
    out_ref[...] = total.astype(jnp.bfloat16)


def add(a, b):
    return pl.pallas_call(
        add_kernel,
        in_specs=[VMEM, VMEM],
        out_specs=VMEM,
        out_shape=bf16(*a.shape),
        compiler_params=params(8),
        cost_estimate=work(0, a, a, a),
        name="add",
    )(a, b)


def place_kernel(parts, index_ref, *refs):
    n = len(parts)
    a_refs, b_refs, out_ref, total, sem = refs[:n], refs[n : 2 * n], *refs[-3:]
    copies, left = [], 0
    for a_ref, b_ref, pieces in zip(a_refs, b_refs, parts):
        add_kernel(a_ref, b_ref, total.at[:, pl.ds(left, a_ref.shape[1])])
        for j, shard, offset, width in pieces:
            start = pl.multiple_of(jnp.bitwise_xor(index_ref[0], j) * shard + offset, 128)
            copies.append(
                pltpu.make_async_copy(
                    total.at[:, pl.ds(left, width)],
                    out_ref.at[:, pl.ds(start, width)],
                    sem.at[len(copies)],
                )
            )
            copies[-1].start()
            left += width
    for copy in copies:
        copy.wait()


def place(mixed, index, first, second, parts, columns):
    every = [piece for pieces in parts for piece in pieces]
    count = first[0].shape[0]
    if any(offset % 128 or width % 128 or shard % 128 for _, shard, offset, width in every):
        if mixed is None:
            mixed = jnp.zeros((count, columns), jnp.bfloat16)
        for a, b, pieces in zip(first, second, parts):
            total, left = add(a, b), 0
            for j, shard, offset, width in pieces:
                start = jnp.bitwise_xor(index[0], j) * shard + offset
                mixed = lax.dynamic_update_slice(mixed, total[:, left : left + width], (0, start))
                left += width
        return mixed
    held = [] if mixed is None else [mixed]
    return pl.pallas_call(
        functools.partial(place_kernel, parts),
        in_specs=[SMEM] + [VMEM] * (2 * len(parts)) + [ANY] * len(held),
        out_specs=ANY,
        out_shape=bf16(count, columns),
        scratch_shapes=[
            pltpu.VMEM((count, sum(piece[3] for piece in every)), jnp.bfloat16),
            pltpu.SemaphoreType.DMA((len(every),)),
        ],
        input_output_aliases={1 + 2 * len(parts): 0} if held else {},
        compiler_params=params(8),
        cost_estimate=work(0, *first, *second),
        name="place",
    )(index, *first, *second, *held)


def swapped(array, n_f, mask):
    return lax.ppermute(array, "fsdp", [(i, i ^ mask) for i in range(n_f)])


def after(array, *others):
    return lax.optimization_barrier((array, *others))[0] if others else array


def chips_away(level, chips):
    return [r for r in range(chips) if bin(r).count("1") == level]


def send_level(held, n_f, cut, axis, level, *before):
    for r in chips_away(level, n_f // 2):
        if level == 1:
            held[r] = [swapped(after(held[0][0], *before), n_f, 2 * r)]
            continue
        held[r] = []
        for half, bit in ((0, r & -r), (1, 1 << (r.bit_length() - 1))):
            parts = held[r ^ bit]
            part = parts[half] if len(parts) == 2 else part_of(parts[0], cut, half, axis)
            held[r].append(swapped(after(part, *before), n_f, 2 * bit))


def send_siblings(held, sibling, n_f, level, *before):
    for r in chips_away(level, n_f // 2):
        others = held[r] if len(held[r]) > 1 else []
        sibling[r] = [swapped(after(part, *others, *before), n_f, 1) for part in held[r]]


def rope_tables(length):
    frequency = np.float32(ROPE_BASE) ** (
        -(np.arange(HALF, dtype=np.float32) * np.float32(2.0) / np.float32(HEAD_SIZE))
    )
    angle = np.arange(length, dtype=np.float32)[:, None] * frequency[None, :].astype(np.float32)
    angle = angle.astype(np.float64)
    cos, sin = np.cos(angle).astype(np.float32), np.sin(angle).astype(np.float32)
    return np.concatenate([cos, cos], axis=1), np.concatenate([-sin, sin], axis=1)


def body(
    n_f,
    n_s,
    tokens,
    norm_gain,
    q_weight,
    key_matrix,
    value_matrix,
    q_bias,
    k_bias,
    value_offset_bias,
    out_weight,
):
    index = jnp.stack([lax.axis_index("fsdp"), lax.axis_index("sp")])
    count = tokens.shape[0]
    chips = n_f // 2
    levels = chips.bit_length() - 1
    shard, q_cols = q_weight.shape
    kv_cols = key_matrix.shape[1]
    wide = 256 if q_cols % 256 == 0 and kv_cols % 256 == 0 else 128
    cut = (q_cols + 2 * kv_cols) // wide // 2 * wide
    cut += wide if cut + wide <= q_cols else 0
    o_cut = shard * 3 // 5 // 128 * 128 or shard // 2 // 16 * 16
    right = [(i, (i + 1) % n_s) for i in range(n_s)]
    left = [(i, (i - 1) % n_s) for i in range(n_s)]
    cos, sin = rope_tables(n_s * count)

    own = normed_pieces(index, tokens, norm_gain, n_f)
    held = {0: [pack(after(q_weight, own), key_matrix, value_matrix)]}
    sibling, o_held, o_sibling = {}, {0: [after(out_weight, held[0][0])]}, {}
    send_level(held, n_f, cut, 1, 1)
    send_siblings(held, sibling, n_f, 0)

    steps = n_s // 2
    offsets, blocks, gate = [0], [own], []
    ahead = behind = own
    for step in range(1, steps + 1):
        if step > 1 and step <= levels:
            send_level(held, n_f, cut, 1, step, *gate)
            send_siblings(held, sibling, n_f, step - 1, *gate)
        if step < steps:
            ahead = lax.ppermute(ahead, "sp", right)
            behind = lax.ppermute(behind, "sp", left)
            offsets += [step, n_s - step]
        else:
            ahead = lax.ppermute(part_of(ahead, count // 2, 0, 0), "sp", right)
            behind = lax.ppermute(part_of(behind, count // 2, 1, 0), "sp", left)
            offsets += [step]
        blocks += [ahead, behind]
        gate = [ahead, behind]
        if step == 1:
            send_siblings(o_held, o_sibling, n_f, 0, *gate)

    def pieces_of(chosen):
        return [side[r] for r in chosen for side in (held, sibling)]

    most = pieces_of(range(chips - 1))
    early = partial(blocks[:-2], most, wide)
    send_siblings(held, sibling, n_f, levels, *gate, early)
    send_level(o_held, n_f, o_cut, 0, 1, early)
    late = partial(blocks[-2:], most, wide)
    mine, others = pieces_of([chips - 1])
    queries, kv = finish(
        index,
        blocks,
        offsets,
        [mine[0], others[0], mine[1], others[1]],
        early,
        late,
        (q_bias, k_bias, value_offset_bias),
        cos,
        sin,
        q_cols,
        2 * shard * (chips - 1),
        wide,
    )
    heads = attend(index, queries, kv, offsets)

    rounds = []
    for level in range(levels + 1):
        gate = []
        if level == 1:
            gate = arrivals[min(1, n_s - 2)][:1]
        elif level > 1:
            gate = arrivals[0] + (rounds[-2][1][1] if n_s > 2 else [])
        if level:
            before = arrivals[0] if level > 1 else gate
            send_siblings(o_held, o_sibling, n_f, level, *before)
            send_level(o_held, n_f, o_cut, 0, level + 1, *before)
        groups = []
        for r in chips_away(level, chips):
            halves = range(len(o_held[r]))
            if len(halves) == 1:
                groups += [((r, 0, 0),), ((r, 0, 1),)]
            else:
                groups += [((r, half, 0), (r, half, 1)) for half in halves]
        groups.sort(key=lambda group: group[0][2])
        terms = []
        for group in groups:
            weights = [(o_sibling if core else o_held)[r][half] for r, half, core in group]
            mixed = mix(after(heads, *gate), weights, n_s)
            terms.append([mixed[offsets.index(d)] for d in range(n_s)])
        totals, arrivals = [term[1] for term in terms], []
        for d in range(2, n_s + 1):
            arrivals.append([lax.ppermute(total, "sp", right) for total in totals])
            others = []
            if level > 1 and d == n_s - 2:
                others = rounds[-2][1][-1]
            if level > 1 and d == n_s - 1:
                others = rounds[-1][1][-1][:2]
            if d < n_s:
                totals = [add(after(a, *others), term[d]) for a, term in zip(arrivals[-1], terms)]
        where = [
            [(2 * r + core, shard, half * o_cut, o_held[r][half].shape[0]) for r, half, core in group]
            for group in groups
        ]
        rounds.append(([term[0] for term in terms], arrivals, where))

    mixed = None
    for chosen in (rounds[:-1], rounds[-1:]):
        mixed = place(
            mixed,
            index,
            [a for _, arrivals, _ in chosen for a in arrivals[-1]],
            [own for owns, _, _ in chosen for own in owns],
            [parts for _, _, where in chosen for parts in where],
            shard * n_f,
        )
    return mixed


def solution(mesh):
    n_f, n_s = mesh.shape["fsdp"], mesh.shape["sp"]
    placed = (
        P(("fsdp", "sp"), None),
        P(),
        P("fsdp", "sp"),
        P("fsdp", "sp"),
        P("fsdp", "sp"),
        P("sp"),
        P("sp"),
        P("sp"),
        P("fsdp", "sp"),
    )
    return jax.shard_map(
        functools.partial(body, n_f, n_s),
        mesh=mesh,
        in_specs=placed,
        out_specs=P(("fsdp", "sp"), None),
        check_vma=False,
    )
```

time: 231 us -> 240 us (1.039)
  starting transfers between devices: 21.8 us -> 32.8 us
  Pallas kernels: 38.1 us -> 31.2 us
  waiting for transfers between devices: 167 us -> 173 us
    ppermute x27 -> x28, waiting for transfers between devices: 94 us -> 147 us  [the longest x24 72.1 us: body(): arrivals.append([lax.ppermute(total, 'sp', right) for total in totals])]
    ppermute x23 -> x18, waiting for transfers between devices: 73.4 us -> 26.4 us  [swapped(): return lax.ppermute(array, 'fsdp', [(i, i ^ mask) for i in range(n_f)])]
    ppermute x27 -> x28, starting transfers between devices: 8.74 us -> 19.9 us  [the longest x24 12.9 us: body(): arrivals.append([lax.ppermute(total, 'sp', right) for total in totals])]
    pallas_call x15 -> x13, Pallas kernels: 26.8 us -> 19.9 us  [the longest x2 8.85 us: partial(): pl.pallas_call(functools.partial(partial_kernel, len(blocks), counts, wid...]
    ppermute x23 -> x18, starting transfers between devices: 13 us -> 12.9 us  [swapped(): return lax.ppermute(array, 'fsdp', [(i, i ^ mask) for i in range(n_f)])]
  transfers between devices with their start and end apart: 50 -> 46, of which waited for: 30 -> 27; matrix products, arithmetic and copies ran while one was open for 0% -> 0% of each run, Pallas kernels for 15% -> 12%
where the time goes in v6:
time: 240 us
  waiting for transfers between devices  173 us (72%)
  starting transfers between devices  32.8 us (14%)
  Pallas kernels  31.2 us (13%)
    ppermute x24, waiting for transfers between devices, body(): arrivals.append([lax.ppermute(total, 'sp', right) for total in totals])  72.1 us
    ppermute x1, waiting for transfers between devices, body(): behind = lax.ppermute(behind, 'sp', left)  29.2 us
    ppermute x1, waiting for transfers between devices, body(): ahead = lax.ppermute(ahead, 'sp', right)  27.2 us
    ppermute x18, waiting for transfers between devices, swapped(): return lax.ppermute(array, 'fsdp', [(i, i ^ mask) for i in range(n_f)])  26.4 us
    ppermute x1, waiting for transfers between devices, body(): ahead = lax.ppermute(part_of(ahead, count // 2, 0, 0), 'sp', right)  13 us
    ppermute x24, starting transfers between devices, body(): arrivals.append([lax.ppermute(total, 'sp', right) for total in totals])  12.9 us
    ppermute x18, starting transfers between devices, swapped(): return lax.ppermute(array, 'fsdp', [(i, i ^ mask) for i in range(n_f)])  12.9 us
    pallas_call x8, Pallas kernels, mix(): pl.pallas_call(functools.partial(mix_kernel, len(parts)), in_specs=[VMEM]...  9.37 us
  transfers between devices with their start and end apart: 46, of which 27 were waited for; matrix products, arithmetic and copies ran while one was open for 0% of the time, Pallas kernels for 12%

profile of v6, /device:TPU:0, one launch (start us, length us, event | category | flops | bytes accessed | tf_op | source)
XLA Modules:
  0.0 240.0 jit_solution(8688853476091285291)
XLA Ops:
  3.7 3.0 %collective-permute-start.6 = (bf16[640,1792]{1,0:T(8,128)(2,1)S(1)}, bf16[640,1792]{1,0:T(8,128)(2,1)S(1)}, u32[]{:S(2)}, u32[]{:S(2)}) collective-permute-start(bf16[640,1792]{1,0:T(8,128)(2,1)S(1)} %pack.1.refs_3_.refs_2_), channel_id=1, source_target_pairs={{0,8},{4,12},{8,0},{12,4},{16,24},{20,28},{24,16},{28,20},{1,9},{5... | collective-permute-start | bytes 6881288 | tf_op jit(solution)/shard_map/ppermute | solution.py:397
  8.2 3.6 %collective-permute-start.1 = (bf16[128,5120]{1,0:T(8,128)(2,1)S(1)}, bf16[128,5120]{1,0:T(8,128)(2,1)S(1)}, u32[]{:S(2)}, u32[]{:S(2)}) collective-permute-start(bf16[128,5120]{1,0:T(8,128)(2,1)S(1)} %norm.1.refs_0_), channel_id=1, source_target_pairs={{0,3},{1,0},{2,1},{3,2},{4,7},{5,4},{6,5},{7,6},{8,11},{9,8},{10,9... | collective-permute-start | bytes 3932168 | tf_op jit(solution)/shard_map/ppermute | solution.py:478
  11.8 29.2 %collective-permute-done.1.ref.refs_2_ = bf16[128,5120]{1,0:T(8,128)(2,1)S(1)} collective-permute-done((bf16[128,5120]{1,0:T(8,128)(2,1)S(1)}, bf16[128,5120]{1,0:T(8,128)(2,1)S(1)}, u32[]{:S(2)}, u32[]{:S(2)}) %collective-permute-start.1) | collective-permute-done | bytes 1310752 | tf_op jit(solution)/shard_map/ppermute | solution.py:478
  41.0 27.2 %collective-permute-done.ref.refs_1_ = bf16[128,5120]{1,0:T(8,128)(2,1)S(1)} collective-permute-done((bf16[128,5120]{1,0:T(8,128)(2,1)S(1)}, bf16[128,5120]{1,0:T(8,128)(2,1)S(1)}, u32[]{:S(2)}, u32[]{:S(2)}) %collective-permute-start) | collective-permute-done | bytes 1310752 | tf_op jit(solution)/shard_map/ppermute | solution.py:477
  70.2 1.8 collective-permute-start.3
  72.7 1.6 collective-permute-start.2
  74.3 1.7 collective-permute-done.10.refs_8_.refs_7_
  76.0 6.5 %partial.2.refs_9_ = f32[384,1792]{1,0:T(8,128)S(1)} custom-call(bf16[128,5120]{1,0:T(8,128)(2,1)S(1)} %norm.1.refs_0_, bf16[128,5120]{1,0:T(8,128)(2,1)S(1)} %collective-permute-done.ref.refs_1_, bf16[128,5120]{1,0:T(8,128)(2,1)S(1)} %collective-permute-done.1.ref.refs_2_, bf16[640,1792]{1,0:T(8,128)(2,1)S(1)} %pack.1.refs_3_.refs_2_, ...), custom_call_target="tpu_custom_call" | custom-call | flops 5284823040 | bytes 20447232 | tf_op jit(solution)/shard_map/partial/pallas_call | solution.py:140
  82.6 5.2 %collective-permute-done.3.refs_1_.refs_4_ = bf16[64,5120]{1,0:T(8,128)(2,1)S(1)} collective-permute-done((bf16[64,5120]{1,0:T(8,128)(2,1)S(1)}, bf16[64,5120]{1,0:T(8,128)(2,1)S(1)}, u32[]{:S(2)}, u32[]{:S(2)}) %collective-permute-start.3) | collective-permute-done | bytes 655392 | tf_op jit(solution)/shard_map/ppermute | solution.py:482
  87.8 13.0 %collective-permute-done.2.refs_0_.refs_3_ = bf16[64,5120]{1,0:T(8,128)(2,1)S(1)} collective-permute-done((bf16[64,5120]{1,0:T(8,128)(2,1)S(1)}, bf16[64,5120]{1,0:T(8,128)(2,1)S(1)}, u32[]{:S(2)}, u32[]{:S(2)}) %collective-permute-start.2) | collective-permute-done | bytes 655392 | tf_op jit(solution)/shard_map/ppermute | solution.py:481
  104.3 2.3 partial.3.refs_10_
  106.7 3.7 %finish.1 = (bf16[512,1280]{1,0:T(8,128)(2,1)S(1)}, bf16[512,512]{1,0:T(8,128)(2,1)S(1)}) custom-call(s32[2]{0:T(128)S(1)} %pad_add_fusion.index_ref, bf16[128,5120]{1,0:T(8,128)(2,1)S(1)} %norm.1.refs_0_, bf16[128,5120]{1,0:T(8,128)(2,1)S(1)} %collective-permute-done.ref.refs_1_, bf16[128,5120]{1,0:T(8,128)(2,1)S(1)} %collective-permute-done.1.ref.refs_2_, ...), custom_call_target="tpu_custom_call" | custom-call | flops 2348810240 | bytes 8257536 | tf_op jit(solution)/shard_map/finish/pallas_call | solution.py:216
  110.4 4.0 %attend.1.heads_ref = bf16[512,1280]{1,0:T(8,128)(2,1)S(1)} custom-call(s32[2]{0:T(128)S(1)} %pad_add_fusion.index_ref, bf16[512,1280]{1,0:T(8,128)(2,1)S(1)} %get-tuple-element.68.q_ref, bf16[512,512]{1,0:T(8,128)(2,1)S(1)} %get-tuple-element.69.kv_ref), custom_call_target="tpu_custom_call" | custom-call | flops 1342177280 | bytes 3145728 | tf_op jit(solution)/shard_map/attend/pallas_call | solution.py:287
  117.1 5.9 %collective-permute-done.13.a_ref = bf16[128,640]{1,0:T(8,128)(2,1)S(1)} collective-permute-done((bf16[128,640]{1,0:T(8,128)(2,1)S(1)}, bf16[128,640]{1,0:T(8,128)(2,1)S(1)}, u32[]{:S(2)}, u32[]{:S(2)}) %collective-permute-start.13) | collective-permute-done | bytes 163872 | tf_op jit(solution)/shard_map/ppermute | solution.py:540
  123.2 15.9 %collective-permute-done.17.refs_0_.ref = bf16[640,1280]{1,0:T(8,128)(2,1)S(1)} collective-permute-done((bf16[640,1280]{1,0:T(8,128)(2,1)S(1)}, bf16[640,1280]{1,0:T(8,128)(2,1)S(1)}, u32[]{:S(2)}, u32[]{:S(2)}) %collective-permute-start.17) | collective-permute-done | bytes 1638432 | tf_op jit(solution)/shard_map/ppermute | solution.py:397
  150.9 3.5 %collective-permute-done.18.a_ref = bf16[128,640]{1,0:T(8,128)(2,1)S(1)} collective-permute-done((bf16[128,640]{1,0:T(8,128)(2,1)S(1)}, bf16[128,640]{1,0:T(8,128)(2,1)S(1)}, u32[]{:S(2)}, u32[]{:S(2)}) %collective-permute-start.18) | collective-permute-done | bytes 163872 | tf_op jit(solution)/shard_map/ppermute | solution.py:540
  154.5 2.4 %collective-permute-done.16.a_ref = bf16[128,640]{1,0:T(8,128)(2,1)S(1)} collective-permute-done((bf16[128,640]{1,0:T(8,128)(2,1)S(1)}, bf16[128,640]{1,0:T(8,128)(2,1)S(1)}, u32[]{:S(2)}, u32[]{:S(2)}) %collective-permute-start.16) | collective-permute-done | bytes 163872 | tf_op jit(solution)/shard_map/ppermute | solution.py:540
  158.9 5.7 %collective-permute-done.26.refs_0_ = bf16[384,1280]{1,0:T(8,128)(2,1)S(1)} collective-permute-done((bf16[384,1280]{1,0:T(8,128)(2,1)S(1)}, bf16[384,1280]{1,0:T(8,128)(2,1)S(1)}, u32[]{:S(2)}, u32[]{:S(2)}) %collective-permute-start.26) | collective-permute-done | bytes 983072 | tf_op jit(solution)/shard_map/ppermute | solution.py:397
  167.9 6.9 %collective-permute-done.24.a_ref = bf16[128,640]{1,0:T(8,128)(2,1)S(1)} collective-permute-done((bf16[128,640]{1,0:T(8,128)(2,1)S(1)}, bf16[128,640]{1,0:T(8,128)(2,1)S(1)}, u32[]{:S(2)}, u32[]{:S(2)}) %collective-permute-start.24) | collective-permute-done | bytes 163872 | tf_op jit(solution)/shard_map/ppermute | solution.py:540
  175.7 8.0 %collective-permute-done.25.a_ref = bf16[128,640]{1,0:T(8,128)(2,1)S(1)} collective-permute-done((bf16[128,640]{1,0:T(8,128)(2,1)S(1)}, bf16[128,640]{1,0:T(8,128)(2,1)S(1)}, u32[]{:S(2)}, u32[]{:S(2)}) %collective-permute-start.25) | collective-permute-done | bytes 163872 | tf_op jit(solution)/shard_map/ppermute | solution.py:540
  185.9 4.3 %collective-permute-start.33 = (bf16[128,640]{1,0:T(8,128)(2,1)S(1)}, bf16[128,640]{1,0:T(8,128)(2,1)S(1)}, u32[]{:S(2)}, u32[]{:S(2)}) collective-permute-start(bf16[128,640]{1,0:T(8,128)(2,1)S(1)} %add.23), channel_id=1, source_target_pairs={{0,1},{1,2},{2,3},{3,0},{4,5},{5,6},{6,7},{7,4},{8,9},{9,10},{10,1... | collective-permute-start | bytes 491528 | tf_op jit(solution)/shard_map/ppermute | solution.py:540
  191.2 6.9 %collective-permute-done.31.refs_1_ = bf16[128,640]{1,0:T(8,128)(2,1)S(1)} collective-permute-done((bf16[128,640]{1,0:T(8,128)(2,1)S(1)}, bf16[128,640]{1,0:T(8,128)(2,1)S(1)}, u32[]{:S(2)}, u32[]{:S(2)}) %collective-permute-start.31) | collective-permute-done | bytes 163872 | tf_op jit(solution)/shard_map/ppermute | solution.py:540
  198.1 3.5 %collective-permute-done.30.refs_0_ = bf16[128,640]{1,0:T(8,128)(2,1)S(1)} collective-permute-done((bf16[128,640]{1,0:T(8,128)(2,1)S(1)}, bf16[128,640]{1,0:T(8,128)(2,1)S(1)}, u32[]{:S(2)}, u32[]{:S(2)}) %collective-permute-start.30) | collective-permute-done | bytes 163872 | tf_op jit(solution)/shard_map/ppermute | solution.py:540
  201.8 3.4 %collective-permute-done.33.a_ref = bf16[128,640]{1,0:T(8,128)(2,1)S(1)} collective-permute-done((bf16[128,640]{1,0:T(8,128)(2,1)S(1)}, bf16[128,640]{1,0:T(8,128)(2,1)S(1)}, u32[]{:S(2)}, u32[]{:S(2)}) %collective-permute-start.33) | collective-permute-done | bytes 163872 | tf_op jit(solution)/shard_map/ppermute | solution.py:540
  205.4 2.5 %collective-permute-done.39.a_ref = bf16[128,512]{1,0:T(8,128)(2,1)S(1)} collective-permute-done((bf16[128,512]{1,0:T(8,128)(2,1)S(1)}, bf16[128,512]{1,0:T(8,128)(2,1)S(1)}, u32[]{:S(2)}, u32[]{:S(2)}) %collective-permute-start.39) | collective-permute-done | bytes 131104 | tf_op jit(solution)/shard_map/ppermute | solution.py:540
  208.0 3.5 %collective-permute-done.36.refs_3_ = bf16[128,640]{1,0:T(8,128)(2,1)S(1)} collective-permute-done((bf16[128,640]{1,0:T(8,128)(2,1)S(1)}, bf16[128,640]{1,0:T(8,128)(2,1)S(1)}, u32[]{:S(2)}, u32[]{:S(2)}) %collective-permute-start.36) | collective-permute-done | bytes 163872 | tf_op jit(solution)/shard_map/ppermute | solution.py:540
  211.5 7.7 %collective-permute-done.34.refs_2_ = bf16[128,640]{1,0:T(8,128)(2,1)S(1)} collective-permute-done((bf16[128,640]{1,0:T(8,128)(2,1)S(1)}, bf16[128,640]{1,0:T(8,128)(2,1)S(1)}, u32[]{:S(2)}, u32[]{:S(2)}) %collective-permute-start.34) | collective-permute-done | bytes 163872 | tf_op jit(solution)/shard_map/ppermute | solution.py:540
  219.3 3.4 %collective-permute-done.44.a_ref = bf16[128,640]{1,0:T(8,128)(2,1)S(1)} collective-permute-done((bf16[128,640]{1,0:T(8,128)(2,1)S(1)}, bf16[128,640]{1,0:T(8,128)(2,1)S(1)}, u32[]{:S(2)}, u32[]{:S(2)}) %collective-permute-start.44) | collective-permute-done | bytes 163872 | tf_op jit(solution)/shard_map/ppermute | solution.py:540
  222.8 3.4 %collective-permute-done.42.a_ref = bf16[128,640]{1,0:T(8,128)(2,1)S(1)} collective-permute-done((bf16[128,640]{1,0:T(8,128)(2,1)S(1)}, bf16[128,640]{1,0:T(8,128)(2,1)S(1)}, u32[]{:S(2)}, u32[]{:S(2)}) %collective-permute-start.42) | collective-permute-done | bytes 163872 | tf_op jit(solution)/shard_map/ppermute | solution.py:540
  226.3 2.7 %collective-permute-done.40.a_ref = bf16[128,512]{1,0:T(8,128)(2,1)S(1)} collective-permute-done((bf16[128,512]{1,0:T(8,128)(2,1)S(1)}, bf16[128,512]{1,0:T(8,128)(2,1)S(1)}, u32[]{:S(2)}, u32[]{:S(2)}) %collective-permute-start.40) | collective-permute-done | bytes 131104 | tf_op jit(solution)/shard_map/ppermute | solution.py:540
  229.1 6.1 %collective-permute-done.45.refs_5_ = bf16[128,640]{1,0:T(8,128)(2,1)S(1)} collective-permute-done((bf16[128,640]{1,0:T(8,128)(2,1)S(1)}, bf16[128,640]{1,0:T(8,128)(2,1)S(1)}, u32[]{:S(2)}, u32[]{:S(2)}) %collective-permute-start.45) | collective-permute-done | bytes 163872 | tf_op jit(solution)/shard_map/ppermute | solution.py:540
  235.2 1.8 collective-permute-done.43.refs_4_
  (121 shorter events, 39.0 us)
Async XLA Ops:
  3.7 64.6 %collective-permute-start.6 = (bf16[640,1792]{1,0:T(8,128)(2,1)S(1)}, bf16[640,1792]{1,0:T(8,128)(2,1)S(1)}, u32[]{:S(2)}, u32[]{:S(2)}) collective-permute-start(bf16[640,1792]{1,0:T(8,128)(2,1)S(1)} %pack.1.refs_3_.refs_2_), channel_id=1, source_target_pairs={{0,8},{4,12},{8,0},{12,4},{16,24},{20,28},{24,16},{28,20},{1,9},{5... | collective-permute-start | bytes 6881288 | tf_op jit(solution)/shard_map/ppermute | solution.py:397
  6.7 61.6 %collective-permute-start.4 = (bf16[640,1792]{1,0:T(8,128)(2,1)S(1)}, bf16[640,1792]{1,0:T(8,128)(2,1)S(1)}, u32[]{:S(2)}, u32[]{:S(2)}) collective-permute-start(bf16[640,1792]{1,0:T(8,128)(2,1)S(1)} %pack.1.refs_3_.refs_2_), channel_id=1, source_target_pairs={{0,16},{4,20},{8,24},{12,28},{16,0},{20,4},{24,8},{28,12},{1,17},{... | collective-permute-start | bytes 6881288 | tf_op jit(solution)/shard_map/ppermute | solution.py:397
  8.2 32.8 %collective-permute-start.1 = (bf16[128,5120]{1,0:T(8,128)(2,1)S(1)}, bf16[128,5120]{1,0:T(8,128)(2,1)S(1)}, u32[]{:S(2)}, u32[]{:S(2)}) collective-permute-start(bf16[128,5120]{1,0:T(8,128)(2,1)S(1)} %norm.1.refs_0_), channel_id=1, source_target_pairs={{0,3},{1,0},{2,1},{3,2},{4,7},{5,4},{6,5},{7,6},{8,11},{9,8},{10,9... | collective-permute-start | bytes 3932168 | tf_op jit(solution)/shard_map/ppermute | solution.py:478
  11.8 56.5 %collective-permute-start = (bf16[128,5120]{1,0:T(8,128)(2,1)S(1)}, bf16[128,5120]{1,0:T(8,128)(2,1)S(1)}, u32[]{:S(2)}, u32[]{:S(2)}) collective-permute-start(bf16[128,5120]{1,0:T(8,128)(2,1)S(1)} %norm.1.refs_0_), channel_id=1, source_target_pairs={{0,1},{1,2},{2,3},{3,0},{4,5},{5,6},{6,7},{7,4},{8,9},{9,10},{10,1... | collective-permute-start | bytes 3932168 | tf_op jit(solution)/shard_map/ppermute | solution.py:477
  11.8 58.4 %collective-permute-start.8 = (bf16[640,1792]{1,0:T(8,128)(2,1)S(1)}, bf16[640,1792]{1,0:T(8,128)(2,1)S(1)}, u32[]{:S(2)}, u32[]{:S(2)}) collective-permute-start(bf16[640,1792]{1,0:T(8,128)(2,1)S(1)} %pack.1.refs_3_.refs_2_), channel_id=1, source_target_pairs={{0,4},{4,0},{8,12},{12,8},{16,20},{20,16},{24,28},{28,24},{1,5},{5... | collective-permute-start | bytes 6881288 | tf_op jit(solution)/shard_map/ppermute | solution.py:397
  68.9 31.9 %collective-permute-start.5 = (bf16[640,1024]{1,0:T(8,128)(2,1)S(1)}, bf16[640,1024]{1,0:T(8,128)(2,1)S(1)}, u32[]{:S(2)}, u32[]{:S(2)}) collective-permute-start(bf16[640,1024]{1,0:T(8,128)(2,1)S(1)} %cut.8), channel_id=1, source_target_pairs={{0,8},{4,12},{8,0},{12,4},{16,24},{20,28},{24,16},{28,20},{1,9},{5... | collective-permute-start | bytes 3932168 | tf_op jit(solution)/shard_map/ppermute | solution.py:397
  69.5 31.2 %collective-permute-start.7 = (bf16[640,768]{1,0:T(8,128)(2,1)S(1)}, bf16[640,768]{1,0:T(8,128)(2,1)S(1)}, u32[]{:S(2)}, u32[]{:S(2)}) collective-permute-start(bf16[640,768]{1,0:T(8,128)(2,1)S(1)} %cut.9), channel_id=1, source_target_pairs={{0,16},{4,20},{8,24},{12,28},{16,0},{20,4},{24,8},{28,12},{1,17},{... | collective-permute-start | bytes 2949128 | tf_op jit(solution)/shard_map/ppermute | solution.py:397
  70.2 17.5 %collective-permute-start.3 = (bf16[64,5120]{1,0:T(8,128)(2,1)S(1)}, bf16[64,5120]{1,0:T(8,128)(2,1)S(1)}, u32[]{:S(2)}, u32[]{:S(2)}) collective-permute-start(bf16[64,5120]{1,0:T(8,128)(2,1)S(1)} %cut.7), channel_id=1, source_target_pairs={{0,3},{1,0},{2,1},{3,2},{4,7},{5,4},{6,5},{7,6},{8,11},{9,8},{10,9... | collective-permute-start | bytes 1966088 | tf_op jit(solution)/shard_map/ppermute | solution.py:482
  72.7 28.0 %collective-permute-start.2 = (bf16[64,5120]{1,0:T(8,128)(2,1)S(1)}, bf16[64,5120]{1,0:T(8,128)(2,1)S(1)}, u32[]{:S(2)}, u32[]{:S(2)}) collective-permute-start(bf16[64,5120]{1,0:T(8,128)(2,1)S(1)} %cut.6), channel_id=1, source_target_pairs={{0,1},{1,2},{2,3},{3,0},{4,5},{5,6},{6,7},{7,4},{8,9},{9,10},{10,1... | collective-permute-start | bytes 1966088 | tf_op jit(solution)/shard_map/ppermute | solution.py:481
  101.3 37.8 %collective-permute-start.17 = (bf16[640,1280]{1,0:T(8,128)(2,1)S(1)}, bf16[640,1280]{1,0:T(8,128)(2,1)S(1)}, u32[]{:S(2)}, u32[]{:S(2)}) collective-permute-start(bf16[640,1280]{1,0:T(8,128)(2,1)S(1)} %copy-done.10), channel_id=1, source_target_pairs={{0,16},{4,20},{8,24},{12,28},{16,0},{20,4},{24,8},{28,12},{1,17},{... | collective-permute-start | bytes 4915208 | tf_op jit(solution)/shard_map/ppermute | solution.py:397
  102.8 37.5 %collective-permute-start.15 = (bf16[640,1280]{1,0:T(8,128)(2,1)S(1)}, bf16[640,1280]{1,0:T(8,128)(2,1)S(1)}, u32[]{:S(2)}, u32[]{:S(2)}) collective-permute-start(bf16[640,1280]{1,0:T(8,128)(2,1)S(1)} %copy-done.10), channel_id=1, source_target_pairs={{0,8},{4,12},{8,0},{12,4},{16,24},{20,28},{24,16},{28,20},{1,9},{5... | collective-permute-start | bytes 4915208 | tf_op jit(solution)/shard_map/ppermute | solution.py:397
  123.1 16.0 %collective-permute-start.14 = (bf16[128,640]{1,0:T(8,128)(2,1)S(1)}, bf16[128,640]{1,0:T(8,128)(2,1)S(1)}, u32[]{:S(2)}, u32[]{:S(2)}) collective-permute-start(bf16[128,640]{1,0:T(8,128)(2,1)S(1)} %add.18), channel_id=1, source_target_pairs={{0,1},{1,2},{2,3},{3,0},{4,5},{5,6},{6,7},{7,4},{8,9},{9,10},{10,1... | collective-permute-start | bytes 491528 | tf_op jit(solution)/shard_map/ppermute | solution.py:540
  140.3 25.3 %collective-permute-start.23 = (bf16[640,1280]{1,0:T(8,128)(2,1)S(1)}, bf16[640,1280]{1,0:T(8,128)(2,1)S(1)}, u32[]{:S(2)}, u32[]{:S(2)}) collective-permute-start(bf16[640,1280]{1,0:T(8,128)(2,1)S(1)} %copy-done.10), channel_id=1, source_target_pairs={{0,4},{4,0},{8,12},{12,8},{16,20},{20,16},{24,28},{28,24},{1,5},{5... | collective-permute-start | bytes 4915208 | tf_op jit(solution)/shard_map/ppermute | solution.py:397
  140.9 23.7 %collective-permute-start.26 = (bf16[384,1280]{1,0:T(8,128)(2,1)S(1)}, bf16[384,1280]{1,0:T(8,128)(2,1)S(1)}, u32[]{:S(2)}, u32[]{:S(2)}) collective-permute-start(bf16[384,1280]{1,0:T(8,128)(2,1)S(1)} %cut.10), channel_id=1, source_target_pairs={{0,8},{4,12},{8,0},{12,4},{16,24},{20,28},{24,16},{28,20},{1,9},{5... | collective-permute-start | bytes 2949128 | tf_op jit(solution)/shard_map/ppermute | solution.py:397
  142.5 16.4 %collective-permute-start.27 = (bf16[256,1280]{1,0:T(8,128)(2,1)S(1)}, bf16[256,1280]{1,0:T(8,128)(2,1)S(1)}, u32[]{:S(2)}, u32[]{:S(2)}) collective-permute-start(bf16[256,1280]{1,0:T(8,128)(2,1)S(1)} %cut.11), channel_id=1, source_target_pairs={{0,16},{4,20},{8,24},{12,28},{16,0},{20,4},{24,8},{28,12},{1,17},{... | collective-permute-start | bytes 1966088 | tf_op jit(solution)/shard_map/ppermute | solution.py:397
  165.1 18.6 %collective-permute-start.28 = (bf16[384,1280]{1,0:T(8,128)(2,1)S(1)}, bf16[384,1280]{1,0:T(8,128)(2,1)S(1)}, u32[]{:S(2)}, u32[]{:S(2)}) collective-permute-start(bf16[384,1280]{1,0:T(8,128)(2,1)S(1)} %collective-permute-done.26.refs_0_), channel_id=1, source_target_pairs={{0,4},{4,0},{8,12},{12,8},{16,20},{20,16},{24,28},{28,24},{1,5},{5... | collective-permute-start | bytes 2949128 | tf_op jit(solution)/shard_map/ppermute | solution.py:397
  165.1 20.8 %collective-permute-start.38 = (bf16[256,1280]{1,0:T(8,128)(2,1)S(1)}, bf16[256,1280]{1,0:T(8,128)(2,1)S(1)}, u32[]{:S(2)}, u32[]{:S(2)}) collective-permute-start(bf16[256,1280]{1,0:T(8,128)(2,1)S(1)} %collective-permute-done.27.refs_0_), channel_id=1, source_target_pairs={{0,4},{4,0},{8,12},{12,8},{16,20},{20,16},{24,28},{28,24},{1,5},{5... | collective-permute-start | bytes 1966088 | tf_op jit(solution)/shard_map/ppermute | solution.py:397
  175.0 16.2 %collective-permute-start.35 = (bf16[128,640]{1,0:T(8,128)(2,1)S(1)}, bf16[128,640]{1,0:T(8,128)(2,1)S(1)}, u32[]{:S(2)}, u32[]{:S(2)}) collective-permute-start(bf16[128,640]{1,0:T(8,128)(2,1)S(1)} %add.25), channel_id=1, source_target_pairs={{0,1},{1,2},{2,3},{3,0},{4,5},{5,6},{6,7},{7,4},{8,9},{9,10},{10,1... | collective-permute-start | bytes 491528 | tf_op jit(solution)/shard_map/ppermute | solution.py:540
  184.9 16.7 %collective-permute-start.29 = (bf16[128,768]{1,0:T(8,128)(2,1)S(1)}, bf16[128,768]{1,0:T(8,128)(2,1)S(1)}, u32[]{:S(2)}, u32[]{:S(2)}) collective-permute-start(bf16[128,768]{1,0:T(8,128)(2,1)S(1)} %get-tuple-element.88), channel_id=1, source_target_pairs={{0,1},{1,2},{2,3},{3,0},{4,5},{5,6},{6,7},{7,4},{8,9},{9,10},{10,1... | collective-permute-start | bytes 589832 | tf_op jit(solution)/shard_map/ppermute | solution.py:540
  185.0 13.1 %collective-permute-start.31 = (bf16[128,640]{1,0:T(8,128)(2,1)S(1)}, bf16[128,640]{1,0:T(8,128)(2,1)S(1)}, u32[]{:S(2)}, u32[]{:S(2)}) collective-permute-start(bf16[128,640]{1,0:T(8,128)(2,1)S(1)} %add.21), channel_id=1, source_target_pairs={{0,1},{1,2},{2,3},{3,0},{4,5},{5,6},{6,7},{7,4},{8,9},{9,10},{10,1... | collective-permute-start | bytes 491528 | tf_op jit(solution)/shard_map/ppermute | solution.py:540
  185.2 16.5 %collective-permute-start.30 = (bf16[128,640]{1,0:T(8,128)(2,1)S(1)}, bf16[128,640]{1,0:T(8,128)(2,1)S(1)}, u32[]{:S(2)}, u32[]{:S(2)}) collective-permute-start(bf16[128,640]{1,0:T(8,128)(2,1)S(1)} %add.20), channel_id=1, source_target_pairs={{0,1},{1,2},{2,3},{3,0},{4,5},{5,6},{6,7},{7,4},{8,9},{9,10},{10,1... | collective-permute-start | bytes 491528 | tf_op jit(solution)/shard_map/ppermute | solution.py:540
  185.9 19.3 %collective-permute-start.33 = (bf16[128,640]{1,0:T(8,128)(2,1)S(1)}, bf16[128,640]{1,0:T(8,128)(2,1)S(1)}, u32[]{:S(2)}, u32[]{:S(2)}) collective-permute-start(bf16[128,640]{1,0:T(8,128)(2,1)S(1)} %add.23), channel_id=1, source_target_pairs={{0,1},{1,2},{2,3},{3,0},{4,5},{5,6},{6,7},{7,4},{8,9},{9,10},{10,1... | collective-permute-start | bytes 491528 | tf_op jit(solution)/shard_map/ppermute | solution.py:540
  191.1 16.8 %collective-permute-start.39 = (bf16[128,512]{1,0:T(8,128)(2,1)S(1)}, bf16[128,512]{1,0:T(8,128)(2,1)S(1)}, u32[]{:S(2)}, u32[]{:S(2)}) collective-permute-start(bf16[128,512]{1,0:T(8,128)(2,1)S(1)} %get-tuple-element.100), channel_id=1, source_target_pairs={{0,1},{1,2},{2,3},{3,0},{4,5},{5,6},{6,7},{7,4},{8,9},{9,10},{10,1... | collective-permute-start | bytes 393224 | tf_op jit(solution)/shard_map/ppermute | solution.py:540
  198.1 13.3 %collective-permute-start.36 = (bf16[128,640]{1,0:T(8,128)(2,1)S(1)}, bf16[128,640]{1,0:T(8,128)(2,1)S(1)}, u32[]{:S(2)}, u32[]{:S(2)}) collective-permute-start(bf16[128,640]{1,0:T(8,128)(2,1)S(1)} %add.26), channel_id=1, source_target_pairs={{0,1},{1,2},{2,3},{3,0},{4,5},{5,6},{6,7},{7,4},{8,9},{9,10},{10,1... | collective-permute-start | bytes 491528 | tf_op jit(solution)/shard_map/ppermute | solution.py:540
  201.7 17.5 %collective-permute-start.32 = (bf16[128,768]{1,0:T(8,128)(2,1)S(1)}, bf16[128,768]{1,0:T(8,128)(2,1)S(1)}, u32[]{:S(2)}, u32[]{:S(2)}) collective-permute-start(bf16[128,768]{1,0:T(8,128)(2,1)S(1)} %add.22), channel_id=1, source_target_pairs={{0,1},{1,2},{2,3},{3,0},{4,5},{5,6},{6,7},{7,4},{8,9},{9,10},{10,1... | collective-permute-start | bytes 589832 | tf_op jit(solution)/shard_map/ppermute | solution.py:540
  205.2 14.0 %collective-permute-start.34 = (bf16[128,640]{1,0:T(8,128)(2,1)S(1)}, bf16[128,640]{1,0:T(8,128)(2,1)S(1)}, u32[]{:S(2)}, u32[]{:S(2)}) collective-permute-start(bf16[128,640]{1,0:T(8,128)(2,1)S(1)} %add.24), channel_id=1, source_target_pairs={{0,1},{1,2},{2,3},{3,0},{4,5},{5,6},{6,7},{7,4},{8,9},{9,10},{10,1... | collective-permute-start | bytes 491528 | tf_op jit(solution)/shard_map/ppermute | solution.py:540
  205.3 17.4 %collective-permute-start.44 = (bf16[128,640]{1,0:T(8,128)(2,1)S(1)}, bf16[128,640]{1,0:T(8,128)(2,1)S(1)}, u32[]{:S(2)}, u32[]{:S(2)}) collective-permute-start(bf16[128,640]{1,0:T(8,128)(2,1)S(1)} %add.32), channel_id=1, source_target_pairs={{0,1},{1,2},{2,3},{3,0},{4,5},{5,6},{6,7},{7,4},{8,9},{9,10},{10,1... | collective-permute-start | bytes 491528 | tf_op jit(solution)/shard_map/ppermute | solution.py:540
  208.0 18.3 %collective-permute-start.42 = (bf16[128,640]{1,0:T(8,128)(2,1)S(1)}, bf16[128,640]{1,0:T(8,128)(2,1)S(1)}, u32[]{:S(2)}, u32[]{:S(2)}) collective-permute-start(bf16[128,640]{1,0:T(8,128)(2,1)S(1)} %add.30), channel_id=1, source_target_pairs={{0,1},{1,2},{2,3},{3,0},{4,5},{5,6},{6,7},{7,4},{8,9},{9,10},{10,1... | collective-permute-start | bytes 491528 | tf_op jit(solution)/shard_map/ppermute | solution.py:540
  211.5 17.6 %collective-permute-start.40 = (bf16[128,512]{1,0:T(8,128)(2,1)S(1)}, bf16[128,512]{1,0:T(8,128)(2,1)S(1)}, u32[]{:S(2)}, u32[]{:S(2)}) collective-permute-start(bf16[128,512]{1,0:T(8,128)(2,1)S(1)} %add.28), channel_id=1, source_target_pairs={{0,1},{1,2},{2,3},{3,0},{4,5},{5,6},{6,7},{7,4},{8,9},{9,10},{10,1... | collective-permute-start | bytes 393224 | tf_op jit(solution)/shard_map/ppermute | solution.py:540
  219.2 19.3 %collective-permute-start.37 = (bf16[128,768]{1,0:T(8,128)(2,1)S(1)}, bf16[128,768]{1,0:T(8,128)(2,1)S(1)}, u32[]{:S(2)}, u32[]{:S(2)}) collective-permute-start(bf16[128,768]{1,0:T(8,128)(2,1)S(1)} %add.27), channel_id=1, source_target_pairs={{0,1},{1,2},{2,3},{3,0},{4,5},{5,6},{6,7},{7,4},{8,9},{9,10},{10,1... | collective-permute-start | bytes 589832 | tf_op jit(solution)/shard_map/ppermute | solution.py:540
  222.7 12.4 %collective-permute-start.45 = (bf16[128,640]{1,0:T(8,128)(2,1)S(1)}, bf16[128,640]{1,0:T(8,128)(2,1)S(1)}, u32[]{:S(2)}, u32[]{:S(2)}) collective-permute-start(bf16[128,640]{1,0:T(8,128)(2,1)S(1)} %add.33), channel_id=1, source_target_pairs={{0,1},{1,2},{2,3},{3,0},{4,5},{5,6},{6,7},{7,4},{8,9},{9,10},{10,1... | collective-permute-start | bytes 491528 | tf_op jit(solution)/shard_map/ppermute | solution.py:540
  226.3 10.7 %collective-permute-start.43 = (bf16[128,640]{1,0:T(8,128)(2,1)S(1)}, bf16[128,640]{1,0:T(8,128)(2,1)S(1)}, u32[]{:S(2)}, u32[]{:S(2)}) collective-permute-start(bf16[128,640]{1,0:T(8,128)(2,1)S(1)} %add.31), channel_id=1, source_target_pairs={{0,1},{1,2},{2,3},{3,0},{4,5},{5,6},{6,7},{7,4},{8,9},{9,10},{10,1... | collective-permute-start | bytes 491528 | tf_op jit(solution)/shard_map/ppermute | solution.py:540
  (25 other events, 267.6 us)

commit v7 on v6

--- a/solution.py
+++ b/solution.py
@@ -29,6 +29,11 @@
 def work(flops, *arrays):
     size = sum(int(np.prod(x.shape)) * x.dtype.itemsize for x in arrays)
     return pl.CostEstimate(flops=flops, bytes_accessed=size, transcendentals=0)
+
+
+def link_time(array, share=2):
+    size = share * int(np.prod(array.shape)) * array.dtype.itemsize
+    return pl.CostEstimate(flops=size * 11000, bytes_accessed=size, transcendentals=0)
 
 
 def normed_kernel(n_f, index_ref, tokens_ref, gain_ref, out_ref):
@@ -337,7 +342,7 @@
         out_specs=VMEM,
         out_shape=bf16(*a.shape),
         compiler_params=params(8),
-        cost_estimate=work(0, a, a, a),
+        cost_estimate=link_time(a),
         name="add",
     )(a, b)
 
@@ -513,15 +518,9 @@
 
     rounds = []
     for level in range(levels + 1):
-        gate = []
-        if level == 1:
-            gate = arrivals[min(1, n_s - 2)][:1]
-        elif level > 1:
-            gate = arrivals[0] + (rounds[-2][1][1] if n_s > 2 else [])
         if level:
-            before = arrivals[0] if level > 1 else gate
-            send_siblings(o_held, o_sibling, n_f, level, *before)
-            send_level(o_held, n_f, o_cut, 0, level + 1, *before)
+            send_siblings(o_held, o_sibling, n_f, level, *sent)
+            send_level(o_held, n_f, o_cut, 0, level + 1, *sent)
         groups = []
         for r in chips_away(level, chips):
             halves = range(len(o_held[r]))
@@ -533,23 +532,19 @@
         terms = []
         for group in groups:
             weights = [(o_sibling if core else o_held)[r][half] for r, half, core in group]
-            mixed = mix(after(heads, *gate), weights, n_s)
+            mixed = mix(heads, weights, n_s)
             terms.append([mixed[offsets.index(d)] for d in range(n_s)])
         totals, arrivals = [term[1] for term in terms], []
         for d in range(2, n_s + 1):
             arrivals.append([lax.ppermute(total, "sp", right) for total in totals])
-            others = []
-            if level > 1 and d == n_s - 2:
-                others = rounds[-2][1][-1]
-            if level > 1 and d == n_s - 1:
-                others = rounds[-1][1][-1][:2]
             if d < n_s:
-                totals = [add(after(a, *others), term[d]) for a, term in zip(arrivals[-1], terms)]
+                totals = [add(a, term[d]) for a, term in zip(arrivals[-1], terms)]
         where = [
             [(2 * r + core, shard, half * o_cut, o_held[r][half].shape[0]) for r, half, core in group]
             for group in groups
         ]
         rounds.append(([term[0] for term in terms], arrivals, where))
+        sent = arrivals[0][:1]
 
     mixed = None
     for chosen in (rounds[:-1], rounds[-1:]):

time: 240 us -> 257 us (1.071)
  waiting for transfers between devices: 173 us -> 191 us
    ppermute x24, waiting for transfers between devices: 72.1 us -> 90.3 us  [body(): arrivals.append([lax.ppermute(total, 'sp', right) for total in totals])]
  transfers between devices with their start and end apart: 46 -> 46, of which waited for: 27 -> 26; matrix products, arithmetic and copies ran while one was open for 0% -> 0% of each run, Pallas kernels for 12% -> 11%
where the time goes in v7:
time: 257 us
  waiting for transfers between devices  191 us (74%)
  Pallas kernels  31.2 us (12%)
  starting transfers between devices  31.2 us (12%)
    ppermute x24, waiting for transfers between devices, body(): arrivals.append([lax.ppermute(total, 'sp', right) for total in totals])  90.3 us
    ppermute x1, waiting for transfers between devices, body(): behind = lax.ppermute(behind, 'sp', left)  29.2 us
    ppermute x1, waiting for transfers between devices, body(): ahead = lax.ppermute(ahead, 'sp', right)  27.2 us
    ppermute x18, waiting for transfers between devices, swapped(): return lax.ppermute(array, 'fsdp', [(i, i ^ mask) for i in range(n_f)])  26.4 us
    ppermute x18, starting transfers between devices, swapped(): return lax.ppermute(array, 'fsdp', [(i, i ^ mask) for i in range(n_f)])  13.2 us
    ppermute x1, waiting for transfers between devices, body(): ahead = lax.ppermute(part_of(ahead, count // 2, 0, 0), 'sp', right)  13 us
    ppermute x24, starting transfers between devices, body(): arrivals.append([lax.ppermute(total, 'sp', right) for total in totals])  10.9 us
    pallas_call x8, Pallas kernels, mix(): pl.pallas_call(functools.partial(mix_kernel, len(parts)), in_specs=[VMEM]...  9.36 us
  transfers between devices with their start and end apart: 46, of which 26 were waited for; matrix products, arithmetic and copies ran while one was open for 0% of the time, Pallas kernels for 11%

profile of v7, /device:TPU:0, one launch (start us, length us, event | category | flops | bytes accessed | tf_op | source)
XLA Modules:
  0.0 256.6 jit_solution(4573036779166603304)
XLA Ops:
  3.7 3.0 %collective-permute-start.6 = (bf16[640,1792]{1,0:T(8,128)(2,1)S(1)}, bf16[640,1792]{1,0:T(8,128)(2,1)S(1)}, u32[]{:S(2)}, u32[]{:S(2)}) collective-permute-start(bf16[640,1792]{1,0:T(8,128)(2,1)S(1)} %pack.1.refs_3_.refs_2_), channel_id=1, source_target_pairs={{0,8},{4,12},{8,0},{12,4},{16,24},{20,28},{24,16},{28,20},{1,9},{5... | collective-permute-start | bytes 6881288 | tf_op jit(solution)/shard_map/ppermute | solution.py:402
  8.2 3.6 %collective-permute-start.1 = (bf16[128,5120]{1,0:T(8,128)(2,1)S(1)}, bf16[128,5120]{1,0:T(8,128)(2,1)S(1)}, u32[]{:S(2)}, u32[]{:S(2)}) collective-permute-start(bf16[128,5120]{1,0:T(8,128)(2,1)S(1)} %norm.1.refs_0_), channel_id=1, source_target_pairs={{0,3},{1,0},{2,1},{3,2},{4,7},{5,4},{6,5},{7,6},{8,11},{9,8},{10,9... | collective-permute-start | bytes 3932168 | tf_op jit(solution)/shard_map/ppermute | solution.py:483
  11.8 29.2 %collective-permute-done.1.ref.refs_2_ = bf16[128,5120]{1,0:T(8,128)(2,1)S(1)} collective-permute-done((bf16[128,5120]{1,0:T(8,128)(2,1)S(1)}, bf16[128,5120]{1,0:T(8,128)(2,1)S(1)}, u32[]{:S(2)}, u32[]{:S(2)}) %collective-permute-start.1) | collective-permute-done | bytes 1310752 | tf_op jit(solution)/shard_map/ppermute | solution.py:483
  41.0 27.2 %collective-permute-done.ref.refs_1_ = bf16[128,5120]{1,0:T(8,128)(2,1)S(1)} collective-permute-done((bf16[128,5120]{1,0:T(8,128)(2,1)S(1)}, bf16[128,5120]{1,0:T(8,128)(2,1)S(1)}, u32[]{:S(2)}, u32[]{:S(2)}) %collective-permute-start) | collective-permute-done | bytes 1310752 | tf_op jit(solution)/shard_map/ppermute | solution.py:482
  70.2 1.8 collective-permute-start.3
  72.7 1.6 collective-permute-start.2
  74.3 1.7 collective-permute-done.10.refs_8_.refs_7_
  76.0 6.5 %partial.2.refs_9_ = f32[384,1792]{1,0:T(8,128)S(1)} custom-call(bf16[128,5120]{1,0:T(8,128)(2,1)S(1)} %norm.1.refs_0_, bf16[128,5120]{1,0:T(8,128)(2,1)S(1)} %collective-permute-done.ref.refs_1_, bf16[128,5120]{1,0:T(8,128)(2,1)S(1)} %collective-permute-done.1.ref.refs_2_, bf16[640,1792]{1,0:T(8,128)(2,1)S(1)} %pack.1.refs_3_.refs_2_, ...), custom_call_target="tpu_custom_call" | custom-call | flops 5284823040 | bytes 20447232 | tf_op jit(solution)/shard_map/partial/pallas_call | solution.py:145
  82.6 5.2 %collective-permute-done.3.refs_1_.refs_4_ = bf16[64,5120]{1,0:T(8,128)(2,1)S(1)} collective-permute-done((bf16[64,5120]{1,0:T(8,128)(2,1)S(1)}, bf16[64,5120]{1,0:T(8,128)(2,1)S(1)}, u32[]{:S(2)}, u32[]{:S(2)}) %collective-permute-start.3) | collective-permute-done | bytes 655392 | tf_op jit(solution)/shard_map/ppermute | solution.py:487
  87.8 13.0 %collective-permute-done.2.refs_0_.refs_3_ = bf16[64,5120]{1,0:T(8,128)(2,1)S(1)} collective-permute-done((bf16[64,5120]{1,0:T(8,128)(2,1)S(1)}, bf16[64,5120]{1,0:T(8,128)(2,1)S(1)}, u32[]{:S(2)}, u32[]{:S(2)}) %collective-permute-start.2) | collective-permute-done | bytes 655392 | tf_op jit(solution)/shard_map/ppermute | solution.py:486
  104.4 2.3 partial.3.refs_10_
  107.6 3.7 %finish.1 = (bf16[512,1280]{1,0:T(8,128)(2,1)S(1)}, bf16[512,512]{1,0:T(8,128)(2,1)S(1)}) custom-call(s32[2]{0:T(128)S(1)} %pad_add_fusion.index_ref, bf16[128,5120]{1,0:T(8,128)(2,1)S(1)} %norm.1.refs_0_, bf16[128,5120]{1,0:T(8,128)(2,1)S(1)} %collective-permute-done.ref.refs_1_, bf16[128,5120]{1,0:T(8,128)(2,1)S(1)} %collective-permute-done.1.ref.refs_2_, ...), custom_call_target="tpu_custom_call" | custom-call | flops 2348810240 | bytes 8257536 | tf_op jit(solution)/shard_map/finish/pallas_call | solution.py:221
  111.3 4.0 %attend.1.heads_ref = bf16[512,1280]{1,0:T(8,128)(2,1)S(1)} custom-call(s32[2]{0:T(128)S(1)} %pad_add_fusion.index_ref, bf16[512,1280]{1,0:T(8,128)(2,1)S(1)} %get-tuple-element.62.q_ref, bf16[512,512]{1,0:T(8,128)(2,1)S(1)} %get-tuple-element.63.kv_ref), custom_call_target="tpu_custom_call" | custom-call | flops 1342177280 | bytes 3145728 | tf_op jit(solution)/shard_map/attend/pallas_call | solution.py:292
  120.8 4.6 %collective-permute-done.30.a_ref = bf16[128,640]{1,0:T(8,128)(2,1)S(1)} collective-permute-done((bf16[128,640]{1,0:T(8,128)(2,1)S(1)}, bf16[128,640]{1,0:T(8,128)(2,1)S(1)}, u32[]{:S(2)}, u32[]{:S(2)}) %collective-permute-start.30) | collective-permute-done | bytes 163872 | tf_op jit(solution)/shard_map/ppermute | solution.py:539
  125.5 2.6 %collective-permute-done.14.a_ref = bf16[128,640]{1,0:T(8,128)(2,1)S(1)} collective-permute-done((bf16[128,640]{1,0:T(8,128)(2,1)S(1)}, bf16[128,640]{1,0:T(8,128)(2,1)S(1)}, u32[]{:S(2)}, u32[]{:S(2)}) %collective-permute-start.14) | collective-permute-done | bytes 163872 | tf_op jit(solution)/shard_map/ppermute | solution.py:539
  128.7 10.8 %collective-permute-done.16.ref.refs_0_ = bf16[640,1280]{1,0:T(8,128)(2,1)S(1)} collective-permute-done((bf16[640,1280]{1,0:T(8,128)(2,1)S(1)}, bf16[640,1280]{1,0:T(8,128)(2,1)S(1)}, u32[]{:S(2)}, u32[]{:S(2)}) %collective-permute-start.16) | collective-permute-done | bytes 1638432 | tf_op jit(solution)/shard_map/ppermute | solution.py:402
  148.6 6.9 %collective-permute-done.35.a_ref = bf16[128,640]{1,0:T(8,128)(2,1)S(1)} collective-permute-done((bf16[128,640]{1,0:T(8,128)(2,1)S(1)}, bf16[128,640]{1,0:T(8,128)(2,1)S(1)}, u32[]{:S(2)}, u32[]{:S(2)}) %collective-permute-start.35) | collective-permute-done | bytes 163872 | tf_op jit(solution)/shard_map/ppermute | solution.py:539
  155.6 2.8 %collective-permute-done.17.refs_0_ = bf16[256,1280]{1,0:T(8,128)(2,1)S(1)} collective-permute-done((bf16[256,1280]{1,0:T(8,128)(2,1)S(1)}, bf16[256,1280]{1,0:T(8,128)(2,1)S(1)}, u32[]{:S(2)}, u32[]{:S(2)}) %collective-permute-start.17) | collective-permute-done | bytes 655392 | tf_op jit(solution)/shard_map/ppermute | solution.py:402
  159.8 9.6 %collective-permute-done.15.refs_0_ = bf16[384,1280]{1,0:T(8,128)(2,1)S(1)} collective-permute-done((bf16[384,1280]{1,0:T(8,128)(2,1)S(1)}, bf16[384,1280]{1,0:T(8,128)(2,1)S(1)}, u32[]{:S(2)}, u32[]{:S(2)}) %collective-permute-start.15) | collective-permute-done | bytes 983072 | tf_op jit(solution)/shard_map/ppermute | solution.py:402
  170.9 6.2 %collective-permute-done.36.a_ref = bf16[128,640]{1,0:T(8,128)(2,1)S(1)} collective-permute-done((bf16[128,640]{1,0:T(8,128)(2,1)S(1)}, bf16[128,640]{1,0:T(8,128)(2,1)S(1)}, u32[]{:S(2)}, u32[]{:S(2)}) %collective-permute-start.36) | collective-permute-done | bytes 163872 | tf_op jit(solution)/shard_map/ppermute | solution.py:539
  182.3 7.8 %collective-permute-done.24.a_ref = bf16[128,512]{1,0:T(8,128)(2,1)S(1)} collective-permute-done((bf16[128,512]{1,0:T(8,128)(2,1)S(1)}, bf16[128,512]{1,0:T(8,128)(2,1)S(1)}, u32[]{:S(2)}, u32[]{:S(2)}) %collective-permute-start.24) | collective-permute-done | bytes 131104 | tf_op jit(solution)/shard_map/ppermute | solution.py:539
  190.1 7.1 %collective-permute-done.39.a_ref = bf16[128,640]{1,0:T(8,128)(2,1)S(1)} collective-permute-done((bf16[128,640]{1,0:T(8,128)(2,1)S(1)}, bf16[128,640]{1,0:T(8,128)(2,1)S(1)}, u32[]{:S(2)}, u32[]{:S(2)}) %collective-permute-start.39) | collective-permute-done | bytes 163872 | tf_op jit(solution)/shard_map/ppermute | solution.py:539
  197.2 7.1 %collective-permute-done.43.a_ref = bf16[128,640]{1,0:T(8,128)(2,1)S(1)} collective-permute-done((bf16[128,640]{1,0:T(8,128)(2,1)S(1)}, bf16[128,640]{1,0:T(8,128)(2,1)S(1)}, u32[]{:S(2)}, u32[]{:S(2)}) %collective-permute-start.43) | collective-permute-done | bytes 163872 | tf_op jit(solution)/shard_map/ppermute | solution.py:539
  205.7 7.0 %collective-permute-done.40.a_ref = bf16[128,640]{1,0:T(8,128)(2,1)S(1)} collective-permute-done((bf16[128,640]{1,0:T(8,128)(2,1)S(1)}, bf16[128,640]{1,0:T(8,128)(2,1)S(1)}, u32[]{:S(2)}, u32[]{:S(2)}) %collective-permute-start.40) | collective-permute-done | bytes 163872 | tf_op jit(solution)/shard_map/ppermute | solution.py:539
  212.7 8.6 %collective-permute-done.20.a_ref = bf16[128,768]{1,0:T(8,128)(2,1)S(1)} collective-permute-done((bf16[128,768]{1,0:T(8,128)(2,1)S(1)}, bf16[128,768]{1,0:T(8,128)(2,1)S(1)}, u32[]{:S(2)}, u32[]{:S(2)}) %collective-permute-start.20) | collective-permute-done | bytes 196640 | tf_op jit(solution)/shard_map/ppermute | solution.py:539
  221.3 8.6 %collective-permute-done.44.a_ref = bf16[128,640]{1,0:T(8,128)(2,1)S(1)} collective-permute-done((bf16[128,640]{1,0:T(8,128)(2,1)S(1)}, bf16[128,640]{1,0:T(8,128)(2,1)S(1)}, u32[]{:S(2)}, u32[]{:S(2)}) %collective-permute-start.44) | collective-permute-done | bytes 163872 | tf_op jit(solution)/shard_map/ppermute | solution.py:539
  230.0 9.5 %collective-permute-done.21.a_ref = bf16[128,768]{1,0:T(8,128)(2,1)S(1)} collective-permute-done((bf16[128,768]{1,0:T(8,128)(2,1)S(1)}, bf16[128,768]{1,0:T(8,128)(2,1)S(1)}, u32[]{:S(2)}, u32[]{:S(2)}) %collective-permute-start.21) | collective-permute-done | bytes 196640 | tf_op jit(solution)/shard_map/ppermute | solution.py:539
  240.3 6.0 %collective-permute-done.25.a_ref = bf16[128,512]{1,0:T(8,128)(2,1)S(1)} collective-permute-done((bf16[128,512]{1,0:T(8,128)(2,1)S(1)}, bf16[128,512]{1,0:T(8,128)(2,1)S(1)}, u32[]{:S(2)}, u32[]{:S(2)}) %collective-permute-start.25) | collective-permute-done | bytes 131104 | tf_op jit(solution)/shard_map/ppermute | solution.py:539
  246.4 1.6 collective-permute-done.41.refs_4_
  248.0 1.8 collective-permute-done.45.refs_5_
  249.8 1.6 place.2.refs_4_
  251.4 3.8 %collective-permute-done.26.refs_1_ = bf16[128,512]{1,0:T(8,128)(2,1)S(1)} collective-permute-done((bf16[128,512]{1,0:T(8,128)(2,1)S(1)}, bf16[128,512]{1,0:T(8,128)(2,1)S(1)}, u32[]{:S(2)}, u32[]{:S(2)}) %collective-permute-start.26) | collective-permute-done | bytes 131104 | tf_op jit(solution)/shard_map/ppermute | solution.py:539
  (121 shorter events, 39.4 us)
Async XLA Ops:
  3.7 64.6 %collective-permute-start.6 = (bf16[640,1792]{1,0:T(8,128)(2,1)S(1)}, bf16[640,1792]{1,0:T(8,128)(2,1)S(1)}, u32[]{:S(2)}, u32[]{:S(2)}) collective-permute-start(bf16[640,1792]{1,0:T(8,128)(2,1)S(1)} %pack.1.refs_3_.refs_2_), channel_id=1, source_target_pairs={{0,8},{4,12},{8,0},{12,4},{16,24},{20,28},{24,16},{28,20},{1,9},{5... | collective-permute-start | bytes 6881288 | tf_op jit(solution)/shard_map/ppermute | solution.py:402
  6.7 61.6 %collective-permute-start.4 = (bf16[640,1792]{1,0:T(8,128)(2,1)S(1)}, bf16[640,1792]{1,0:T(8,128)(2,1)S(1)}, u32[]{:S(2)}, u32[]{:S(2)}) collective-permute-start(bf16[640,1792]{1,0:T(8,128)(2,1)S(1)} %pack.1.refs_3_.refs_2_), channel_id=1, source_target_pairs={{0,16},{4,20},{8,24},{12,28},{16,0},{20,4},{24,8},{28,12},{1,17},{... | collective-permute-start | bytes 6881288 | tf_op jit(solution)/shard_map/ppermute | solution.py:402
  8.2 32.8 %collective-permute-start.1 = (bf16[128,5120]{1,0:T(8,128)(2,1)S(1)}, bf16[128,5120]{1,0:T(8,128)(2,1)S(1)}, u32[]{:S(2)}, u32[]{:S(2)}) collective-permute-start(bf16[128,5120]{1,0:T(8,128)(2,1)S(1)} %norm.1.refs_0_), channel_id=1, source_target_pairs={{0,3},{1,0},{2,1},{3,2},{4,7},{5,4},{6,5},{7,6},{8,11},{9,8},{10,9... | collective-permute-start | bytes 3932168 | tf_op jit(solution)/shard_map/ppermute | solution.py:483
  11.8 56.5 %collective-permute-start = (bf16[128,5120]{1,0:T(8,128)(2,1)S(1)}, bf16[128,5120]{1,0:T(8,128)(2,1)S(1)}, u32[]{:S(2)}, u32[]{:S(2)}) collective-permute-start(bf16[128,5120]{1,0:T(8,128)(2,1)S(1)} %norm.1.refs_0_), channel_id=1, source_target_pairs={{0,1},{1,2},{2,3},{3,0},{4,5},{5,6},{6,7},{7,4},{8,9},{9,10},{10,1... | collective-permute-start | bytes 3932168 | tf_op jit(solution)/shard_map/ppermute | solution.py:482
  11.8 58.4 %collective-permute-start.8 = (bf16[640,1792]{1,0:T(8,128)(2,1)S(1)}, bf16[640,1792]{1,0:T(8,128)(2,1)S(1)}, u32[]{:S(2)}, u32[]{:S(2)}) collective-permute-start(bf16[640,1792]{1,0:T(8,128)(2,1)S(1)} %pack.1.refs_3_.refs_2_), channel_id=1, source_target_pairs={{0,4},{4,0},{8,12},{12,8},{16,20},{20,16},{24,28},{28,24},{1,5},{5... | collective-permute-start | bytes 6881288 | tf_op jit(solution)/shard_map/ppermute | solution.py:402
  68.9 31.9 %collective-permute-start.5 = (bf16[640,1024]{1,0:T(8,128)(2,1)S(1)}, bf16[640,1024]{1,0:T(8,128)(2,1)S(1)}, u32[]{:S(2)}, u32[]{:S(2)}) collective-permute-start(bf16[640,1024]{1,0:T(8,128)(2,1)S(1)} %cut.8), channel_id=1, source_target_pairs={{0,8},{4,12},{8,0},{12,4},{16,24},{20,28},{24,16},{28,20},{1,9},{5... | collective-permute-start | bytes 3932168 | tf_op jit(solution)/shard_map/ppermute | solution.py:402
  69.5 31.2 %collective-permute-start.7 = (bf16[640,768]{1,0:T(8,128)(2,1)S(1)}, bf16[640,768]{1,0:T(8,128)(2,1)S(1)}, u32[]{:S(2)}, u32[]{:S(2)}) collective-permute-start(bf16[640,768]{1,0:T(8,128)(2,1)S(1)} %cut.9), channel_id=1, source_target_pairs={{0,16},{4,20},{8,24},{12,28},{16,0},{20,4},{24,8},{28,12},{1,17},{... | collective-permute-start | bytes 2949128 | tf_op jit(solution)/shard_map/ppermute | solution.py:402
  70.2 17.5 %collective-permute-start.3 = (bf16[64,5120]{1,0:T(8,128)(2,1)S(1)}, bf16[64,5120]{1,0:T(8,128)(2,1)S(1)}, u32[]{:S(2)}, u32[]{:S(2)}) collective-permute-start(bf16[64,5120]{1,0:T(8,128)(2,1)S(1)} %cut.7), channel_id=1, source_target_pairs={{0,3},{1,0},{2,1},{3,2},{4,7},{5,4},{6,5},{7,6},{8,11},{9,8},{10,9... | collective-permute-start | bytes 1966088 | tf_op jit(solution)/shard_map/ppermute | solution.py:487
  72.7 28.0 %collective-permute-start.2 = (bf16[64,5120]{1,0:T(8,128)(2,1)S(1)}, bf16[64,5120]{1,0:T(8,128)(2,1)S(1)}, u32[]{:S(2)}, u32[]{:S(2)}) collective-permute-start(bf16[64,5120]{1,0:T(8,128)(2,1)S(1)} %cut.6), channel_id=1, source_target_pairs={{0,1},{1,2},{2,3},{3,0},{4,5},{5,6},{6,7},{7,4},{8,9},{9,10},{10,1... | collective-permute-start | bytes 1966088 | tf_op jit(solution)/shard_map/ppermute | solution.py:486
  100.8 14.5 %collective-permute-start.29 = (bf16[640,1280]{1,0:T(8,128)(2,1)S(1)}, bf16[640,1280]{1,0:T(8,128)(2,1)S(1)}, u32[]{:S(2)}, u32[]{:S(2)}) collective-permute-start(bf16[640,1280]{1,0:T(8,128)(2,1)S(1)} %copy-done.10), channel_id=1, source_target_pairs={{0,4},{4,0},{8,12},{12,8},{16,20},{20,16},{24,28},{28,24},{1,5},{5... | collective-permute-start | bytes 4915208 | tf_op jit(solution)/shard_map/ppermute | solution.py:402
  101.4 38.1 %collective-permute-start.16 = (bf16[640,1280]{1,0:T(8,128)(2,1)S(1)}, bf16[640,1280]{1,0:T(8,128)(2,1)S(1)}, u32[]{:S(2)}, u32[]{:S(2)}) collective-permute-start(bf16[640,1280]{1,0:T(8,128)(2,1)S(1)} %copy-done.10), channel_id=1, source_target_pairs={{0,8},{4,12},{8,0},{12,4},{16,24},{20,28},{24,16},{28,20},{1,9},{5... | collective-permute-start | bytes 4915208 | tf_op jit(solution)/shard_map/ppermute | solution.py:402
  102.8 41.0 %collective-permute-start.13 = (bf16[640,1280]{1,0:T(8,128)(2,1)S(1)}, bf16[640,1280]{1,0:T(8,128)(2,1)S(1)}, u32[]{:S(2)}, u32[]{:S(2)}) collective-permute-start(bf16[640,1280]{1,0:T(8,128)(2,1)S(1)} %copy-done.10), channel_id=1, source_target_pairs={{0,16},{4,20},{8,24},{12,28},{16,0},{20,4},{24,8},{28,12},{1,17},{... | collective-permute-start | bytes 4915208 | tf_op jit(solution)/shard_map/ppermute | solution.py:402
  116.5 8.9 %collective-permute-start.30 = (bf16[128,640]{1,0:T(8,128)(2,1)S(1)}, bf16[128,640]{1,0:T(8,128)(2,1)S(1)}, u32[]{:S(2)}, u32[]{:S(2)}) collective-permute-start(bf16[128,640]{1,0:T(8,128)(2,1)S(1)} %get-tuple-element.83), channel_id=1, source_target_pairs={{0,1},{1,2},{2,3},{3,0},{4,5},{5,6},{6,7},{7,4},{8,9},{9,10},{10,1... | collective-permute-start | bytes 491528 | tf_op jit(solution)/shard_map/ppermute | solution.py:539
  119.3 8.8 %collective-permute-start.14 = (bf16[128,640]{1,0:T(8,128)(2,1)S(1)}, bf16[128,640]{1,0:T(8,128)(2,1)S(1)}, u32[]{:S(2)}, u32[]{:S(2)}) collective-permute-start(bf16[128,640]{1,0:T(8,128)(2,1)S(1)} %get-tuple-element.66), channel_id=1, source_target_pairs={{0,1},{1,2},{2,3},{3,0},{4,5},{5,6},{6,7},{7,4},{8,9},{9,10},{10,1... | collective-permute-start | bytes 491528 | tf_op jit(solution)/shard_map/ppermute | solution.py:539
  125.4 19.7 %collective-permute-start.31 = (bf16[128,640]{1,0:T(8,128)(2,1)S(1)}, bf16[128,640]{1,0:T(8,128)(2,1)S(1)}, u32[]{:S(2)}, u32[]{:S(2)}) collective-permute-start(bf16[128,640]{1,0:T(8,128)(2,1)S(1)} %add.24), channel_id=1, source_target_pairs={{0,1},{1,2},{2,3},{3,0},{4,5},{5,6},{6,7},{7,4},{8,9},{9,10},{10,1... | collective-permute-start | bytes 491528 | tf_op jit(solution)/shard_map/ppermute | solution.py:539
  128.1 18.6 %collective-permute-start.27 = (bf16[128,640]{1,0:T(8,128)(2,1)S(1)}, bf16[128,640]{1,0:T(8,128)(2,1)S(1)}, u32[]{:S(2)}, u32[]{:S(2)}) collective-permute-start(bf16[128,640]{1,0:T(8,128)(2,1)S(1)} %add.22), channel_id=1, source_target_pairs={{0,1},{1,2},{2,3},{3,0},{4,5},{5,6},{6,7},{7,4},{8,9},{9,10},{10,1... | collective-permute-start | bytes 491528 | tf_op jit(solution)/shard_map/ppermute | solution.py:539
  142.3 16.0 %collective-permute-start.17 = (bf16[256,1280]{1,0:T(8,128)(2,1)S(1)}, bf16[256,1280]{1,0:T(8,128)(2,1)S(1)}, u32[]{:S(2)}, u32[]{:S(2)}) collective-permute-start(bf16[256,1280]{1,0:T(8,128)(2,1)S(1)} %cut.11), channel_id=1, source_target_pairs={{0,16},{4,20},{8,24},{12,28},{16,0},{20,4},{24,8},{28,12},{1,17},{... | collective-permute-start | bytes 1966088 | tf_op jit(solution)/shard_map/ppermute | solution.py:402
  143.9 35.2 %collective-permute-start.38 = (bf16[640,1280]{1,0:T(8,128)(2,1)S(1)}, bf16[640,1280]{1,0:T(8,128)(2,1)S(1)}, u32[]{:S(2)}, u32[]{:S(2)}) collective-permute-start(bf16[640,1280]{1,0:T(8,128)(2,1)S(1)} %collective-permute-done.16.ref.refs_0_), channel_id=1, source_target_pairs={{0,4},{4,0},{8,12},{12,8},{16,20},{20,16},{24,28},{28,24},{1,5},{5... | collective-permute-start | bytes 4915208 | tf_op jit(solution)/shard_map/ppermute | solution.py:402
  145.2 24.2 %collective-permute-start.15 = (bf16[384,1280]{1,0:T(8,128)(2,1)S(1)}, bf16[384,1280]{1,0:T(8,128)(2,1)S(1)}, u32[]{:S(2)}, u32[]{:S(2)}) collective-permute-start(bf16[384,1280]{1,0:T(8,128)(2,1)S(1)} %cut.10), channel_id=1, source_target_pairs={{0,8},{4,12},{8,0},{12,4},{16,24},{20,28},{24,16},{28,20},{1,9},{5... | collective-permute-start | bytes 2949128 | tf_op jit(solution)/shard_map/ppermute | solution.py:402
  146.8 34.2 %collective-permute-start.42 = (bf16[640,1280]{1,0:T(8,128)(2,1)S(1)}, bf16[640,1280]{1,0:T(8,128)(2,1)S(1)}, u32[]{:S(2)}, u32[]{:S(2)}) collective-permute-start(bf16[640,1280]{1,0:T(8,128)(2,1)S(1)} %collective-permute-done.13.ref.refs_0_), channel_id=1, source_target_pairs={{0,4},{4,0},{8,12},{12,8},{16,20},{20,16},{24,28},{28,24},{1,5},{5... | collective-permute-start | bytes 4915208 | tf_op jit(solution)/shard_map/ppermute | solution.py:402
  155.5 15.3 %collective-permute-start.33 = (bf16[128,640]{1,0:T(8,128)(2,1)S(1)}, bf16[128,640]{1,0:T(8,128)(2,1)S(1)}, u32[]{:S(2)}, u32[]{:S(2)}) collective-permute-start(bf16[128,640]{1,0:T(8,128)(2,1)S(1)} %add.26), channel_id=1, source_target_pairs={{0,1},{1,2},{2,3},{3,0},{4,5},{5,6},{6,7},{7,4},{8,9},{9,10},{10,1... | collective-permute-start | bytes 491528 | tf_op jit(solution)/shard_map/ppermute | solution.py:539
  158.4 81.2 %collective-permute-start.32 = (bf16[128,640]{1,0:T(8,128)(2,1)S(1)}, bf16[128,640]{1,0:T(8,128)(2,1)S(1)}, u32[]{:S(2)}, u32[]{:S(2)}) collective-permute-start(bf16[128,640]{1,0:T(8,128)(2,1)S(1)} %add.25), channel_id=1, source_target_pairs={{0,1},{1,2},{2,3},{3,0},{4,5},{5,6},{6,7},{7,4},{8,9},{9,10},{10,1... | collective-permute-start | bytes 491528 | tf_op jit(solution)/shard_map/ppermute | solution.py:539
  177.0 62.6 %collective-permute-start.28 = (bf16[128,640]{1,0:T(8,128)(2,1)S(1)}, bf16[128,640]{1,0:T(8,128)(2,1)S(1)}, u32[]{:S(2)}, u32[]{:S(2)}) collective-permute-start(bf16[128,640]{1,0:T(8,128)(2,1)S(1)} %add.23), channel_id=1, source_target_pairs={{0,1},{1,2},{2,3},{3,0},{4,5},{5,6},{6,7},{7,4},{8,9},{9,10},{10,1... | collective-permute-start | bytes 491528 | tf_op jit(solution)/shard_map/ppermute | solution.py:539
  177.1 69.2 %collective-permute-start.34 = (bf16[128,640]{1,0:T(8,128)(2,1)S(1)}, bf16[128,640]{1,0:T(8,128)(2,1)S(1)}, u32[]{:S(2)}, u32[]{:S(2)}) collective-permute-start(bf16[128,640]{1,0:T(8,128)(2,1)S(1)} %add.27), channel_id=1, source_target_pairs={{0,1},{1,2},{2,3},{3,0},{4,5},{5,6},{6,7},{7,4},{8,9},{9,10},{10,1... | collective-permute-start | bytes 491528 | tf_op jit(solution)/shard_map/ppermute | solution.py:539
  179.1 11.0 %collective-permute-start.24 = (bf16[128,512]{1,0:T(8,128)(2,1)S(1)}, bf16[128,512]{1,0:T(8,128)(2,1)S(1)}, u32[]{:S(2)}, u32[]{:S(2)}) collective-permute-start(bf16[128,512]{1,0:T(8,128)(2,1)S(1)} %get-tuple-element.75), channel_id=1, source_target_pairs={{0,1},{1,2},{2,3},{3,0},{4,5},{5,6},{6,7},{7,4},{8,9},{9,10},{10,1... | collective-permute-start | bytes 393224 | tf_op jit(solution)/shard_map/ppermute | solution.py:539
  181.0 23.4 %collective-permute-start.19 = (bf16[384,1280]{1,0:T(8,128)(2,1)S(1)}, bf16[384,1280]{1,0:T(8,128)(2,1)S(1)}, u32[]{:S(2)}, u32[]{:S(2)}) collective-permute-start(bf16[384,1280]{1,0:T(8,128)(2,1)S(1)} %collective-permute-done.15.refs_0_), channel_id=1, source_target_pairs={{0,4},{4,0},{8,12},{12,8},{16,20},{20,16},{24,28},{28,24},{1,5},{5... | collective-permute-start | bytes 2949128 | tf_op jit(solution)/shard_map/ppermute | solution.py:402
  204.4 42.0 %collective-permute-start.37 = (bf16[128,640]{1,0:T(8,128)(2,1)S(1)}, bf16[128,640]{1,0:T(8,128)(2,1)S(1)}, u32[]{:S(2)}, u32[]{:S(2)}) collective-permute-start(bf16[128,640]{1,0:T(8,128)(2,1)S(1)} %add.29), channel_id=1, source_target_pairs={{0,1},{1,2},{2,3},{3,0},{4,5},{5,6},{6,7},{7,4},{8,9},{9,10},{10,1... | collective-permute-start | bytes 491528 | tf_op jit(solution)/shard_map/ppermute | solution.py:539
  221.3 8.7 %collective-permute-start.44 = (bf16[128,640]{1,0:T(8,128)(2,1)S(1)}, bf16[128,640]{1,0:T(8,128)(2,1)S(1)}, u32[]{:S(2)}, u32[]{:S(2)}) collective-permute-start(bf16[128,640]{1,0:T(8,128)(2,1)S(1)} %add.32), channel_id=1, source_target_pairs={{0,1},{1,2},{2,3},{3,0},{4,5},{5,6},{6,7},{7,4},{8,9},{9,10},{10,1... | collective-permute-start | bytes 491528 | tf_op jit(solution)/shard_map/ppermute | solution.py:539
  229.9 9.6 %collective-permute-start.21 = (bf16[128,768]{1,0:T(8,128)(2,1)S(1)}, bf16[128,768]{1,0:T(8,128)(2,1)S(1)}, u32[]{:S(2)}, u32[]{:S(2)}) collective-permute-start(bf16[128,768]{1,0:T(8,128)(2,1)S(1)} %add.18), channel_id=1, source_target_pairs={{0,1},{1,2},{2,3},{3,0},{4,5},{5,6},{6,7},{7,4},{8,9},{9,10},{10,1... | collective-permute-start | bytes 589832 | tf_op jit(solution)/shard_map/ppermute | solution.py:539
  239.6 10.1 %collective-permute-start.45 = (bf16[128,640]{1,0:T(8,128)(2,1)S(1)}, bf16[128,640]{1,0:T(8,128)(2,1)S(1)}, u32[]{:S(2)}, u32[]{:S(2)}) collective-permute-start(bf16[128,640]{1,0:T(8,128)(2,1)S(1)} %add.33), channel_id=1, source_target_pairs={{0,1},{1,2},{2,3},{3,0},{4,5},{5,6},{6,7},{7,4},{8,9},{9,10},{10,1... | collective-permute-start | bytes 491528 | tf_op jit(solution)/shard_map/ppermute | solution.py:539
  246.3 8.9 %collective-permute-start.22 = (bf16[128,768]{1,0:T(8,128)(2,1)S(1)}, bf16[128,768]{1,0:T(8,128)(2,1)S(1)}, u32[]{:S(2)}, u32[]{:S(2)}) collective-permute-start(bf16[128,768]{1,0:T(8,128)(2,1)S(1)} %add.19), channel_id=1, source_target_pairs={{0,1},{1,2},{2,3},{3,0},{4,5},{5,6},{6,7},{7,4},{8,9},{9,10},{10,1... | collective-permute-start | bytes 589832 | tf_op jit(solution)/shard_map/ppermute | solution.py:539
  246.3 8.8 %collective-permute-start.26 = (bf16[128,512]{1,0:T(8,128)(2,1)S(1)}, bf16[128,512]{1,0:T(8,128)(2,1)S(1)}, u32[]{:S(2)}, u32[]{:S(2)}) collective-permute-start(bf16[128,512]{1,0:T(8,128)(2,1)S(1)} %add.21), channel_id=1, source_target_pairs={{0,1},{1,2},{2,3},{3,0},{4,5},{5,6},{6,7},{7,4},{8,9},{9,10},{10,1... | collective-permute-start | bytes 393224 | tf_op jit(solution)/shard_map/ppermute | solution.py:539
  (25 other events, 264.0 us)

commit v8 on v7

--- a/solution.py
+++ b/solution.py
@@ -33,7 +33,7 @@
 
 def link_time(array, share=2):
     size = share * int(np.prod(array.shape)) * array.dtype.itemsize
-    return pl.CostEstimate(flops=size * 11000, bytes_accessed=size, transcendentals=0)
+    return pl.CostEstimate(flops=size * 2000, bytes_accessed=size, transcendentals=0)
 
 
 def normed_kernel(n_f, index_ref, tokens_ref, gain_ref, out_ref):
@@ -518,9 +518,13 @@
 
     rounds = []
     for level in range(levels + 1):
+        if level == 1:
+            for r in chips_away(1, chips):
+                o_held[r] = [after(part, *arrivals[min(1, n_s - 2)]) for part in o_held[r]]
         if level:
-            send_siblings(o_held, o_sibling, n_f, level, *sent)
-            send_level(o_held, n_f, o_cut, 0, level + 1, *sent)
+            before = arrivals[0] + arrivals[min(1, n_s - 2)][:2] if level > 1 else []
+            send_siblings(o_held, o_sibling, n_f, level, *before)
+            send_level(o_held, n_f, o_cut, 0, level + 1, *before)
         groups = []
         for r in chips_away(level, chips):
             halves = range(len(o_held[r]))
@@ -544,7 +548,6 @@
             for group in groups
         ]
         rounds.append(([term[0] for term in terms], arrivals, where))
-        sent = arrivals[0][:1]
 
     mixed = None
     for chosen in (rounds[:-1], rounds[-1:]):

time: 257 us -> 230 us (0.89)
  waiting for transfers between devices: 191 us -> 163 us
    ppermute x24, waiting for transfers between devices: 90.3 us -> 71.2 us  [body(): arrivals.append([lax.ppermute(total, 'sp', right) for total in totals])]
    ppermute x18, waiting for transfers between devices: 26.4 us -> 17.2 us  [swapped(): return lax.ppermute(array, 'fsdp', [(i, i ^ mask) for i in range(n_f)])]
  transfers between devices with their start and end apart: 46 -> 46, of which waited for: 26 -> 28; matrix products, arithmetic and copies ran while one was open for 0% -> 0% of each run, Pallas kernels for 11% -> 12%
where the time goes in v8:
time: 230 us
  waiting for transfers between devices  163 us (71%)
  starting transfers between devices  32.8 us (14%)
  Pallas kernels  31.2 us (14%)
    ppermute x24, waiting for transfers between devices, body(): arrivals.append([lax.ppermute(total, 'sp', right) for total in totals])  71.2 us
    ppermute x1, waiting for transfers between devices, body(): behind = lax.ppermute(behind, 'sp', left)  29.2 us
    ppermute x1, waiting for transfers between devices, body(): ahead = lax.ppermute(ahead, 'sp', right)  27.2 us
    ppermute x18, waiting for transfers between devices, swapped(): return lax.ppermute(array, 'fsdp', [(i, i ^ mask) for i in range(n_f)])  17.2 us
    ppermute x24, starting transfers between devices, body(): arrivals.append([lax.ppermute(total, 'sp', right) for total in totals])  13 us
    ppermute x1, waiting for transfers between devices, body(): ahead = lax.ppermute(part_of(ahead, count // 2, 0, 0), 'sp', right)  13 us
    ppermute x18, starting transfers between devices, swapped(): return lax.ppermute(array, 'fsdp', [(i, i ^ mask) for i in range(n_f)])  12.8 us
    pallas_call x8, Pallas kernels, mix(): pl.pallas_call(functools.partial(mix_kernel, len(parts)), in_specs=[VMEM]...  9.37 us
  transfers between devices with their start and end apart: 46, of which 28 were waited for; matrix products, arithmetic and copies ran while one was open for 0% of the time, Pallas kernels for 12%

profile of v8, /device:TPU:0, one launch (start us, length us, event | category | flops | bytes accessed | tf_op | source)
XLA Modules:
  0.0 230.0 jit_solution(5999082119948772000)
XLA Ops:
  3.7 3.0 %collective-permute-start.6 = (bf16[640,1792]{1,0:T(8,128)(2,1)S(1)}, bf16[640,1792]{1,0:T(8,128)(2,1)S(1)}, u32[]{:S(2)}, u32[]{:S(2)}) collective-permute-start(bf16[640,1792]{1,0:T(8,128)(2,1)S(1)} %pack.1.refs_3_.refs_2_), channel_id=1, source_target_pairs={{0,8},{4,12},{8,0},{12,4},{16,24},{20,28},{24,16},{28,20},{1,9},{5... | collective-permute-start | bytes 6881288 | tf_op jit(solution)/shard_map/ppermute | solution.py:402
  8.2 3.6 %collective-permute-start.1 = (bf16[128,5120]{1,0:T(8,128)(2,1)S(1)}, bf16[128,5120]{1,0:T(8,128)(2,1)S(1)}, u32[]{:S(2)}, u32[]{:S(2)}) collective-permute-start(bf16[128,5120]{1,0:T(8,128)(2,1)S(1)} %norm.1.refs_0_), channel_id=1, source_target_pairs={{0,3},{1,0},{2,1},{3,2},{4,7},{5,4},{6,5},{7,6},{8,11},{9,8},{10,9... | collective-permute-start | bytes 3932168 | tf_op jit(solution)/shard_map/ppermute | solution.py:483
  11.8 29.2 %collective-permute-done.1.ref.refs_2_ = bf16[128,5120]{1,0:T(8,128)(2,1)S(1)} collective-permute-done((bf16[128,5120]{1,0:T(8,128)(2,1)S(1)}, bf16[128,5120]{1,0:T(8,128)(2,1)S(1)}, u32[]{:S(2)}, u32[]{:S(2)}) %collective-permute-start.1) | collective-permute-done | bytes 1310752 | tf_op jit(solution)/shard_map/ppermute | solution.py:483
  41.0 27.2 %collective-permute-done.ref.refs_1_ = bf16[128,5120]{1,0:T(8,128)(2,1)S(1)} collective-permute-done((bf16[128,5120]{1,0:T(8,128)(2,1)S(1)}, bf16[128,5120]{1,0:T(8,128)(2,1)S(1)}, u32[]{:S(2)}, u32[]{:S(2)}) %collective-permute-start) | collective-permute-done | bytes 1310752 | tf_op jit(solution)/shard_map/ppermute | solution.py:482
  70.2 1.8 collective-permute-start.3
  76.0 6.5 %partial.2.refs_9_ = f32[384,1792]{1,0:T(8,128)S(1)} custom-call(bf16[128,5120]{1,0:T(8,128)(2,1)S(1)} %norm.1.refs_0_, bf16[128,5120]{1,0:T(8,128)(2,1)S(1)} %collective-permute-done.ref.refs_1_, bf16[128,5120]{1,0:T(8,128)(2,1)S(1)} %collective-permute-done.1.ref.refs_2_, bf16[640,1792]{1,0:T(8,128)(2,1)S(1)} %pack.1.refs_3_.refs_2_, ...), custom_call_target="tpu_custom_call" | custom-call | flops 5284823040 | bytes 20447232 | tf_op jit(solution)/shard_map/partial/pallas_call | solution.py:145
  82.6 5.2 %collective-permute-done.3.refs_1_.refs_4_ = bf16[64,5120]{1,0:T(8,128)(2,1)S(1)} collective-permute-done((bf16[64,5120]{1,0:T(8,128)(2,1)S(1)}, bf16[64,5120]{1,0:T(8,128)(2,1)S(1)}, u32[]{:S(2)}, u32[]{:S(2)}) %collective-permute-start.3) | collective-permute-done | bytes 655392 | tf_op jit(solution)/shard_map/ppermute | solution.py:487
  87.8 13.0 %collective-permute-done.2.refs_0_.refs_3_ = bf16[64,5120]{1,0:T(8,128)(2,1)S(1)} collective-permute-done((bf16[64,5120]{1,0:T(8,128)(2,1)S(1)}, bf16[64,5120]{1,0:T(8,128)(2,1)S(1)}, u32[]{:S(2)}, u32[]{:S(2)}) %collective-permute-start.2) | collective-permute-done | bytes 655392 | tf_op jit(solution)/shard_map/ppermute | solution.py:486
  104.4 2.3 %partial.3.refs_10_ = f32[128,1792]{1,0:T(8,128)S(1)} custom-call(bf16[64,5120]{1,0:T(8,128)(2,1)S(1)} %collective-permute-done.2.refs_0_.refs_3_, bf16[64,5120]{1,0:T(8,128)(2,1)S(1)} %collective-permute-done.3.refs_1_.refs_4_, bf16[640,1792]{1,0:T(8,128)(2,1)S(1)} %pack.1.refs_3_.refs_2_, bf16[640,1792]{1,0:T(8,128)(2,1)S(1)} %collective-permute-done.8.refs_4_.refs_3_, ...), custom_call_target="tpu_custom_call" | custom-call | flops 1761607680 | bytes 15990784 | tf_op jit(solution)/shard_map/partial/pallas_call | solution.py:145
  107.6 3.7 %finish.1 = (bf16[512,1280]{1,0:T(8,128)(2,1)S(1)}, bf16[512,512]{1,0:T(8,128)(2,1)S(1)}) custom-call(s32[2]{0:T(128)S(1)} %pad_add_fusion.index_ref, bf16[128,5120]{1,0:T(8,128)(2,1)S(1)} %norm.1.refs_0_, bf16[128,5120]{1,0:T(8,128)(2,1)S(1)} %collective-permute-done.ref.refs_1_, bf16[128,5120]{1,0:T(8,128)(2,1)S(1)} %collective-permute-done.1.ref.refs_2_, ...), custom_call_target="tpu_custom_call" | custom-call | flops 2348810240 | bytes 8257536 | tf_op jit(solution)/shard_map/finish/pallas_call | solution.py:221
  111.3 4.0 %attend.1.heads_ref = bf16[512,1280]{1,0:T(8,128)(2,1)S(1)} custom-call(s32[2]{0:T(128)S(1)} %pad_add_fusion.index_ref, bf16[512,1280]{1,0:T(8,128)(2,1)S(1)} %get-tuple-element.60.q_ref, bf16[512,512]{1,0:T(8,128)(2,1)S(1)} %get-tuple-element.61.kv_ref), custom_call_target="tpu_custom_call" | custom-call | flops 1342177280 | bytes 3145728 | tf_op jit(solution)/shard_map/attend/pallas_call | solution.py:292
  120.8 4.6 %collective-permute-done.17.a_ref = bf16[128,640]{1,0:T(8,128)(2,1)S(1)} collective-permute-done((bf16[128,640]{1,0:T(8,128)(2,1)S(1)}, bf16[128,640]{1,0:T(8,128)(2,1)S(1)}, u32[]{:S(2)}, u32[]{:S(2)}) %collective-permute-start.17) | collective-permute-done | bytes 163872 | tf_op jit(solution)/shard_map/ppermute | solution.py:543
  125.5 2.6 %collective-permute-done.14.a_ref = bf16[128,640]{1,0:T(8,128)(2,1)S(1)} collective-permute-done((bf16[128,640]{1,0:T(8,128)(2,1)S(1)}, bf16[128,640]{1,0:T(8,128)(2,1)S(1)}, u32[]{:S(2)}, u32[]{:S(2)}) %collective-permute-start.14) | collective-permute-done | bytes 163872 | tf_op jit(solution)/shard_map/ppermute | solution.py:543
  128.7 10.8 %collective-permute-done.20.ref.refs_0_ = bf16[640,1280]{1,0:T(8,128)(2,1)S(1)} collective-permute-done((bf16[640,1280]{1,0:T(8,128)(2,1)S(1)}, bf16[640,1280]{1,0:T(8,128)(2,1)S(1)}, u32[]{:S(2)}, u32[]{:S(2)}) %collective-permute-start.20) | collective-permute-done | bytes 1638432 | tf_op jit(solution)/shard_map/ppermute | solution.py:402
  147.3 3.5 %collective-permute-done.22.a_ref = bf16[128,640]{1,0:T(8,128)(2,1)S(1)} collective-permute-done((bf16[128,640]{1,0:T(8,128)(2,1)S(1)}, bf16[128,640]{1,0:T(8,128)(2,1)S(1)}, u32[]{:S(2)}, u32[]{:S(2)}) %collective-permute-start.22) | collective-permute-done | bytes 163872 | tf_op jit(solution)/shard_map/ppermute | solution.py:543
  150.8 7.1 %collective-permute-done.23.a_ref = bf16[128,640]{1,0:T(8,128)(2,1)S(1)} collective-permute-done((bf16[128,640]{1,0:T(8,128)(2,1)S(1)}, bf16[128,640]{1,0:T(8,128)(2,1)S(1)}, u32[]{:S(2)}, u32[]{:S(2)}) %collective-permute-start.23) | collective-permute-done | bytes 163872 | tf_op jit(solution)/shard_map/ppermute | solution.py:543
  161.3 5.5 %collective-permute-done.28.a_ref = bf16[128,640]{1,0:T(8,128)(2,1)S(1)} collective-permute-done((bf16[128,640]{1,0:T(8,128)(2,1)S(1)}, bf16[128,640]{1,0:T(8,128)(2,1)S(1)}, u32[]{:S(2)}, u32[]{:S(2)}) %collective-permute-start.28) | collective-permute-done | bytes 163872 | tf_op jit(solution)/shard_map/ppermute | solution.py:543
  166.9 3.5 %collective-permute-done.29.a_ref = bf16[128,640]{1,0:T(8,128)(2,1)S(1)} collective-permute-done((bf16[128,640]{1,0:T(8,128)(2,1)S(1)}, bf16[128,640]{1,0:T(8,128)(2,1)S(1)}, u32[]{:S(2)}, u32[]{:S(2)}) %collective-permute-start.29) | collective-permute-done | bytes 163872 | tf_op jit(solution)/shard_map/ppermute | solution.py:543
  170.4 2.2 collective-permute-done.25.a_ref
  172.6 1.8 collective-permute-done.27.a_ref
  174.9 1.9 collective-permute-done.30.refs_1_
  178.4 3.0 %collective-permute-start.42 = (bf16[128,640]{1,0:T(8,128)(2,1)S(1)}, bf16[128,640]{1,0:T(8,128)(2,1)S(1)}, u32[]{:S(2)}, u32[]{:S(2)}) collective-permute-start(bf16[128,640]{1,0:T(8,128)(2,1)S(1)} %add.30), channel_id=1, source_target_pairs={{0,1},{1,2},{2,3},{3,0},{4,5},{5,6},{6,7},{7,4},{8,9},{9,10},{10,1... | collective-permute-start | bytes 491528 | tf_op jit(solution)/shard_map/ppermute | solution.py:543
  182.3 2.0 collective-permute-start.35
  184.3 3.4 %collective-permute-done.31.a_ref = bf16[128,768]{1,0:T(8,128)(2,1)S(1)} collective-permute-done((bf16[128,768]{1,0:T(8,128)(2,1)S(1)}, bf16[128,768]{1,0:T(8,128)(2,1)S(1)}, u32[]{:S(2)}, u32[]{:S(2)}) %collective-permute-start.31) | collective-permute-done | bytes 196640 | tf_op jit(solution)/shard_map/ppermute | solution.py:543
  187.9 6.8 %collective-permute-done.42.a_ref = bf16[128,640]{1,0:T(8,128)(2,1)S(1)} collective-permute-done((bf16[128,640]{1,0:T(8,128)(2,1)S(1)}, bf16[128,640]{1,0:T(8,128)(2,1)S(1)}, u32[]{:S(2)}, u32[]{:S(2)}) %collective-permute-start.42) | collective-permute-done | bytes 163872 | tf_op jit(solution)/shard_map/ppermute | solution.py:543
  194.8 2.8 %collective-permute-done.35.a_ref = bf16[128,512]{1,0:T(8,128)(2,1)S(1)} collective-permute-done((bf16[128,512]{1,0:T(8,128)(2,1)S(1)}, bf16[128,512]{1,0:T(8,128)(2,1)S(1)}, u32[]{:S(2)}, u32[]{:S(2)}) %collective-permute-start.35) | collective-permute-done | bytes 131104 | tf_op jit(solution)/shard_map/ppermute | solution.py:543
  197.6 4.2 %collective-permute-done.32.a_ref = bf16[128,768]{1,0:T(8,128)(2,1)S(1)} collective-permute-done((bf16[128,768]{1,0:T(8,128)(2,1)S(1)}, bf16[128,768]{1,0:T(8,128)(2,1)S(1)}, u32[]{:S(2)}, u32[]{:S(2)}) %collective-permute-start.32) | collective-permute-done | bytes 196640 | tf_op jit(solution)/shard_map/ppermute | solution.py:543
  201.8 3.5 %collective-permute-done.44.a_ref = bf16[128,640]{1,0:T(8,128)(2,1)S(1)} collective-permute-done((bf16[128,640]{1,0:T(8,128)(2,1)S(1)}, bf16[128,640]{1,0:T(8,128)(2,1)S(1)}, u32[]{:S(2)}, u32[]{:S(2)}) %collective-permute-start.44) | collective-permute-done | bytes 163872 | tf_op jit(solution)/shard_map/ppermute | solution.py:543
  206.9 4.7 %collective-permute-done.36.a_ref = bf16[128,512]{1,0:T(8,128)(2,1)S(1)} collective-permute-done((bf16[128,512]{1,0:T(8,128)(2,1)S(1)}, bf16[128,512]{1,0:T(8,128)(2,1)S(1)}, u32[]{:S(2)}, u32[]{:S(2)}) %collective-permute-start.36) | collective-permute-done | bytes 131104 | tf_op jit(solution)/shard_map/ppermute | solution.py:543
  211.7 7.6 %collective-permute-done.41.refs_3_ = bf16[128,640]{1,0:T(8,128)(2,1)S(1)} collective-permute-done((bf16[128,640]{1,0:T(8,128)(2,1)S(1)}, bf16[128,640]{1,0:T(8,128)(2,1)S(1)}, u32[]{:S(2)}, u32[]{:S(2)}) %collective-permute-start.41) | collective-permute-done | bytes 163872 | tf_op jit(solution)/shard_map/ppermute | solution.py:543
  219.3 3.5 %collective-permute-done.43.refs_4_ = bf16[128,640]{1,0:T(8,128)(2,1)S(1)} collective-permute-done((bf16[128,640]{1,0:T(8,128)(2,1)S(1)}, bf16[128,640]{1,0:T(8,128)(2,1)S(1)}, u32[]{:S(2)}, u32[]{:S(2)}) %collective-permute-start.43) | collective-permute-done | bytes 163872 | tf_op jit(solution)/shard_map/ppermute | solution.py:543
  222.8 3.5 %collective-permute-done.45.refs_5_ = bf16[128,640]{1,0:T(8,128)(2,1)S(1)} collective-permute-done((bf16[128,640]{1,0:T(8,128)(2,1)S(1)}, bf16[128,640]{1,0:T(8,128)(2,1)S(1)}, u32[]{:S(2)}, u32[]{:S(2)}) %collective-permute-start.45) | collective-permute-done | bytes 163872 | tf_op jit(solution)/shard_map/ppermute | solution.py:543
  (121 shorter events, 41.4 us)
Async XLA Ops:
  3.7 64.6 %collective-permute-start.6 = (bf16[640,1792]{1,0:T(8,128)(2,1)S(1)}, bf16[640,1792]{1,0:T(8,128)(2,1)S(1)}, u32[]{:S(2)}, u32[]{:S(2)}) collective-permute-start(bf16[640,1792]{1,0:T(8,128)(2,1)S(1)} %pack.1.refs_3_.refs_2_), channel_id=1, source_target_pairs={{0,8},{4,12},{8,0},{12,4},{16,24},{20,28},{24,16},{28,20},{1,9},{5... | collective-permute-start | bytes 6881288 | tf_op jit(solution)/shard_map/ppermute | solution.py:402
  6.7 61.6 %collective-permute-start.4 = (bf16[640,1792]{1,0:T(8,128)(2,1)S(1)}, bf16[640,1792]{1,0:T(8,128)(2,1)S(1)}, u32[]{:S(2)}, u32[]{:S(2)}) collective-permute-start(bf16[640,1792]{1,0:T(8,128)(2,1)S(1)} %pack.1.refs_3_.refs_2_), channel_id=1, source_target_pairs={{0,16},{4,20},{8,24},{12,28},{16,0},{20,4},{24,8},{28,12},{1,17},{... | collective-permute-start | bytes 6881288 | tf_op jit(solution)/shard_map/ppermute | solution.py:402
  8.2 32.8 %collective-permute-start.1 = (bf16[128,5120]{1,0:T(8,128)(2,1)S(1)}, bf16[128,5120]{1,0:T(8,128)(2,1)S(1)}, u32[]{:S(2)}, u32[]{:S(2)}) collective-permute-start(bf16[128,5120]{1,0:T(8,128)(2,1)S(1)} %norm.1.refs_0_), channel_id=1, source_target_pairs={{0,3},{1,0},{2,1},{3,2},{4,7},{5,4},{6,5},{7,6},{8,11},{9,8},{10,9... | collective-permute-start | bytes 3932168 | tf_op jit(solution)/shard_map/ppermute | solution.py:483
  11.8 56.5 %collective-permute-start = (bf16[128,5120]{1,0:T(8,128)(2,1)S(1)}, bf16[128,5120]{1,0:T(8,128)(2,1)S(1)}, u32[]{:S(2)}, u32[]{:S(2)}) collective-permute-start(bf16[128,5120]{1,0:T(8,128)(2,1)S(1)} %norm.1.refs_0_), channel_id=1, source_target_pairs={{0,1},{1,2},{2,3},{3,0},{4,5},{5,6},{6,7},{7,4},{8,9},{9,10},{10,1... | collective-permute-start | bytes 3932168 | tf_op jit(solution)/shard_map/ppermute | solution.py:482
  11.8 58.4 %collective-permute-start.8 = (bf16[640,1792]{1,0:T(8,128)(2,1)S(1)}, bf16[640,1792]{1,0:T(8,128)(2,1)S(1)}, u32[]{:S(2)}, u32[]{:S(2)}) collective-permute-start(bf16[640,1792]{1,0:T(8,128)(2,1)S(1)} %pack.1.refs_3_.refs_2_), channel_id=1, source_target_pairs={{0,4},{4,0},{8,12},{12,8},{16,20},{20,16},{24,28},{28,24},{1,5},{5... | collective-permute-start | bytes 6881288 | tf_op jit(solution)/shard_map/ppermute | solution.py:402
  68.9 31.9 %collective-permute-start.5 = (bf16[640,1024]{1,0:T(8,128)(2,1)S(1)}, bf16[640,1024]{1,0:T(8,128)(2,1)S(1)}, u32[]{:S(2)}, u32[]{:S(2)}) collective-permute-start(bf16[640,1024]{1,0:T(8,128)(2,1)S(1)} %cut.8), channel_id=1, source_target_pairs={{0,8},{4,12},{8,0},{12,4},{16,24},{20,28},{24,16},{28,20},{1,9},{5... | collective-permute-start | bytes 3932168 | tf_op jit(solution)/shard_map/ppermute | solution.py:402
  69.5 31.2 %collective-permute-start.7 = (bf16[640,768]{1,0:T(8,128)(2,1)S(1)}, bf16[640,768]{1,0:T(8,128)(2,1)S(1)}, u32[]{:S(2)}, u32[]{:S(2)}) collective-permute-start(bf16[640,768]{1,0:T(8,128)(2,1)S(1)} %cut.9), channel_id=1, source_target_pairs={{0,16},{4,20},{8,24},{12,28},{16,0},{20,4},{24,8},{28,12},{1,17},{... | collective-permute-start | bytes 2949128 | tf_op jit(solution)/shard_map/ppermute | solution.py:402
  70.2 17.5 %collective-permute-start.3 = (bf16[64,5120]{1,0:T(8,128)(2,1)S(1)}, bf16[64,5120]{1,0:T(8,128)(2,1)S(1)}, u32[]{:S(2)}, u32[]{:S(2)}) collective-permute-start(bf16[64,5120]{1,0:T(8,128)(2,1)S(1)} %cut.7), channel_id=1, source_target_pairs={{0,3},{1,0},{2,1},{3,2},{4,7},{5,4},{6,5},{7,6},{8,11},{9,8},{10,9... | collective-permute-start | bytes 1966088 | tf_op jit(solution)/shard_map/ppermute | solution.py:487
  72.7 28.0 %collective-permute-start.2 = (bf16[64,5120]{1,0:T(8,128)(2,1)S(1)}, bf16[64,5120]{1,0:T(8,128)(2,1)S(1)}, u32[]{:S(2)}, u32[]{:S(2)}) collective-permute-start(bf16[64,5120]{1,0:T(8,128)(2,1)S(1)} %cut.6), channel_id=1, source_target_pairs={{0,1},{1,2},{2,3},{3,0},{4,5},{5,6},{6,7},{7,4},{8,9},{9,10},{10,1... | collective-permute-start | bytes 1966088 | tf_op jit(solution)/shard_map/ppermute | solution.py:486
  100.8 14.5 %collective-permute-start.16 = (bf16[640,1280]{1,0:T(8,128)(2,1)S(1)}, bf16[640,1280]{1,0:T(8,128)(2,1)S(1)}, u32[]{:S(2)}, u32[]{:S(2)}) collective-permute-start(bf16[640,1280]{1,0:T(8,128)(2,1)S(1)} %copy-done.10), channel_id=1, source_target_pairs={{0,4},{4,0},{8,12},{12,8},{16,20},{20,16},{24,28},{28,24},{1,5},{5... | collective-permute-start | bytes 4915208 | tf_op jit(solution)/shard_map/ppermute | solution.py:402
  101.4 38.1 %collective-permute-start.20 = (bf16[640,1280]{1,0:T(8,128)(2,1)S(1)}, bf16[640,1280]{1,0:T(8,128)(2,1)S(1)}, u32[]{:S(2)}, u32[]{:S(2)}) collective-permute-start(bf16[640,1280]{1,0:T(8,128)(2,1)S(1)} %copy-done.10), channel_id=1, source_target_pairs={{0,8},{4,12},{8,0},{12,4},{16,24},{20,28},{24,16},{28,20},{1,9},{5... | collective-permute-start | bytes 4915208 | tf_op jit(solution)/shard_map/ppermute | solution.py:402
  102.8 37.9 %collective-permute-start.13 = (bf16[640,1280]{1,0:T(8,128)(2,1)S(1)}, bf16[640,1280]{1,0:T(8,128)(2,1)S(1)}, u32[]{:S(2)}, u32[]{:S(2)}) collective-permute-start(bf16[640,1280]{1,0:T(8,128)(2,1)S(1)} %copy-done.10), channel_id=1, source_target_pairs={{0,16},{4,20},{8,24},{12,28},{16,0},{20,4},{24,8},{28,12},{1,17},{... | collective-permute-start | bytes 4915208 | tf_op jit(solution)/shard_map/ppermute | solution.py:402
  125.4 14.1 %collective-permute-start.18 = (bf16[128,640]{1,0:T(8,128)(2,1)S(1)}, bf16[128,640]{1,0:T(8,128)(2,1)S(1)}, u32[]{:S(2)}, u32[]{:S(2)}) collective-permute-start(bf16[128,640]{1,0:T(8,128)(2,1)S(1)} %add.19), channel_id=1, source_target_pairs={{0,1},{1,2},{2,3},{3,0},{4,5},{5,6},{6,7},{7,4},{8,9},{9,10},{10,1... | collective-permute-start | bytes 491528 | tf_op jit(solution)/shard_map/ppermute | solution.py:543
  128.1 11.4 %collective-permute-start.15 = (bf16[128,640]{1,0:T(8,128)(2,1)S(1)}, bf16[128,640]{1,0:T(8,128)(2,1)S(1)}, u32[]{:S(2)}, u32[]{:S(2)}) collective-permute-start(bf16[128,640]{1,0:T(8,128)(2,1)S(1)} %add.18), channel_id=1, source_target_pairs={{0,1},{1,2},{2,3},{3,0},{4,5},{5,6},{6,7},{7,4},{8,9},{9,10},{10,1... | collective-permute-start | bytes 491528 | tf_op jit(solution)/shard_map/ppermute | solution.py:543
  139.5 18.4 %collective-permute-start.24 = (bf16[640,1280]{1,0:T(8,128)(2,1)S(1)}, bf16[640,1280]{1,0:T(8,128)(2,1)S(1)}, u32[]{:S(2)}, u32[]{:S(2)}) collective-permute-start(bf16[640,1280]{1,0:T(8,128)(2,1)S(1)} %collective-permute-done.20.ref.refs_0_), channel_id=1, source_target_pairs={{0,4},{4,0},{8,12},{12,8},{16,20},{20,16},{24,28},{28,24},{1,5},{5... | collective-permute-start | bytes 4915208 | tf_op jit(solution)/shard_map/ppermute | solution.py:402
  140.7 18.5 %collective-permute-start.26 = (bf16[640,1280]{1,0:T(8,128)(2,1)S(1)}, bf16[640,1280]{1,0:T(8,128)(2,1)S(1)}, u32[]{:S(2)}, u32[]{:S(2)}) collective-permute-start(bf16[640,1280]{1,0:T(8,128)(2,1)S(1)} %collective-permute-done.13.ref.refs_0_), channel_id=1, source_target_pairs={{0,4},{4,0},{8,12},{12,8},{16,20},{20,16},{24,28},{28,24},{1,5},{5... | collective-permute-start | bytes 4915208 | tf_op jit(solution)/shard_map/ppermute | solution.py:402
  140.8 29.6 %collective-permute-start.19 = (bf16[384,1280]{1,0:T(8,128)(2,1)S(1)}, bf16[384,1280]{1,0:T(8,128)(2,1)S(1)}, u32[]{:S(2)}, u32[]{:S(2)}) collective-permute-start(bf16[384,1280]{1,0:T(8,128)(2,1)S(1)} %cut.10), channel_id=1, source_target_pairs={{0,8},{4,12},{8,0},{12,4},{16,24},{20,28},{24,16},{28,20},{1,9},{5... | collective-permute-start | bytes 2949128 | tf_op jit(solution)/shard_map/ppermute | solution.py:402
  144.5 25.9 %collective-permute-start.21 = (bf16[256,1280]{1,0:T(8,128)(2,1)S(1)}, bf16[256,1280]{1,0:T(8,128)(2,1)S(1)}, u32[]{:S(2)}, u32[]{:S(2)}) collective-permute-start(bf16[256,1280]{1,0:T(8,128)(2,1)S(1)} %cut.11), channel_id=1, source_target_pairs={{0,16},{4,20},{8,24},{12,28},{16,0},{20,4},{24,8},{28,12},{1,17},{... | collective-permute-start | bytes 1966088 | tf_op jit(solution)/shard_map/ppermute | solution.py:402
  158.0 12.4 %collective-permute-start.29 = (bf16[128,640]{1,0:T(8,128)(2,1)S(1)}, bf16[128,640]{1,0:T(8,128)(2,1)S(1)}, u32[]{:S(2)}, u32[]{:S(2)}) collective-permute-start(bf16[128,640]{1,0:T(8,128)(2,1)S(1)} %add.21), channel_id=1, source_target_pairs={{0,1},{1,2},{2,3},{3,0},{4,5},{5,6},{6,7},{7,4},{8,9},{9,10},{10,1... | collective-permute-start | bytes 491528 | tf_op jit(solution)/shard_map/ppermute | solution.py:543
  159.3 13.3 %collective-permute-start.25 = (bf16[128,640]{1,0:T(8,128)(2,1)S(1)}, bf16[128,640]{1,0:T(8,128)(2,1)S(1)}, u32[]{:S(2)}, u32[]{:S(2)}) collective-permute-start(bf16[128,640]{1,0:T(8,128)(2,1)S(1)} %get-tuple-element.73), channel_id=1, source_target_pairs={{0,1},{1,2},{2,3},{3,0},{4,5},{5,6},{6,7},{7,4},{8,9},{9,10},{10,1... | collective-permute-start | bytes 491528 | tf_op jit(solution)/shard_map/ppermute | solution.py:543
  174.9 30.4 %collective-permute-start.39 = (bf16[128,640]{1,0:T(8,128)(2,1)S(1)}, bf16[128,640]{1,0:T(8,128)(2,1)S(1)}, u32[]{:S(2)}, u32[]{:S(2)}) collective-permute-start(bf16[128,640]{1,0:T(8,128)(2,1)S(1)} %add.27), channel_id=1, source_target_pairs={{0,1},{1,2},{2,3},{3,0},{4,5},{5,6},{6,7},{7,4},{8,9},{9,10},{10,1... | collective-permute-start | bytes 491528 | tf_op jit(solution)/shard_map/ppermute | solution.py:543
  178.2 27.2 %collective-permute-start.38 = (bf16[128,640]{1,0:T(8,128)(2,1)S(1)}, bf16[128,640]{1,0:T(8,128)(2,1)S(1)}, u32[]{:S(2)}, u32[]{:S(2)}) collective-permute-start(bf16[128,640]{1,0:T(8,128)(2,1)S(1)} %add.26), channel_id=1, source_target_pairs={{0,1},{1,2},{2,3},{3,0},{4,5},{5,6},{6,7},{7,4},{8,9},{9,10},{10,1... | collective-permute-start | bytes 491528 | tf_op jit(solution)/shard_map/ppermute | solution.py:543
  178.4 16.3 %collective-permute-start.42 = (bf16[128,640]{1,0:T(8,128)(2,1)S(1)}, bf16[128,640]{1,0:T(8,128)(2,1)S(1)}, u32[]{:S(2)}, u32[]{:S(2)}) collective-permute-start(bf16[128,640]{1,0:T(8,128)(2,1)S(1)} %add.30), channel_id=1, source_target_pairs={{0,1},{1,2},{2,3},{3,0},{4,5},{5,6},{6,7},{7,4},{8,9},{9,10},{10,1... | collective-permute-start | bytes 491528 | tf_op jit(solution)/shard_map/ppermute | solution.py:543
  182.3 15.2 %collective-permute-start.35 = (bf16[128,512]{1,0:T(8,128)(2,1)S(1)}, bf16[128,512]{1,0:T(8,128)(2,1)S(1)}, u32[]{:S(2)}, u32[]{:S(2)}) collective-permute-start(bf16[128,512]{1,0:T(8,128)(2,1)S(1)} %get-tuple-element.82), channel_id=1, source_target_pairs={{0,1},{1,2},{2,3},{3,0},{4,5},{5,6},{6,7},{7,4},{8,9},{9,10},{10,1... | collective-permute-start | bytes 393224 | tf_op jit(solution)/shard_map/ppermute | solution.py:543
  187.7 14.0 %collective-permute-start.32 = (bf16[128,768]{1,0:T(8,128)(2,1)S(1)}, bf16[128,768]{1,0:T(8,128)(2,1)S(1)}, u32[]{:S(2)}, u32[]{:S(2)}) collective-permute-start(bf16[128,768]{1,0:T(8,128)(2,1)S(1)} %add.22), channel_id=1, source_target_pairs={{0,1},{1,2},{2,3},{3,0},{4,5},{5,6},{6,7},{7,4},{8,9},{9,10},{10,1... | collective-permute-start | bytes 589832 | tf_op jit(solution)/shard_map/ppermute | solution.py:543
  194.7 10.5 %collective-permute-start.44 = (bf16[128,640]{1,0:T(8,128)(2,1)S(1)}, bf16[128,640]{1,0:T(8,128)(2,1)S(1)}, u32[]{:S(2)}, u32[]{:S(2)}) collective-permute-start(bf16[128,640]{1,0:T(8,128)(2,1)S(1)} %add.32), channel_id=1, source_target_pairs={{0,1},{1,2},{2,3},{3,0},{4,5},{5,6},{6,7},{7,4},{8,9},{9,10},{10,1... | collective-permute-start | bytes 491528 | tf_op jit(solution)/shard_map/ppermute | solution.py:543
  197.5 14.1 %collective-permute-start.40 = (bf16[128,640]{1,0:T(8,128)(2,1)S(1)}, bf16[128,640]{1,0:T(8,128)(2,1)S(1)}, u32[]{:S(2)}, u32[]{:S(2)}) collective-permute-start(bf16[128,640]{1,0:T(8,128)(2,1)S(1)} %add.28), channel_id=1, source_target_pairs={{0,1},{1,2},{2,3},{3,0},{4,5},{5,6},{6,7},{7,4},{8,9},{9,10},{10,1... | collective-permute-start | bytes 491528 | tf_op jit(solution)/shard_map/ppermute | solution.py:543
  205.3 23.2 %collective-permute-start.33 = (bf16[128,768]{1,0:T(8,128)(2,1)S(1)}, bf16[128,768]{1,0:T(8,128)(2,1)S(1)}, u32[]{:S(2)}, u32[]{:S(2)}) collective-permute-start(bf16[128,768]{1,0:T(8,128)(2,1)S(1)} %add.23), channel_id=1, source_target_pairs={{0,1},{1,2},{2,3},{3,0},{4,5},{5,6},{6,7},{7,4},{8,9},{9,10},{10,1... | collective-permute-start | bytes 589832 | tf_op jit(solution)/shard_map/ppermute | solution.py:543
  205.3 14.0 %collective-permute-start.41 = (bf16[128,640]{1,0:T(8,128)(2,1)S(1)}, bf16[128,640]{1,0:T(8,128)(2,1)S(1)}, u32[]{:S(2)}, u32[]{:S(2)}) collective-permute-start(bf16[128,640]{1,0:T(8,128)(2,1)S(1)} %add.29), channel_id=1, source_target_pairs={{0,1},{1,2},{2,3},{3,0},{4,5},{5,6},{6,7},{7,4},{8,9},{9,10},{10,1... | collective-permute-start | bytes 491528 | tf_op jit(solution)/shard_map/ppermute | solution.py:543
  205.4 17.4 %collective-permute-start.43 = (bf16[128,640]{1,0:T(8,128)(2,1)S(1)}, bf16[128,640]{1,0:T(8,128)(2,1)S(1)}, u32[]{:S(2)}, u32[]{:S(2)}) collective-permute-start(bf16[128,640]{1,0:T(8,128)(2,1)S(1)} %add.31), channel_id=1, source_target_pairs={{0,1},{1,2},{2,3},{3,0},{4,5},{5,6},{6,7},{7,4},{8,9},{9,10},{10,1... | collective-permute-start | bytes 491528 | tf_op jit(solution)/shard_map/ppermute | solution.py:543
  211.6 14.7 %collective-permute-start.45 = (bf16[128,640]{1,0:T(8,128)(2,1)S(1)}, bf16[128,640]{1,0:T(8,128)(2,1)S(1)}, u32[]{:S(2)}, u32[]{:S(2)}) collective-permute-start(bf16[128,640]{1,0:T(8,128)(2,1)S(1)} %add.33), channel_id=1, source_target_pairs={{0,1},{1,2},{2,3},{3,0},{4,5},{5,6},{6,7},{7,4},{8,9},{9,10},{10,1... | collective-permute-start | bytes 491528 | tf_op jit(solution)/shard_map/ppermute | solution.py:543
  211.6 16.8 %collective-permute-start.37 = (bf16[128,512]{1,0:T(8,128)(2,1)S(1)}, bf16[128,512]{1,0:T(8,128)(2,1)S(1)}, u32[]{:S(2)}, u32[]{:S(2)}) collective-permute-start(bf16[128,512]{1,0:T(8,128)(2,1)S(1)} %add.25), channel_id=1, source_target_pairs={{0,1},{1,2},{2,3},{3,0},{4,5},{5,6},{6,7},{7,4},{8,9},{9,10},{10,1... | collective-permute-start | bytes 393224 | tf_op jit(solution)/shard_map/ppermute | solution.py:543
  (25 other events, 267.2 us)

commit v9 on v7

--- a/solution.py
+++ b/solution.py
@@ -12,6 +12,7 @@
 HALF = HEAD_SIZE // 2
 ROPE_BASE = 1000000.0
 LOG2E = 1.4426950408889634
+EXCHANGE = 11500000000
 NT = (((1,), (1,)), ((), ()))
 VMEM = pl.BlockSpec(memory_space=pltpu.VMEM)
 SMEM = pl.BlockSpec(memory_space=pltpu.SMEM)
@@ -33,7 +34,7 @@
 
 def link_time(array, share=2):
     size = share * int(np.prod(array.shape)) * array.dtype.itemsize
-    return pl.CostEstimate(flops=size * 11000, bytes_accessed=size, transcendentals=0)
+    return pl.CostEstimate(flops=size * 300, bytes_accessed=size, transcendentals=0)
 
 
 def normed_kernel(n_f, index_ref, tokens_ref, gain_ref, out_ref):
@@ -93,7 +94,7 @@
     out_ref[...] = ref[rows, columns]
 
 
-def part_of(array, cut, half, axis):
+def part_of(array, cut, half, axis, cost=0):
     bounds = [slice(0, size) for size in array.shape]
     bounds[axis] = slice(cut, array.shape[axis]) if half else slice(0, cut)
     return pl.pallas_call(
@@ -102,7 +103,7 @@
         out_specs=VMEM,
         out_shape=bf16(*[bound.stop - bound.start for bound in bounds]),
         compiler_params=params(16),
-        cost_estimate=work(0, array),
+        cost_estimate=work(cost, array),
         name="cut",
     )(array)
 
@@ -135,7 +136,7 @@
         out_ref[:, col : col + wide] = total
 
 
-def partial(blocks, pieces, wide):
+def partial(blocks, pieces, wide, declared):
     weights = [part for piece in pieces for part in piece]
     length = sum(block.shape[0] for block in blocks)
     depth = len(pieces) * weights[0].shape[0]
@@ -149,7 +150,7 @@
         out_shape=out,
         scratch_shapes=[pltpu.VMEM((length, depth), jnp.bfloat16)],
         compiler_params=params(16),
-        cost_estimate=work(2 * length * depth * columns, *blocks, *weights, out),
+        cost_estimate=work(2 * length * depth * columns if declared else 0),
         name="partial",
     )(*blocks, *weights)
 
@@ -229,7 +230,7 @@
             pltpu.VMEM((length, HEAD_SIZE), jnp.float32),
         ],
         compiler_params=params(16),
-        cost_estimate=work(4 * length * shard * columns, *weights, early, late),
+        cost_estimate=work(0),
         name="finish",
     )(index, *blocks, *weights, early, late, *biases, cos, sin)
 
@@ -299,7 +300,7 @@
             pltpu.VMEM((length, kv_half), jnp.bfloat16),
         ],
         compiler_params=params(16),
-        cost_estimate=work(4 * length * length * q_cols, queries, queries, kv),
+        cost_estimate=work(0),
         name="attend",
     )(index, queries, kv)
 
@@ -325,7 +326,7 @@
         out_specs=[VMEM] * blocks,
         out_shape=[bf16(length // blocks, columns)] * blocks,
         compiler_params=params(16),
-        cost_estimate=work(2 * length * columns * features, heads, *parts),
+        cost_estimate=work(0),
         name="mix",
     )(heads, *parts)
 
@@ -483,11 +484,14 @@
             behind = lax.ppermute(behind, "sp", left)
             offsets += [step, n_s - step]
         else:
-            ahead = lax.ppermute(part_of(ahead, count // 2, 0, 0), "sp", right)
-            behind = lax.ppermute(part_of(behind, count // 2, 1, 0), "sp", left)
+            ahead = lax.ppermute(halves[0], "sp", right)
+            behind = lax.ppermute(halves[1], "sp", left)
             offsets += [step]
         blocks += [ahead, behind]
         gate = [ahead, behind]
+        if step == steps - 1:
+            halves = [part_of(x, count // 2, i, 0, EXCHANGE) for i, x in enumerate(gate)]
+            gate = halves[1:]
         if step == 1:
             send_siblings(o_held, o_sibling, n_f, 0, *gate)
 
@@ -495,10 +499,10 @@
         return [side[r] for r in chosen for side in (held, sibling)]
 
     most = pieces_of(range(chips - 1))
-    early = partial(blocks[:-2], most, wide)
-    send_siblings(held, sibling, n_f, levels, *gate, early)
+    early = partial(blocks[:-2], most, wide, True)
+    send_siblings(held, sibling, n_f, levels, early)
     send_level(o_held, n_f, o_cut, 0, 1, early)
-    late = partial(blocks[-2:], most, wide)
+    late = partial(blocks[-2:], most, wide, False)
     mine, others = pieces_of([chips - 1])
     queries, kv = finish(
         index,
@@ -516,35 +520,60 @@
     )
     heads = attend(index, queries, kv, offsets)
 
-    rounds = []
-    for level in range(levels + 1):
-        if level:
-            send_siblings(o_held, o_sibling, n_f, level, *sent)
-            send_level(o_held, n_f, o_cut, 0, level + 1, *sent)
-        groups = []
-        for r in chips_away(level, chips):
-            halves = range(len(o_held[r]))
-            if len(halves) == 1:
-                groups += [((r, 0, 0),), ((r, 0, 1),)]
-            else:
-                groups += [((r, half, 0), (r, half, 1)) for half in halves]
-        groups.sort(key=lambda group: group[0][2])
+    sets = []
+
+    def start(level, groups):
         terms = []
         for group in groups:
             weights = [(o_sibling if core else o_held)[r][half] for r, half, core in group]
             mixed = mix(heads, weights, n_s)
             terms.append([mixed[offsets.index(d)] for d in range(n_s)])
-        totals, arrivals = [term[1] for term in terms], []
-        for d in range(2, n_s + 1):
-            arrivals.append([lax.ppermute(total, "sp", right) for total in totals])
-            if d < n_s:
-                totals = [add(a, term[d]) for a, term in zip(arrivals[-1], terms)]
         where = [
             [(2 * r + core, shard, half * o_cut, o_held[r][half].shape[0]) for r, half, core in group]
             for group in groups
         ]
-        rounds.append(([term[0] for term in terms], arrivals, where))
-        sent = arrivals[0][:1]
+        arrived = [lax.ppermute(term[1], "sp", right) for term in terms]
+        sets.append((terms, [arrived], where))
+
+    def advance(which, *before):
+        terms, arrivals, _ = which
+        d = len(arrivals) + 1
+        totals = [add(after(a, *before), term[d]) for a, term in zip(arrivals[-1], terms)]
+        arrivals.append([lax.ppermute(total, "sp", right) for total in totals])
+
+    def complete(which, *before):
+        while len(which[1]) < n_s - 1:
+            advance(which, *before)
+            before = ()
+
+    for level in range(levels + 1):
+        near = chips_away(level, chips)
+        if level == 1:
+            for r in near:
+                o_held[r] = [after(part, *sets[0][1][0]) for part in o_held[r]]
+        if level:
+            before = sets[-1][1][0] if level > 1 else []
+            send_siblings(o_held, o_sibling, n_f, level, *before)
+            send_level(o_held, n_f, o_cut, 0, level + 1, *before)
+        if level == 0:
+            plans = [[tuple((r, 0, core) for r in near for core in (0, 1))]]
+        elif level == 1:
+            plans = [[tuple((r, 0, core) for r in near)] for core in (0, 1)]
+        else:
+            plans = [[tuple((r, half, core) for r in near for half in (0, 1) for core in (0, 1))]]
+        for groups in plans:
+            start(level, groups)
+            current = sets[-1]
+            if len(sets) == 1:
+                advance(current, *current[1][0])
+            elif len(sets) == 2:
+                complete(sets[-2])
+                advance(current, *current[1][0], *sets[-2][1][-1])
+            else:
+                complete(sets[-2], *current[1][0])
+                advance(current, *current[1][0], *sets[-2][1][1])
+    complete(sets[-1])
+    rounds = [([term[0] for term in terms], arrivals, where) for terms, arrivals, where in sets]
 
     mixed = None
     for chosen in (rounds[:-1], rounds[-1:]):

time: 257 us -> 243 us (0.946)
  waiting for transfers between devices: 191 us -> 183 us
  starting transfers between devices: 31.2 us -> 27.9 us
    ppermute x18, waiting for transfers between devices: 26.4 us -> 81.7 us  [swapped(): return lax.ppermute(array, 'fsdp', [(i, i ^ mask) for i in range(n_f)])]
    ppermute x26 -> x14, waiting for transfers between devices: 108 us -> 70.7 us  [the longest x8 56.5 us: advance(): arrivals.append([lax.ppermute(total, 'sp', right) for total in totals])]
    ppermute x1, waiting for transfers between devices: 27.2 us -> 4.85 us  [body(): ahead = lax.ppermute(ahead, 'sp', right)]
    ppermute x18, starting transfers between devices: 13.2 us -> 9.53 us  [swapped(): return lax.ppermute(array, 'fsdp', [(i, i ^ mask) for i in range(n_f)])]
    ppermute x1, waiting for transfers between devices: 29.2 us -> 26 us  [body(): behind = lax.ppermute(behind, 'sp', left)]
    pallas_call x8 -> x4, Pallas kernels: 9.36 us -> 7.57 us  [mix(): pl.pallas_call(functools.partial(mix_kernel, len(parts)), in_specs=[VMEM]...]
    ppermute x26 -> x14, starting transfers between devices: 14.3 us -> 13.2 us  [the longest x8 5.9 us: advance(): arrivals.append([lax.ppermute(total, 'sp', right) for total in totals])]
  transfers between devices with their start and end apart: 46 -> 34, of which waited for: 26 -> 22; matrix products, arithmetic and copies ran while one was open for 0% -> 0% of each run, Pallas kernels for 11% -> 11%
where the time goes in v9:
time: 243 us
  waiting for transfers between devices  183 us (75%)
  Pallas kernels  29.4 us (12%)
  starting transfers between devices  27.9 us (11%)
    ppermute x18, waiting for transfers between devices, swapped(): return lax.ppermute(array, 'fsdp', [(i, i ^ mask) for i in range(n_f)])  81.7 us
    ppermute x8, waiting for transfers between devices, advance(): arrivals.append([lax.ppermute(total, 'sp', right) for total in totals])  56.5 us
    ppermute x1, waiting for transfers between devices, body(): behind = lax.ppermute(behind, 'sp', left)  26 us
    ppermute x4, waiting for transfers between devices, start(): arrived = [lax.ppermute(term[1], 'sp', right) for term in terms]  14.1 us
    ppermute x18, starting transfers between devices, swapped(): return lax.ppermute(array, 'fsdp', [(i, i ^ mask) for i in range(n_f)])  9.53 us
    pallas_call x2, Pallas kernels, partial(): pl.pallas_call(functools.partial(partial_kernel, len(blocks), counts, wid...  8.87 us
    pallas_call x4, Pallas kernels, mix(): pl.pallas_call(functools.partial(mix_kernel, len(parts)), in_specs=[VMEM]...  7.57 us
    ppermute x8, starting transfers between devices, advance(): arrivals.append([lax.ppermute(total, 'sp', right) for total in totals])  5.9 us
  transfers between devices with their start and end apart: 34, of which 22 were waited for; matrix products, arithmetic and copies ran while one was open for 0% of the time, Pallas kernels for 11%

profile of v9, /device:TPU:0, one launch (start us, length us, event | category | flops | bytes accessed | tf_op | source)
XLA Modules:
  0.0 243.2 jit_solution(7444469488879052364)
XLA Ops:
  3.5 5.1 %collective-permute-start.1 = (bf16[128,5120]{1,0:T(8,128)(2,1)S(1)}, bf16[128,5120]{1,0:T(8,128)(2,1)S(1)}, u32[]{:S(2)}, u32[]{:S(2)}) collective-permute-start(bf16[128,5120]{1,0:T(8,128)(2,1)S(1)} %norm.1.refs_0_), channel_id=1, source_target_pairs={{0,3},{1,0},{2,1},{3,2},{4,7},{5,4},{6,5},{7,6},{8,11},{9,8},{10,9... | collective-permute-start | bytes 3932168 | tf_op jit(solution)/shard_map/ppermute | solution.py:484
  11.8 26.0 %collective-permute-done.1.ref.refs_2_ = bf16[128,5120]{1,0:T(8,128)(2,1)S(1)} collective-permute-done((bf16[128,5120]{1,0:T(8,128)(2,1)S(1)}, bf16[128,5120]{1,0:T(8,128)(2,1)S(1)}, u32[]{:S(2)}, u32[]{:S(2)}) %collective-permute-start.1) | collective-permute-done | bytes 1310752 | tf_op jit(solution)/shard_map/ppermute | solution.py:484
  37.9 22.3 %collective-permute-done.6.ref.refs_5_.refs_4_ = bf16[640,1792]{1,0:T(8,128)(2,1)S(1)} collective-permute-done((bf16[640,1792]{1,0:T(8,128)(2,1)S(1)}, bf16[640,1792]{1,0:T(8,128)(2,1)S(1)}, u32[]{:S(2)}, u32[]{:S(2)}) %collective-permute-start.6) | collective-permute-done | bytes 2293792 | tf_op jit(solution)/shard_map/ppermute | solution.py:403
  62.0 4.9 %collective-permute-done.ref.refs_1_ = bf16[128,5120]{1,0:T(8,128)(2,1)S(1)} collective-permute-done((bf16[128,5120]{1,0:T(8,128)(2,1)S(1)}, bf16[128,5120]{1,0:T(8,128)(2,1)S(1)}, u32[]{:S(2)}, u32[]{:S(2)}) %collective-permute-start) | collective-permute-done | bytes 1310752 | tf_op jit(solution)/shard_map/ppermute | solution.py:483
  71.5 6.6 %partial.2.refs_9_ = f32[384,1792]{1,0:T(8,128)S(1)} custom-call(bf16[128,5120]{1,0:T(8,128)(2,1)S(1)} %norm.1.refs_0_, bf16[128,5120]{1,0:T(8,128)(2,1)S(1)} %collective-permute-done.ref.refs_1_, bf16[128,5120]{1,0:T(8,128)(2,1)S(1)} %collective-permute-done.1.ref.refs_2_, bf16[640,1792]{1,0:T(8,128)(2,1)S(1)} %pack.1.refs_3_.refs_2_, ...), custom_call_target="tpu_custom_call" | custom-call | flops 5284823040 | tf_op jit(solution)/shard_map/partial/pallas_call | solution.py:146
  78.1 10.2 %collective-permute-done.7.refs_7_ = bf16[640,768]{1,0:T(8,128)(2,1)S(1)} collective-permute-done((bf16[640,768]{1,0:T(8,128)(2,1)S(1)}, bf16[640,768]{1,0:T(8,128)(2,1)S(1)}, u32[]{:S(2)}, u32[]{:S(2)}) %collective-permute-start.7) | collective-permute-done | bytes 983072 | tf_op jit(solution)/shard_map/ppermute | solution.py:403
  88.3 8.3 %collective-permute-done.5.refs_5_ = bf16[640,1024]{1,0:T(8,128)(2,1)S(1)} collective-permute-done((bf16[640,1024]{1,0:T(8,128)(2,1)S(1)}, bf16[640,1024]{1,0:T(8,128)(2,1)S(1)}, u32[]{:S(2)}, u32[]{:S(2)}) %collective-permute-start.5) | collective-permute-done | bytes 1310752 | tf_op jit(solution)/shard_map/ppermute | solution.py:403
  98.5 2.3 partial.3.refs_10_
  101.2 3.7 %finish.1 = (bf16[512,1280]{1,0:T(8,128)(2,1)S(1)}, bf16[512,512]{1,0:T(8,128)(2,1)S(1)}) custom-call(s32[2]{0:T(128)S(1)} %pad_add_fusion.index_ref, bf16[128,5120]{1,0:T(8,128)(2,1)S(1)} %norm.1.refs_0_, bf16[128,5120]{1,0:T(8,128)(2,1)S(1)} %collective-permute-done.ref.refs_1_, bf16[128,5120]{1,0:T(8,128)(2,1)S(1)} %collective-permute-done.1.ref.refs_2_, ...), custom_call_target="tpu_custom_call" | custom-call | tf_op jit(solution)/shard_map/finish/pallas_call | solution.py:222
  104.9 4.0 %attend.1.heads_ref = bf16[512,1280]{1,0:T(8,128)(2,1)S(1)} custom-call(s32[2]{0:T(128)S(1)} %pad_add_fusion.index_ref, bf16[512,1280]{1,0:T(8,128)(2,1)S(1)} %get-tuple-element.50.q_ref, bf16[512,512]{1,0:T(8,128)(2,1)S(1)} %get-tuple-element.51.kv_ref), custom_call_target="tpu_custom_call" | custom-call | tf_op jit(solution)/shard_map/attend/pallas_call | solution.py:293
  108.8 1.9 mix.4
  110.7 1.9 collective-permute-start.15
  112.6 22.2 %collective-permute-done.17.ref.refs_0_ = bf16[640,1280]{1,0:T(8,128)(2,1)S(1)} collective-permute-done((bf16[640,1280]{1,0:T(8,128)(2,1)S(1)}, bf16[640,1280]{1,0:T(8,128)(2,1)S(1)}, u32[]{:S(2)}, u32[]{:S(2)}) %collective-permute-start.17) | collective-permute-done | bytes 1638432 | tf_op jit(solution)/shard_map/ppermute | solution.py:403
  138.3 2.3 collective-permute-done.20.refs_1_
  140.6 1.9 mix.5
  142.5 1.7 collective-permute-start.21
  144.3 3.0 %collective-permute-start.26 = (bf16[128,1280]{1,0:T(8,128)(2,1)S(1)}, bf16[128,1280]{1,0:T(8,128)(2,1)S(1)}, u32[]{:S(2)}, u32[]{:S(2)}) collective-permute-start(bf16[128,1280]{1,0:T(8,128)(2,1)S(1)} %add.10), channel_id=1, source_target_pairs={{0,1},{1,2},{2,3},{3,0},{4,5},{5,6},{6,7},{7,4},{8,9},{9,10},{10,1... | collective-permute-start | bytes 983048 | tf_op jit(solution)/shard_map/ppermute | solution.py:542
  147.3 6.4 %collective-permute-done.18.refs_2_ = bf16[256,1280]{1,0:T(8,128)(2,1)S(1)} collective-permute-done((bf16[256,1280]{1,0:T(8,128)(2,1)S(1)}, bf16[256,1280]{1,0:T(8,128)(2,1)S(1)}, u32[]{:S(2)}, u32[]{:S(2)}) %collective-permute-start.18) | collective-permute-done | bytes 655392 | tf_op jit(solution)/shard_map/ppermute | solution.py:403
  153.6 6.7 %collective-permute-done.16.refs_0_ = bf16[384,1280]{1,0:T(8,128)(2,1)S(1)} collective-permute-done((bf16[384,1280]{1,0:T(8,128)(2,1)S(1)}, bf16[384,1280]{1,0:T(8,128)(2,1)S(1)}, u32[]{:S(2)}, u32[]{:S(2)}) %collective-permute-start.16) | collective-permute-done | bytes 983072 | tf_op jit(solution)/shard_map/ppermute | solution.py:403
  160.3 1.9 mix.7
  162.2 1.7 collective-permute-start.25
  163.9 2.0 collective-permute-start.27
  165.9 9.1 %collective-permute-done.25.a_ref = bf16[128,1280]{1,0:T(8,128)(2,1)S(1)} collective-permute-done((bf16[128,1280]{1,0:T(8,128)(2,1)S(1)}, bf16[128,1280]{1,0:T(8,128)(2,1)S(1)}, u32[]{:S(2)}, u32[]{:S(2)}) %collective-permute-start.25) | collective-permute-done | bytes 327712 | tf_op jit(solution)/shard_map/ppermute | solution.py:535
  175.0 6.8 %collective-permute-done.27.refs_0_ = bf16[128,1280]{1,0:T(8,128)(2,1)S(1)} collective-permute-done((bf16[128,1280]{1,0:T(8,128)(2,1)S(1)}, bf16[128,1280]{1,0:T(8,128)(2,1)S(1)}, u32[]{:S(2)}, u32[]{:S(2)}) %collective-permute-start.27) | collective-permute-done | bytes 327712 | tf_op jit(solution)/shard_map/ppermute | solution.py:542
  182.0 11.3 %collective-permute-done.28.a_ref = bf16[128,1280]{1,0:T(8,128)(2,1)S(1)} collective-permute-done((bf16[128,1280]{1,0:T(8,128)(2,1)S(1)}, bf16[128,1280]{1,0:T(8,128)(2,1)S(1)}, u32[]{:S(2)}, u32[]{:S(2)}) %collective-permute-start.28) | collective-permute-done | bytes 327712 | tf_op jit(solution)/shard_map/ppermute | solution.py:542
  193.5 1.9 mix.6
  195.4 10.4 %collective-permute-done.29.a_ref = bf16[128,1280]{1,0:T(8,128)(2,1)S(1)} collective-permute-done((bf16[128,1280]{1,0:T(8,128)(2,1)S(1)}, bf16[128,1280]{1,0:T(8,128)(2,1)S(1)}, u32[]{:S(2)}, u32[]{:S(2)}) %collective-permute-start.29) | collective-permute-done | bytes 327712 | tf_op jit(solution)/shard_map/ppermute | solution.py:542
  205.9 5.1 %collective-permute-done.24.a_ref = bf16[128,1280]{1,0:T(8,128)(2,1)S(1)} collective-permute-done((bf16[128,1280]{1,0:T(8,128)(2,1)S(1)}, bf16[128,1280]{1,0:T(8,128)(2,1)S(1)}, u32[]{:S(2)}, u32[]{:S(2)}) %collective-permute-start.24) | collective-permute-done | bytes 327712 | tf_op jit(solution)/shard_map/ppermute | solution.py:535
  212.0 11.5 %collective-permute-done.30.a_ref = bf16[128,1280]{1,0:T(8,128)(2,1)S(1)} collective-permute-done((bf16[128,1280]{1,0:T(8,128)(2,1)S(1)}, bf16[128,1280]{1,0:T(8,128)(2,1)S(1)}, u32[]{:S(2)}, u32[]{:S(2)}) %collective-permute-start.30) | collective-permute-done | bytes 327712 | tf_op jit(solution)/shard_map/ppermute | solution.py:542
  223.7 6.9 %collective-permute-done.32.refs_1_ = bf16[128,1280]{1,0:T(8,128)(2,1)S(1)} collective-permute-done((bf16[128,1280]{1,0:T(8,128)(2,1)S(1)}, bf16[128,1280]{1,0:T(8,128)(2,1)S(1)}, u32[]{:S(2)}, u32[]{:S(2)}) %collective-permute-start.32) | collective-permute-done | bytes 327712 | tf_op jit(solution)/shard_map/ppermute | solution.py:542
  230.5 7.0 %collective-permute-done.33.refs_2_ = bf16[128,1280]{1,0:T(8,128)(2,1)S(1)} collective-permute-done((bf16[128,1280]{1,0:T(8,128)(2,1)S(1)}, bf16[128,1280]{1,0:T(8,128)(2,1)S(1)}, u32[]{:S(2)}, u32[]{:S(2)}) %collective-permute-start.33) | collective-permute-done | bytes 327712 | tf_op jit(solution)/shard_map/ppermute | solution.py:542
  239.2 2.5 %collective-permute-done.31.refs_0_ = bf16[128,1280]{1,0:T(8,128)(2,1)S(1)} collective-permute-done((bf16[128,1280]{1,0:T(8,128)(2,1)S(1)}, bf16[128,1280]{1,0:T(8,128)(2,1)S(1)}, u32[]{:S(2)}, u32[]{:S(2)}) %collective-permute-start.31) | collective-permute-done | bytes 327712 | tf_op jit(solution)/shard_map/ppermute | solution.py:542
  (85 shorter events, 23.6 us)
Async XLA Ops:
  3.5 34.3 %collective-permute-start.1 = (bf16[128,5120]{1,0:T(8,128)(2,1)S(1)}, bf16[128,5120]{1,0:T(8,128)(2,1)S(1)}, u32[]{:S(2)}, u32[]{:S(2)}) collective-permute-start(bf16[128,5120]{1,0:T(8,128)(2,1)S(1)} %norm.1.refs_0_), channel_id=1, source_target_pairs={{0,3},{1,0},{2,1},{3,2},{4,7},{5,4},{6,5},{7,6},{8,11},{9,8},{10,9... | collective-permute-start | bytes 3932168 | tf_op jit(solution)/shard_map/ppermute | solution.py:484
  8.7 51.4 %collective-permute-start.6 = (bf16[640,1792]{1,0:T(8,128)(2,1)S(1)}, bf16[640,1792]{1,0:T(8,128)(2,1)S(1)}, u32[]{:S(2)}, u32[]{:S(2)}) collective-permute-start(bf16[640,1792]{1,0:T(8,128)(2,1)S(1)} %pack.1.refs_3_.refs_2_), channel_id=1, source_target_pairs={{0,8},{4,12},{8,0},{12,4},{16,24},{20,28},{24,16},{28,20},{1,9},{5... | collective-permute-start | bytes 6881288 | tf_op jit(solution)/shard_map/ppermute | solution.py:403
  10.3 51.0 %collective-permute-start.4 = (bf16[640,1792]{1,0:T(8,128)(2,1)S(1)}, bf16[640,1792]{1,0:T(8,128)(2,1)S(1)}, u32[]{:S(2)}, u32[]{:S(2)}) collective-permute-start(bf16[640,1792]{1,0:T(8,128)(2,1)S(1)} %pack.1.refs_3_.refs_2_), channel_id=1, source_target_pairs={{0,16},{4,20},{8,24},{12,28},{16,0},{20,4},{24,8},{28,12},{1,17},{... | collective-permute-start | bytes 6881288 | tf_op jit(solution)/shard_map/ppermute | solution.py:403
  11.8 55.0 %collective-permute-start = (bf16[128,5120]{1,0:T(8,128)(2,1)S(1)}, bf16[128,5120]{1,0:T(8,128)(2,1)S(1)}, u32[]{:S(2)}, u32[]{:S(2)}) collective-permute-start(bf16[128,5120]{1,0:T(8,128)(2,1)S(1)} %norm.1.refs_0_), channel_id=1, source_target_pairs={{0,1},{1,2},{2,3},{3,0},{4,5},{5,6},{6,7},{7,4},{8,9},{9,10},{10,1... | collective-permute-start | bytes 3932168 | tf_op jit(solution)/shard_map/ppermute | solution.py:483
  11.8 56.5 %collective-permute-start.8 = (bf16[640,1792]{1,0:T(8,128)(2,1)S(1)}, bf16[640,1792]{1,0:T(8,128)(2,1)S(1)}, u32[]{:S(2)}, u32[]{:S(2)}) collective-permute-start(bf16[640,1792]{1,0:T(8,128)(2,1)S(1)} %pack.1.refs_3_.refs_2_), channel_id=1, source_target_pairs={{0,4},{4,0},{8,12},{12,8},{16,20},{20,16},{24,28},{28,24},{1,5},{5... | collective-permute-start | bytes 6881288 | tf_op jit(solution)/shard_map/ppermute | solution.py:403
  60.1 9.8 %collective-permute-start.9 = (bf16[640,1792]{1,0:T(8,128)(2,1)S(1)}, bf16[640,1792]{1,0:T(8,128)(2,1)S(1)}, u32[]{:S(2)}, u32[]{:S(2)}) collective-permute-start(bf16[640,1792]{1,0:T(8,128)(2,1)S(1)} %collective-permute-done.6.ref.refs_5_.refs_4_), channel_id=1, source_target_pairs={{0,4},{4,0},{8,12},{12,8},{16,20},{20,16},{24,28},{28,24},{1,5},{5... | collective-permute-start | bytes 6881288 | tf_op jit(solution)/shard_map/ppermute | solution.py:403
  61.3 10.1 %collective-permute-start.10 = (bf16[640,1792]{1,0:T(8,128)(2,1)S(1)}, bf16[640,1792]{1,0:T(8,128)(2,1)S(1)}, u32[]{:S(2)}, u32[]{:S(2)}) collective-permute-start(bf16[640,1792]{1,0:T(8,128)(2,1)S(1)} %collective-permute-done.4.ref.refs_7_.refs_6_), channel_id=1, source_target_pairs={{0,4},{4,0},{8,12},{12,8},{16,20},{20,16},{24,28},{28,24},{1,5},{5... | collective-permute-start | bytes 6881288 | tf_op jit(solution)/shard_map/ppermute | solution.py:403
  61.3 36.7 %collective-permute-start.3 = (bf16[64,5120]{1,0:T(8,128)(2,1)S(1)}, bf16[64,5120]{1,0:T(8,128)(2,1)S(1)}, u32[]{:S(2)}, u32[]{:S(2)}) collective-permute-start(bf16[64,5120]{1,0:T(8,128)(2,1)S(1)} %cut.7), channel_id=1, source_target_pairs={{0,3},{1,0},{2,1},{3,2},{4,7},{5,4},{6,5},{7,6},{8,11},{9,8},{10,9... | collective-permute-start | bytes 1966088 | tf_op jit(solution)/shard_map/ppermute | solution.py:488
  66.8 21.5 %collective-permute-start.7 = (bf16[640,768]{1,0:T(8,128)(2,1)S(1)}, bf16[640,768]{1,0:T(8,128)(2,1)S(1)}, u32[]{:S(2)}, u32[]{:S(2)}) collective-permute-start(bf16[640,768]{1,0:T(8,128)(2,1)S(1)} %cut.9), channel_id=1, source_target_pairs={{0,16},{4,20},{8,24},{12,28},{16,0},{20,4},{24,8},{28,12},{1,17},{... | collective-permute-start | bytes 2949128 | tf_op jit(solution)/shard_map/ppermute | solution.py:403
  68.3 28.2 %collective-permute-start.5 = (bf16[640,1024]{1,0:T(8,128)(2,1)S(1)}, bf16[640,1024]{1,0:T(8,128)(2,1)S(1)}, u32[]{:S(2)}, u32[]{:S(2)}) collective-permute-start(bf16[640,1024]{1,0:T(8,128)(2,1)S(1)} %cut.8), channel_id=1, source_target_pairs={{0,8},{4,12},{8,0},{12,4},{16,24},{20,28},{24,16},{28,20},{1,9},{5... | collective-permute-start | bytes 3932168 | tf_op jit(solution)/shard_map/ppermute | solution.py:403
  69.9 28.7 %collective-permute-start.2 = (bf16[64,5120]{1,0:T(8,128)(2,1)S(1)}, bf16[64,5120]{1,0:T(8,128)(2,1)S(1)}, u32[]{:S(2)}, u32[]{:S(2)}) collective-permute-start(bf16[64,5120]{1,0:T(8,128)(2,1)S(1)} %cut.6), channel_id=1, source_target_pairs={{0,1},{1,2},{2,3},{3,0},{4,5},{5,6},{6,7},{7,4},{8,9},{9,10},{10,1... | collective-permute-start | bytes 1966088 | tf_op jit(solution)/shard_map/ppermute | solution.py:487
  71.5 37.4 %collective-permute-start.14 = (bf16[640,1280]{1,0:T(8,128)(2,1)S(1)}, bf16[640,1280]{1,0:T(8,128)(2,1)S(1)}, u32[]{:S(2)}, u32[]{:S(2)}) collective-permute-start(bf16[640,1280]{1,0:T(8,128)(2,1)S(1)} %copy-done.1), channel_id=1, source_target_pairs={{0,4},{4,0},{8,12},{12,8},{16,20},{20,16},{24,28},{28,24},{1,5},{5... | collective-permute-start | bytes 4915208 | tf_op jit(solution)/shard_map/ppermute | solution.py:403
  96.5 4.6 %collective-permute-start.11 = (bf16[640,1024]{1,0:T(8,128)(2,1)S(1)}, bf16[640,1024]{1,0:T(8,128)(2,1)S(1)}, u32[]{:S(2)}, u32[]{:S(2)}) collective-permute-start(bf16[640,1024]{1,0:T(8,128)(2,1)S(1)} %collective-permute-done.5.refs_5_), channel_id=1, source_target_pairs={{0,4},{4,0},{8,12},{12,8},{16,20},{20,16},{24,28},{28,24},{1,5},{5... | collective-permute-start | bytes 3932168 | tf_op jit(solution)/shard_map/ppermute | solution.py:403
  96.5 38.2 %collective-permute-start.17 = (bf16[640,1280]{1,0:T(8,128)(2,1)S(1)}, bf16[640,1280]{1,0:T(8,128)(2,1)S(1)}, u32[]{:S(2)}, u32[]{:S(2)}) collective-permute-start(bf16[640,1280]{1,0:T(8,128)(2,1)S(1)} %copy-done.1), channel_id=1, source_target_pairs={{0,8},{4,12},{8,0},{12,4},{16,24},{20,28},{24,16},{28,20},{1,9},{5... | collective-permute-start | bytes 4915208 | tf_op jit(solution)/shard_map/ppermute | solution.py:403
  98.0 37.9 %collective-permute-start.13 = (bf16[640,1280]{1,0:T(8,128)(2,1)S(1)}, bf16[640,1280]{1,0:T(8,128)(2,1)S(1)}, u32[]{:S(2)}, u32[]{:S(2)}) collective-permute-start(bf16[640,1280]{1,0:T(8,128)(2,1)S(1)} %copy-done.1), channel_id=1, source_target_pairs={{0,16},{4,20},{8,24},{12,28},{16,0},{20,4},{24,8},{28,12},{1,17},{... | collective-permute-start | bytes 4915208 | tf_op jit(solution)/shard_map/ppermute | solution.py:403
  110.7 24.0 %collective-permute-start.15 = (bf16[128,1280]{1,0:T(8,128)(2,1)S(1)}, bf16[128,1280]{1,0:T(8,128)(2,1)S(1)}, u32[]{:S(2)}, u32[]{:S(2)}) collective-permute-start(bf16[128,1280]{1,0:T(8,128)(2,1)S(1)} %get-tuple-element.55), channel_id=1, source_target_pairs={{0,1},{1,2},{2,3},{3,0},{4,5},{5,6},{6,7},{7,4},{8,9},{9,10},{10,1... | collective-permute-start | bytes 983048 | tf_op jit(solution)/shard_map/ppermute | solution.py:535
  136.0 4.6 %collective-permute-start.20 = (bf16[640,1280]{1,0:T(8,128)(2,1)S(1)}, bf16[640,1280]{1,0:T(8,128)(2,1)S(1)}, u32[]{:S(2)}, u32[]{:S(2)}) collective-permute-start(bf16[640,1280]{1,0:T(8,128)(2,1)S(1)} %collective-permute-done.13.ref.refs_1_), channel_id=1, source_target_pairs={{0,4},{4,0},{8,12},{12,8},{16,20},{20,16},{24,28},{28,24},{1,5},{5... | collective-permute-start | bytes 4915208 | tf_op jit(solution)/shard_map/ppermute | solution.py:403
  136.0 24.2 %collective-permute-start.16 = (bf16[384,1280]{1,0:T(8,128)(2,1)S(1)}, bf16[384,1280]{1,0:T(8,128)(2,1)S(1)}, u32[]{:S(2)}, u32[]{:S(2)}) collective-permute-start(bf16[384,1280]{1,0:T(8,128)(2,1)S(1)} %cut.10), channel_id=1, source_target_pairs={{0,8},{4,12},{8,0},{12,4},{16,24},{20,28},{24,16},{28,20},{1,9},{5... | collective-permute-start | bytes 2949128 | tf_op jit(solution)/shard_map/ppermute | solution.py:403
  136.9 16.7 %collective-permute-start.18 = (bf16[256,1280]{1,0:T(8,128)(2,1)S(1)}, bf16[256,1280]{1,0:T(8,128)(2,1)S(1)}, u32[]{:S(2)}, u32[]{:S(2)}) collective-permute-start(bf16[256,1280]{1,0:T(8,128)(2,1)S(1)} %cut.11), channel_id=1, source_target_pairs={{0,16},{4,20},{8,24},{12,28},{16,0},{20,4},{24,8},{28,12},{1,17},{... | collective-permute-start | bytes 1966088 | tf_op jit(solution)/shard_map/ppermute | solution.py:403
  142.5 17.8 %collective-permute-start.21 = (bf16[128,1280]{1,0:T(8,128)(2,1)S(1)}, bf16[128,1280]{1,0:T(8,128)(2,1)S(1)}, u32[]{:S(2)}, u32[]{:S(2)}) collective-permute-start(bf16[128,1280]{1,0:T(8,128)(2,1)S(1)} %get-tuple-element.58), channel_id=1, source_target_pairs={{0,1},{1,2},{2,3},{3,0},{4,5},{5,6},{6,7},{7,4},{8,9},{9,10},{10,1... | collective-permute-start | bytes 983048 | tf_op jit(solution)/shard_map/ppermute | solution.py:535
  144.3 19.6 %collective-permute-start.26 = (bf16[128,1280]{1,0:T(8,128)(2,1)S(1)}, bf16[128,1280]{1,0:T(8,128)(2,1)S(1)}, u32[]{:S(2)}, u32[]{:S(2)}) collective-permute-start(bf16[128,1280]{1,0:T(8,128)(2,1)S(1)} %add.10), channel_id=1, source_target_pairs={{0,1},{1,2},{2,3},{3,0},{4,5},{5,6},{6,7},{7,4},{8,9},{9,10},{10,1... | collective-permute-start | bytes 983048 | tf_op jit(solution)/shard_map/ppermute | solution.py:542
  160.3 33.2 %collective-permute-start.22 = (bf16[384,1280]{1,0:T(8,128)(2,1)S(1)}, bf16[384,1280]{1,0:T(8,128)(2,1)S(1)}, u32[]{:S(2)}, u32[]{:S(2)}) collective-permute-start(bf16[384,1280]{1,0:T(8,128)(2,1)S(1)} %collective-permute-done.16.refs_0_), channel_id=1, source_target_pairs={{0,4},{4,0},{8,12},{12,8},{16,20},{20,16},{24,28},{28,24},{1,5},{5... | collective-permute-start | bytes 2949128 | tf_op jit(solution)/shard_map/ppermute | solution.py:403
  162.2 12.8 %collective-permute-start.25 = (bf16[128,1280]{1,0:T(8,128)(2,1)S(1)}, bf16[128,1280]{1,0:T(8,128)(2,1)S(1)}, u32[]{:S(2)}, u32[]{:S(2)}) collective-permute-start(bf16[128,1280]{1,0:T(8,128)(2,1)S(1)} %get-tuple-element.62), channel_id=1, source_target_pairs={{0,1},{1,2},{2,3},{3,0},{4,5},{5,6},{6,7},{7,4},{8,9},{9,10},{10,1... | collective-permute-start | bytes 983048 | tf_op jit(solution)/shard_map/ppermute | solution.py:535
  163.9 17.9 %collective-permute-start.27 = (bf16[128,1280]{1,0:T(8,128)(2,1)S(1)}, bf16[128,1280]{1,0:T(8,128)(2,1)S(1)}, u32[]{:S(2)}, u32[]{:S(2)}) collective-permute-start(bf16[128,1280]{1,0:T(8,128)(2,1)S(1)} %add.11), channel_id=1, source_target_pairs={{0,1},{1,2},{2,3},{3,0},{4,5},{5,6},{6,7},{7,4},{8,9},{9,10},{10,1... | collective-permute-start | bytes 983048 | tf_op jit(solution)/shard_map/ppermute | solution.py:542
  165.9 27.5 %collective-permute-start.23 = (bf16[256,1280]{1,0:T(8,128)(2,1)S(1)}, bf16[256,1280]{1,0:T(8,128)(2,1)S(1)}, u32[]{:S(2)}, u32[]{:S(2)}) collective-permute-start(bf16[256,1280]{1,0:T(8,128)(2,1)S(1)} %collective-permute-done.18.refs_2_), channel_id=1, source_target_pairs={{0,4},{4,0},{8,12},{12,8},{16,20},{20,16},{24,28},{28,24},{1,5},{5... | collective-permute-start | bytes 1966088 | tf_op jit(solution)/shard_map/ppermute | solution.py:403
  181.9 11.4 %collective-permute-start.28 = (bf16[128,1280]{1,0:T(8,128)(2,1)S(1)}, bf16[128,1280]{1,0:T(8,128)(2,1)S(1)}, u32[]{:S(2)}, u32[]{:S(2)}) collective-permute-start(bf16[128,1280]{1,0:T(8,128)(2,1)S(1)} %add.12), channel_id=1, source_target_pairs={{0,1},{1,2},{2,3},{3,0},{4,5},{5,6},{6,7},{7,4},{8,9},{9,10},{10,1... | collective-permute-start | bytes 983048 | tf_op jit(solution)/shard_map/ppermute | solution.py:542
  193.4 12.5 %collective-permute-start.29 = (bf16[128,1280]{1,0:T(8,128)(2,1)S(1)}, bf16[128,1280]{1,0:T(8,128)(2,1)S(1)}, u32[]{:S(2)}, u32[]{:S(2)}) collective-permute-start(bf16[128,1280]{1,0:T(8,128)(2,1)S(1)} %add.13), channel_id=1, source_target_pairs={{0,1},{1,2},{2,3},{3,0},{4,5},{5,6},{6,7},{7,4},{8,9},{9,10},{10,1... | collective-permute-start | bytes 983048 | tf_op jit(solution)/shard_map/ppermute | solution.py:542
  195.4 15.6 %collective-permute-start.24 = (bf16[128,1280]{1,0:T(8,128)(2,1)S(1)}, bf16[128,1280]{1,0:T(8,128)(2,1)S(1)}, u32[]{:S(2)}, u32[]{:S(2)}) collective-permute-start(bf16[128,1280]{1,0:T(8,128)(2,1)S(1)} %get-tuple-element.61), channel_id=1, source_target_pairs={{0,1},{1,2},{2,3},{3,0},{4,5},{5,6},{6,7},{7,4},{8,9},{9,10},{10,1... | collective-permute-start | bytes 983048 | tf_op jit(solution)/shard_map/ppermute | solution.py:535
  211.0 12.5 %collective-permute-start.30 = (bf16[128,1280]{1,0:T(8,128)(2,1)S(1)}, bf16[128,1280]{1,0:T(8,128)(2,1)S(1)}, u32[]{:S(2)}, u32[]{:S(2)}) collective-permute-start(bf16[128,1280]{1,0:T(8,128)(2,1)S(1)} %add.14), channel_id=1, source_target_pairs={{0,1},{1,2},{2,3},{3,0},{4,5},{5,6},{6,7},{7,4},{8,9},{9,10},{10,1... | collective-permute-start | bytes 983048 | tf_op jit(solution)/shard_map/ppermute | solution.py:542
  211.2 19.4 %collective-permute-start.32 = (bf16[128,1280]{1,0:T(8,128)(2,1)S(1)}, bf16[128,1280]{1,0:T(8,128)(2,1)S(1)}, u32[]{:S(2)}, u32[]{:S(2)}) collective-permute-start(bf16[128,1280]{1,0:T(8,128)(2,1)S(1)} %add.16), channel_id=1, source_target_pairs={{0,1},{1,2},{2,3},{3,0},{4,5},{5,6},{6,7},{7,4},{8,9},{9,10},{10,1... | collective-permute-start | bytes 983048 | tf_op jit(solution)/shard_map/ppermute | solution.py:542
  211.3 26.2 %collective-permute-start.33 = (bf16[128,1280]{1,0:T(8,128)(2,1)S(1)}, bf16[128,1280]{1,0:T(8,128)(2,1)S(1)}, u32[]{:S(2)}, u32[]{:S(2)}) collective-permute-start(bf16[128,1280]{1,0:T(8,128)(2,1)S(1)} %add.17), channel_id=1, source_target_pairs={{0,1},{1,2},{2,3},{3,0},{4,5},{5,6},{6,7},{7,4},{8,9},{9,10},{10,1... | collective-permute-start | bytes 983048 | tf_op jit(solution)/shard_map/ppermute | solution.py:542
  223.6 18.1 %collective-permute-start.31 = (bf16[128,1280]{1,0:T(8,128)(2,1)S(1)}, bf16[128,1280]{1,0:T(8,128)(2,1)S(1)}, u32[]{:S(2)}, u32[]{:S(2)}) collective-permute-start(bf16[128,1280]{1,0:T(8,128)(2,1)S(1)} %add.15), channel_id=1, source_target_pairs={{0,1},{1,2},{2,3},{3,0},{4,5},{5,6},{6,7},{7,4},{8,9},{9,10},{10,1... | collective-permute-start | bytes 983048 | tf_op jit(solution)/shard_map/ppermute | solution.py:542
  (13 other events, 154.4 us)

commit v10 on v7

--- a/solution.py
+++ b/solution.py
@@ -12,6 +12,7 @@
 HALF = HEAD_SIZE // 2
 ROPE_BASE = 1000000.0
 LOG2E = 1.4426950408889634
+EXCHANGE = 11500000000
 NT = (((1,), (1,)), ((), ()))
 VMEM = pl.BlockSpec(memory_space=pltpu.VMEM)
 SMEM = pl.BlockSpec(memory_space=pltpu.SMEM)
@@ -29,11 +30,6 @@
 def work(flops, *arrays):
     size = sum(int(np.prod(x.shape)) * x.dtype.itemsize for x in arrays)
     return pl.CostEstimate(flops=flops, bytes_accessed=size, transcendentals=0)
-
-
-def link_time(array, share=2):
-    size = share * int(np.prod(array.shape)) * array.dtype.itemsize
-    return pl.CostEstimate(flops=size * 11000, bytes_accessed=size, transcendentals=0)
 
 
 def normed_kernel(n_f, index_ref, tokens_ref, gain_ref, out_ref):
@@ -93,7 +89,7 @@
     out_ref[...] = ref[rows, columns]
 
 
-def part_of(array, cut, half, axis):
+def part_of(array, cut, half, axis, cost=0):
     bounds = [slice(0, size) for size in array.shape]
     bounds[axis] = slice(cut, array.shape[axis]) if half else slice(0, cut)
     return pl.pallas_call(
@@ -102,7 +98,7 @@
         out_specs=VMEM,
         out_shape=bf16(*[bound.stop - bound.start for bound in bounds]),
         compiler_params=params(16),
-        cost_estimate=work(0, array),
+        cost_estimate=work(cost, array),
         name="cut",
     )(array)
 
@@ -135,7 +131,7 @@
         out_ref[:, col : col + wide] = total
 
 
-def partial(blocks, pieces, wide):
+def partial(blocks, pieces, wide, declared):
     weights = [part for piece in pieces for part in piece]
     length = sum(block.shape[0] for block in blocks)
     depth = len(pieces) * weights[0].shape[0]
@@ -149,7 +145,7 @@
         out_shape=out,
         scratch_shapes=[pltpu.VMEM((length, depth), jnp.bfloat16)],
         compiler_params=params(16),
-        cost_estimate=work(2 * length * depth * columns, *blocks, *weights, out),
+        cost_estimate=work(2 * length * depth * columns if declared else 0),
         name="partial",
     )(*blocks, *weights)
 
@@ -229,7 +225,7 @@
             pltpu.VMEM((length, HEAD_SIZE), jnp.float32),
         ],
         compiler_params=params(16),
-        cost_estimate=work(4 * length * shard * columns, *weights, early, late),
+        cost_estimate=work(0),
         name="finish",
     )(index, *blocks, *weights, early, late, *biases, cos, sin)
 
@@ -299,7 +295,7 @@
             pltpu.VMEM((length, kv_half), jnp.bfloat16),
         ],
         compiler_params=params(16),
-        cost_estimate=work(4 * length * length * q_cols, queries, queries, kv),
+        cost_estimate=work(0),
         name="attend",
     )(index, queries, kv)
 
@@ -342,7 +338,7 @@
         out_specs=VMEM,
         out_shape=bf16(*a.shape),
         compiler_params=params(8),
-        cost_estimate=link_time(a),
+        cost_estimate=work(0, a, a, a),
         name="add",
     )(a, b)
 
@@ -483,11 +479,14 @@
             behind = lax.ppermute(behind, "sp", left)
             offsets += [step, n_s - step]
         else:
-            ahead = lax.ppermute(part_of(ahead, count // 2, 0, 0), "sp", right)
-            behind = lax.ppermute(part_of(behind, count // 2, 1, 0), "sp", left)
+            ahead = lax.ppermute(halves[0], "sp", right)
+            behind = lax.ppermute(halves[1], "sp", left)
             offsets += [step]
         blocks += [ahead, behind]
         gate = [ahead, behind]
+        if step == steps - 1:
+            halves = [part_of(x, count // 2, i, 0, EXCHANGE) for i, x in enumerate(gate)]
+            gate = halves[1:]
         if step == 1:
             send_siblings(o_held, o_sibling, n_f, 0, *gate)
 
@@ -495,10 +494,10 @@
         return [side[r] for r in chosen for side in (held, sibling)]
 
     most = pieces_of(range(chips - 1))
-    early = partial(blocks[:-2], most, wide)
-    send_siblings(held, sibling, n_f, levels, *gate, early)
+    early = partial(blocks[:-2], most, wide, True)
+    send_siblings(held, sibling, n_f, levels, early)
     send_level(o_held, n_f, o_cut, 0, 1, early)
-    late = partial(blocks[-2:], most, wide)
+    late = partial(blocks[-2:], most, wide, False)
     mine, others = pieces_of([chips - 1])
     queries, kv = finish(
         index,
@@ -516,35 +515,34 @@
     )
     heads = attend(index, queries, kv, offsets)
 
-    rounds = []
+    gate, behind, rounds = [], [], []
     for level in range(levels + 1):
+        near = chips_away(level, chips)
         if level:
-            send_siblings(o_held, o_sibling, n_f, level, *sent)
-            send_level(o_held, n_f, o_cut, 0, level + 1, *sent)
-        groups = []
-        for r in chips_away(level, chips):
-            halves = range(len(o_held[r]))
-            if len(halves) == 1:
-                groups += [((r, 0, 0),), ((r, 0, 1),)]
-            else:
-                groups += [((r, half, 0), (r, half, 1)) for half in halves]
-        groups.sort(key=lambda group: group[0][2])
+            send_siblings(o_held, o_sibling, n_f, level, *gate)
+            send_level(o_held, n_f, o_cut, 0, level + 1, *gate)
+        if level < 2:
+            groups = [((r, 0, core),) for core in (0, 1) for r in near]
+        else:
+            groups = [((r, half, 0), (r, half, 1)) for r in near for half in (0, 1)]
         terms = []
         for group in groups:
             weights = [(o_sibling if core else o_held)[r][half] for r, half, core in group]
-            mixed = mix(heads, weights, n_s)
+            mixed = mix(after(heads, *gate), weights, n_s)
             terms.append([mixed[offsets.index(d)] for d in range(n_s)])
         totals, arrivals = [term[1] for term in terms], []
         for d in range(2, n_s + 1):
             arrivals.append([lax.ppermute(total, "sp", right) for total in totals])
+            others = behind if d == n_s - 1 else []
             if d < n_s:
-                totals = [add(a, term[d]) for a, term in zip(arrivals[-1], terms)]
+                totals = [add(after(a, *others), term[d]) for a, term in zip(arrivals[-1], terms)]
         where = [
             [(2 * r + core, shard, half * o_cut, o_held[r][half].shape[0]) for r, half, core in group]
             for group in groups
         ]
         rounds.append(([term[0] for term in terms], arrivals, where))
-        sent = arrivals[0][:1]
+        gate = arrivals[-1] if level == 0 else arrivals[0] + arrivals[min(1, n_s - 2)][:2]
+        behind = arrivals[-1][:2] if level else []
 
     mixed = None
     for chosen in (rounds[:-1], rounds[-1:]):

time: 257 us -> 226 us (0.88)
  waiting for transfers between devices: 191 us -> 164 us
  starting transfers between devices: 31.2 us -> 27.3 us
    ppermute x1, waiting for transfers between devices: 27.2 us -> 2.53 us  [body(): ahead = lax.ppermute(ahead, 'sp', right)]
    ppermute x18, waiting for transfers between devices: 26.4 us -> 44.7 us  [swapped(): return lax.ppermute(array, 'fsdp', [(i, i ^ mask) for i in range(n_f)])]
    ppermute x2, waiting for transfers between devices: 18.2 us -> 2.45 us  [the longest x1 2.45 us: body(): ahead = lax.ppermute(halves[0], 'sp', right)]
    ppermute x24, starting transfers between devices: 10.9 us -> 7.06 us  [body(): arrivals.append([lax.ppermute(total, 'sp', right) for total in totals])]
    ppermute x1, waiting for transfers between devices: 29.2 us -> 26 us  [body(): behind = lax.ppermute(behind, 'sp', left)]
  transfers between devices with their start and end apart: 46 -> 46, of which waited for: 26 -> 31; matrix products, arithmetic and copies ran while one was open for 0% -> 0% of each run, Pallas kernels for 11% -> 13%
where the time goes in v10:
time: 226 us
  waiting for transfers between devices  164 us (73%)
  Pallas kernels  31.2 us (14%)
  starting transfers between devices  27.3 us (12%)
    ppermute x24, waiting for transfers between devices, body(): arrivals.append([lax.ppermute(total, 'sp', right) for total in totals])  88.5 us
    ppermute x18, waiting for transfers between devices, swapped(): return lax.ppermute(array, 'fsdp', [(i, i ^ mask) for i in range(n_f)])  44.7 us
    ppermute x1, waiting for transfers between devices, body(): behind = lax.ppermute(behind, 'sp', left)  26 us
    ppermute x18, starting transfers between devices, swapped(): return lax.ppermute(array, 'fsdp', [(i, i ^ mask) for i in range(n_f)])  11.6 us
    pallas_call x8, Pallas kernels, mix(): pl.pallas_call(functools.partial(mix_kernel, len(parts)), in_specs=[VMEM]...  9.37 us
    pallas_call x2, Pallas kernels, partial(): pl.pallas_call(functools.partial(partial_kernel, len(blocks), counts, wid...  8.88 us
    ppermute x24, starting transfers between devices, body(): arrivals.append([lax.ppermute(total, 'sp', right) for total in totals])  7.06 us
    ppermute x1, starting transfers between devices, body(): behind = lax.ppermute(behind, 'sp', left)  5.1 us
  transfers between devices with their start and end apart: 46, of which 31 were waited for; matrix products, arithmetic and copies ran while one was open for 0% of the time, Pallas kernels for 13%

profile of v10, /device:TPU:0, one launch (start us, length us, event | category | flops | bytes accessed | tf_op | source)
XLA Modules:
  0.0 225.7 jit_solution(17285667464804957424)
XLA Ops:
  3.5 5.1 %collective-permute-start.1 = (bf16[128,5120]{1,0:T(8,128)(2,1)S(1)}, bf16[128,5120]{1,0:T(8,128)(2,1)S(1)}, u32[]{:S(2)}, u32[]{:S(2)}) collective-permute-start(bf16[128,5120]{1,0:T(8,128)(2,1)S(1)} %norm.1.refs_0_), channel_id=1, source_target_pairs={{0,3},{1,0},{2,1},{3,2},{4,7},{5,4},{6,5},{7,6},{8,11},{9,8},{10,9... | collective-permute-start | bytes 3932168 | tf_op jit(solution)/shard_map/ppermute | solution.py:479
  11.8 26.0 %collective-permute-done.1.ref.refs_2_ = bf16[128,5120]{1,0:T(8,128)(2,1)S(1)} collective-permute-done((bf16[128,5120]{1,0:T(8,128)(2,1)S(1)}, bf16[128,5120]{1,0:T(8,128)(2,1)S(1)}, u32[]{:S(2)}, u32[]{:S(2)}) %collective-permute-start.1) | collective-permute-done | bytes 1310752 | tf_op jit(solution)/shard_map/ppermute | solution.py:479
  37.9 22.3 %collective-permute-done.6.ref.refs_5_.refs_4_ = bf16[640,1792]{1,0:T(8,128)(2,1)S(1)} collective-permute-done((bf16[640,1792]{1,0:T(8,128)(2,1)S(1)}, bf16[640,1792]{1,0:T(8,128)(2,1)S(1)}, u32[]{:S(2)}, u32[]{:S(2)}) %collective-permute-start.6) | collective-permute-done | bytes 2293792 | tf_op jit(solution)/shard_map/ppermute | solution.py:398
  63.1 2.5 %collective-permute-done.ref.refs_1_ = bf16[128,5120]{1,0:T(8,128)(2,1)S(1)} collective-permute-done((bf16[128,5120]{1,0:T(8,128)(2,1)S(1)}, bf16[128,5120]{1,0:T(8,128)(2,1)S(1)}, u32[]{:S(2)}, u32[]{:S(2)}) %collective-permute-start) | collective-permute-done | bytes 1310752 | tf_op jit(solution)/shard_map/ppermute | solution.py:478
  67.2 3.5 %collective-permute-start.3 = (bf16[64,5120]{1,0:T(8,128)(2,1)S(1)}, bf16[64,5120]{1,0:T(8,128)(2,1)S(1)}, u32[]{:S(2)}, u32[]{:S(2)}) collective-permute-start(bf16[64,5120]{1,0:T(8,128)(2,1)S(1)} %cut.7), channel_id=1, source_target_pairs={{0,3},{1,0},{2,1},{3,2},{4,7},{5,4},{6,5},{7,6},{8,11},{9,8},{10,9... | collective-permute-start | bytes 1966088 | tf_op jit(solution)/shard_map/ppermute | solution.py:483
  70.8 6.6 %partial.2.refs_9_ = f32[384,1792]{1,0:T(8,128)S(1)} custom-call(bf16[128,5120]{1,0:T(8,128)(2,1)S(1)} %norm.1.refs_0_, bf16[128,5120]{1,0:T(8,128)(2,1)S(1)} %collective-permute-done.ref.refs_1_, bf16[128,5120]{1,0:T(8,128)(2,1)S(1)} %collective-permute-done.1.ref.refs_2_, bf16[640,1792]{1,0:T(8,128)(2,1)S(1)} %pack.1.refs_3_.refs_2_, ...), custom_call_target="tpu_custom_call" | custom-call | flops 5284823040 | tf_op jit(solution)/shard_map/partial/pallas_call | solution.py:141
  77.4 8.2 %collective-permute-done.7.refs_7_ = bf16[640,768]{1,0:T(8,128)(2,1)S(1)} collective-permute-done((bf16[640,768]{1,0:T(8,128)(2,1)S(1)}, bf16[640,768]{1,0:T(8,128)(2,1)S(1)}, u32[]{:S(2)}, u32[]{:S(2)}) %collective-permute-start.7) | collective-permute-done | bytes 983072 | tf_op jit(solution)/shard_map/ppermute | solution.py:398
  85.6 9.6 %collective-permute-done.5.refs_5_ = bf16[640,1024]{1,0:T(8,128)(2,1)S(1)} collective-permute-done((bf16[640,1024]{1,0:T(8,128)(2,1)S(1)}, bf16[640,1024]{1,0:T(8,128)(2,1)S(1)}, u32[]{:S(2)}, u32[]{:S(2)}) %collective-permute-start.5) | collective-permute-done | bytes 1310752 | tf_op jit(solution)/shard_map/ppermute | solution.py:398
  97.0 2.4 %collective-permute-done.2.refs_0_.refs_3_ = bf16[64,5120]{1,0:T(8,128)(2,1)S(1)} collective-permute-done((bf16[64,5120]{1,0:T(8,128)(2,1)S(1)}, bf16[64,5120]{1,0:T(8,128)(2,1)S(1)}, u32[]{:S(2)}, u32[]{:S(2)}) %collective-permute-start.2) | collective-permute-done | bytes 655392 | tf_op jit(solution)/shard_map/ppermute | solution.py:482
  100.1 2.3 %partial.3.refs_10_ = f32[128,1792]{1,0:T(8,128)S(1)} custom-call(bf16[64,5120]{1,0:T(8,128)(2,1)S(1)} %collective-permute-done.2.refs_0_.refs_3_, bf16[64,5120]{1,0:T(8,128)(2,1)S(1)} %collective-permute-done.3.refs_1_.refs_4_, bf16[640,1792]{1,0:T(8,128)(2,1)S(1)} %pack.1.refs_3_.refs_2_, bf16[640,1792]{1,0:T(8,128)(2,1)S(1)} %collective-permute-done.8.refs_4_.refs_3_, ...), custom_call_target="tpu_custom_call" | custom-call | tf_op jit(solution)/shard_map/partial/pallas_call | solution.py:141
  102.5 3.7 %finish.1 = (bf16[512,1280]{1,0:T(8,128)(2,1)S(1)}, bf16[512,512]{1,0:T(8,128)(2,1)S(1)}) custom-call(s32[2]{0:T(128)S(1)} %pad_add_fusion.index_ref, bf16[128,5120]{1,0:T(8,128)(2,1)S(1)} %norm.1.refs_0_, bf16[128,5120]{1,0:T(8,128)(2,1)S(1)} %collective-permute-done.ref.refs_1_, bf16[128,5120]{1,0:T(8,128)(2,1)S(1)} %collective-permute-done.1.ref.refs_2_, ...), custom_call_target="tpu_custom_call" | custom-call | tf_op jit(solution)/shard_map/finish/pallas_call | solution.py:217
  106.2 4.0 %attend.1.heads_ref = bf16[512,1280]{1,0:T(8,128)(2,1)S(1)} custom-call(s32[2]{0:T(128)S(1)} %pad_add_fusion.index_ref, bf16[512,1280]{1,0:T(8,128)(2,1)S(1)} %get-tuple-element.66.q_ref, bf16[512,512]{1,0:T(8,128)(2,1)S(1)} %get-tuple-element.67.kv_ref), custom_call_target="tpu_custom_call" | custom-call | tf_op jit(solution)/shard_map/attend/pallas_call | solution.py:288
  114.2 6.0 %collective-permute-done.17.a_ref = bf16[128,640]{1,0:T(8,128)(2,1)S(1)} collective-permute-done((bf16[128,640]{1,0:T(8,128)(2,1)S(1)}, bf16[128,640]{1,0:T(8,128)(2,1)S(1)}, u32[]{:S(2)}, u32[]{:S(2)}) %collective-permute-start.17) | collective-permute-done | bytes 163872 | tf_op jit(solution)/shard_map/ppermute | solution.py:535
  120.3 3.3 %collective-permute-done.13.a_ref = bf16[128,640]{1,0:T(8,128)(2,1)S(1)} collective-permute-done((bf16[128,640]{1,0:T(8,128)(2,1)S(1)}, bf16[128,640]{1,0:T(8,128)(2,1)S(1)}, u32[]{:S(2)}, u32[]{:S(2)}) %collective-permute-start.13) | collective-permute-done | bytes 163872 | tf_op jit(solution)/shard_map/ppermute | solution.py:535
  123.7 5.1 %collective-permute-done.18.a_ref = bf16[128,640]{1,0:T(8,128)(2,1)S(1)} collective-permute-done((bf16[128,640]{1,0:T(8,128)(2,1)S(1)}, bf16[128,640]{1,0:T(8,128)(2,1)S(1)}, u32[]{:S(2)}, u32[]{:S(2)}) %collective-permute-start.18) | collective-permute-done | bytes 163872 | tf_op jit(solution)/shard_map/ppermute | solution.py:535
  128.9 3.1 %collective-permute-done.14.a_ref = bf16[128,640]{1,0:T(8,128)(2,1)S(1)} collective-permute-done((bf16[128,640]{1,0:T(8,128)(2,1)S(1)}, bf16[128,640]{1,0:T(8,128)(2,1)S(1)}, u32[]{:S(2)}, u32[]{:S(2)}) %collective-permute-start.14) | collective-permute-done | bytes 163872 | tf_op jit(solution)/shard_map/ppermute | solution.py:535
  133.5 2.6 %collective-permute-done.19.refs_1_ = bf16[128,640]{1,0:T(8,128)(2,1)S(1)} collective-permute-done((bf16[128,640]{1,0:T(8,128)(2,1)S(1)}, bf16[128,640]{1,0:T(8,128)(2,1)S(1)}, u32[]{:S(2)}, u32[]{:S(2)}) %collective-permute-start.19) | collective-permute-done | bytes 163872 | tf_op jit(solution)/shard_map/ppermute | solution.py:535
  136.1 3.2 %collective-permute-done.15.refs_0_ = bf16[128,640]{1,0:T(8,128)(2,1)S(1)} collective-permute-done((bf16[128,640]{1,0:T(8,128)(2,1)S(1)}, bf16[128,640]{1,0:T(8,128)(2,1)S(1)}, u32[]{:S(2)}, u32[]{:S(2)}) %collective-permute-start.15) | collective-permute-done | bytes 163872 | tf_op jit(solution)/shard_map/ppermute | solution.py:535
  144.4 6.0 %collective-permute-done.23.a_ref = bf16[128,640]{1,0:T(8,128)(2,1)S(1)} collective-permute-done((bf16[128,640]{1,0:T(8,128)(2,1)S(1)}, bf16[128,640]{1,0:T(8,128)(2,1)S(1)}, u32[]{:S(2)}, u32[]{:S(2)}) %collective-permute-start.23) | collective-permute-done | bytes 163872 | tf_op jit(solution)/shard_map/ppermute | solution.py:535
  150.5 7.1 %collective-permute-done.21.a_ref = bf16[128,640]{1,0:T(8,128)(2,1)S(1)} collective-permute-done((bf16[128,640]{1,0:T(8,128)(2,1)S(1)}, bf16[128,640]{1,0:T(8,128)(2,1)S(1)}, u32[]{:S(2)}, u32[]{:S(2)}) %collective-permute-start.21) | collective-permute-done | bytes 163872 | tf_op jit(solution)/shard_map/ppermute | solution.py:535
  160.8 5.6 %collective-permute-done.29.a_ref = bf16[128,640]{1,0:T(8,128)(2,1)S(1)} collective-permute-done((bf16[128,640]{1,0:T(8,128)(2,1)S(1)}, bf16[128,640]{1,0:T(8,128)(2,1)S(1)}, u32[]{:S(2)}, u32[]{:S(2)}) %collective-permute-start.29) | collective-permute-done | bytes 163872 | tf_op jit(solution)/shard_map/ppermute | solution.py:535
  166.5 3.5 %collective-permute-done.28.a_ref = bf16[128,640]{1,0:T(8,128)(2,1)S(1)} collective-permute-done((bf16[128,640]{1,0:T(8,128)(2,1)S(1)}, bf16[128,640]{1,0:T(8,128)(2,1)S(1)}, u32[]{:S(2)}, u32[]{:S(2)}) %collective-permute-start.28) | collective-permute-done | bytes 163872 | tf_op jit(solution)/shard_map/ppermute | solution.py:535
  170.0 1.9 collective-permute-done.27.a_ref
  174.2 2.1 collective-permute-done.32.refs_1_
  179.2 7.8 %collective-permute-done.33.a_ref = bf16[128,768]{1,0:T(8,128)(2,1)S(1)} collective-permute-done((bf16[128,768]{1,0:T(8,128)(2,1)S(1)}, bf16[128,768]{1,0:T(8,128)(2,1)S(1)}, u32[]{:S(2)}, u32[]{:S(2)}) %collective-permute-start.33) | collective-permute-done | bytes 196640 | tf_op jit(solution)/shard_map/ppermute | solution.py:535
  189.9 2.5 %collective-permute-start.42 = (bf16[128,640]{1,0:T(8,128)(2,1)S(1)}, bf16[128,640]{1,0:T(8,128)(2,1)S(1)}, u32[]{:S(2)}, u32[]{:S(2)}) collective-permute-start(bf16[128,640]{1,0:T(8,128)(2,1)S(1)} %add.30), channel_id=1, source_target_pairs={{0,1},{1,2},{2,3},{3,0},{4,5},{5,6},{6,7},{7,4},{8,9},{9,10},{10,1... | collective-permute-start | bytes 491528 | tf_op jit(solution)/shard_map/ppermute | solution.py:535
  193.4 7.7 %collective-permute-done.35.refs_2_ = bf16[128,640]{1,0:T(8,128)(2,1)S(1)} collective-permute-done((bf16[128,640]{1,0:T(8,128)(2,1)S(1)}, bf16[128,640]{1,0:T(8,128)(2,1)S(1)}, u32[]{:S(2)}, u32[]{:S(2)}) %collective-permute-start.35) | collective-permute-done | bytes 163872 | tf_op jit(solution)/shard_map/ppermute | solution.py:535
  201.2 3.4 %collective-permute-done.44.a_ref = bf16[128,640]{1,0:T(8,128)(2,1)S(1)} collective-permute-done((bf16[128,640]{1,0:T(8,128)(2,1)S(1)}, bf16[128,640]{1,0:T(8,128)(2,1)S(1)}, u32[]{:S(2)}, u32[]{:S(2)}) %collective-permute-start.44) | collective-permute-done | bytes 163872 | tf_op jit(solution)/shard_map/ppermute | solution.py:535
  204.7 3.4 %collective-permute-done.42.a_ref = bf16[128,640]{1,0:T(8,128)(2,1)S(1)} collective-permute-done((bf16[128,640]{1,0:T(8,128)(2,1)S(1)}, bf16[128,640]{1,0:T(8,128)(2,1)S(1)}, u32[]{:S(2)}, u32[]{:S(2)}) %collective-permute-start.42) | collective-permute-done | bytes 163872 | tf_op jit(solution)/shard_map/ppermute | solution.py:535
  208.2 2.7 %collective-permute-done.40.a_ref = bf16[128,512]{1,0:T(8,128)(2,1)S(1)} collective-permute-done((bf16[128,512]{1,0:T(8,128)(2,1)S(1)}, bf16[128,512]{1,0:T(8,128)(2,1)S(1)}, u32[]{:S(2)}, u32[]{:S(2)}) %collective-permute-start.40) | collective-permute-done | bytes 131104 | tf_op jit(solution)/shard_map/ppermute | solution.py:535
  211.0 7.6 %collective-permute-done.45.refs_5_ = bf16[128,640]{1,0:T(8,128)(2,1)S(1)} collective-permute-done((bf16[128,640]{1,0:T(8,128)(2,1)S(1)}, bf16[128,640]{1,0:T(8,128)(2,1)S(1)}, u32[]{:S(2)}, u32[]{:S(2)}) %collective-permute-start.45) | collective-permute-done | bytes 163872 | tf_op jit(solution)/shard_map/ppermute | solution.py:535
  218.6 3.5 %collective-permute-done.43.refs_4_ = bf16[128,640]{1,0:T(8,128)(2,1)S(1)} collective-permute-done((bf16[128,640]{1,0:T(8,128)(2,1)S(1)}, bf16[128,640]{1,0:T(8,128)(2,1)S(1)}, u32[]{:S(2)}, u32[]{:S(2)}) %collective-permute-start.43) | collective-permute-done | bytes 163872 | tf_op jit(solution)/shard_map/ppermute | solution.py:535
  (121 shorter events, 40.6 us)
Async XLA Ops:
  3.5 34.3 %collective-permute-start.1 = (bf16[128,5120]{1,0:T(8,128)(2,1)S(1)}, bf16[128,5120]{1,0:T(8,128)(2,1)S(1)}, u32[]{:S(2)}, u32[]{:S(2)}) collective-permute-start(bf16[128,5120]{1,0:T(8,128)(2,1)S(1)} %norm.1.refs_0_), channel_id=1, source_target_pairs={{0,3},{1,0},{2,1},{3,2},{4,7},{5,4},{6,5},{7,6},{8,11},{9,8},{10,9... | collective-permute-start | bytes 3932168 | tf_op jit(solution)/shard_map/ppermute | solution.py:479
  8.7 51.4 %collective-permute-start.6 = (bf16[640,1792]{1,0:T(8,128)(2,1)S(1)}, bf16[640,1792]{1,0:T(8,128)(2,1)S(1)}, u32[]{:S(2)}, u32[]{:S(2)}) collective-permute-start(bf16[640,1792]{1,0:T(8,128)(2,1)S(1)} %pack.1.refs_3_.refs_2_), channel_id=1, source_target_pairs={{0,8},{4,12},{8,0},{12,4},{16,24},{20,28},{24,16},{28,20},{1,9},{5... | collective-permute-start | bytes 6881288 | tf_op jit(solution)/shard_map/ppermute | solution.py:398
  10.3 51.0 %collective-permute-start.4 = (bf16[640,1792]{1,0:T(8,128)(2,1)S(1)}, bf16[640,1792]{1,0:T(8,128)(2,1)S(1)}, u32[]{:S(2)}, u32[]{:S(2)}) collective-permute-start(bf16[640,1792]{1,0:T(8,128)(2,1)S(1)} %pack.1.refs_3_.refs_2_), channel_id=1, source_target_pairs={{0,16},{4,20},{8,24},{12,28},{16,0},{20,4},{24,8},{28,12},{1,17},{... | collective-permute-start | bytes 6881288 | tf_op jit(solution)/shard_map/ppermute | solution.py:398
  11.8 53.8 %collective-permute-start = (bf16[128,5120]{1,0:T(8,128)(2,1)S(1)}, bf16[128,5120]{1,0:T(8,128)(2,1)S(1)}, u32[]{:S(2)}, u32[]{:S(2)}) collective-permute-start(bf16[128,5120]{1,0:T(8,128)(2,1)S(1)} %norm.1.refs_0_), channel_id=1, source_target_pairs={{0,1},{1,2},{2,3},{3,0},{4,5},{5,6},{6,7},{7,4},{8,9},{9,10},{10,1... | collective-permute-start | bytes 3932168 | tf_op jit(solution)/shard_map/ppermute | solution.py:478
  11.8 55.3 %collective-permute-start.8 = (bf16[640,1792]{1,0:T(8,128)(2,1)S(1)}, bf16[640,1792]{1,0:T(8,128)(2,1)S(1)}, u32[]{:S(2)}, u32[]{:S(2)}) collective-permute-start(bf16[640,1792]{1,0:T(8,128)(2,1)S(1)} %pack.1.refs_3_.refs_2_), channel_id=1, source_target_pairs={{0,4},{4,0},{8,12},{12,8},{16,20},{20,16},{24,28},{28,24},{1,5},{5... | collective-permute-start | bytes 6881288 | tf_op jit(solution)/shard_map/ppermute | solution.py:398
  60.1 10.6 %collective-permute-start.9 = (bf16[640,1792]{1,0:T(8,128)(2,1)S(1)}, bf16[640,1792]{1,0:T(8,128)(2,1)S(1)}, u32[]{:S(2)}, u32[]{:S(2)}) collective-permute-start(bf16[640,1792]{1,0:T(8,128)(2,1)S(1)} %collective-permute-done.6.ref.refs_5_.refs_4_), channel_id=1, source_target_pairs={{0,4},{4,0},{8,12},{12,8},{16,20},{20,16},{24,28},{28,24},{1,5},{5... | collective-permute-start | bytes 6881288 | tf_op jit(solution)/shard_map/ppermute | solution.py:398
  61.4 24.2 %collective-permute-start.7 = (bf16[640,768]{1,0:T(8,128)(2,1)S(1)}, bf16[640,768]{1,0:T(8,128)(2,1)S(1)}, u32[]{:S(2)}, u32[]{:S(2)}) collective-permute-start(bf16[640,768]{1,0:T(8,128)(2,1)S(1)} %cut.9), channel_id=1, source_target_pairs={{0,16},{4,20},{8,24},{12,28},{16,0},{20,4},{24,8},{28,12},{1,17},{... | collective-permute-start | bytes 2949128 | tf_op jit(solution)/shard_map/ppermute | solution.py:398
  65.6 29.6 %collective-permute-start.5 = (bf16[640,1024]{1,0:T(8,128)(2,1)S(1)}, bf16[640,1024]{1,0:T(8,128)(2,1)S(1)}, u32[]{:S(2)}, u32[]{:S(2)}) collective-permute-start(bf16[640,1024]{1,0:T(8,128)(2,1)S(1)} %cut.8), channel_id=1, source_target_pairs={{0,8},{4,12},{8,0},{12,4},{16,24},{20,28},{24,16},{28,20},{1,9},{5... | collective-permute-start | bytes 3932168 | tf_op jit(solution)/shard_map/ppermute | solution.py:398
  67.2 29.6 %collective-permute-start.3 = (bf16[64,5120]{1,0:T(8,128)(2,1)S(1)}, bf16[64,5120]{1,0:T(8,128)(2,1)S(1)}, u32[]{:S(2)}, u32[]{:S(2)}) collective-permute-start(bf16[64,5120]{1,0:T(8,128)(2,1)S(1)} %cut.7), channel_id=1, source_target_pairs={{0,3},{1,0},{2,1},{3,2},{4,7},{5,4},{6,5},{7,6},{8,11},{9,8},{10,9... | collective-permute-start | bytes 1966088 | tf_op jit(solution)/shard_map/ppermute | solution.py:483
  70.7 28.8 %collective-permute-start.2 = (bf16[64,5120]{1,0:T(8,128)(2,1)S(1)}, bf16[64,5120]{1,0:T(8,128)(2,1)S(1)}, u32[]{:S(2)}, u32[]{:S(2)}) collective-permute-start(bf16[64,5120]{1,0:T(8,128)(2,1)S(1)} %cut.6), channel_id=1, source_target_pairs={{0,1},{1,2},{2,3},{3,0},{4,5},{5,6},{6,7},{7,4},{8,9},{9,10},{10,1... | collective-permute-start | bytes 1966088 | tf_op jit(solution)/shard_map/ppermute | solution.py:482
  70.7 39.5 %collective-permute-start.16 = (bf16[640,1280]{1,0:T(8,128)(2,1)S(1)}, bf16[640,1280]{1,0:T(8,128)(2,1)S(1)}, u32[]{:S(2)}, u32[]{:S(2)}) collective-permute-start(bf16[640,1280]{1,0:T(8,128)(2,1)S(1)} %copy-done.10), channel_id=1, source_target_pairs={{0,4},{4,0},{8,12},{12,8},{16,20},{20,16},{24,28},{28,24},{1,5},{5... | collective-permute-start | bytes 4915208 | tf_op jit(solution)/shard_map/ppermute | solution.py:398
  95.3 38.2 %collective-permute-start.22 = (bf16[640,1280]{1,0:T(8,128)(2,1)S(1)}, bf16[640,1280]{1,0:T(8,128)(2,1)S(1)}, u32[]{:S(2)}, u32[]{:S(2)}) collective-permute-start(bf16[640,1280]{1,0:T(8,128)(2,1)S(1)} %copy-done.10), channel_id=1, source_target_pairs={{0,16},{4,20},{8,24},{12,28},{16,0},{20,4},{24,8},{28,12},{1,17},{... | collective-permute-start | bytes 4915208 | tf_op jit(solution)/shard_map/ppermute | solution.py:398
  99.5 39.8 %collective-permute-start.20 = (bf16[640,1280]{1,0:T(8,128)(2,1)S(1)}, bf16[640,1280]{1,0:T(8,128)(2,1)S(1)}, u32[]{:S(2)}, u32[]{:S(2)}) collective-permute-start(bf16[640,1280]{1,0:T(8,128)(2,1)S(1)} %copy-done.10), channel_id=1, source_target_pairs={{0,8},{4,12},{8,0},{12,4},{16,24},{20,28},{24,16},{28,20},{1,9},{5... | collective-permute-start | bytes 4915208 | tf_op jit(solution)/shard_map/ppermute | solution.py:398
  114.1 9.5 %collective-permute-start.13 = (bf16[128,640]{1,0:T(8,128)(2,1)S(1)}, bf16[128,640]{1,0:T(8,128)(2,1)S(1)}, u32[]{:S(2)}, u32[]{:S(2)}) collective-permute-start(bf16[128,640]{1,0:T(8,128)(2,1)S(1)} %get-tuple-element.69), channel_id=1, source_target_pairs={{0,1},{1,2},{2,3},{3,0},{4,5},{5,6},{6,7},{7,4},{8,9},{9,10},{10,1... | collective-permute-start | bytes 491528 | tf_op jit(solution)/shard_map/ppermute | solution.py:535
  139.3 18.3 %collective-permute-start.26 = (bf16[640,1280]{1,0:T(8,128)(2,1)S(1)}, bf16[640,1280]{1,0:T(8,128)(2,1)S(1)}, u32[]{:S(2)}, u32[]{:S(2)}) collective-permute-start(bf16[640,1280]{1,0:T(8,128)(2,1)S(1)} %collective-permute-done.22.refs_0_.ref), channel_id=1, source_target_pairs={{0,4},{4,0},{8,12},{12,8},{16,20},{20,16},{24,28},{28,24},{1,5},{5... | collective-permute-start | bytes 4915208 | tf_op jit(solution)/shard_map/ppermute | solution.py:398
  139.3 19.6 %collective-permute-start.24 = (bf16[640,1280]{1,0:T(8,128)(2,1)S(1)}, bf16[640,1280]{1,0:T(8,128)(2,1)S(1)}, u32[]{:S(2)}, u32[]{:S(2)}) collective-permute-start(bf16[640,1280]{1,0:T(8,128)(2,1)S(1)} %collective-permute-done.20.refs_0_.ref), channel_id=1, source_target_pairs={{0,4},{4,0},{8,12},{12,8},{16,20},{20,16},{24,28},{28,24},{1,5},{5... | collective-permute-start | bytes 4915208 | tf_op jit(solution)/shard_map/ppermute | solution.py:398
  139.9 30.1 %collective-permute-start.30 = (bf16[384,1280]{1,0:T(8,128)(2,1)S(1)}, bf16[384,1280]{1,0:T(8,128)(2,1)S(1)}, u32[]{:S(2)}, u32[]{:S(2)}) collective-permute-start(bf16[384,1280]{1,0:T(8,128)(2,1)S(1)} %cut.10), channel_id=1, source_target_pairs={{0,8},{4,12},{8,0},{12,4},{16,24},{20,28},{24,16},{28,20},{1,9},{5... | collective-permute-start | bytes 2949128 | tf_op jit(solution)/shard_map/ppermute | solution.py:398
  142.8 27.2 %collective-permute-start.31 = (bf16[256,1280]{1,0:T(8,128)(2,1)S(1)}, bf16[256,1280]{1,0:T(8,128)(2,1)S(1)}, u32[]{:S(2)}, u32[]{:S(2)}) collective-permute-start(bf16[256,1280]{1,0:T(8,128)(2,1)S(1)} %cut.11), channel_id=1, source_target_pairs={{0,16},{4,20},{8,24},{12,28},{16,0},{20,4},{24,8},{28,12},{1,17},{... | collective-permute-start | bytes 1966088 | tf_op jit(solution)/shard_map/ppermute | solution.py:398
  157.6 12.4 %collective-permute-start.28 = (bf16[128,640]{1,0:T(8,128)(2,1)S(1)}, bf16[128,640]{1,0:T(8,128)(2,1)S(1)}, u32[]{:S(2)}, u32[]{:S(2)}) collective-permute-start(bf16[128,640]{1,0:T(8,128)(2,1)S(1)} %add.22), channel_id=1, source_target_pairs={{0,1},{1,2},{2,3},{3,0},{4,5},{5,6},{6,7},{7,4},{8,9},{9,10},{10,1... | collective-permute-start | bytes 491528 | tf_op jit(solution)/shard_map/ppermute | solution.py:535
  158.9 13.0 %collective-permute-start.27 = (bf16[128,640]{1,0:T(8,128)(2,1)S(1)}, bf16[128,640]{1,0:T(8,128)(2,1)S(1)}, u32[]{:S(2)}, u32[]{:S(2)}) collective-permute-start(bf16[128,640]{1,0:T(8,128)(2,1)S(1)} %get-tuple-element.83), channel_id=1, source_target_pairs={{0,1},{1,2},{2,3},{3,0},{4,5},{5,6},{6,7},{7,4},{8,9},{9,10},{10,1... | collective-permute-start | bytes 491528 | tf_op jit(solution)/shard_map/ppermute | solution.py:535
  177.4 9.6 %collective-permute-start.33 = (bf16[128,768]{1,0:T(8,128)(2,1)S(1)}, bf16[128,768]{1,0:T(8,128)(2,1)S(1)}, u32[]{:S(2)}, u32[]{:S(2)}) collective-permute-start(bf16[128,768]{1,0:T(8,128)(2,1)S(1)} %get-tuple-element.90), channel_id=1, source_target_pairs={{0,1},{1,2},{2,3},{3,0},{4,5},{5,6},{6,7},{7,4},{8,9},{9,10},{10,1... | collective-permute-start | bytes 589832 | tf_op jit(solution)/shard_map/ppermute | solution.py:535
  178.4 11.4 %collective-permute-start.39 = (bf16[128,512]{1,0:T(8,128)(2,1)S(1)}, bf16[128,512]{1,0:T(8,128)(2,1)S(1)}, u32[]{:S(2)}, u32[]{:S(2)}) collective-permute-start(bf16[128,512]{1,0:T(8,128)(2,1)S(1)} %get-tuple-element.97), channel_id=1, source_target_pairs={{0,1},{1,2},{2,3},{3,0},{4,5},{5,6},{6,7},{7,4},{8,9},{9,10},{10,1... | collective-permute-start | bytes 393224 | tf_op jit(solution)/shard_map/ppermute | solution.py:535
  178.5 14.8 %collective-permute-start.36 = (bf16[128,640]{1,0:T(8,128)(2,1)S(1)}, bf16[128,640]{1,0:T(8,128)(2,1)S(1)}, u32[]{:S(2)}, u32[]{:S(2)}) collective-permute-start(bf16[128,640]{1,0:T(8,128)(2,1)S(1)} %add.26), channel_id=1, source_target_pairs={{0,1},{1,2},{2,3},{3,0},{4,5},{5,6},{6,7},{7,4},{8,9},{9,10},{10,1... | collective-permute-start | bytes 491528 | tf_op jit(solution)/shard_map/ppermute | solution.py:535
  187.1 14.0 %collective-permute-start.34 = (bf16[128,768]{1,0:T(8,128)(2,1)S(1)}, bf16[128,768]{1,0:T(8,128)(2,1)S(1)}, u32[]{:S(2)}, u32[]{:S(2)}) collective-permute-start(bf16[128,768]{1,0:T(8,128)(2,1)S(1)} %add.24), channel_id=1, source_target_pairs={{0,1},{1,2},{2,3},{3,0},{4,5},{5,6},{6,7},{7,4},{8,9},{9,10},{10,1... | collective-permute-start | bytes 589832 | tf_op jit(solution)/shard_map/ppermute | solution.py:535
  187.2 13.9 %collective-permute-start.35 = (bf16[128,640]{1,0:T(8,128)(2,1)S(1)}, bf16[128,640]{1,0:T(8,128)(2,1)S(1)}, u32[]{:S(2)}, u32[]{:S(2)}) collective-permute-start(bf16[128,640]{1,0:T(8,128)(2,1)S(1)} %add.25), channel_id=1, source_target_pairs={{0,1},{1,2},{2,3},{3,0},{4,5},{5,6},{6,7},{7,4},{8,9},{9,10},{10,1... | collective-permute-start | bytes 491528 | tf_op jit(solution)/shard_map/ppermute | solution.py:535
  187.3 17.3 %collective-permute-start.44 = (bf16[128,640]{1,0:T(8,128)(2,1)S(1)}, bf16[128,640]{1,0:T(8,128)(2,1)S(1)}, u32[]{:S(2)}, u32[]{:S(2)}) collective-permute-start(bf16[128,640]{1,0:T(8,128)(2,1)S(1)} %add.32), channel_id=1, source_target_pairs={{0,1},{1,2},{2,3},{3,0},{4,5},{5,6},{6,7},{7,4},{8,9},{9,10},{10,1... | collective-permute-start | bytes 491528 | tf_op jit(solution)/shard_map/ppermute | solution.py:535
  189.9 18.3 %collective-permute-start.42 = (bf16[128,640]{1,0:T(8,128)(2,1)S(1)}, bf16[128,640]{1,0:T(8,128)(2,1)S(1)}, u32[]{:S(2)}, u32[]{:S(2)}) collective-permute-start(bf16[128,640]{1,0:T(8,128)(2,1)S(1)} %add.30), channel_id=1, source_target_pairs={{0,1},{1,2},{2,3},{3,0},{4,5},{5,6},{6,7},{7,4},{8,9},{9,10},{10,1... | collective-permute-start | bytes 491528 | tf_op jit(solution)/shard_map/ppermute | solution.py:535
  193.4 17.6 %collective-permute-start.40 = (bf16[128,512]{1,0:T(8,128)(2,1)S(1)}, bf16[128,512]{1,0:T(8,128)(2,1)S(1)}, u32[]{:S(2)}, u32[]{:S(2)}) collective-permute-start(bf16[128,512]{1,0:T(8,128)(2,1)S(1)} %add.28), channel_id=1, source_target_pairs={{0,1},{1,2},{2,3},{3,0},{4,5},{5,6},{6,7},{7,4},{8,9},{9,10},{10,1... | collective-permute-start | bytes 393224 | tf_op jit(solution)/shard_map/ppermute | solution.py:535
  201.1 23.0 %collective-permute-start.37 = (bf16[128,768]{1,0:T(8,128)(2,1)S(1)}, bf16[128,768]{1,0:T(8,128)(2,1)S(1)}, u32[]{:S(2)}, u32[]{:S(2)}) collective-permute-start(bf16[128,768]{1,0:T(8,128)(2,1)S(1)} %add.27), channel_id=1, source_target_pairs={{0,1},{1,2},{2,3},{3,0},{4,5},{5,6},{6,7},{7,4},{8,9},{9,10},{10,1... | collective-permute-start | bytes 589832 | tf_op jit(solution)/shard_map/ppermute | solution.py:535
  204.6 14.0 %collective-permute-start.45 = (bf16[128,640]{1,0:T(8,128)(2,1)S(1)}, bf16[128,640]{1,0:T(8,128)(2,1)S(1)}, u32[]{:S(2)}, u32[]{:S(2)}) collective-permute-start(bf16[128,640]{1,0:T(8,128)(2,1)S(1)} %add.33), channel_id=1, source_target_pairs={{0,1},{1,2},{2,3},{3,0},{4,5},{5,6},{6,7},{7,4},{8,9},{9,10},{10,1... | collective-permute-start | bytes 491528 | tf_op jit(solution)/shard_map/ppermute | solution.py:535
  208.2 14.0 %collective-permute-start.43 = (bf16[128,640]{1,0:T(8,128)(2,1)S(1)}, bf16[128,640]{1,0:T(8,128)(2,1)S(1)}, u32[]{:S(2)}, u32[]{:S(2)}) collective-permute-start(bf16[128,640]{1,0:T(8,128)(2,1)S(1)} %add.31), channel_id=1, source_target_pairs={{0,1},{1,2},{2,3},{3,0},{4,5},{5,6},{6,7},{7,4},{8,9},{9,10},{10,1... | collective-permute-start | bytes 491528 | tf_op jit(solution)/shard_map/ppermute | solution.py:535
  211.0 13.2 %collective-permute-start.41 = (bf16[128,512]{1,0:T(8,128)(2,1)S(1)}, bf16[128,512]{1,0:T(8,128)(2,1)S(1)}, u32[]{:S(2)}, u32[]{:S(2)}) collective-permute-start(bf16[128,512]{1,0:T(8,128)(2,1)S(1)} %add.29), channel_id=1, source_target_pairs={{0,1},{1,2},{2,3},{3,0},{4,5},{5,6},{6,7},{7,4},{8,9},{9,10},{10,1... | collective-permute-start | bytes 393224 | tf_op jit(solution)/shard_map/ppermute | solution.py:535
  (25 other events, 256.1 us)

commit v11 on v10

--- a/solution.py
+++ b/solution.py
@@ -522,7 +522,7 @@
             send_siblings(o_held, o_sibling, n_f, level, *gate)
             send_level(o_held, n_f, o_cut, 0, level + 1, *gate)
         if level < 2:
-            groups = [((r, 0, core),) for core in (0, 1) for r in near]
+            groups = [tuple((r, 0, core) for r in near) for core in (0, 1)]
         else:
             groups = [((r, half, 0), (r, half, 1)) for r in near for half in (0, 1)]
         terms = []
@@ -541,8 +541,8 @@
             for group in groups
         ]
         rounds.append(([term[0] for term in terms], arrivals, where))
-        gate = arrivals[-1] if level == 0 else arrivals[0] + arrivals[min(1, n_s - 2)][:2]
-        behind = arrivals[-1][:2] if level else []
+        gate = arrivals[-1] if level == 0 else arrivals[min(1, n_s - 2)]
+        behind = arrivals[-1][:1] if level else []
 
     mixed = None
     for chosen in (rounds[:-1], rounds[-1:]):

time: 226 us -> 220 us (0.973)
  starting transfers between devices: 27.3 us -> 23.7 us
    ppermute x24 -> x18, starting transfers between devices: 7.06 us -> 3.94 us  [body(): arrivals.append([lax.ppermute(total, 'sp', right) for total in totals])]
    ppermute x18, waiting for transfers between devices: 44.7 us -> 47.8 us  [swapped(): return lax.ppermute(array, 'fsdp', [(i, i ^ mask) for i in range(n_f)])]
    ppermute x24 -> x18, waiting for transfers between devices: 88.5 us -> 86 us  [body(): arrivals.append([lax.ppermute(total, 'sp', right) for total in totals])]
    pallas_call x8 -> x6, Pallas kernels: 9.37 us -> 8.27 us  [mix(): pl.pallas_call(functools.partial(mix_kernel, len(parts)), in_specs=[VMEM]...]
  transfers between devices with their start and end apart: 46 -> 40, of which waited for: 31 -> 27; matrix products, arithmetic and copies ran while one was open for 0% -> 0% of each run, Pallas kernels for 13% -> 13%
where the time goes in v11:
time: 220 us
  waiting for transfers between devices  163 us (74%)
  Pallas kernels  30.1 us (14%)
  starting transfers between devices  23.7 us (11%)
  local copies, waits for them, and re-layouts  2.2 us (1%)
    ppermute x18, waiting for transfers between devices, body(): arrivals.append([lax.ppermute(total, 'sp', right) for total in totals])  86 us
    ppermute x18, waiting for transfers between devices, swapped(): return lax.ppermute(array, 'fsdp', [(i, i ^ mask) for i in range(n_f)])  47.8 us
    ppermute x1, waiting for transfers between devices, body(): behind = lax.ppermute(behind, 'sp', left)  26 us
    ppermute x18, starting transfers between devices, swapped(): return lax.ppermute(array, 'fsdp', [(i, i ^ mask) for i in range(n_f)])  11.1 us
    pallas_call x2, Pallas kernels, partial(): pl.pallas_call(functools.partial(partial_kernel, len(blocks), counts, wid...  8.88 us
    pallas_call x6, Pallas kernels, mix(): pl.pallas_call(functools.partial(mix_kernel, len(parts)), in_specs=[VMEM]...  8.27 us
    ppermute x1, starting transfers between devices, body(): behind = lax.ppermute(behind, 'sp', left)  5.1 us
  transfers between devices with their start and end apart: 40, of which 27 were waited for; matrix products, arithmetic and copies ran while one was open for 0% of the time, Pallas kernels for 13%

profile of v11, /device:TPU:0, one launch (start us, length us, event | category | flops | bytes accessed | tf_op | source)
XLA Modules:
  0.0 220.1 jit_solution(9495465343701105640)
XLA Ops:
  3.5 5.1 %collective-permute-start.1 = (bf16[128,5120]{1,0:T(8,128)(2,1)S(1)}, bf16[128,5120]{1,0:T(8,128)(2,1)S(1)}, u32[]{:S(2)}, u32[]{:S(2)}) collective-permute-start(bf16[128,5120]{1,0:T(8,128)(2,1)S(1)} %norm.1.refs_0_), channel_id=1, source_target_pairs={{0,3},{1,0},{2,1},{3,2},{4,7},{5,4},{6,5},{7,6},{8,11},{9,8},{10,9... | collective-permute-start | bytes 3932168 | tf_op jit(solution)/shard_map/ppermute | solution.py:479
  11.8 26.0 %collective-permute-done.1.ref.refs_2_ = bf16[128,5120]{1,0:T(8,128)(2,1)S(1)} collective-permute-done((bf16[128,5120]{1,0:T(8,128)(2,1)S(1)}, bf16[128,5120]{1,0:T(8,128)(2,1)S(1)}, u32[]{:S(2)}, u32[]{:S(2)}) %collective-permute-start.1) | collective-permute-done | bytes 1310752 | tf_op jit(solution)/shard_map/ppermute | solution.py:479
  37.9 22.3 %collective-permute-done.6.ref.refs_5_.refs_4_ = bf16[640,1792]{1,0:T(8,128)(2,1)S(1)} collective-permute-done((bf16[640,1792]{1,0:T(8,128)(2,1)S(1)}, bf16[640,1792]{1,0:T(8,128)(2,1)S(1)}, u32[]{:S(2)}, u32[]{:S(2)}) %collective-permute-start.6) | collective-permute-done | bytes 2293792 | tf_op jit(solution)/shard_map/ppermute | solution.py:398
  63.1 2.5 %collective-permute-done.ref.refs_1_ = bf16[128,5120]{1,0:T(8,128)(2,1)S(1)} collective-permute-done((bf16[128,5120]{1,0:T(8,128)(2,1)S(1)}, bf16[128,5120]{1,0:T(8,128)(2,1)S(1)}, u32[]{:S(2)}, u32[]{:S(2)}) %collective-permute-start) | collective-permute-done | bytes 1310752 | tf_op jit(solution)/shard_map/ppermute | solution.py:478
  67.2 3.5 %collective-permute-start.3 = (bf16[64,5120]{1,0:T(8,128)(2,1)S(1)}, bf16[64,5120]{1,0:T(8,128)(2,1)S(1)}, u32[]{:S(2)}, u32[]{:S(2)}) collective-permute-start(bf16[64,5120]{1,0:T(8,128)(2,1)S(1)} %cut.7), channel_id=1, source_target_pairs={{0,3},{1,0},{2,1},{3,2},{4,7},{5,4},{6,5},{7,6},{8,11},{9,8},{10,9... | collective-permute-start | bytes 1966088 | tf_op jit(solution)/shard_map/ppermute | solution.py:483
  70.8 6.6 %partial.2.refs_9_ = f32[384,1792]{1,0:T(8,128)S(1)} custom-call(bf16[128,5120]{1,0:T(8,128)(2,1)S(1)} %norm.1.refs_0_, bf16[128,5120]{1,0:T(8,128)(2,1)S(1)} %collective-permute-done.ref.refs_1_, bf16[128,5120]{1,0:T(8,128)(2,1)S(1)} %collective-permute-done.1.ref.refs_2_, bf16[640,1792]{1,0:T(8,128)(2,1)S(1)} %pack.1.refs_3_.refs_2_, ...), custom_call_target="tpu_custom_call" | custom-call | flops 5284823040 | tf_op jit(solution)/shard_map/partial/pallas_call | solution.py:141
  77.4 8.2 %collective-permute-done.7.refs_7_ = bf16[640,768]{1,0:T(8,128)(2,1)S(1)} collective-permute-done((bf16[640,768]{1,0:T(8,128)(2,1)S(1)}, bf16[640,768]{1,0:T(8,128)(2,1)S(1)}, u32[]{:S(2)}, u32[]{:S(2)}) %collective-permute-start.7) | collective-permute-done | bytes 983072 | tf_op jit(solution)/shard_map/ppermute | solution.py:398
  85.6 9.6 %collective-permute-done.5.refs_5_ = bf16[640,1024]{1,0:T(8,128)(2,1)S(1)} collective-permute-done((bf16[640,1024]{1,0:T(8,128)(2,1)S(1)}, bf16[640,1024]{1,0:T(8,128)(2,1)S(1)}, u32[]{:S(2)}, u32[]{:S(2)}) %collective-permute-start.5) | collective-permute-done | bytes 1310752 | tf_op jit(solution)/shard_map/ppermute | solution.py:398
  99.5 2.3 %partial.3.refs_10_ = f32[128,1792]{1,0:T(8,128)S(1)} custom-call(bf16[64,5120]{1,0:T(8,128)(2,1)S(1)} %collective-permute-done.2.refs_0_.refs_3_, bf16[64,5120]{1,0:T(8,128)(2,1)S(1)} %collective-permute-done.3.refs_1_.refs_4_, bf16[640,1792]{1,0:T(8,128)(2,1)S(1)} %pack.1.refs_3_.refs_2_, bf16[640,1792]{1,0:T(8,128)(2,1)S(1)} %collective-permute-done.8.refs_4_.refs_3_, ...), custom_call_target="tpu_custom_call" | custom-call | tf_op jit(solution)/shard_map/partial/pallas_call | solution.py:141
  102.1 3.7 %finish.1 = (bf16[512,1280]{1,0:T(8,128)(2,1)S(1)}, bf16[512,512]{1,0:T(8,128)(2,1)S(1)}) custom-call(s32[2]{0:T(128)S(1)} %pad_add_fusion.index_ref, bf16[128,5120]{1,0:T(8,128)(2,1)S(1)} %norm.1.refs_0_, bf16[128,5120]{1,0:T(8,128)(2,1)S(1)} %collective-permute-done.ref.refs_1_, bf16[128,5120]{1,0:T(8,128)(2,1)S(1)} %collective-permute-done.1.ref.refs_2_, ...), custom_call_target="tpu_custom_call" | custom-call | tf_op jit(solution)/shard_map/finish/pallas_call | solution.py:217
  105.8 4.0 %attend.1.heads_ref = bf16[512,1280]{1,0:T(8,128)(2,1)S(1)} custom-call(s32[2]{0:T(128)S(1)} %pad_add_fusion.index_ref, bf16[512,1280]{1,0:T(8,128)(2,1)S(1)} %get-tuple-element.58.q_ref, bf16[512,512]{1,0:T(8,128)(2,1)S(1)} %get-tuple-element.59.kv_ref), custom_call_target="tpu_custom_call" | custom-call | tf_op jit(solution)/shard_map/attend/pallas_call | solution.py:288
  111.0 1.7 collective-permute-start.17
  114.1 5.8 %collective-permute-done.17.a_ref = bf16[128,640]{1,0:T(8,128)(2,1)S(1)} collective-permute-done((bf16[128,640]{1,0:T(8,128)(2,1)S(1)}, bf16[128,640]{1,0:T(8,128)(2,1)S(1)}, u32[]{:S(2)}, u32[]{:S(2)}) %collective-permute-start.17) | collective-permute-done | bytes 163872 | tf_op jit(solution)/shard_map/ppermute | solution.py:535
  120.0 2.8 %collective-permute-done.13.a_ref = bf16[128,640]{1,0:T(8,128)(2,1)S(1)} collective-permute-done((bf16[128,640]{1,0:T(8,128)(2,1)S(1)}, bf16[128,640]{1,0:T(8,128)(2,1)S(1)}, u32[]{:S(2)}, u32[]{:S(2)}) %collective-permute-start.13) | collective-permute-done | bytes 163872 | tf_op jit(solution)/shard_map/ppermute | solution.py:535
  123.3 4.0 %collective-permute-done.18.a_ref = bf16[128,640]{1,0:T(8,128)(2,1)S(1)} collective-permute-done((bf16[128,640]{1,0:T(8,128)(2,1)S(1)}, bf16[128,640]{1,0:T(8,128)(2,1)S(1)}, u32[]{:S(2)}, u32[]{:S(2)}) %collective-permute-start.18) | collective-permute-done | bytes 163872 | tf_op jit(solution)/shard_map/ppermute | solution.py:535
  127.5 4.3 %collective-permute-done.14.a_ref = bf16[128,640]{1,0:T(8,128)(2,1)S(1)} collective-permute-done((bf16[128,640]{1,0:T(8,128)(2,1)S(1)}, bf16[128,640]{1,0:T(8,128)(2,1)S(1)}, u32[]{:S(2)}, u32[]{:S(2)}) %collective-permute-start.14) | collective-permute-done | bytes 163872 | tf_op jit(solution)/shard_map/ppermute | solution.py:535
  131.9 1.6 collective-permute-done.21.refs_1_.ref
  133.5 1.7 collective-permute-done.19.refs_1_
  135.2 3.8 %collective-permute-done.15.refs_0_ = bf16[128,640]{1,0:T(8,128)(2,1)S(1)} collective-permute-done((bf16[128,640]{1,0:T(8,128)(2,1)S(1)}, bf16[128,640]{1,0:T(8,128)(2,1)S(1)}, u32[]{:S(2)}, u32[]{:S(2)}) %collective-permute-start.15) | collective-permute-done | bytes 163872 | tf_op jit(solution)/shard_map/ppermute | solution.py:535
  140.3 1.9 mix.8
  142.5 2.3 %collective-permute-done.24.refs_0_ = bf16[640,1280]{1,0:T(8,128)(2,1)S(1)} collective-permute-done((bf16[640,1280]{1,0:T(8,128)(2,1)S(1)}, bf16[640,1280]{1,0:T(8,128)(2,1)S(1)}, u32[]{:S(2)}, u32[]{:S(2)}) %collective-permute-start.24) | collective-permute-done | bytes 1638432 | tf_op jit(solution)/shard_map/ppermute | solution.py:398
  144.8 1.9 mix.9
  147.0 7.7 %collective-permute-done.22.a_ref = bf16[128,1280]{1,0:T(8,128)(2,1)S(1)} collective-permute-done((bf16[128,1280]{1,0:T(8,128)(2,1)S(1)}, bf16[128,1280]{1,0:T(8,128)(2,1)S(1)}, u32[]{:S(2)}, u32[]{:S(2)}) %collective-permute-start.22) | collective-permute-done | bytes 327712 | tf_op jit(solution)/shard_map/ppermute | solution.py:535
  154.8 6.9 %collective-permute-done.26.a_ref = bf16[128,1280]{1,0:T(8,128)(2,1)S(1)} collective-permute-done((bf16[128,1280]{1,0:T(8,128)(2,1)S(1)}, bf16[128,1280]{1,0:T(8,128)(2,1)S(1)}, u32[]{:S(2)}, u32[]{:S(2)}) %collective-permute-start.26) | collective-permute-done | bytes 327712 | tf_op jit(solution)/shard_map/ppermute | solution.py:535
  161.8 6.9 %collective-permute-done.23.a_ref = bf16[128,1280]{1,0:T(8,128)(2,1)S(1)} collective-permute-done((bf16[128,1280]{1,0:T(8,128)(2,1)S(1)}, bf16[128,1280]{1,0:T(8,128)(2,1)S(1)}, u32[]{:S(2)}, u32[]{:S(2)}) %collective-permute-start.23) | collective-permute-done | bytes 327712 | tf_op jit(solution)/shard_map/ppermute | solution.py:535
  168.7 5.7 %collective-permute-done.27.a_ref = bf16[128,1280]{1,0:T(8,128)(2,1)S(1)} collective-permute-done((bf16[128,1280]{1,0:T(8,128)(2,1)S(1)}, bf16[128,1280]{1,0:T(8,128)(2,1)S(1)}, u32[]{:S(2)}, u32[]{:S(2)}) %collective-permute-start.27) | collective-permute-done | bytes 327712 | tf_op jit(solution)/shard_map/ppermute | solution.py:535
  175.0 2.1 collective-permute-done.30.refs_1_
  180.1 7.8 %collective-permute-done.31.a_ref = bf16[128,768]{1,0:T(8,128)(2,1)S(1)} collective-permute-done((bf16[128,768]{1,0:T(8,128)(2,1)S(1)}, bf16[128,768]{1,0:T(8,128)(2,1)S(1)}, u32[]{:S(2)}, u32[]{:S(2)}) %collective-permute-start.31) | collective-permute-done | bytes 196640 | tf_op jit(solution)/shard_map/ppermute | solution.py:535
  188.1 9.6 %collective-permute-done.36.a_ref = bf16[128,512]{1,0:T(8,128)(2,1)S(1)} collective-permute-done((bf16[128,512]{1,0:T(8,128)(2,1)S(1)}, bf16[128,512]{1,0:T(8,128)(2,1)S(1)}, u32[]{:S(2)}, u32[]{:S(2)}) %collective-permute-start.36) | collective-permute-done | bytes 131104 | tf_op jit(solution)/shard_map/ppermute | solution.py:535
  197.8 4.1 %collective-permute-done.32.a_ref = bf16[128,768]{1,0:T(8,128)(2,1)S(1)} collective-permute-done((bf16[128,768]{1,0:T(8,128)(2,1)S(1)}, bf16[128,768]{1,0:T(8,128)(2,1)S(1)}, u32[]{:S(2)}, u32[]{:S(2)}) %collective-permute-start.32) | collective-permute-done | bytes 196640 | tf_op jit(solution)/shard_map/ppermute | solution.py:535
  202.0 9.7 %collective-permute-done.37.a_ref = bf16[128,512]{1,0:T(8,128)(2,1)S(1)} collective-permute-done((bf16[128,512]{1,0:T(8,128)(2,1)S(1)}, bf16[128,512]{1,0:T(8,128)(2,1)S(1)}, u32[]{:S(2)}, u32[]{:S(2)}) %collective-permute-start.37) | collective-permute-done | bytes 131104 | tf_op jit(solution)/shard_map/ppermute | solution.py:535
  213.4 5.2 %collective-permute-done.38.refs_1_ = bf16[128,512]{1,0:T(8,128)(2,1)S(1)} collective-permute-done((bf16[128,512]{1,0:T(8,128)(2,1)S(1)}, bf16[128,512]{1,0:T(8,128)(2,1)S(1)}, u32[]{:S(2)}, u32[]{:S(2)}) %collective-permute-start.38) | collective-permute-done | bytes 131104 | tf_op jit(solution)/shard_map/ppermute | solution.py:535
  (103 shorter events, 28.3 us)
Async XLA Ops:
  3.5 34.3 %collective-permute-start.1 = (bf16[128,5120]{1,0:T(8,128)(2,1)S(1)}, bf16[128,5120]{1,0:T(8,128)(2,1)S(1)}, u32[]{:S(2)}, u32[]{:S(2)}) collective-permute-start(bf16[128,5120]{1,0:T(8,128)(2,1)S(1)} %norm.1.refs_0_), channel_id=1, source_target_pairs={{0,3},{1,0},{2,1},{3,2},{4,7},{5,4},{6,5},{7,6},{8,11},{9,8},{10,9... | collective-permute-start | bytes 3932168 | tf_op jit(solution)/shard_map/ppermute | solution.py:479
  8.7 51.4 %collective-permute-start.6 = (bf16[640,1792]{1,0:T(8,128)(2,1)S(1)}, bf16[640,1792]{1,0:T(8,128)(2,1)S(1)}, u32[]{:S(2)}, u32[]{:S(2)}) collective-permute-start(bf16[640,1792]{1,0:T(8,128)(2,1)S(1)} %pack.1.refs_3_.refs_2_), channel_id=1, source_target_pairs={{0,8},{4,12},{8,0},{12,4},{16,24},{20,28},{24,16},{28,20},{1,9},{5... | collective-permute-start | bytes 6881288 | tf_op jit(solution)/shard_map/ppermute | solution.py:398
  10.3 51.0 %collective-permute-start.4 = (bf16[640,1792]{1,0:T(8,128)(2,1)S(1)}, bf16[640,1792]{1,0:T(8,128)(2,1)S(1)}, u32[]{:S(2)}, u32[]{:S(2)}) collective-permute-start(bf16[640,1792]{1,0:T(8,128)(2,1)S(1)} %pack.1.refs_3_.refs_2_), channel_id=1, source_target_pairs={{0,16},{4,20},{8,24},{12,28},{16,0},{20,4},{24,8},{28,12},{1,17},{... | collective-permute-start | bytes 6881288 | tf_op jit(solution)/shard_map/ppermute | solution.py:398
  11.8 53.8 %collective-permute-start = (bf16[128,5120]{1,0:T(8,128)(2,1)S(1)}, bf16[128,5120]{1,0:T(8,128)(2,1)S(1)}, u32[]{:S(2)}, u32[]{:S(2)}) collective-permute-start(bf16[128,5120]{1,0:T(8,128)(2,1)S(1)} %norm.1.refs_0_), channel_id=1, source_target_pairs={{0,1},{1,2},{2,3},{3,0},{4,5},{5,6},{6,7},{7,4},{8,9},{9,10},{10,1... | collective-permute-start | bytes 3932168 | tf_op jit(solution)/shard_map/ppermute | solution.py:478
  11.8 55.3 %collective-permute-start.8 = (bf16[640,1792]{1,0:T(8,128)(2,1)S(1)}, bf16[640,1792]{1,0:T(8,128)(2,1)S(1)}, u32[]{:S(2)}, u32[]{:S(2)}) collective-permute-start(bf16[640,1792]{1,0:T(8,128)(2,1)S(1)} %pack.1.refs_3_.refs_2_), channel_id=1, source_target_pairs={{0,4},{4,0},{8,12},{12,8},{16,20},{20,16},{24,28},{28,24},{1,5},{5... | collective-permute-start | bytes 6881288 | tf_op jit(solution)/shard_map/ppermute | solution.py:398
  60.1 10.6 %collective-permute-start.9 = (bf16[640,1792]{1,0:T(8,128)(2,1)S(1)}, bf16[640,1792]{1,0:T(8,128)(2,1)S(1)}, u32[]{:S(2)}, u32[]{:S(2)}) collective-permute-start(bf16[640,1792]{1,0:T(8,128)(2,1)S(1)} %collective-permute-done.6.ref.refs_5_.refs_4_), channel_id=1, source_target_pairs={{0,4},{4,0},{8,12},{12,8},{16,20},{20,16},{24,28},{28,24},{1,5},{5... | collective-permute-start | bytes 6881288 | tf_op jit(solution)/shard_map/ppermute | solution.py:398
  61.3 9.4 %collective-permute-start.10 = (bf16[640,1792]{1,0:T(8,128)(2,1)S(1)}, bf16[640,1792]{1,0:T(8,128)(2,1)S(1)}, u32[]{:S(2)}, u32[]{:S(2)}) collective-permute-start(bf16[640,1792]{1,0:T(8,128)(2,1)S(1)} %collective-permute-done.4.ref.refs_7_.refs_6_), channel_id=1, source_target_pairs={{0,4},{4,0},{8,12},{12,8},{16,20},{20,16},{24,28},{28,24},{1,5},{5... | collective-permute-start | bytes 6881288 | tf_op jit(solution)/shard_map/ppermute | solution.py:398
  61.4 24.2 %collective-permute-start.7 = (bf16[640,768]{1,0:T(8,128)(2,1)S(1)}, bf16[640,768]{1,0:T(8,128)(2,1)S(1)}, u32[]{:S(2)}, u32[]{:S(2)}) collective-permute-start(bf16[640,768]{1,0:T(8,128)(2,1)S(1)} %cut.9), channel_id=1, source_target_pairs={{0,16},{4,20},{8,24},{12,28},{16,0},{20,4},{24,8},{28,12},{1,17},{... | collective-permute-start | bytes 2949128 | tf_op jit(solution)/shard_map/ppermute | solution.py:398
  65.6 29.6 %collective-permute-start.5 = (bf16[640,1024]{1,0:T(8,128)(2,1)S(1)}, bf16[640,1024]{1,0:T(8,128)(2,1)S(1)}, u32[]{:S(2)}, u32[]{:S(2)}) collective-permute-start(bf16[640,1024]{1,0:T(8,128)(2,1)S(1)} %cut.8), channel_id=1, source_target_pairs={{0,8},{4,12},{8,0},{12,4},{16,24},{20,28},{24,16},{28,20},{1,9},{5... | collective-permute-start | bytes 3932168 | tf_op jit(solution)/shard_map/ppermute | solution.py:398
  67.2 29.6 %collective-permute-start.3 = (bf16[64,5120]{1,0:T(8,128)(2,1)S(1)}, bf16[64,5120]{1,0:T(8,128)(2,1)S(1)}, u32[]{:S(2)}, u32[]{:S(2)}) collective-permute-start(bf16[64,5120]{1,0:T(8,128)(2,1)S(1)} %cut.7), channel_id=1, source_target_pairs={{0,3},{1,0},{2,1},{3,2},{4,7},{5,4},{6,5},{7,6},{8,11},{9,8},{10,9... | collective-permute-start | bytes 1966088 | tf_op jit(solution)/shard_map/ppermute | solution.py:483
  70.7 28.8 %collective-permute-start.2 = (bf16[64,5120]{1,0:T(8,128)(2,1)S(1)}, bf16[64,5120]{1,0:T(8,128)(2,1)S(1)}, u32[]{:S(2)}, u32[]{:S(2)}) collective-permute-start(bf16[64,5120]{1,0:T(8,128)(2,1)S(1)} %cut.6), channel_id=1, source_target_pairs={{0,1},{1,2},{2,3},{3,0},{4,5},{5,6},{6,7},{7,4},{8,9},{9,10},{10,1... | collective-permute-start | bytes 1966088 | tf_op jit(solution)/shard_map/ppermute | solution.py:482
  70.7 39.1 %collective-permute-start.16 = (bf16[640,1280]{1,0:T(8,128)(2,1)S(1)}, bf16[640,1280]{1,0:T(8,128)(2,1)S(1)}, u32[]{:S(2)}, u32[]{:S(2)}) collective-permute-start(bf16[640,1280]{1,0:T(8,128)(2,1)S(1)} %copy-done.10), channel_id=1, source_target_pairs={{0,4},{4,0},{8,12},{12,8},{16,20},{20,16},{24,28},{28,24},{1,5},{5... | collective-permute-start | bytes 4915208 | tf_op jit(solution)/shard_map/ppermute | solution.py:398
  95.3 38.2 %collective-permute-start.21 = (bf16[640,1280]{1,0:T(8,128)(2,1)S(1)}, bf16[640,1280]{1,0:T(8,128)(2,1)S(1)}, u32[]{:S(2)}, u32[]{:S(2)}) collective-permute-start(bf16[640,1280]{1,0:T(8,128)(2,1)S(1)} %copy-done.10), channel_id=1, source_target_pairs={{0,16},{4,20},{8,24},{12,28},{16,0},{20,4},{24,8},{28,12},{1,17},{... | collective-permute-start | bytes 4915208 | tf_op jit(solution)/shard_map/ppermute | solution.py:398
  96.8 42.2 %collective-permute-start.20 = (bf16[640,1280]{1,0:T(8,128)(2,1)S(1)}, bf16[640,1280]{1,0:T(8,128)(2,1)S(1)}, u32[]{:S(2)}, u32[]{:S(2)}) collective-permute-start(bf16[640,1280]{1,0:T(8,128)(2,1)S(1)} %copy-done.10), channel_id=1, source_target_pairs={{0,8},{4,12},{8,0},{12,4},{16,24},{20,28},{24,16},{28,20},{1,9},{5... | collective-permute-start | bytes 4915208 | tf_op jit(solution)/shard_map/ppermute | solution.py:398
  111.0 8.9 %collective-permute-start.17 = (bf16[128,640]{1,0:T(8,128)(2,1)S(1)}, bf16[128,640]{1,0:T(8,128)(2,1)S(1)}, u32[]{:S(2)}, u32[]{:S(2)}) collective-permute-start(bf16[128,640]{1,0:T(8,128)(2,1)S(1)} %get-tuple-element.65), channel_id=1, source_target_pairs={{0,1},{1,2},{2,3},{3,0},{4,5},{5,6},{6,7},{7,4},{8,9},{9,10},{10,1... | collective-permute-start | bytes 491528 | tf_op jit(solution)/shard_map/ppermute | solution.py:535
  113.9 8.8 %collective-permute-start.13 = (bf16[128,640]{1,0:T(8,128)(2,1)S(1)}, bf16[128,640]{1,0:T(8,128)(2,1)S(1)}, u32[]{:S(2)}, u32[]{:S(2)}) collective-permute-start(bf16[128,640]{1,0:T(8,128)(2,1)S(1)} %get-tuple-element.61), channel_id=1, source_target_pairs={{0,1},{1,2},{2,3},{3,0},{4,5},{5,6},{6,7},{7,4},{8,9},{9,10},{10,1... | collective-permute-start | bytes 491528 | tf_op jit(solution)/shard_map/ppermute | solution.py:535
  119.9 7.5 %collective-permute-start.18 = (bf16[128,640]{1,0:T(8,128)(2,1)S(1)}, bf16[128,640]{1,0:T(8,128)(2,1)S(1)}, u32[]{:S(2)}, u32[]{:S(2)}) collective-permute-start(bf16[128,640]{1,0:T(8,128)(2,1)S(1)} %add.16), channel_id=1, source_target_pairs={{0,1},{1,2},{2,3},{3,0},{4,5},{5,6},{6,7},{7,4},{8,9},{9,10},{10,1... | collective-permute-start | bytes 491528 | tf_op jit(solution)/shard_map/ppermute | solution.py:535
  122.8 9.0 %collective-permute-start.14 = (bf16[128,640]{1,0:T(8,128)(2,1)S(1)}, bf16[128,640]{1,0:T(8,128)(2,1)S(1)}, u32[]{:S(2)}, u32[]{:S(2)}) collective-permute-start(bf16[128,640]{1,0:T(8,128)(2,1)S(1)} %add.14), channel_id=1, source_target_pairs={{0,1},{1,2},{2,3},{3,0},{4,5},{5,6},{6,7},{7,4},{8,9},{9,10},{10,1... | collective-permute-start | bytes 491528 | tf_op jit(solution)/shard_map/ppermute | solution.py:535
  127.4 7.7 %collective-permute-start.19 = (bf16[128,640]{1,0:T(8,128)(2,1)S(1)}, bf16[128,640]{1,0:T(8,128)(2,1)S(1)}, u32[]{:S(2)}, u32[]{:S(2)}) collective-permute-start(bf16[128,640]{1,0:T(8,128)(2,1)S(1)} %add.17), channel_id=1, source_target_pairs={{0,1},{1,2},{2,3},{3,0},{4,5},{5,6},{6,7},{7,4},{8,9},{9,10},{10,1... | collective-permute-start | bytes 491528 | tf_op jit(solution)/shard_map/ppermute | solution.py:535
  139.6 29.2 %collective-permute-start.28 = (bf16[384,1280]{1,0:T(8,128)(2,1)S(1)}, bf16[384,1280]{1,0:T(8,128)(2,1)S(1)}, u32[]{:S(2)}, u32[]{:S(2)}) collective-permute-start(bf16[384,1280]{1,0:T(8,128)(2,1)S(1)} %cut.10), channel_id=1, source_target_pairs={{0,8},{4,12},{8,0},{12,4},{16,24},{20,28},{24,16},{28,20},{1,9},{5... | collective-permute-start | bytes 2949128 | tf_op jit(solution)/shard_map/ppermute | solution.py:398
  142.2 12.5 %collective-permute-start.22 = (bf16[128,1280]{1,0:T(8,128)(2,1)S(1)}, bf16[128,1280]{1,0:T(8,128)(2,1)S(1)}, u32[]{:S(2)}, u32[]{:S(2)}) collective-permute-start(bf16[128,1280]{1,0:T(8,128)(2,1)S(1)} %get-tuple-element.70), channel_id=1, source_target_pairs={{0,1},{1,2},{2,3},{3,0},{4,5},{5,6},{6,7},{7,4},{8,9},{9,10},{10,1... | collective-permute-start | bytes 983048 | tf_op jit(solution)/shard_map/ppermute | solution.py:535
  146.7 15.0 %collective-permute-start.26 = (bf16[128,1280]{1,0:T(8,128)(2,1)S(1)}, bf16[128,1280]{1,0:T(8,128)(2,1)S(1)}, u32[]{:S(2)}, u32[]{:S(2)}) collective-permute-start(bf16[128,1280]{1,0:T(8,128)(2,1)S(1)} %get-tuple-element.74), channel_id=1, source_target_pairs={{0,1},{1,2},{2,3},{3,0},{4,5},{5,6},{6,7},{7,4},{8,9},{9,10},{10,1... | collective-permute-start | bytes 983048 | tf_op jit(solution)/shard_map/ppermute | solution.py:535
  146.8 21.9 %collective-permute-start.29 = (bf16[256,1280]{1,0:T(8,128)(2,1)S(1)}, bf16[256,1280]{1,0:T(8,128)(2,1)S(1)}, u32[]{:S(2)}, u32[]{:S(2)}) collective-permute-start(bf16[256,1280]{1,0:T(8,128)(2,1)S(1)} %cut.11), channel_id=1, source_target_pairs={{0,16},{4,20},{8,24},{12,28},{16,0},{20,4},{24,8},{28,12},{1,17},{... | collective-permute-start | bytes 1966088 | tf_op jit(solution)/shard_map/ppermute | solution.py:398
  154.8 14.0 %collective-permute-start.23 = (bf16[128,1280]{1,0:T(8,128)(2,1)S(1)}, bf16[128,1280]{1,0:T(8,128)(2,1)S(1)}, u32[]{:S(2)}, u32[]{:S(2)}) collective-permute-start(bf16[128,1280]{1,0:T(8,128)(2,1)S(1)} %add.18), channel_id=1, source_target_pairs={{0,1},{1,2},{2,3},{3,0},{4,5},{5,6},{6,7},{7,4},{8,9},{9,10},{10,1... | collective-permute-start | bytes 983048 | tf_op jit(solution)/shard_map/ppermute | solution.py:535
  161.8 12.7 %collective-permute-start.27 = (bf16[128,1280]{1,0:T(8,128)(2,1)S(1)}, bf16[128,1280]{1,0:T(8,128)(2,1)S(1)}, u32[]{:S(2)}, u32[]{:S(2)}) collective-permute-start(bf16[128,1280]{1,0:T(8,128)(2,1)S(1)} %add.19), channel_id=1, source_target_pairs={{0,1},{1,2},{2,3},{3,0},{4,5},{5,6},{6,7},{7,4},{8,9},{9,10},{10,1... | collective-permute-start | bytes 983048 | tf_op jit(solution)/shard_map/ppermute | solution.py:535
  178.3 9.6 %collective-permute-start.31 = (bf16[128,768]{1,0:T(8,128)(2,1)S(1)}, bf16[128,768]{1,0:T(8,128)(2,1)S(1)}, u32[]{:S(2)}, u32[]{:S(2)}) collective-permute-start(bf16[128,768]{1,0:T(8,128)(2,1)S(1)} %get-tuple-element.80), channel_id=1, source_target_pairs={{0,1},{1,2},{2,3},{3,0},{4,5},{5,6},{6,7},{7,4},{8,9},{9,10},{10,1... | collective-permute-start | bytes 589832 | tf_op jit(solution)/shard_map/ppermute | solution.py:535
  178.4 19.4 %collective-permute-start.33 = (bf16[128,1280]{1,0:T(8,128)(2,1)S(1)}, bf16[128,1280]{1,0:T(8,128)(2,1)S(1)}, u32[]{:S(2)}, u32[]{:S(2)}) collective-permute-start(bf16[128,1280]{1,0:T(8,128)(2,1)S(1)} %add.21), channel_id=1, source_target_pairs={{0,1},{1,2},{2,3},{3,0},{4,5},{5,6},{6,7},{7,4},{8,9},{9,10},{10,1... | collective-permute-start | bytes 983048 | tf_op jit(solution)/shard_map/ppermute | solution.py:535
  179.4 18.3 %collective-permute-start.36 = (bf16[128,512]{1,0:T(8,128)(2,1)S(1)}, bf16[128,512]{1,0:T(8,128)(2,1)S(1)}, u32[]{:S(2)}, u32[]{:S(2)}) collective-permute-start(bf16[128,512]{1,0:T(8,128)(2,1)S(1)} %get-tuple-element.86), channel_id=1, source_target_pairs={{0,1},{1,2},{2,3},{3,0},{4,5},{5,6},{6,7},{7,4},{8,9},{9,10},{10,1... | collective-permute-start | bytes 393224 | tf_op jit(solution)/shard_map/ppermute | solution.py:535
  187.9 14.0 %collective-permute-start.32 = (bf16[128,768]{1,0:T(8,128)(2,1)S(1)}, bf16[128,768]{1,0:T(8,128)(2,1)S(1)}, u32[]{:S(2)}, u32[]{:S(2)}) collective-permute-start(bf16[128,768]{1,0:T(8,128)(2,1)S(1)} %add.20), channel_id=1, source_target_pairs={{0,1},{1,2},{2,3},{3,0},{4,5},{5,6},{6,7},{7,4},{8,9},{9,10},{10,1... | collective-permute-start | bytes 589832 | tf_op jit(solution)/shard_map/ppermute | solution.py:535
  188.1 23.8 %collective-permute-start.39 = (bf16[128,1280]{1,0:T(8,128)(2,1)S(1)}, bf16[128,1280]{1,0:T(8,128)(2,1)S(1)}, u32[]{:S(2)}, u32[]{:S(2)}) collective-permute-start(bf16[128,1280]{1,0:T(8,128)(2,1)S(1)} %add.25), channel_id=1, source_target_pairs={{0,1},{1,2},{2,3},{3,0},{4,5},{5,6},{6,7},{7,4},{8,9},{9,10},{10,1... | collective-permute-start | bytes 983048 | tf_op jit(solution)/shard_map/ppermute | solution.py:535
  197.7 14.0 %collective-permute-start.37 = (bf16[128,512]{1,0:T(8,128)(2,1)S(1)}, bf16[128,512]{1,0:T(8,128)(2,1)S(1)}, u32[]{:S(2)}, u32[]{:S(2)}) collective-permute-start(bf16[128,512]{1,0:T(8,128)(2,1)S(1)} %add.23), channel_id=1, source_target_pairs={{0,1},{1,2},{2,3},{3,0},{4,5},{5,6},{6,7},{7,4},{8,9},{9,10},{10,1... | collective-permute-start | bytes 393224 | tf_op jit(solution)/shard_map/ppermute | solution.py:535
  201.9 16.6 %collective-permute-start.34 = (bf16[128,768]{1,0:T(8,128)(2,1)S(1)}, bf16[128,768]{1,0:T(8,128)(2,1)S(1)}, u32[]{:S(2)}, u32[]{:S(2)}) collective-permute-start(bf16[128,768]{1,0:T(8,128)(2,1)S(1)} %add.22), channel_id=1, source_target_pairs={{0,1},{1,2},{2,3},{3,0},{4,5},{5,6},{6,7},{7,4},{8,9},{9,10},{10,1... | collective-permute-start | bytes 589832 | tf_op jit(solution)/shard_map/ppermute | solution.py:535
  (19 other events, 193.7 us)

commit v12 on v11

--- a/solution.py
+++ b/solution.py
@@ -533,7 +533,7 @@
         totals, arrivals = [term[1] for term in terms], []
         for d in range(2, n_s + 1):
             arrivals.append([lax.ppermute(total, "sp", right) for total in totals])
-            others = behind if d == n_s - 1 else []
+            others = behind if d == (2 if level == 1 else n_s - 1) else []
             if d < n_s:
                 totals = [add(after(a, *others), term[d]) for a, term in zip(arrivals[-1], terms)]
         where = [
@@ -541,8 +541,8 @@
             for group in groups
         ]
         rounds.append(([term[0] for term in terms], arrivals, where))
-        gate = arrivals[-1] if level == 0 else arrivals[min(1, n_s - 2)]
-        behind = arrivals[-1][:1] if level else []
+        gate = arrivals[min(1, n_s - 2)]
+        behind = arrivals[-1][:1] if level else arrivals[-1]
 
     mixed = None
     for chosen in (rounds[:-1], rounds[-1:]):

time: 220 us -> 228 us (1.036)
  starting transfers between devices: 23.7 us -> 32.3 us
    ppermute x18, starting transfers between devices: 3.94 us -> 13.9 us  [body(): arrivals.append([lax.ppermute(total, 'sp', right) for total in totals])]
    ppermute x18, waiting for transfers between devices: 86 us -> 76.7 us  [body(): arrivals.append([lax.ppermute(total, 'sp', right) for total in totals])]
    ppermute x18, waiting for transfers between devices: 47.8 us -> 55.4 us  [swapped(): return lax.ppermute(array, 'fsdp', [(i, i ^ mask) for i in range(n_f)])]
    ppermute x1, starting transfers between devices: 3.51 us -> 0.45 us  [body(): behind = lax.ppermute(halves[1], 'sp', left)]
    ppermute x1, waiting for transfers between devices: 2.53 us -> 4.85 us  [body(): ahead = lax.ppermute(ahead, 'sp', right)]
  transfers between devices with their start and end apart: 40 -> 40, of which waited for: 27 -> 20; matrix products, arithmetic and copies ran while one was open for 0% -> 0% of each run, Pallas kernels for 13% -> 12%
where the time goes in v12:
time: 228 us
  waiting for transfers between devices  163 us (71%)
  starting transfers between devices  32.3 us (14%)
  Pallas kernels  30.1 us (13%)
    ppermute x18, waiting for transfers between devices, body(): arrivals.append([lax.ppermute(total, 'sp', right) for total in totals])  76.7 us
    ppermute x18, waiting for transfers between devices, swapped(): return lax.ppermute(array, 'fsdp', [(i, i ^ mask) for i in range(n_f)])  55.4 us
    ppermute x1, waiting for transfers between devices, body(): behind = lax.ppermute(behind, 'sp', left)  26 us
    ppermute x18, starting transfers between devices, body(): arrivals.append([lax.ppermute(total, 'sp', right) for total in totals])  13.9 us
    ppermute x18, starting transfers between devices, swapped(): return lax.ppermute(array, 'fsdp', [(i, i ^ mask) for i in range(n_f)])  11.2 us
    pallas_call x2, Pallas kernels, partial(): pl.pallas_call(functools.partial(partial_kernel, len(blocks), counts, wid...  8.87 us
    pallas_call x6, Pallas kernels, mix(): pl.pallas_call(functools.partial(mix_kernel, len(parts)), in_specs=[VMEM]...  8.3 us
    ppermute x1, starting transfers between devices, body(): behind = lax.ppermute(behind, 'sp', left)  5.1 us
  transfers between devices with their start and end apart: 40, of which 20 were waited for; matrix products, arithmetic and copies ran while one was open for 0% of the time, Pallas kernels for 12%

profile of v12, /device:TPU:0, one launch (start us, length us, event | category | flops | bytes accessed | tf_op | source)
XLA Modules:
  0.0 228.2 jit_solution(10626898693352589375)
XLA Ops:
  3.5 5.1 %collective-permute-start.1 = (bf16[128,5120]{1,0:T(8,128)(2,1)S(1)}, bf16[128,5120]{1,0:T(8,128)(2,1)S(1)}, u32[]{:S(2)}, u32[]{:S(2)}) collective-permute-start(bf16[128,5120]{1,0:T(8,128)(2,1)S(1)} %norm.1.refs_0_), channel_id=1, source_target_pairs={{0,3},{1,0},{2,1},{3,2},{4,7},{5,4},{6,5},{7,6},{8,11},{9,8},{10,9... | collective-permute-start | bytes 3932168 | tf_op jit(solution)/shard_map/ppermute | solution.py:479
  11.8 26.0 %collective-permute-done.1.ref.refs_2_ = bf16[128,5120]{1,0:T(8,128)(2,1)S(1)} collective-permute-done((bf16[128,5120]{1,0:T(8,128)(2,1)S(1)}, bf16[128,5120]{1,0:T(8,128)(2,1)S(1)}, u32[]{:S(2)}, u32[]{:S(2)}) %collective-permute-start.1) | collective-permute-done | bytes 1310752 | tf_op jit(solution)/shard_map/ppermute | solution.py:479
  37.9 22.3 %collective-permute-done.6.ref.refs_5_.refs_4_ = bf16[640,1792]{1,0:T(8,128)(2,1)S(1)} collective-permute-done((bf16[640,1792]{1,0:T(8,128)(2,1)S(1)}, bf16[640,1792]{1,0:T(8,128)(2,1)S(1)}, u32[]{:S(2)}, u32[]{:S(2)}) %collective-permute-start.6) | collective-permute-done | bytes 2293792 | tf_op jit(solution)/shard_map/ppermute | solution.py:398
  62.0 4.9 %collective-permute-done.ref.refs_1_ = bf16[128,5120]{1,0:T(8,128)(2,1)S(1)} collective-permute-done((bf16[128,5120]{1,0:T(8,128)(2,1)S(1)}, bf16[128,5120]{1,0:T(8,128)(2,1)S(1)}, u32[]{:S(2)}, u32[]{:S(2)}) %collective-permute-start) | collective-permute-done | bytes 1310752 | tf_op jit(solution)/shard_map/ppermute | solution.py:478
  69.9 1.6 collective-permute-start.2
  71.5 6.6 %partial.2.refs_9_ = f32[384,1792]{1,0:T(8,128)S(1)} custom-call(bf16[128,5120]{1,0:T(8,128)(2,1)S(1)} %norm.1.refs_0_, bf16[128,5120]{1,0:T(8,128)(2,1)S(1)} %collective-permute-done.ref.refs_1_, bf16[128,5120]{1,0:T(8,128)(2,1)S(1)} %collective-permute-done.1.ref.refs_2_, bf16[640,1792]{1,0:T(8,128)(2,1)S(1)} %pack.1.refs_3_.refs_2_, ...), custom_call_target="tpu_custom_call" | custom-call | flops 5284823040 | tf_op jit(solution)/shard_map/partial/pallas_call | solution.py:141
  78.1 10.2 %collective-permute-done.7.refs_7_ = bf16[640,768]{1,0:T(8,128)(2,1)S(1)} collective-permute-done((bf16[640,768]{1,0:T(8,128)(2,1)S(1)}, bf16[640,768]{1,0:T(8,128)(2,1)S(1)}, u32[]{:S(2)}, u32[]{:S(2)}) %collective-permute-start.7) | collective-permute-done | bytes 983072 | tf_op jit(solution)/shard_map/ppermute | solution.py:398
  88.3 8.3 %collective-permute-done.5.refs_5_ = bf16[640,1024]{1,0:T(8,128)(2,1)S(1)} collective-permute-done((bf16[640,1024]{1,0:T(8,128)(2,1)S(1)}, bf16[640,1024]{1,0:T(8,128)(2,1)S(1)}, u32[]{:S(2)}, u32[]{:S(2)}) %collective-permute-start.5) | collective-permute-done | bytes 1310752 | tf_op jit(solution)/shard_map/ppermute | solution.py:398
  98.5 2.3 %partial.3.refs_10_ = f32[128,1792]{1,0:T(8,128)S(1)} custom-call(bf16[64,5120]{1,0:T(8,128)(2,1)S(1)} %collective-permute-done.2.refs_0_.refs_3_, bf16[64,5120]{1,0:T(8,128)(2,1)S(1)} %collective-permute-done.3.refs_1_.refs_4_, bf16[640,1792]{1,0:T(8,128)(2,1)S(1)} %pack.1.refs_3_.refs_2_, bf16[640,1792]{1,0:T(8,128)(2,1)S(1)} %collective-permute-done.8.refs_4_.refs_3_, ...), custom_call_target="tpu_custom_call" | custom-call | tf_op jit(solution)/shard_map/partial/pallas_call | solution.py:141
  101.2 3.7 %finish.1 = (bf16[512,1280]{1,0:T(8,128)(2,1)S(1)}, bf16[512,512]{1,0:T(8,128)(2,1)S(1)}) custom-call(s32[2]{0:T(128)S(1)} %pad_add_fusion.index_ref, bf16[128,5120]{1,0:T(8,128)(2,1)S(1)} %norm.1.refs_0_, bf16[128,5120]{1,0:T(8,128)(2,1)S(1)} %collective-permute-done.ref.refs_1_, bf16[128,5120]{1,0:T(8,128)(2,1)S(1)} %collective-permute-done.1.ref.refs_2_, ...), custom_call_target="tpu_custom_call" | custom-call | tf_op jit(solution)/shard_map/finish/pallas_call | solution.py:217
  104.9 4.0 %attend.1.heads_ref = bf16[512,1280]{1,0:T(8,128)(2,1)S(1)} custom-call(s32[2]{0:T(128)S(1)} %pad_add_fusion.index_ref, bf16[512,1280]{1,0:T(8,128)(2,1)S(1)} %get-tuple-element.60.q_ref, bf16[512,512]{1,0:T(8,128)(2,1)S(1)} %get-tuple-element.61.kv_ref), custom_call_target="tpu_custom_call" | custom-call | tf_op jit(solution)/shard_map/attend/pallas_call | solution.py:288
  110.1 1.9 collective-permute-start.16
  113.2 3.0 %collective-permute-start.13 = (bf16[128,640]{1,0:T(8,128)(2,1)S(1)}, bf16[128,640]{1,0:T(8,128)(2,1)S(1)}, u32[]{:S(2)}, u32[]{:S(2)}) collective-permute-start(bf16[128,640]{1,0:T(8,128)(2,1)S(1)} %get-tuple-element.63), channel_id=1, source_target_pairs={{0,1},{1,2},{2,3},{3,0},{4,5},{5,6},{6,7},{7,4},{8,9},{9,10},{10,1... | collective-permute-start | bytes 491528 | tf_op jit(solution)/shard_map/ppermute | solution.py:535
  116.2 4.3 %collective-permute-done.16.a_ref = bf16[128,640]{1,0:T(8,128)(2,1)S(1)} collective-permute-done((bf16[128,640]{1,0:T(8,128)(2,1)S(1)}, bf16[128,640]{1,0:T(8,128)(2,1)S(1)}, u32[]{:S(2)}, u32[]{:S(2)}) %collective-permute-start.16) | collective-permute-done | bytes 163872 | tf_op jit(solution)/shard_map/ppermute | solution.py:535
  120.6 3.1 %collective-permute-done.13.a_ref = bf16[128,640]{1,0:T(8,128)(2,1)S(1)} collective-permute-done((bf16[128,640]{1,0:T(8,128)(2,1)S(1)}, bf16[128,640]{1,0:T(8,128)(2,1)S(1)}, u32[]{:S(2)}, u32[]{:S(2)}) %collective-permute-start.13) | collective-permute-done | bytes 163872 | tf_op jit(solution)/shard_map/ppermute | solution.py:535
  123.8 10.9 %collective-permute-done.19.refs_1_.ref = bf16[640,1280]{1,0:T(8,128)(2,1)S(1)} collective-permute-done((bf16[640,1280]{1,0:T(8,128)(2,1)S(1)}, bf16[640,1280]{1,0:T(8,128)(2,1)S(1)}, u32[]{:S(2)}, u32[]{:S(2)}) %collective-permute-start.19) | collective-permute-done | bytes 1638432 | tf_op jit(solution)/shard_map/ppermute | solution.py:398
  135.3 1.6 collective-permute-start.28
  137.0 1.7 collective-permute-start.22
  138.7 1.9 mix.8
  140.6 2.9 %collective-permute-start.20 = (bf16[128,1280]{1,0:T(8,128)(2,1)S(1)}, bf16[128,1280]{1,0:T(8,128)(2,1)S(1)}, u32[]{:S(2)}, u32[]{:S(2)}) collective-permute-start(bf16[128,1280]{1,0:T(8,128)(2,1)S(1)} %get-tuple-element.70), channel_id=1, source_target_pairs={{0,1},{1,2},{2,3},{3,0},{4,5},{5,6},{6,7},{7,4},{8,9},{9,10},{10,1... | collective-permute-start | bytes 983048 | tf_op jit(solution)/shard_map/ppermute | solution.py:535
  143.5 1.9 mix.9
  145.4 1.8 collective-permute-start.26
  148.2 16.1 %collective-permute-done.21.refs_0_ = bf16[128,640]{1,0:T(8,128)(2,1)S(1)} collective-permute-done((bf16[128,640]{1,0:T(8,128)(2,1)S(1)}, bf16[128,640]{1,0:T(8,128)(2,1)S(1)}, u32[]{:S(2)}, u32[]{:S(2)}) %collective-permute-start.21) | collective-permute-done | bytes 163872 | tf_op jit(solution)/shard_map/ppermute | solution.py:535
  165.7 11.2 %collective-permute-done.23.a_ref = bf16[128,1280]{1,0:T(8,128)(2,1)S(1)} collective-permute-done((bf16[128,1280]{1,0:T(8,128)(2,1)S(1)}, bf16[128,1280]{1,0:T(8,128)(2,1)S(1)}, u32[]{:S(2)}, u32[]{:S(2)}) %collective-permute-start.23) | collective-permute-done | bytes 327712 | tf_op jit(solution)/shard_map/ppermute | solution.py:535
  176.9 5.7 %collective-permute-done.27.a_ref = bf16[128,1280]{1,0:T(8,128)(2,1)S(1)} collective-permute-done((bf16[128,1280]{1,0:T(8,128)(2,1)S(1)}, bf16[128,1280]{1,0:T(8,128)(2,1)S(1)}, u32[]{:S(2)}, u32[]{:S(2)}) %collective-permute-start.27) | collective-permute-done | bytes 327712 | tf_op jit(solution)/shard_map/ppermute | solution.py:535
  183.1 2.1 collective-permute-done.30.refs_1_
  188.3 7.7 %collective-permute-done.31.a_ref = bf16[128,768]{1,0:T(8,128)(2,1)S(1)} collective-permute-done((bf16[128,768]{1,0:T(8,128)(2,1)S(1)}, bf16[128,768]{1,0:T(8,128)(2,1)S(1)}, u32[]{:S(2)}, u32[]{:S(2)}) %collective-permute-start.31) | collective-permute-done | bytes 196640 | tf_op jit(solution)/shard_map/ppermute | solution.py:535
  196.3 9.6 %collective-permute-done.36.a_ref = bf16[128,512]{1,0:T(8,128)(2,1)S(1)} collective-permute-done((bf16[128,512]{1,0:T(8,128)(2,1)S(1)}, bf16[128,512]{1,0:T(8,128)(2,1)S(1)}, u32[]{:S(2)}, u32[]{:S(2)}) %collective-permute-start.36) | collective-permute-done | bytes 131104 | tf_op jit(solution)/shard_map/ppermute | solution.py:535
  206.0 4.1 %collective-permute-done.32.a_ref = bf16[128,768]{1,0:T(8,128)(2,1)S(1)} collective-permute-done((bf16[128,768]{1,0:T(8,128)(2,1)S(1)}, bf16[128,768]{1,0:T(8,128)(2,1)S(1)}, u32[]{:S(2)}, u32[]{:S(2)}) %collective-permute-start.32) | collective-permute-done | bytes 196640 | tf_op jit(solution)/shard_map/ppermute | solution.py:535
  210.2 9.7 %collective-permute-done.37.a_ref = bf16[128,512]{1,0:T(8,128)(2,1)S(1)} collective-permute-done((bf16[128,512]{1,0:T(8,128)(2,1)S(1)}, bf16[128,512]{1,0:T(8,128)(2,1)S(1)}, u32[]{:S(2)}, u32[]{:S(2)}) %collective-permute-start.37) | collective-permute-done | bytes 131104 | tf_op jit(solution)/shard_map/ppermute | solution.py:535
  220.0 1.6 place.2.refs_4_
  221.6 5.2 %collective-permute-done.38.refs_1_ = bf16[128,512]{1,0:T(8,128)(2,1)S(1)} collective-permute-done((bf16[128,512]{1,0:T(8,128)(2,1)S(1)}, bf16[128,512]{1,0:T(8,128)(2,1)S(1)}, u32[]{:S(2)}, u32[]{:S(2)}) %collective-permute-start.38) | collective-permute-done | bytes 131104 | tf_op jit(solution)/shard_map/ppermute | solution.py:535
  (103 shorter events, 25.0 us)
Async XLA Ops:
  3.5 34.3 %collective-permute-start.1 = (bf16[128,5120]{1,0:T(8,128)(2,1)S(1)}, bf16[128,5120]{1,0:T(8,128)(2,1)S(1)}, u32[]{:S(2)}, u32[]{:S(2)}) collective-permute-start(bf16[128,5120]{1,0:T(8,128)(2,1)S(1)} %norm.1.refs_0_), channel_id=1, source_target_pairs={{0,3},{1,0},{2,1},{3,2},{4,7},{5,4},{6,5},{7,6},{8,11},{9,8},{10,9... | collective-permute-start | bytes 3932168 | tf_op jit(solution)/shard_map/ppermute | solution.py:479
  8.7 51.4 %collective-permute-start.6 = (bf16[640,1792]{1,0:T(8,128)(2,1)S(1)}, bf16[640,1792]{1,0:T(8,128)(2,1)S(1)}, u32[]{:S(2)}, u32[]{:S(2)}) collective-permute-start(bf16[640,1792]{1,0:T(8,128)(2,1)S(1)} %pack.1.refs_3_.refs_2_), channel_id=1, source_target_pairs={{0,8},{4,12},{8,0},{12,4},{16,24},{20,28},{24,16},{28,20},{1,9},{5... | collective-permute-start | bytes 6881288 | tf_op jit(solution)/shard_map/ppermute | solution.py:398
  10.3 51.0 %collective-permute-start.4 = (bf16[640,1792]{1,0:T(8,128)(2,1)S(1)}, bf16[640,1792]{1,0:T(8,128)(2,1)S(1)}, u32[]{:S(2)}, u32[]{:S(2)}) collective-permute-start(bf16[640,1792]{1,0:T(8,128)(2,1)S(1)} %pack.1.refs_3_.refs_2_), channel_id=1, source_target_pairs={{0,16},{4,20},{8,24},{12,28},{16,0},{20,4},{24,8},{28,12},{1,17},{... | collective-permute-start | bytes 6881288 | tf_op jit(solution)/shard_map/ppermute | solution.py:398
  11.8 55.0 %collective-permute-start = (bf16[128,5120]{1,0:T(8,128)(2,1)S(1)}, bf16[128,5120]{1,0:T(8,128)(2,1)S(1)}, u32[]{:S(2)}, u32[]{:S(2)}) collective-permute-start(bf16[128,5120]{1,0:T(8,128)(2,1)S(1)} %norm.1.refs_0_), channel_id=1, source_target_pairs={{0,1},{1,2},{2,3},{3,0},{4,5},{5,6},{6,7},{7,4},{8,9},{9,10},{10,1... | collective-permute-start | bytes 3932168 | tf_op jit(solution)/shard_map/ppermute | solution.py:478
  11.8 56.5 %collective-permute-start.8 = (bf16[640,1792]{1,0:T(8,128)(2,1)S(1)}, bf16[640,1792]{1,0:T(8,128)(2,1)S(1)}, u32[]{:S(2)}, u32[]{:S(2)}) collective-permute-start(bf16[640,1792]{1,0:T(8,128)(2,1)S(1)} %pack.1.refs_3_.refs_2_), channel_id=1, source_target_pairs={{0,4},{4,0},{8,12},{12,8},{16,20},{20,16},{24,28},{28,24},{1,5},{5... | collective-permute-start | bytes 6881288 | tf_op jit(solution)/shard_map/ppermute | solution.py:398
  60.1 9.8 %collective-permute-start.9 = (bf16[640,1792]{1,0:T(8,128)(2,1)S(1)}, bf16[640,1792]{1,0:T(8,128)(2,1)S(1)}, u32[]{:S(2)}, u32[]{:S(2)}) collective-permute-start(bf16[640,1792]{1,0:T(8,128)(2,1)S(1)} %collective-permute-done.6.ref.refs_5_.refs_4_), channel_id=1, source_target_pairs={{0,4},{4,0},{8,12},{12,8},{16,20},{20,16},{24,28},{28,24},{1,5},{5... | collective-permute-start | bytes 6881288 | tf_op jit(solution)/shard_map/ppermute | solution.py:398
  61.3 10.1 %collective-permute-start.10 = (bf16[640,1792]{1,0:T(8,128)(2,1)S(1)}, bf16[640,1792]{1,0:T(8,128)(2,1)S(1)}, u32[]{:S(2)}, u32[]{:S(2)}) collective-permute-start(bf16[640,1792]{1,0:T(8,128)(2,1)S(1)} %collective-permute-done.4.ref.refs_7_.refs_6_), channel_id=1, source_target_pairs={{0,4},{4,0},{8,12},{12,8},{16,20},{20,16},{24,28},{28,24},{1,5},{5... | collective-permute-start | bytes 6881288 | tf_op jit(solution)/shard_map/ppermute | solution.py:398
  61.3 35.7 %collective-permute-start.3 = (bf16[64,5120]{1,0:T(8,128)(2,1)S(1)}, bf16[64,5120]{1,0:T(8,128)(2,1)S(1)}, u32[]{:S(2)}, u32[]{:S(2)}) collective-permute-start(bf16[64,5120]{1,0:T(8,128)(2,1)S(1)} %cut.7), channel_id=1, source_target_pairs={{0,3},{1,0},{2,1},{3,2},{4,7},{5,4},{6,5},{7,6},{8,11},{9,8},{10,9... | collective-permute-start | bytes 1966088 | tf_op jit(solution)/shard_map/ppermute | solution.py:483
  66.8 21.5 %collective-permute-start.7 = (bf16[640,768]{1,0:T(8,128)(2,1)S(1)}, bf16[640,768]{1,0:T(8,128)(2,1)S(1)}, u32[]{:S(2)}, u32[]{:S(2)}) collective-permute-start(bf16[640,768]{1,0:T(8,128)(2,1)S(1)} %cut.9), channel_id=1, source_target_pairs={{0,16},{4,20},{8,24},{12,28},{16,0},{20,4},{24,8},{28,12},{1,17},{... | collective-permute-start | bytes 2949128 | tf_op jit(solution)/shard_map/ppermute | solution.py:398
  68.3 28.2 %collective-permute-start.5 = (bf16[640,1024]{1,0:T(8,128)(2,1)S(1)}, bf16[640,1024]{1,0:T(8,128)(2,1)S(1)}, u32[]{:S(2)}, u32[]{:S(2)}) collective-permute-start(bf16[640,1024]{1,0:T(8,128)(2,1)S(1)} %cut.8), channel_id=1, source_target_pairs={{0,8},{4,12},{8,0},{12,4},{16,24},{20,28},{24,16},{28,20},{1,9},{5... | collective-permute-start | bytes 3932168 | tf_op jit(solution)/shard_map/ppermute | solution.py:398
  69.9 28.7 %collective-permute-start.2 = (bf16[64,5120]{1,0:T(8,128)(2,1)S(1)}, bf16[64,5120]{1,0:T(8,128)(2,1)S(1)}, u32[]{:S(2)}, u32[]{:S(2)}) collective-permute-start(bf16[64,5120]{1,0:T(8,128)(2,1)S(1)} %cut.6), channel_id=1, source_target_pairs={{0,1},{1,2},{2,3},{3,0},{4,5},{5,6},{6,7},{7,4},{8,9},{9,10},{10,1... | collective-permute-start | bytes 1966088 | tf_op jit(solution)/shard_map/ppermute | solution.py:482
  71.5 37.4 %collective-permute-start.15 = (bf16[640,1280]{1,0:T(8,128)(2,1)S(1)}, bf16[640,1280]{1,0:T(8,128)(2,1)S(1)}, u32[]{:S(2)}, u32[]{:S(2)}) collective-permute-start(bf16[640,1280]{1,0:T(8,128)(2,1)S(1)} %copy-done.10), channel_id=1, source_target_pairs={{0,4},{4,0},{8,12},{12,8},{16,20},{20,16},{24,28},{28,24},{1,5},{5... | collective-permute-start | bytes 4915208 | tf_op jit(solution)/shard_map/ppermute | solution.py:398
  96.5 38.2 %collective-permute-start.19 = (bf16[640,1280]{1,0:T(8,128)(2,1)S(1)}, bf16[640,1280]{1,0:T(8,128)(2,1)S(1)}, u32[]{:S(2)}, u32[]{:S(2)}) collective-permute-start(bf16[640,1280]{1,0:T(8,128)(2,1)S(1)} %copy-done.10), channel_id=1, source_target_pairs={{0,16},{4,20},{8,24},{12,28},{16,0},{20,4},{24,8},{28,12},{1,17},{... | collective-permute-start | bytes 4915208 | tf_op jit(solution)/shard_map/ppermute | solution.py:398
  97.1 37.9 %collective-permute-start.18 = (bf16[640,1280]{1,0:T(8,128)(2,1)S(1)}, bf16[640,1280]{1,0:T(8,128)(2,1)S(1)}, u32[]{:S(2)}, u32[]{:S(2)}) collective-permute-start(bf16[640,1280]{1,0:T(8,128)(2,1)S(1)} %copy-done.10), channel_id=1, source_target_pairs={{0,8},{4,12},{8,0},{12,4},{16,24},{20,28},{24,16},{28,20},{1,9},{5... | collective-permute-start | bytes 4915208 | tf_op jit(solution)/shard_map/ppermute | solution.py:398
  110.1 10.4 %collective-permute-start.16 = (bf16[128,640]{1,0:T(8,128)(2,1)S(1)}, bf16[128,640]{1,0:T(8,128)(2,1)S(1)}, u32[]{:S(2)}, u32[]{:S(2)}) collective-permute-start(bf16[128,640]{1,0:T(8,128)(2,1)S(1)} %get-tuple-element.66), channel_id=1, source_target_pairs={{0,1},{1,2},{2,3},{3,0},{4,5},{5,6},{6,7},{7,4},{8,9},{9,10},{10,1... | collective-permute-start | bytes 491528 | tf_op jit(solution)/shard_map/ppermute | solution.py:535
  113.2 10.5 %collective-permute-start.13 = (bf16[128,640]{1,0:T(8,128)(2,1)S(1)}, bf16[128,640]{1,0:T(8,128)(2,1)S(1)}, u32[]{:S(2)}, u32[]{:S(2)}) collective-permute-start(bf16[128,640]{1,0:T(8,128)(2,1)S(1)} %get-tuple-element.63), channel_id=1, source_target_pairs={{0,1},{1,2},{2,3},{3,0},{4,5},{5,6},{6,7},{7,4},{8,9},{9,10},{10,1... | collective-permute-start | bytes 491528 | tf_op jit(solution)/shard_map/ppermute | solution.py:535
  120.6 14.2 %collective-permute-start.17 = (bf16[128,640]{1,0:T(8,128)(2,1)S(1)}, bf16[128,640]{1,0:T(8,128)(2,1)S(1)}, u32[]{:S(2)}, u32[]{:S(2)}) collective-permute-start(bf16[128,640]{1,0:T(8,128)(2,1)S(1)} %add.15), channel_id=1, source_target_pairs={{0,1},{1,2},{2,3},{3,0},{4,5},{5,6},{6,7},{7,4},{8,9},{9,10},{10,1... | collective-permute-start | bytes 491528 | tf_op jit(solution)/shard_map/ppermute | solution.py:535
  123.8 11.0 %collective-permute-start.14 = (bf16[128,640]{1,0:T(8,128)(2,1)S(1)}, bf16[128,640]{1,0:T(8,128)(2,1)S(1)}, u32[]{:S(2)}, u32[]{:S(2)}) collective-permute-start(bf16[128,640]{1,0:T(8,128)(2,1)S(1)} %add.14), channel_id=1, source_target_pairs={{0,1},{1,2},{2,3},{3,0},{4,5},{5,6},{6,7},{7,4},{8,9},{9,10},{10,1... | collective-permute-start | bytes 491528 | tf_op jit(solution)/shard_map/ppermute | solution.py:535
  135.3 41.5 %collective-permute-start.28 = (bf16[384,1280]{1,0:T(8,128)(2,1)S(1)}, bf16[384,1280]{1,0:T(8,128)(2,1)S(1)}, u32[]{:S(2)}, u32[]{:S(2)}) collective-permute-start(bf16[384,1280]{1,0:T(8,128)(2,1)S(1)} %cut.10), channel_id=1, source_target_pairs={{0,8},{4,12},{8,0},{12,4},{16,24},{20,28},{24,16},{28,20},{1,9},{5... | collective-permute-start | bytes 2949128 | tf_op jit(solution)/shard_map/ppermute | solution.py:398
  137.0 11.0 %collective-permute-start.22 = (bf16[128,640]{1,0:T(8,128)(2,1)S(1)}, bf16[128,640]{1,0:T(8,128)(2,1)S(1)}, u32[]{:S(2)}, u32[]{:S(2)}) collective-permute-start(bf16[128,640]{1,0:T(8,128)(2,1)S(1)} %add.17), channel_id=1, source_target_pairs={{0,1},{1,2},{2,3},{3,0},{4,5},{5,6},{6,7},{7,4},{8,9},{9,10},{10,1... | collective-permute-start | bytes 491528 | tf_op jit(solution)/shard_map/ppermute | solution.py:535
  140.6 23.8 %collective-permute-start.20 = (bf16[128,1280]{1,0:T(8,128)(2,1)S(1)}, bf16[128,1280]{1,0:T(8,128)(2,1)S(1)}, u32[]{:S(2)}, u32[]{:S(2)}) collective-permute-start(bf16[128,1280]{1,0:T(8,128)(2,1)S(1)} %get-tuple-element.70), channel_id=1, source_target_pairs={{0,1},{1,2},{2,3},{3,0},{4,5},{5,6},{6,7},{7,4},{8,9},{9,10},{10,1... | collective-permute-start | bytes 983048 | tf_op jit(solution)/shard_map/ppermute | solution.py:535
  145.4 19.1 %collective-permute-start.26 = (bf16[128,1280]{1,0:T(8,128)(2,1)S(1)}, bf16[128,1280]{1,0:T(8,128)(2,1)S(1)}, u32[]{:S(2)}, u32[]{:S(2)}) collective-permute-start(bf16[128,1280]{1,0:T(8,128)(2,1)S(1)} %get-tuple-element.77), channel_id=1, source_target_pairs={{0,1},{1,2},{2,3},{3,0},{4,5},{5,6},{6,7},{7,4},{8,9},{9,10},{10,1... | collective-permute-start | bytes 983048 | tf_op jit(solution)/shard_map/ppermute | solution.py:535
  147.2 29.7 %collective-permute-start.29 = (bf16[256,1280]{1,0:T(8,128)(2,1)S(1)}, bf16[256,1280]{1,0:T(8,128)(2,1)S(1)}, u32[]{:S(2)}, u32[]{:S(2)}) collective-permute-start(bf16[256,1280]{1,0:T(8,128)(2,1)S(1)} %cut.11), channel_id=1, source_target_pairs={{0,16},{4,20},{8,24},{12,28},{16,0},{20,4},{24,8},{28,12},{1,17},{... | collective-permute-start | bytes 1966088 | tf_op jit(solution)/shard_map/ppermute | solution.py:398
  148.1 16.3 %collective-permute-start.21 = (bf16[128,640]{1,0:T(8,128)(2,1)S(1)}, bf16[128,640]{1,0:T(8,128)(2,1)S(1)}, u32[]{:S(2)}, u32[]{:S(2)}) collective-permute-start(bf16[128,640]{1,0:T(8,128)(2,1)S(1)} %add.16), channel_id=1, source_target_pairs={{0,1},{1,2},{2,3},{3,0},{4,5},{5,6},{6,7},{7,4},{8,9},{9,10},{10,1... | collective-permute-start | bytes 491528 | tf_op jit(solution)/shard_map/ppermute | solution.py:535
  164.4 12.5 %collective-permute-start.23 = (bf16[128,1280]{1,0:T(8,128)(2,1)S(1)}, bf16[128,1280]{1,0:T(8,128)(2,1)S(1)}, u32[]{:S(2)}, u32[]{:S(2)}) collective-permute-start(bf16[128,1280]{1,0:T(8,128)(2,1)S(1)} %add.18), channel_id=1, source_target_pairs={{0,1},{1,2},{2,3},{3,0},{4,5},{5,6},{6,7},{7,4},{8,9},{9,10},{10,1... | collective-permute-start | bytes 983048 | tf_op jit(solution)/shard_map/ppermute | solution.py:535
  164.6 18.1 %collective-permute-start.27 = (bf16[128,1280]{1,0:T(8,128)(2,1)S(1)}, bf16[128,1280]{1,0:T(8,128)(2,1)S(1)}, u32[]{:S(2)}, u32[]{:S(2)}) collective-permute-start(bf16[128,1280]{1,0:T(8,128)(2,1)S(1)} %add.19), channel_id=1, source_target_pairs={{0,1},{1,2},{2,3},{3,0},{4,5},{5,6},{6,7},{7,4},{8,9},{9,10},{10,1... | collective-permute-start | bytes 983048 | tf_op jit(solution)/shard_map/ppermute | solution.py:535
  186.6 19.4 %collective-permute-start.33 = (bf16[128,1280]{1,0:T(8,128)(2,1)S(1)}, bf16[128,1280]{1,0:T(8,128)(2,1)S(1)}, u32[]{:S(2)}, u32[]{:S(2)}) collective-permute-start(bf16[128,1280]{1,0:T(8,128)(2,1)S(1)} %add.21), channel_id=1, source_target_pairs={{0,1},{1,2},{2,3},{3,0},{4,5},{5,6},{6,7},{7,4},{8,9},{9,10},{10,1... | collective-permute-start | bytes 983048 | tf_op jit(solution)/shard_map/ppermute | solution.py:535
  187.5 18.3 %collective-permute-start.36 = (bf16[128,512]{1,0:T(8,128)(2,1)S(1)}, bf16[128,512]{1,0:T(8,128)(2,1)S(1)}, u32[]{:S(2)}, u32[]{:S(2)}) collective-permute-start(bf16[128,512]{1,0:T(8,128)(2,1)S(1)} %get-tuple-element.90), channel_id=1, source_target_pairs={{0,1},{1,2},{2,3},{3,0},{4,5},{5,6},{6,7},{7,4},{8,9},{9,10},{10,1... | collective-permute-start | bytes 393224 | tf_op jit(solution)/shard_map/ppermute | solution.py:535
  196.1 14.0 %collective-permute-start.32 = (bf16[128,768]{1,0:T(8,128)(2,1)S(1)}, bf16[128,768]{1,0:T(8,128)(2,1)S(1)}, u32[]{:S(2)}, u32[]{:S(2)}) collective-permute-start(bf16[128,768]{1,0:T(8,128)(2,1)S(1)} %add.20), channel_id=1, source_target_pairs={{0,1},{1,2},{2,3},{3,0},{4,5},{5,6},{6,7},{7,4},{8,9},{9,10},{10,1... | collective-permute-start | bytes 589832 | tf_op jit(solution)/shard_map/ppermute | solution.py:535
  196.2 23.8 %collective-permute-start.39 = (bf16[128,1280]{1,0:T(8,128)(2,1)S(1)}, bf16[128,1280]{1,0:T(8,128)(2,1)S(1)}, u32[]{:S(2)}, u32[]{:S(2)}) collective-permute-start(bf16[128,1280]{1,0:T(8,128)(2,1)S(1)} %add.25), channel_id=1, source_target_pairs={{0,1},{1,2},{2,3},{3,0},{4,5},{5,6},{6,7},{7,4},{8,9},{9,10},{10,1... | collective-permute-start | bytes 983048 | tf_op jit(solution)/shard_map/ppermute | solution.py:535
  205.9 14.0 %collective-permute-start.37 = (bf16[128,512]{1,0:T(8,128)(2,1)S(1)}, bf16[128,512]{1,0:T(8,128)(2,1)S(1)}, u32[]{:S(2)}, u32[]{:S(2)}) collective-permute-start(bf16[128,512]{1,0:T(8,128)(2,1)S(1)} %add.23), channel_id=1, source_target_pairs={{0,1},{1,2},{2,3},{3,0},{4,5},{5,6},{6,7},{7,4},{8,9},{9,10},{10,1... | collective-permute-start | bytes 393224 | tf_op jit(solution)/shard_map/ppermute | solution.py:535
  210.1 16.6 %collective-permute-start.34 = (bf16[128,768]{1,0:T(8,128)(2,1)S(1)}, bf16[128,768]{1,0:T(8,128)(2,1)S(1)}, u32[]{:S(2)}, u32[]{:S(2)}) collective-permute-start(bf16[128,768]{1,0:T(8,128)(2,1)S(1)} %add.22), channel_id=1, source_target_pairs={{0,1},{1,2},{2,3},{3,0},{4,5},{5,6},{6,7},{7,4},{8,9},{9,10},{10,1... | collective-permute-start | bytes 589832 | tf_op jit(solution)/shard_map/ppermute | solution.py:535
  (19 other events, 195.7 us)

commit v13 on v11

--- a/solution.py
+++ b/solution.py
@@ -533,7 +533,7 @@
         totals, arrivals = [term[1] for term in terms], []
         for d in range(2, n_s + 1):
             arrivals.append([lax.ppermute(total, "sp", right) for total in totals])
-            others = behind if d == n_s - 1 else []
+            others = behind if d == 2 else []
             if d < n_s:
                 totals = [add(after(a, *others), term[d]) for a, term in zip(arrivals[-1], terms)]
         where = [

time: 220 us -> 219 us (level)
  transfers between devices with their start and end apart: 40 -> 40, of which waited for: 27 -> 28; matrix products, arithmetic and copies ran while one was open for 0% -> 0% of each run, Pallas kernels for 13% -> 13%
where the time goes in v13:
time: 219 us
  waiting for transfers between devices  163 us (74%)
  Pallas kernels  30.1 us (14%)
  starting transfers between devices  23 us (11%)
  local copies, waits for them, and re-layouts  2.2 us (1%)
    ppermute x18, waiting for transfers between devices, body(): arrivals.append([lax.ppermute(total, 'sp', right) for total in totals])  85.9 us
    ppermute x18, waiting for transfers between devices, swapped(): return lax.ppermute(array, 'fsdp', [(i, i ^ mask) for i in range(n_f)])  47.6 us
    ppermute x1, waiting for transfers between devices, body(): behind = lax.ppermute(behind, 'sp', left)  26 us
    ppermute x18, starting transfers between devices, swapped(): return lax.ppermute(array, 'fsdp', [(i, i ^ mask) for i in range(n_f)])  11.1 us
    pallas_call x2, Pallas kernels, partial(): pl.pallas_call(functools.partial(partial_kernel, len(blocks), counts, wid...  8.88 us
    pallas_call x6, Pallas kernels, mix(): pl.pallas_call(functools.partial(mix_kernel, len(parts)), in_specs=[VMEM]...  8.27 us
    ppermute x1, starting transfers between devices, body(): behind = lax.ppermute(behind, 'sp', left)  5.1 us
  transfers between devices with their start and end apart: 40, of which 28 were waited for; matrix products, arithmetic and copies ran while one was open for 0% of the time, Pallas kernels for 13%

profile of v13, /device:TPU:0, one launch (start us, length us, event | category | flops | bytes accessed | tf_op | source)
XLA Modules:
  0.0 219.2 jit_solution(3702680697181764583)
XLA Ops:
  3.5 5.1 %collective-permute-start.1 = (bf16[128,5120]{1,0:T(8,128)(2,1)S(1)}, bf16[128,5120]{1,0:T(8,128)(2,1)S(1)}, u32[]{:S(2)}, u32[]{:S(2)}) collective-permute-start(bf16[128,5120]{1,0:T(8,128)(2,1)S(1)} %norm.1.refs_0_), channel_id=1, source_target_pairs={{0,3},{1,0},{2,1},{3,2},{4,7},{5,4},{6,5},{7,6},{8,11},{9,8},{10,9... | collective-permute-start | bytes 3932168 | tf_op jit(solution)/shard_map/ppermute | solution.py:479
  11.8 26.0 %collective-permute-done.1.ref.refs_2_ = bf16[128,5120]{1,0:T(8,128)(2,1)S(1)} collective-permute-done((bf16[128,5120]{1,0:T(8,128)(2,1)S(1)}, bf16[128,5120]{1,0:T(8,128)(2,1)S(1)}, u32[]{:S(2)}, u32[]{:S(2)}) %collective-permute-start.1) | collective-permute-done | bytes 1310752 | tf_op jit(solution)/shard_map/ppermute | solution.py:479
  37.9 22.3 %collective-permute-done.6.ref.refs_5_.refs_4_ = bf16[640,1792]{1,0:T(8,128)(2,1)S(1)} collective-permute-done((bf16[640,1792]{1,0:T(8,128)(2,1)S(1)}, bf16[640,1792]{1,0:T(8,128)(2,1)S(1)}, u32[]{:S(2)}, u32[]{:S(2)}) %collective-permute-start.6) | collective-permute-done | bytes 2293792 | tf_op jit(solution)/shard_map/ppermute | solution.py:398
  63.1 2.5 %collective-permute-done.ref.refs_1_ = bf16[128,5120]{1,0:T(8,128)(2,1)S(1)} collective-permute-done((bf16[128,5120]{1,0:T(8,128)(2,1)S(1)}, bf16[128,5120]{1,0:T(8,128)(2,1)S(1)}, u32[]{:S(2)}, u32[]{:S(2)}) %collective-permute-start) | collective-permute-done | bytes 1310752 | tf_op jit(solution)/shard_map/ppermute | solution.py:478
  67.2 3.5 %collective-permute-start.3 = (bf16[64,5120]{1,0:T(8,128)(2,1)S(1)}, bf16[64,5120]{1,0:T(8,128)(2,1)S(1)}, u32[]{:S(2)}, u32[]{:S(2)}) collective-permute-start(bf16[64,5120]{1,0:T(8,128)(2,1)S(1)} %cut.7), channel_id=1, source_target_pairs={{0,3},{1,0},{2,1},{3,2},{4,7},{5,4},{6,5},{7,6},{8,11},{9,8},{10,9... | collective-permute-start | bytes 1966088 | tf_op jit(solution)/shard_map/ppermute | solution.py:483
  70.8 6.6 %partial.2.refs_9_ = f32[384,1792]{1,0:T(8,128)S(1)} custom-call(bf16[128,5120]{1,0:T(8,128)(2,1)S(1)} %norm.1.refs_0_, bf16[128,5120]{1,0:T(8,128)(2,1)S(1)} %collective-permute-done.ref.refs_1_, bf16[128,5120]{1,0:T(8,128)(2,1)S(1)} %collective-permute-done.1.ref.refs_2_, bf16[640,1792]{1,0:T(8,128)(2,1)S(1)} %pack.1.refs_3_.refs_2_, ...), custom_call_target="tpu_custom_call" | custom-call | flops 5284823040 | tf_op jit(solution)/shard_map/partial/pallas_call | solution.py:141
  77.4 8.2 %collective-permute-done.7.refs_7_ = bf16[640,768]{1,0:T(8,128)(2,1)S(1)} collective-permute-done((bf16[640,768]{1,0:T(8,128)(2,1)S(1)}, bf16[640,768]{1,0:T(8,128)(2,1)S(1)}, u32[]{:S(2)}, u32[]{:S(2)}) %collective-permute-start.7) | collective-permute-done | bytes 983072 | tf_op jit(solution)/shard_map/ppermute | solution.py:398
  85.6 9.6 %collective-permute-done.5.refs_5_ = bf16[640,1024]{1,0:T(8,128)(2,1)S(1)} collective-permute-done((bf16[640,1024]{1,0:T(8,128)(2,1)S(1)}, bf16[640,1024]{1,0:T(8,128)(2,1)S(1)}, u32[]{:S(2)}, u32[]{:S(2)}) %collective-permute-start.5) | collective-permute-done | bytes 1310752 | tf_op jit(solution)/shard_map/ppermute | solution.py:398
  99.5 2.3 %partial.3.refs_10_ = f32[128,1792]{1,0:T(8,128)S(1)} custom-call(bf16[64,5120]{1,0:T(8,128)(2,1)S(1)} %collective-permute-done.2.refs_0_.refs_3_, bf16[64,5120]{1,0:T(8,128)(2,1)S(1)} %collective-permute-done.3.refs_1_.refs_4_, bf16[640,1792]{1,0:T(8,128)(2,1)S(1)} %pack.1.refs_3_.refs_2_, bf16[640,1792]{1,0:T(8,128)(2,1)S(1)} %collective-permute-done.8.refs_4_.refs_3_, ...), custom_call_target="tpu_custom_call" | custom-call | tf_op jit(solution)/shard_map/partial/pallas_call | solution.py:141
  102.1 3.7 %finish.1 = (bf16[512,1280]{1,0:T(8,128)(2,1)S(1)}, bf16[512,512]{1,0:T(8,128)(2,1)S(1)}) custom-call(s32[2]{0:T(128)S(1)} %pad_add_fusion.index_ref, bf16[128,5120]{1,0:T(8,128)(2,1)S(1)} %norm.1.refs_0_, bf16[128,5120]{1,0:T(8,128)(2,1)S(1)} %collective-permute-done.ref.refs_1_, bf16[128,5120]{1,0:T(8,128)(2,1)S(1)} %collective-permute-done.1.ref.refs_2_, ...), custom_call_target="tpu_custom_call" | custom-call | tf_op jit(solution)/shard_map/finish/pallas_call | solution.py:217
  105.8 4.0 %attend.1.heads_ref = bf16[512,1280]{1,0:T(8,128)(2,1)S(1)} custom-call(s32[2]{0:T(128)S(1)} %pad_add_fusion.index_ref, bf16[512,1280]{1,0:T(8,128)(2,1)S(1)} %get-tuple-element.58.q_ref, bf16[512,512]{1,0:T(8,128)(2,1)S(1)} %get-tuple-element.59.kv_ref), custom_call_target="tpu_custom_call" | custom-call | tf_op jit(solution)/shard_map/attend/pallas_call | solution.py:288
  111.0 1.7 collective-permute-start.17
  114.1 5.8 %collective-permute-done.17.a_ref = bf16[128,640]{1,0:T(8,128)(2,1)S(1)} collective-permute-done((bf16[128,640]{1,0:T(8,128)(2,1)S(1)}, bf16[128,640]{1,0:T(8,128)(2,1)S(1)}, u32[]{:S(2)}, u32[]{:S(2)}) %collective-permute-start.17) | collective-permute-done | bytes 163872 | tf_op jit(solution)/shard_map/ppermute | solution.py:535
  120.0 2.8 %collective-permute-done.13.a_ref = bf16[128,640]{1,0:T(8,128)(2,1)S(1)} collective-permute-done((bf16[128,640]{1,0:T(8,128)(2,1)S(1)}, bf16[128,640]{1,0:T(8,128)(2,1)S(1)}, u32[]{:S(2)}, u32[]{:S(2)}) %collective-permute-start.13) | collective-permute-done | bytes 163872 | tf_op jit(solution)/shard_map/ppermute | solution.py:535
  123.3 4.0 %collective-permute-done.18.a_ref = bf16[128,640]{1,0:T(8,128)(2,1)S(1)} collective-permute-done((bf16[128,640]{1,0:T(8,128)(2,1)S(1)}, bf16[128,640]{1,0:T(8,128)(2,1)S(1)}, u32[]{:S(2)}, u32[]{:S(2)}) %collective-permute-start.18) | collective-permute-done | bytes 163872 | tf_op jit(solution)/shard_map/ppermute | solution.py:535
  127.5 4.3 %collective-permute-done.14.a_ref = bf16[128,640]{1,0:T(8,128)(2,1)S(1)} collective-permute-done((bf16[128,640]{1,0:T(8,128)(2,1)S(1)}, bf16[128,640]{1,0:T(8,128)(2,1)S(1)}, u32[]{:S(2)}, u32[]{:S(2)}) %collective-permute-start.14) | collective-permute-done | bytes 163872 | tf_op jit(solution)/shard_map/ppermute | solution.py:535
  131.9 1.6 collective-permute-done.21.refs_1_.ref
  133.5 1.7 collective-permute-done.19.refs_1_
  135.2 3.8 %collective-permute-done.15.refs_0_ = bf16[128,640]{1,0:T(8,128)(2,1)S(1)} collective-permute-done((bf16[128,640]{1,0:T(8,128)(2,1)S(1)}, bf16[128,640]{1,0:T(8,128)(2,1)S(1)}, u32[]{:S(2)}, u32[]{:S(2)}) %collective-permute-start.15) | collective-permute-done | bytes 163872 | tf_op jit(solution)/shard_map/ppermute | solution.py:535
  140.3 1.9 mix.8
  142.5 2.3 %collective-permute-done.24.refs_0_ = bf16[640,1280]{1,0:T(8,128)(2,1)S(1)} collective-permute-done((bf16[640,1280]{1,0:T(8,128)(2,1)S(1)}, bf16[640,1280]{1,0:T(8,128)(2,1)S(1)}, u32[]{:S(2)}, u32[]{:S(2)}) %collective-permute-start.24) | collective-permute-done | bytes 1638432 | tf_op jit(solution)/shard_map/ppermute | solution.py:398
  144.8 1.9 mix.9
  147.0 7.7 %collective-permute-done.22.a_ref = bf16[128,1280]{1,0:T(8,128)(2,1)S(1)} collective-permute-done((bf16[128,1280]{1,0:T(8,128)(2,1)S(1)}, bf16[128,1280]{1,0:T(8,128)(2,1)S(1)}, u32[]{:S(2)}, u32[]{:S(2)}) %collective-permute-start.22) | collective-permute-done | bytes 327712 | tf_op jit(solution)/shard_map/ppermute | solution.py:535
  154.8 6.9 %collective-permute-done.26.a_ref = bf16[128,1280]{1,0:T(8,128)(2,1)S(1)} collective-permute-done((bf16[128,1280]{1,0:T(8,128)(2,1)S(1)}, bf16[128,1280]{1,0:T(8,128)(2,1)S(1)}, u32[]{:S(2)}, u32[]{:S(2)}) %collective-permute-start.26) | collective-permute-done | bytes 327712 | tf_op jit(solution)/shard_map/ppermute | solution.py:535
  161.8 6.9 %collective-permute-done.23.a_ref = bf16[128,1280]{1,0:T(8,128)(2,1)S(1)} collective-permute-done((bf16[128,1280]{1,0:T(8,128)(2,1)S(1)}, bf16[128,1280]{1,0:T(8,128)(2,1)S(1)}, u32[]{:S(2)}, u32[]{:S(2)}) %collective-permute-start.23) | collective-permute-done | bytes 327712 | tf_op jit(solution)/shard_map/ppermute | solution.py:535
  168.7 5.7 %collective-permute-done.27.a_ref = bf16[128,1280]{1,0:T(8,128)(2,1)S(1)} collective-permute-done((bf16[128,1280]{1,0:T(8,128)(2,1)S(1)}, bf16[128,1280]{1,0:T(8,128)(2,1)S(1)}, u32[]{:S(2)}, u32[]{:S(2)}) %collective-permute-start.27) | collective-permute-done | bytes 327712 | tf_op jit(solution)/shard_map/ppermute | solution.py:535
  175.1 1.9 collective-permute-done.30.refs_1_
  179.3 8.2 %collective-permute-done.32.refs_2_ = bf16[128,1280]{1,0:T(8,128)(2,1)S(1)} collective-permute-done((bf16[128,1280]{1,0:T(8,128)(2,1)S(1)}, bf16[128,1280]{1,0:T(8,128)(2,1)S(1)}, u32[]{:S(2)}, u32[]{:S(2)}) %collective-permute-start.32) | collective-permute-done | bytes 327712 | tf_op jit(solution)/shard_map/ppermute | solution.py:535
  187.5 4.2 %collective-permute-done.31.a_ref = bf16[128,768]{1,0:T(8,128)(2,1)S(1)} collective-permute-done((bf16[128,768]{1,0:T(8,128)(2,1)S(1)}, bf16[128,768]{1,0:T(8,128)(2,1)S(1)}, u32[]{:S(2)}, u32[]{:S(2)}) %collective-permute-start.31) | collective-permute-done | bytes 196640 | tf_op jit(solution)/shard_map/ppermute | solution.py:535
  193.7 7.8 %collective-permute-done.33.a_ref = bf16[128,768]{1,0:T(8,128)(2,1)S(1)} collective-permute-done((bf16[128,768]{1,0:T(8,128)(2,1)S(1)}, bf16[128,768]{1,0:T(8,128)(2,1)S(1)}, u32[]{:S(2)}, u32[]{:S(2)}) %collective-permute-start.33) | collective-permute-done | bytes 196640 | tf_op jit(solution)/shard_map/ppermute | solution.py:535
  201.6 9.3 %collective-permute-done.37.a_ref = bf16[128,512]{1,0:T(8,128)(2,1)S(1)} collective-permute-done((bf16[128,512]{1,0:T(8,128)(2,1)S(1)}, bf16[128,512]{1,0:T(8,128)(2,1)S(1)}, u32[]{:S(2)}, u32[]{:S(2)}) %collective-permute-start.37) | collective-permute-done | bytes 131104 | tf_op jit(solution)/shard_map/ppermute | solution.py:535
  212.5 5.2 %collective-permute-done.38.refs_1_ = bf16[128,512]{1,0:T(8,128)(2,1)S(1)} collective-permute-done((bf16[128,512]{1,0:T(8,128)(2,1)S(1)}, bf16[128,512]{1,0:T(8,128)(2,1)S(1)}, u32[]{:S(2)}, u32[]{:S(2)}) %collective-permute-start.38) | collective-permute-done | bytes 131104 | tf_op jit(solution)/shard_map/ppermute | solution.py:535
  (103 shorter events, 29.2 us)
Async XLA Ops:
  3.5 34.3 %collective-permute-start.1 = (bf16[128,5120]{1,0:T(8,128)(2,1)S(1)}, bf16[128,5120]{1,0:T(8,128)(2,1)S(1)}, u32[]{:S(2)}, u32[]{:S(2)}) collective-permute-start(bf16[128,5120]{1,0:T(8,128)(2,1)S(1)} %norm.1.refs_0_), channel_id=1, source_target_pairs={{0,3},{1,0},{2,1},{3,2},{4,7},{5,4},{6,5},{7,6},{8,11},{9,8},{10,9... | collective-permute-start | bytes 3932168 | tf_op jit(solution)/shard_map/ppermute | solution.py:479
  8.7 51.4 %collective-permute-start.6 = (bf16[640,1792]{1,0:T(8,128)(2,1)S(1)}, bf16[640,1792]{1,0:T(8,128)(2,1)S(1)}, u32[]{:S(2)}, u32[]{:S(2)}) collective-permute-start(bf16[640,1792]{1,0:T(8,128)(2,1)S(1)} %pack.1.refs_3_.refs_2_), channel_id=1, source_target_pairs={{0,8},{4,12},{8,0},{12,4},{16,24},{20,28},{24,16},{28,20},{1,9},{5... | collective-permute-start | bytes 6881288 | tf_op jit(solution)/shard_map/ppermute | solution.py:398
  10.3 51.0 %collective-permute-start.4 = (bf16[640,1792]{1,0:T(8,128)(2,1)S(1)}, bf16[640,1792]{1,0:T(8,128)(2,1)S(1)}, u32[]{:S(2)}, u32[]{:S(2)}) collective-permute-start(bf16[640,1792]{1,0:T(8,128)(2,1)S(1)} %pack.1.refs_3_.refs_2_), channel_id=1, source_target_pairs={{0,16},{4,20},{8,24},{12,28},{16,0},{20,4},{24,8},{28,12},{1,17},{... | collective-permute-start | bytes 6881288 | tf_op jit(solution)/shard_map/ppermute | solution.py:398
  11.8 53.8 %collective-permute-start = (bf16[128,5120]{1,0:T(8,128)(2,1)S(1)}, bf16[128,5120]{1,0:T(8,128)(2,1)S(1)}, u32[]{:S(2)}, u32[]{:S(2)}) collective-permute-start(bf16[128,5120]{1,0:T(8,128)(2,1)S(1)} %norm.1.refs_0_), channel_id=1, source_target_pairs={{0,1},{1,2},{2,3},{3,0},{4,5},{5,6},{6,7},{7,4},{8,9},{9,10},{10,1... | collective-permute-start | bytes 3932168 | tf_op jit(solution)/shard_map/ppermute | solution.py:478
  11.8 55.3 %collective-permute-start.8 = (bf16[640,1792]{1,0:T(8,128)(2,1)S(1)}, bf16[640,1792]{1,0:T(8,128)(2,1)S(1)}, u32[]{:S(2)}, u32[]{:S(2)}) collective-permute-start(bf16[640,1792]{1,0:T(8,128)(2,1)S(1)} %pack.1.refs_3_.refs_2_), channel_id=1, source_target_pairs={{0,4},{4,0},{8,12},{12,8},{16,20},{20,16},{24,28},{28,24},{1,5},{5... | collective-permute-start | bytes 6881288 | tf_op jit(solution)/shard_map/ppermute | solution.py:398
  60.1 10.6 %collective-permute-start.9 = (bf16[640,1792]{1,0:T(8,128)(2,1)S(1)}, bf16[640,1792]{1,0:T(8,128)(2,1)S(1)}, u32[]{:S(2)}, u32[]{:S(2)}) collective-permute-start(bf16[640,1792]{1,0:T(8,128)(2,1)S(1)} %collective-permute-done.6.ref.refs_5_.refs_4_), channel_id=1, source_target_pairs={{0,4},{4,0},{8,12},{12,8},{16,20},{20,16},{24,28},{28,24},{1,5},{5... | collective-permute-start | bytes 6881288 | tf_op jit(solution)/shard_map/ppermute | solution.py:398
  61.3 9.4 %collective-permute-start.10 = (bf16[640,1792]{1,0:T(8,128)(2,1)S(1)}, bf16[640,1792]{1,0:T(8,128)(2,1)S(1)}, u32[]{:S(2)}, u32[]{:S(2)}) collective-permute-start(bf16[640,1792]{1,0:T(8,128)(2,1)S(1)} %collective-permute-done.4.ref.refs_7_.refs_6_), channel_id=1, source_target_pairs={{0,4},{4,0},{8,12},{12,8},{16,20},{20,16},{24,28},{28,24},{1,5},{5... | collective-permute-start | bytes 6881288 | tf_op jit(solution)/shard_map/ppermute | solution.py:398
  61.4 24.2 %collective-permute-start.7 = (bf16[640,768]{1,0:T(8,128)(2,1)S(1)}, bf16[640,768]{1,0:T(8,128)(2,1)S(1)}, u32[]{:S(2)}, u32[]{:S(2)}) collective-permute-start(bf16[640,768]{1,0:T(8,128)(2,1)S(1)} %cut.9), channel_id=1, source_target_pairs={{0,16},{4,20},{8,24},{12,28},{16,0},{20,4},{24,8},{28,12},{1,17},{... | collective-permute-start | bytes 2949128 | tf_op jit(solution)/shard_map/ppermute | solution.py:398
  65.6 29.6 %collective-permute-start.5 = (bf16[640,1024]{1,0:T(8,128)(2,1)S(1)}, bf16[640,1024]{1,0:T(8,128)(2,1)S(1)}, u32[]{:S(2)}, u32[]{:S(2)}) collective-permute-start(bf16[640,1024]{1,0:T(8,128)(2,1)S(1)} %cut.8), channel_id=1, source_target_pairs={{0,8},{4,12},{8,0},{12,4},{16,24},{20,28},{24,16},{28,20},{1,9},{5... | collective-permute-start | bytes 3932168 | tf_op jit(solution)/shard_map/ppermute | solution.py:398
  67.2 29.6 %collective-permute-start.3 = (bf16[64,5120]{1,0:T(8,128)(2,1)S(1)}, bf16[64,5120]{1,0:T(8,128)(2,1)S(1)}, u32[]{:S(2)}, u32[]{:S(2)}) collective-permute-start(bf16[64,5120]{1,0:T(8,128)(2,1)S(1)} %cut.7), channel_id=1, source_target_pairs={{0,3},{1,0},{2,1},{3,2},{4,7},{5,4},{6,5},{7,6},{8,11},{9,8},{10,9... | collective-permute-start | bytes 1966088 | tf_op jit(solution)/shard_map/ppermute | solution.py:483
  70.7 28.8 %collective-permute-start.2 = (bf16[64,5120]{1,0:T(8,128)(2,1)S(1)}, bf16[64,5120]{1,0:T(8,128)(2,1)S(1)}, u32[]{:S(2)}, u32[]{:S(2)}) collective-permute-start(bf16[64,5120]{1,0:T(8,128)(2,1)S(1)} %cut.6), channel_id=1, source_target_pairs={{0,1},{1,2},{2,3},{3,0},{4,5},{5,6},{6,7},{7,4},{8,9},{9,10},{10,1... | collective-permute-start | bytes 1966088 | tf_op jit(solution)/shard_map/ppermute | solution.py:482
  70.7 39.1 %collective-permute-start.16 = (bf16[640,1280]{1,0:T(8,128)(2,1)S(1)}, bf16[640,1280]{1,0:T(8,128)(2,1)S(1)}, u32[]{:S(2)}, u32[]{:S(2)}) collective-permute-start(bf16[640,1280]{1,0:T(8,128)(2,1)S(1)} %copy-done.10), channel_id=1, source_target_pairs={{0,4},{4,0},{8,12},{12,8},{16,20},{20,16},{24,28},{28,24},{1,5},{5... | collective-permute-start | bytes 4915208 | tf_op jit(solution)/shard_map/ppermute | solution.py:398
  95.3 38.2 %collective-permute-start.21 = (bf16[640,1280]{1,0:T(8,128)(2,1)S(1)}, bf16[640,1280]{1,0:T(8,128)(2,1)S(1)}, u32[]{:S(2)}, u32[]{:S(2)}) collective-permute-start(bf16[640,1280]{1,0:T(8,128)(2,1)S(1)} %copy-done.10), channel_id=1, source_target_pairs={{0,16},{4,20},{8,24},{12,28},{16,0},{20,4},{24,8},{28,12},{1,17},{... | collective-permute-start | bytes 4915208 | tf_op jit(solution)/shard_map/ppermute | solution.py:398
  96.8 42.2 %collective-permute-start.20 = (bf16[640,1280]{1,0:T(8,128)(2,1)S(1)}, bf16[640,1280]{1,0:T(8,128)(2,1)S(1)}, u32[]{:S(2)}, u32[]{:S(2)}) collective-permute-start(bf16[640,1280]{1,0:T(8,128)(2,1)S(1)} %copy-done.10), channel_id=1, source_target_pairs={{0,8},{4,12},{8,0},{12,4},{16,24},{20,28},{24,16},{28,20},{1,9},{5... | collective-permute-start | bytes 4915208 | tf_op jit(solution)/shard_map/ppermute | solution.py:398
  111.0 8.9 %collective-permute-start.17 = (bf16[128,640]{1,0:T(8,128)(2,1)S(1)}, bf16[128,640]{1,0:T(8,128)(2,1)S(1)}, u32[]{:S(2)}, u32[]{:S(2)}) collective-permute-start(bf16[128,640]{1,0:T(8,128)(2,1)S(1)} %get-tuple-element.65), channel_id=1, source_target_pairs={{0,1},{1,2},{2,3},{3,0},{4,5},{5,6},{6,7},{7,4},{8,9},{9,10},{10,1... | collective-permute-start | bytes 491528 | tf_op jit(solution)/shard_map/ppermute | solution.py:535
  113.9 8.8 %collective-permute-start.13 = (bf16[128,640]{1,0:T(8,128)(2,1)S(1)}, bf16[128,640]{1,0:T(8,128)(2,1)S(1)}, u32[]{:S(2)}, u32[]{:S(2)}) collective-permute-start(bf16[128,640]{1,0:T(8,128)(2,1)S(1)} %get-tuple-element.61), channel_id=1, source_target_pairs={{0,1},{1,2},{2,3},{3,0},{4,5},{5,6},{6,7},{7,4},{8,9},{9,10},{10,1... | collective-permute-start | bytes 491528 | tf_op jit(solution)/shard_map/ppermute | solution.py:535
  119.9 7.5 %collective-permute-start.18 = (bf16[128,640]{1,0:T(8,128)(2,1)S(1)}, bf16[128,640]{1,0:T(8,128)(2,1)S(1)}, u32[]{:S(2)}, u32[]{:S(2)}) collective-permute-start(bf16[128,640]{1,0:T(8,128)(2,1)S(1)} %add.16), channel_id=1, source_target_pairs={{0,1},{1,2},{2,3},{3,0},{4,5},{5,6},{6,7},{7,4},{8,9},{9,10},{10,1... | collective-permute-start | bytes 491528 | tf_op jit(solution)/shard_map/ppermute | solution.py:535
  122.8 9.0 %collective-permute-start.14 = (bf16[128,640]{1,0:T(8,128)(2,1)S(1)}, bf16[128,640]{1,0:T(8,128)(2,1)S(1)}, u32[]{:S(2)}, u32[]{:S(2)}) collective-permute-start(bf16[128,640]{1,0:T(8,128)(2,1)S(1)} %add.14), channel_id=1, source_target_pairs={{0,1},{1,2},{2,3},{3,0},{4,5},{5,6},{6,7},{7,4},{8,9},{9,10},{10,1... | collective-permute-start | bytes 491528 | tf_op jit(solution)/shard_map/ppermute | solution.py:535
  127.4 7.7 %collective-permute-start.19 = (bf16[128,640]{1,0:T(8,128)(2,1)S(1)}, bf16[128,640]{1,0:T(8,128)(2,1)S(1)}, u32[]{:S(2)}, u32[]{:S(2)}) collective-permute-start(bf16[128,640]{1,0:T(8,128)(2,1)S(1)} %add.17), channel_id=1, source_target_pairs={{0,1},{1,2},{2,3},{3,0},{4,5},{5,6},{6,7},{7,4},{8,9},{9,10},{10,1... | collective-permute-start | bytes 491528 | tf_op jit(solution)/shard_map/ppermute | solution.py:535
  139.6 29.2 %collective-permute-start.28 = (bf16[384,1280]{1,0:T(8,128)(2,1)S(1)}, bf16[384,1280]{1,0:T(8,128)(2,1)S(1)}, u32[]{:S(2)}, u32[]{:S(2)}) collective-permute-start(bf16[384,1280]{1,0:T(8,128)(2,1)S(1)} %cut.10), channel_id=1, source_target_pairs={{0,8},{4,12},{8,0},{12,4},{16,24},{20,28},{24,16},{28,20},{1,9},{5... | collective-permute-start | bytes 2949128 | tf_op jit(solution)/shard_map/ppermute | solution.py:398
  142.2 12.5 %collective-permute-start.22 = (bf16[128,1280]{1,0:T(8,128)(2,1)S(1)}, bf16[128,1280]{1,0:T(8,128)(2,1)S(1)}, u32[]{:S(2)}, u32[]{:S(2)}) collective-permute-start(bf16[128,1280]{1,0:T(8,128)(2,1)S(1)} %get-tuple-element.70), channel_id=1, source_target_pairs={{0,1},{1,2},{2,3},{3,0},{4,5},{5,6},{6,7},{7,4},{8,9},{9,10},{10,1... | collective-permute-start | bytes 983048 | tf_op jit(solution)/shard_map/ppermute | solution.py:535
  146.7 15.0 %collective-permute-start.26 = (bf16[128,1280]{1,0:T(8,128)(2,1)S(1)}, bf16[128,1280]{1,0:T(8,128)(2,1)S(1)}, u32[]{:S(2)}, u32[]{:S(2)}) collective-permute-start(bf16[128,1280]{1,0:T(8,128)(2,1)S(1)} %get-tuple-element.74), channel_id=1, source_target_pairs={{0,1},{1,2},{2,3},{3,0},{4,5},{5,6},{6,7},{7,4},{8,9},{9,10},{10,1... | collective-permute-start | bytes 983048 | tf_op jit(solution)/shard_map/ppermute | solution.py:535
  146.8 21.9 %collective-permute-start.29 = (bf16[256,1280]{1,0:T(8,128)(2,1)S(1)}, bf16[256,1280]{1,0:T(8,128)(2,1)S(1)}, u32[]{:S(2)}, u32[]{:S(2)}) collective-permute-start(bf16[256,1280]{1,0:T(8,128)(2,1)S(1)} %cut.11), channel_id=1, source_target_pairs={{0,16},{4,20},{8,24},{12,28},{16,0},{20,4},{24,8},{28,12},{1,17},{... | collective-permute-start | bytes 1966088 | tf_op jit(solution)/shard_map/ppermute | solution.py:398
  154.8 14.0 %collective-permute-start.23 = (bf16[128,1280]{1,0:T(8,128)(2,1)S(1)}, bf16[128,1280]{1,0:T(8,128)(2,1)S(1)}, u32[]{:S(2)}, u32[]{:S(2)}) collective-permute-start(bf16[128,1280]{1,0:T(8,128)(2,1)S(1)} %add.18), channel_id=1, source_target_pairs={{0,1},{1,2},{2,3},{3,0},{4,5},{5,6},{6,7},{7,4},{8,9},{9,10},{10,1... | collective-permute-start | bytes 983048 | tf_op jit(solution)/shard_map/ppermute | solution.py:535
  161.8 12.7 %collective-permute-start.27 = (bf16[128,1280]{1,0:T(8,128)(2,1)S(1)}, bf16[128,1280]{1,0:T(8,128)(2,1)S(1)}, u32[]{:S(2)}, u32[]{:S(2)}) collective-permute-start(bf16[128,1280]{1,0:T(8,128)(2,1)S(1)} %add.19), channel_id=1, source_target_pairs={{0,1},{1,2},{2,3},{3,0},{4,5},{5,6},{6,7},{7,4},{8,9},{9,10},{10,1... | collective-permute-start | bytes 983048 | tf_op jit(solution)/shard_map/ppermute | solution.py:535
  175.1 12.4 %collective-permute-start.32 = (bf16[128,1280]{1,0:T(8,128)(2,1)S(1)}, bf16[128,1280]{1,0:T(8,128)(2,1)S(1)}, u32[]{:S(2)}, u32[]{:S(2)}) collective-permute-start(bf16[128,1280]{1,0:T(8,128)(2,1)S(1)} %add.20), channel_id=1, source_target_pairs={{0,1},{1,2},{2,3},{3,0},{4,5},{5,6},{6,7},{7,4},{8,9},{9,10},{10,1... | collective-permute-start | bytes 983048 | tf_op jit(solution)/shard_map/ppermute | solution.py:535
  178.3 13.5 %collective-permute-start.31 = (bf16[128,768]{1,0:T(8,128)(2,1)S(1)}, bf16[128,768]{1,0:T(8,128)(2,1)S(1)}, u32[]{:S(2)}, u32[]{:S(2)}) collective-permute-start(bf16[128,768]{1,0:T(8,128)(2,1)S(1)} %get-tuple-element.80), channel_id=1, source_target_pairs={{0,1},{1,2},{2,3},{3,0},{4,5},{5,6},{6,7},{7,4},{8,9},{9,10},{10,1... | collective-permute-start | bytes 589832 | tf_op jit(solution)/shard_map/ppermute | solution.py:535
  179.2 14.3 %collective-permute-start.36 = (bf16[128,512]{1,0:T(8,128)(2,1)S(1)}, bf16[128,512]{1,0:T(8,128)(2,1)S(1)}, u32[]{:S(2)}, u32[]{:S(2)}) collective-permute-start(bf16[128,512]{1,0:T(8,128)(2,1)S(1)} %get-tuple-element.86), channel_id=1, source_target_pairs={{0,1},{1,2},{2,3},{3,0},{4,5},{5,6},{6,7},{7,4},{8,9},{9,10},{10,1... | collective-permute-start | bytes 393224 | tf_op jit(solution)/shard_map/ppermute | solution.py:535
  191.8 9.7 %collective-permute-start.33 = (bf16[128,768]{1,0:T(8,128)(2,1)S(1)}, bf16[128,768]{1,0:T(8,128)(2,1)S(1)}, u32[]{:S(2)}, u32[]{:S(2)}) collective-permute-start(bf16[128,768]{1,0:T(8,128)(2,1)S(1)} %add.21), channel_id=1, source_target_pairs={{0,1},{1,2},{2,3},{3,0},{4,5},{5,6},{6,7},{7,4},{8,9},{9,10},{10,1... | collective-permute-start | bytes 589832 | tf_op jit(solution)/shard_map/ppermute | solution.py:535
  191.9 19.0 %collective-permute-start.39 = (bf16[128,1280]{1,0:T(8,128)(2,1)S(1)}, bf16[128,1280]{1,0:T(8,128)(2,1)S(1)}, u32[]{:S(2)}, u32[]{:S(2)}) collective-permute-start(bf16[128,1280]{1,0:T(8,128)(2,1)S(1)} %add.25), channel_id=1, source_target_pairs={{0,1},{1,2},{2,3},{3,0},{4,5},{5,6},{6,7},{7,4},{8,9},{9,10},{10,1... | collective-permute-start | bytes 983048 | tf_op jit(solution)/shard_map/ppermute | solution.py:535
  193.6 17.2 %collective-permute-start.37 = (bf16[128,512]{1,0:T(8,128)(2,1)S(1)}, bf16[128,512]{1,0:T(8,128)(2,1)S(1)}, u32[]{:S(2)}, u32[]{:S(2)}) collective-permute-start(bf16[128,512]{1,0:T(8,128)(2,1)S(1)} %add.23), channel_id=1, source_target_pairs={{0,1},{1,2},{2,3},{3,0},{4,5},{5,6},{6,7},{7,4},{8,9},{9,10},{10,1... | collective-permute-start | bytes 393224 | tf_op jit(solution)/shard_map/ppermute | solution.py:535
  201.5 16.2 %collective-permute-start.34 = (bf16[128,768]{1,0:T(8,128)(2,1)S(1)}, bf16[128,768]{1,0:T(8,128)(2,1)S(1)}, u32[]{:S(2)}, u32[]{:S(2)}) collective-permute-start(bf16[128,768]{1,0:T(8,128)(2,1)S(1)} %add.22), channel_id=1, source_target_pairs={{0,1},{1,2},{2,3},{3,0},{4,5},{5,6},{6,7},{7,4},{8,9},{9,10},{10,1... | collective-permute-start | bytes 589832 | tf_op jit(solution)/shard_map/ppermute | solution.py:535
  (19 other events, 193.5 us)

commit v14 on v12

--- a/solution.py
+++ b/solution.py
@@ -533,7 +533,7 @@
         totals, arrivals = [term[1] for term in terms], []
         for d in range(2, n_s + 1):
             arrivals.append([lax.ppermute(total, "sp", right) for total in totals])
-            others = behind if d == (2 if level == 1 else n_s - 1) else []
+            others = behind if level > 1 and d == n_s - 1 else []
             if d < n_s:
                 totals = [add(after(a, *others), term[d]) for a, term in zip(arrivals[-1], terms)]
         where = [
@@ -542,7 +542,7 @@
         ]
         rounds.append(([term[0] for term in terms], arrivals, where))
         gate = arrivals[min(1, n_s - 2)]
-        behind = arrivals[-1][:1] if level else arrivals[-1]
+        behind = (arrivals[-1][:1] if level else []) + rounds[0][1][-1]
 
     mixed = None
     for chosen in (rounds[:-1], rounds[-1:]):

time: 228 us -> 226 us (level)
  waiting for transfers between devices: 163 us -> 159 us
    ppermute x18, waiting for transfers between devices: 76.7 us -> 73.1 us  [body(): arrivals.append([lax.ppermute(total, 'sp', right) for total in totals])]
  transfers between devices with their start and end apart: 40 -> 40, of which waited for: 20 -> 23; matrix products, arithmetic and copies ran while one was open for 0% -> 0% of each run, Pallas kernels for 12% -> 12%
where the time goes in v14:
time: 226 us
  waiting for transfers between devices  159 us (70%)
  starting transfers between devices  33.4 us (15%)
  Pallas kernels  30.1 us (13%)
    ppermute x18, waiting for transfers between devices, body(): arrivals.append([lax.ppermute(total, 'sp', right) for total in totals])  73.1 us
    ppermute x18, waiting for transfers between devices, swapped(): return lax.ppermute(array, 'fsdp', [(i, i ^ mask) for i in range(n_f)])  55.5 us
    ppermute x1, waiting for transfers between devices, body(): behind = lax.ppermute(behind, 'sp', left)  26 us
    ppermute x18, starting transfers between devices, body(): arrivals.append([lax.ppermute(total, 'sp', right) for total in totals])  15 us
    ppermute x18, starting transfers between devices, swapped(): return lax.ppermute(array, 'fsdp', [(i, i ^ mask) for i in range(n_f)])  11.3 us
    pallas_call x2, Pallas kernels, partial(): pl.pallas_call(functools.partial(partial_kernel, len(blocks), counts, wid...  8.87 us
    pallas_call x6, Pallas kernels, mix(): pl.pallas_call(functools.partial(mix_kernel, len(parts)), in_specs=[VMEM]...  8.29 us
    ppermute x1, starting transfers between devices, body(): behind = lax.ppermute(behind, 'sp', left)  5.1 us
  transfers between devices with their start and end apart: 40, of which 23 were waited for; matrix products, arithmetic and copies ran while one was open for 0% of the time, Pallas kernels for 12%

profile of v14, /device:TPU:0, one launch (start us, length us, event | category | flops | bytes accessed | tf_op | source)
XLA Modules:
  0.0 225.8 jit_solution(16478878160665568904)
XLA Ops:
  3.5 5.1 %collective-permute-start.1 = (bf16[128,5120]{1,0:T(8,128)(2,1)S(1)}, bf16[128,5120]{1,0:T(8,128)(2,1)S(1)}, u32[]{:S(2)}, u32[]{:S(2)}) collective-permute-start(bf16[128,5120]{1,0:T(8,128)(2,1)S(1)} %norm.1.refs_0_), channel_id=1, source_target_pairs={{0,3},{1,0},{2,1},{3,2},{4,7},{5,4},{6,5},{7,6},{8,11},{9,8},{10,9... | collective-permute-start | bytes 3932168 | tf_op jit(solution)/shard_map/ppermute | solution.py:479
  11.8 26.0 %collective-permute-done.1.ref.refs_2_ = bf16[128,5120]{1,0:T(8,128)(2,1)S(1)} collective-permute-done((bf16[128,5120]{1,0:T(8,128)(2,1)S(1)}, bf16[128,5120]{1,0:T(8,128)(2,1)S(1)}, u32[]{:S(2)}, u32[]{:S(2)}) %collective-permute-start.1) | collective-permute-done | bytes 1310752 | tf_op jit(solution)/shard_map/ppermute | solution.py:479
  37.9 22.3 %collective-permute-done.6.ref.refs_5_.refs_4_ = bf16[640,1792]{1,0:T(8,128)(2,1)S(1)} collective-permute-done((bf16[640,1792]{1,0:T(8,128)(2,1)S(1)}, bf16[640,1792]{1,0:T(8,128)(2,1)S(1)}, u32[]{:S(2)}, u32[]{:S(2)}) %collective-permute-start.6) | collective-permute-done | bytes 2293792 | tf_op jit(solution)/shard_map/ppermute | solution.py:398
  62.0 4.9 %collective-permute-done.ref.refs_1_ = bf16[128,5120]{1,0:T(8,128)(2,1)S(1)} collective-permute-done((bf16[128,5120]{1,0:T(8,128)(2,1)S(1)}, bf16[128,5120]{1,0:T(8,128)(2,1)S(1)}, u32[]{:S(2)}, u32[]{:S(2)}) %collective-permute-start) | collective-permute-done | bytes 1310752 | tf_op jit(solution)/shard_map/ppermute | solution.py:478
  71.5 6.6 %partial.2.refs_9_ = f32[384,1792]{1,0:T(8,128)S(1)} custom-call(bf16[128,5120]{1,0:T(8,128)(2,1)S(1)} %norm.1.refs_0_, bf16[128,5120]{1,0:T(8,128)(2,1)S(1)} %collective-permute-done.ref.refs_1_, bf16[128,5120]{1,0:T(8,128)(2,1)S(1)} %collective-permute-done.1.ref.refs_2_, bf16[640,1792]{1,0:T(8,128)(2,1)S(1)} %pack.1.refs_3_.refs_2_, ...), custom_call_target="tpu_custom_call" | custom-call | flops 5284823040 | tf_op jit(solution)/shard_map/partial/pallas_call | solution.py:141
  78.1 10.2 %collective-permute-done.7.refs_7_ = bf16[640,768]{1,0:T(8,128)(2,1)S(1)} collective-permute-done((bf16[640,768]{1,0:T(8,128)(2,1)S(1)}, bf16[640,768]{1,0:T(8,128)(2,1)S(1)}, u32[]{:S(2)}, u32[]{:S(2)}) %collective-permute-start.7) | collective-permute-done | bytes 983072 | tf_op jit(solution)/shard_map/ppermute | solution.py:398
  88.3 8.3 %collective-permute-done.5.refs_5_ = bf16[640,1024]{1,0:T(8,128)(2,1)S(1)} collective-permute-done((bf16[640,1024]{1,0:T(8,128)(2,1)S(1)}, bf16[640,1024]{1,0:T(8,128)(2,1)S(1)}, u32[]{:S(2)}, u32[]{:S(2)}) %collective-permute-start.5) | collective-permute-done | bytes 1310752 | tf_op jit(solution)/shard_map/ppermute | solution.py:398
  98.5 2.3 %partial.3.refs_10_ = f32[128,1792]{1,0:T(8,128)S(1)} custom-call(bf16[64,5120]{1,0:T(8,128)(2,1)S(1)} %collective-permute-done.2.refs_0_.refs_3_, bf16[64,5120]{1,0:T(8,128)(2,1)S(1)} %collective-permute-done.3.refs_1_.refs_4_, bf16[640,1792]{1,0:T(8,128)(2,1)S(1)} %pack.1.refs_3_.refs_2_, bf16[640,1792]{1,0:T(8,128)(2,1)S(1)} %collective-permute-done.8.refs_4_.refs_3_, ...), custom_call_target="tpu_custom_call" | custom-call | tf_op jit(solution)/shard_map/partial/pallas_call | solution.py:141
  101.2 3.7 %finish.1 = (bf16[512,1280]{1,0:T(8,128)(2,1)S(1)}, bf16[512,512]{1,0:T(8,128)(2,1)S(1)}) custom-call(s32[2]{0:T(128)S(1)} %pad_add_fusion.index_ref, bf16[128,5120]{1,0:T(8,128)(2,1)S(1)} %norm.1.refs_0_, bf16[128,5120]{1,0:T(8,128)(2,1)S(1)} %collective-permute-done.ref.refs_1_, bf16[128,5120]{1,0:T(8,128)(2,1)S(1)} %collective-permute-done.1.ref.refs_2_, ...), custom_call_target="tpu_custom_call" | custom-call | tf_op jit(solution)/shard_map/finish/pallas_call | solution.py:217
  104.9 4.0 %attend.1.heads_ref = bf16[512,1280]{1,0:T(8,128)(2,1)S(1)} custom-call(s32[2]{0:T(128)S(1)} %pad_add_fusion.index_ref, bf16[512,1280]{1,0:T(8,128)(2,1)S(1)} %get-tuple-element.58.q_ref, bf16[512,512]{1,0:T(8,128)(2,1)S(1)} %get-tuple-element.59.kv_ref), custom_call_target="tpu_custom_call" | custom-call | tf_op jit(solution)/shard_map/attend/pallas_call | solution.py:288
  110.1 1.9 collective-permute-start.16
  113.2 3.0 %collective-permute-start.13 = (bf16[128,640]{1,0:T(8,128)(2,1)S(1)}, bf16[128,640]{1,0:T(8,128)(2,1)S(1)}, u32[]{:S(2)}, u32[]{:S(2)}) collective-permute-start(bf16[128,640]{1,0:T(8,128)(2,1)S(1)} %get-tuple-element.61), channel_id=1, source_target_pairs={{0,1},{1,2},{2,3},{3,0},{4,5},{5,6},{6,7},{7,4},{8,9},{9,10},{10,1... | collective-permute-start | bytes 491528 | tf_op jit(solution)/shard_map/ppermute | solution.py:535
  116.2 4.3 %collective-permute-done.16.a_ref = bf16[128,640]{1,0:T(8,128)(2,1)S(1)} collective-permute-done((bf16[128,640]{1,0:T(8,128)(2,1)S(1)}, bf16[128,640]{1,0:T(8,128)(2,1)S(1)}, u32[]{:S(2)}, u32[]{:S(2)}) %collective-permute-start.16) | collective-permute-done | bytes 163872 | tf_op jit(solution)/shard_map/ppermute | solution.py:535
  120.6 3.1 %collective-permute-done.13.a_ref = bf16[128,640]{1,0:T(8,128)(2,1)S(1)} collective-permute-done((bf16[128,640]{1,0:T(8,128)(2,1)S(1)}, bf16[128,640]{1,0:T(8,128)(2,1)S(1)}, u32[]{:S(2)}, u32[]{:S(2)}) %collective-permute-start.13) | collective-permute-done | bytes 163872 | tf_op jit(solution)/shard_map/ppermute | solution.py:535
  123.8 10.9 %collective-permute-done.19.refs_1_.ref = bf16[640,1280]{1,0:T(8,128)(2,1)S(1)} collective-permute-done((bf16[640,1280]{1,0:T(8,128)(2,1)S(1)}, bf16[640,1280]{1,0:T(8,128)(2,1)S(1)}, u32[]{:S(2)}, u32[]{:S(2)}) %collective-permute-start.19) | collective-permute-done | bytes 1638432 | tf_op jit(solution)/shard_map/ppermute | solution.py:398
  137.0 1.9 mix.8
  138.8 1.7 collective-permute-start.20
  140.6 1.9 mix.9
  142.5 2.9 %collective-permute-start.24 = (bf16[128,1280]{1,0:T(8,128)(2,1)S(1)}, bf16[128,1280]{1,0:T(8,128)(2,1)S(1)}, u32[]{:S(2)}, u32[]{:S(2)}) collective-permute-start(bf16[128,1280]{1,0:T(8,128)(2,1)S(1)} %get-tuple-element.72), channel_id=1, source_target_pairs={{0,1},{1,2},{2,3},{3,0},{4,5},{5,6},{6,7},{7,4},{8,9},{9,10},{10,1... | collective-permute-start | bytes 983048 | tf_op jit(solution)/shard_map/ppermute | solution.py:535
  146.2 6.4 %collective-permute-done.20.a_ref = bf16[128,1280]{1,0:T(8,128)(2,1)S(1)} collective-permute-done((bf16[128,1280]{1,0:T(8,128)(2,1)S(1)}, bf16[128,1280]{1,0:T(8,128)(2,1)S(1)}, u32[]{:S(2)}, u32[]{:S(2)}) %collective-permute-start.20) | collective-permute-done | bytes 327712 | tf_op jit(solution)/shard_map/ppermute | solution.py:535
  152.7 6.9 %collective-permute-done.24.a_ref = bf16[128,1280]{1,0:T(8,128)(2,1)S(1)} collective-permute-done((bf16[128,1280]{1,0:T(8,128)(2,1)S(1)}, bf16[128,1280]{1,0:T(8,128)(2,1)S(1)}, u32[]{:S(2)}, u32[]{:S(2)}) %collective-permute-start.24) | collective-permute-done | bytes 327712 | tf_op jit(solution)/shard_map/ppermute | solution.py:535
  159.7 6.9 %collective-permute-done.21.a_ref = bf16[128,1280]{1,0:T(8,128)(2,1)S(1)} collective-permute-done((bf16[128,1280]{1,0:T(8,128)(2,1)S(1)}, bf16[128,1280]{1,0:T(8,128)(2,1)S(1)}, u32[]{:S(2)}, u32[]{:S(2)}) %collective-permute-start.21) | collective-permute-done | bytes 327712 | tf_op jit(solution)/shard_map/ppermute | solution.py:535
  166.6 6.6 %collective-permute-done.25.a_ref = bf16[128,1280]{1,0:T(8,128)(2,1)S(1)} collective-permute-done((bf16[128,1280]{1,0:T(8,128)(2,1)S(1)}, bf16[128,1280]{1,0:T(8,128)(2,1)S(1)}, u32[]{:S(2)}, u32[]{:S(2)}) %collective-permute-start.25) | collective-permute-done | bytes 327712 | tf_op jit(solution)/shard_map/ppermute | solution.py:535
  173.7 2.1 collective-permute-done.28.refs_1_
  179.2 1.8 collective-permute-start.36
  181.0 2.1 collective-permute-start.33
  183.1 3.4 %collective-permute-done.29.a_ref = bf16[128,768]{1,0:T(8,128)(2,1)S(1)} collective-permute-done((bf16[128,768]{1,0:T(8,128)(2,1)S(1)}, bf16[128,768]{1,0:T(8,128)(2,1)S(1)}, u32[]{:S(2)}, u32[]{:S(2)}) %collective-permute-start.29) | collective-permute-done | bytes 196640 | tf_op jit(solution)/shard_map/ppermute | solution.py:535
  186.9 9.5 %collective-permute-done.36.a_ref = bf16[128,512]{1,0:T(8,128)(2,1)S(1)} collective-permute-done((bf16[128,512]{1,0:T(8,128)(2,1)S(1)}, bf16[128,512]{1,0:T(8,128)(2,1)S(1)}, u32[]{:S(2)}, u32[]{:S(2)}) %collective-permute-start.36) | collective-permute-done | bytes 131104 | tf_op jit(solution)/shard_map/ppermute | solution.py:535
  196.4 3.5 %collective-permute-done.33.refs_1_ = bf16[128,640]{1,0:T(8,128)(2,1)S(1)} collective-permute-done((bf16[128,640]{1,0:T(8,128)(2,1)S(1)}, bf16[128,640]{1,0:T(8,128)(2,1)S(1)}, u32[]{:S(2)}, u32[]{:S(2)}) %collective-permute-start.33) | collective-permute-done | bytes 163872 | tf_op jit(solution)/shard_map/ppermute | solution.py:535
  199.9 7.7 %collective-permute-done.32.refs_0_ = bf16[128,640]{1,0:T(8,128)(2,1)S(1)} collective-permute-done((bf16[128,640]{1,0:T(8,128)(2,1)S(1)}, bf16[128,640]{1,0:T(8,128)(2,1)S(1)}, u32[]{:S(2)}, u32[]{:S(2)}) %collective-permute-start.32) | collective-permute-done | bytes 163872 | tf_op jit(solution)/shard_map/ppermute | solution.py:535
  207.8 9.7 %collective-permute-done.37.a_ref = bf16[128,512]{1,0:T(8,128)(2,1)S(1)} collective-permute-done((bf16[128,512]{1,0:T(8,128)(2,1)S(1)}, bf16[128,512]{1,0:T(8,128)(2,1)S(1)}, u32[]{:S(2)}, u32[]{:S(2)}) %collective-permute-start.37) | collective-permute-done | bytes 131104 | tf_op jit(solution)/shard_map/ppermute | solution.py:535
  219.2 5.2 %collective-permute-done.38.refs_1_ = bf16[128,512]{1,0:T(8,128)(2,1)S(1)} collective-permute-done((bf16[128,512]{1,0:T(8,128)(2,1)S(1)}, bf16[128,512]{1,0:T(8,128)(2,1)S(1)}, u32[]{:S(2)}, u32[]{:S(2)}) %collective-permute-start.38) | collective-permute-done | bytes 131104 | tf_op jit(solution)/shard_map/ppermute | solution.py:535
  (103 shorter events, 28.8 us)
Async XLA Ops:
  3.5 34.3 %collective-permute-start.1 = (bf16[128,5120]{1,0:T(8,128)(2,1)S(1)}, bf16[128,5120]{1,0:T(8,128)(2,1)S(1)}, u32[]{:S(2)}, u32[]{:S(2)}) collective-permute-start(bf16[128,5120]{1,0:T(8,128)(2,1)S(1)} %norm.1.refs_0_), channel_id=1, source_target_pairs={{0,3},{1,0},{2,1},{3,2},{4,7},{5,4},{6,5},{7,6},{8,11},{9,8},{10,9... | collective-permute-start | bytes 3932168 | tf_op jit(solution)/shard_map/ppermute | solution.py:479
  8.7 51.4 %collective-permute-start.6 = (bf16[640,1792]{1,0:T(8,128)(2,1)S(1)}, bf16[640,1792]{1,0:T(8,128)(2,1)S(1)}, u32[]{:S(2)}, u32[]{:S(2)}) collective-permute-start(bf16[640,1792]{1,0:T(8,128)(2,1)S(1)} %pack.1.refs_3_.refs_2_), channel_id=1, source_target_pairs={{0,8},{4,12},{8,0},{12,4},{16,24},{20,28},{24,16},{28,20},{1,9},{5... | collective-permute-start | bytes 6881288 | tf_op jit(solution)/shard_map/ppermute | solution.py:398
  10.3 51.0 %collective-permute-start.4 = (bf16[640,1792]{1,0:T(8,128)(2,1)S(1)}, bf16[640,1792]{1,0:T(8,128)(2,1)S(1)}, u32[]{:S(2)}, u32[]{:S(2)}) collective-permute-start(bf16[640,1792]{1,0:T(8,128)(2,1)S(1)} %pack.1.refs_3_.refs_2_), channel_id=1, source_target_pairs={{0,16},{4,20},{8,24},{12,28},{16,0},{20,4},{24,8},{28,12},{1,17},{... | collective-permute-start | bytes 6881288 | tf_op jit(solution)/shard_map/ppermute | solution.py:398
  11.8 55.0 %collective-permute-start = (bf16[128,5120]{1,0:T(8,128)(2,1)S(1)}, bf16[128,5120]{1,0:T(8,128)(2,1)S(1)}, u32[]{:S(2)}, u32[]{:S(2)}) collective-permute-start(bf16[128,5120]{1,0:T(8,128)(2,1)S(1)} %norm.1.refs_0_), channel_id=1, source_target_pairs={{0,1},{1,2},{2,3},{3,0},{4,5},{5,6},{6,7},{7,4},{8,9},{9,10},{10,1... | collective-permute-start | bytes 3932168 | tf_op jit(solution)/shard_map/ppermute | solution.py:478
  11.8 56.5 %collective-permute-start.8 = (bf16[640,1792]{1,0:T(8,128)(2,1)S(1)}, bf16[640,1792]{1,0:T(8,128)(2,1)S(1)}, u32[]{:S(2)}, u32[]{:S(2)}) collective-permute-start(bf16[640,1792]{1,0:T(8,128)(2,1)S(1)} %pack.1.refs_3_.refs_2_), channel_id=1, source_target_pairs={{0,4},{4,0},{8,12},{12,8},{16,20},{20,16},{24,28},{28,24},{1,5},{5... | collective-permute-start | bytes 6881288 | tf_op jit(solution)/shard_map/ppermute | solution.py:398
  60.1 9.8 %collective-permute-start.9 = (bf16[640,1792]{1,0:T(8,128)(2,1)S(1)}, bf16[640,1792]{1,0:T(8,128)(2,1)S(1)}, u32[]{:S(2)}, u32[]{:S(2)}) collective-permute-start(bf16[640,1792]{1,0:T(8,128)(2,1)S(1)} %collective-permute-done.6.ref.refs_5_.refs_4_), channel_id=1, source_target_pairs={{0,4},{4,0},{8,12},{12,8},{16,20},{20,16},{24,28},{28,24},{1,5},{5... | collective-permute-start | bytes 6881288 | tf_op jit(solution)/shard_map/ppermute | solution.py:398
  61.3 10.1 %collective-permute-start.10 = (bf16[640,1792]{1,0:T(8,128)(2,1)S(1)}, bf16[640,1792]{1,0:T(8,128)(2,1)S(1)}, u32[]{:S(2)}, u32[]{:S(2)}) collective-permute-start(bf16[640,1792]{1,0:T(8,128)(2,1)S(1)} %collective-permute-done.4.ref.refs_7_.refs_6_), channel_id=1, source_target_pairs={{0,4},{4,0},{8,12},{12,8},{16,20},{20,16},{24,28},{28,24},{1,5},{5... | collective-permute-start | bytes 6881288 | tf_op jit(solution)/shard_map/ppermute | solution.py:398
  61.3 35.7 %collective-permute-start.3 = (bf16[64,5120]{1,0:T(8,128)(2,1)S(1)}, bf16[64,5120]{1,0:T(8,128)(2,1)S(1)}, u32[]{:S(2)}, u32[]{:S(2)}) collective-permute-start(bf16[64,5120]{1,0:T(8,128)(2,1)S(1)} %cut.7), channel_id=1, source_target_pairs={{0,3},{1,0},{2,1},{3,2},{4,7},{5,4},{6,5},{7,6},{8,11},{9,8},{10,9... | collective-permute-start | bytes 1966088 | tf_op jit(solution)/shard_map/ppermute | solution.py:483
  66.8 21.5 %collective-permute-start.7 = (bf16[640,768]{1,0:T(8,128)(2,1)S(1)}, bf16[640,768]{1,0:T(8,128)(2,1)S(1)}, u32[]{:S(2)}, u32[]{:S(2)}) collective-permute-start(bf16[640,768]{1,0:T(8,128)(2,1)S(1)} %cut.9), channel_id=1, source_target_pairs={{0,16},{4,20},{8,24},{12,28},{16,0},{20,4},{24,8},{28,12},{1,17},{... | collective-permute-start | bytes 2949128 | tf_op jit(solution)/shard_map/ppermute | solution.py:398
  68.3 28.2 %collective-permute-start.5 = (bf16[640,1024]{1,0:T(8,128)(2,1)S(1)}, bf16[640,1024]{1,0:T(8,128)(2,1)S(1)}, u32[]{:S(2)}, u32[]{:S(2)}) collective-permute-start(bf16[640,1024]{1,0:T(8,128)(2,1)S(1)} %cut.8), channel_id=1, source_target_pairs={{0,8},{4,12},{8,0},{12,4},{16,24},{20,28},{24,16},{28,20},{1,9},{5... | collective-permute-start | bytes 3932168 | tf_op jit(solution)/shard_map/ppermute | solution.py:398
  69.9 28.7 %collective-permute-start.2 = (bf16[64,5120]{1,0:T(8,128)(2,1)S(1)}, bf16[64,5120]{1,0:T(8,128)(2,1)S(1)}, u32[]{:S(2)}, u32[]{:S(2)}) collective-permute-start(bf16[64,5120]{1,0:T(8,128)(2,1)S(1)} %cut.6), channel_id=1, source_target_pairs={{0,1},{1,2},{2,3},{3,0},{4,5},{5,6},{6,7},{7,4},{8,9},{9,10},{10,1... | collective-permute-start | bytes 1966088 | tf_op jit(solution)/shard_map/ppermute | solution.py:482
  71.5 37.4 %collective-permute-start.15 = (bf16[640,1280]{1,0:T(8,128)(2,1)S(1)}, bf16[640,1280]{1,0:T(8,128)(2,1)S(1)}, u32[]{:S(2)}, u32[]{:S(2)}) collective-permute-start(bf16[640,1280]{1,0:T(8,128)(2,1)S(1)} %copy-done.10), channel_id=1, source_target_pairs={{0,4},{4,0},{8,12},{12,8},{16,20},{20,16},{24,28},{28,24},{1,5},{5... | collective-permute-start | bytes 4915208 | tf_op jit(solution)/shard_map/ppermute | solution.py:398
  96.5 38.2 %collective-permute-start.19 = (bf16[640,1280]{1,0:T(8,128)(2,1)S(1)}, bf16[640,1280]{1,0:T(8,128)(2,1)S(1)}, u32[]{:S(2)}, u32[]{:S(2)}) collective-permute-start(bf16[640,1280]{1,0:T(8,128)(2,1)S(1)} %copy-done.10), channel_id=1, source_target_pairs={{0,16},{4,20},{8,24},{12,28},{16,0},{20,4},{24,8},{28,12},{1,17},{... | collective-permute-start | bytes 4915208 | tf_op jit(solution)/shard_map/ppermute | solution.py:398
  97.1 37.9 %collective-permute-start.18 = (bf16[640,1280]{1,0:T(8,128)(2,1)S(1)}, bf16[640,1280]{1,0:T(8,128)(2,1)S(1)}, u32[]{:S(2)}, u32[]{:S(2)}) collective-permute-start(bf16[640,1280]{1,0:T(8,128)(2,1)S(1)} %copy-done.10), channel_id=1, source_target_pairs={{0,8},{4,12},{8,0},{12,4},{16,24},{20,28},{24,16},{28,20},{1,9},{5... | collective-permute-start | bytes 4915208 | tf_op jit(solution)/shard_map/ppermute | solution.py:398
  110.1 10.4 %collective-permute-start.16 = (bf16[128,640]{1,0:T(8,128)(2,1)S(1)}, bf16[128,640]{1,0:T(8,128)(2,1)S(1)}, u32[]{:S(2)}, u32[]{:S(2)}) collective-permute-start(bf16[128,640]{1,0:T(8,128)(2,1)S(1)} %get-tuple-element.64), channel_id=1, source_target_pairs={{0,1},{1,2},{2,3},{3,0},{4,5},{5,6},{6,7},{7,4},{8,9},{9,10},{10,1... | collective-permute-start | bytes 491528 | tf_op jit(solution)/shard_map/ppermute | solution.py:535
  113.2 10.5 %collective-permute-start.13 = (bf16[128,640]{1,0:T(8,128)(2,1)S(1)}, bf16[128,640]{1,0:T(8,128)(2,1)S(1)}, u32[]{:S(2)}, u32[]{:S(2)}) collective-permute-start(bf16[128,640]{1,0:T(8,128)(2,1)S(1)} %get-tuple-element.61), channel_id=1, source_target_pairs={{0,1},{1,2},{2,3},{3,0},{4,5},{5,6},{6,7},{7,4},{8,9},{9,10},{10,1... | collective-permute-start | bytes 491528 | tf_op jit(solution)/shard_map/ppermute | solution.py:535
  120.6 14.2 %collective-permute-start.17 = (bf16[128,640]{1,0:T(8,128)(2,1)S(1)}, bf16[128,640]{1,0:T(8,128)(2,1)S(1)}, u32[]{:S(2)}, u32[]{:S(2)}) collective-permute-start(bf16[128,640]{1,0:T(8,128)(2,1)S(1)} %add.15), channel_id=1, source_target_pairs={{0,1},{1,2},{2,3},{3,0},{4,5},{5,6},{6,7},{7,4},{8,9},{9,10},{10,1... | collective-permute-start | bytes 491528 | tf_op jit(solution)/shard_map/ppermute | solution.py:535
  123.8 11.0 %collective-permute-start.14 = (bf16[128,640]{1,0:T(8,128)(2,1)S(1)}, bf16[128,640]{1,0:T(8,128)(2,1)S(1)}, u32[]{:S(2)}, u32[]{:S(2)}) collective-permute-start(bf16[128,640]{1,0:T(8,128)(2,1)S(1)} %add.14), channel_id=1, source_target_pairs={{0,1},{1,2},{2,3},{3,0},{4,5},{5,6},{6,7},{7,4},{8,9},{9,10},{10,1... | collective-permute-start | bytes 491528 | tf_op jit(solution)/shard_map/ppermute | solution.py:535
  135.3 31.2 %collective-permute-start.26 = (bf16[384,1280]{1,0:T(8,128)(2,1)S(1)}, bf16[384,1280]{1,0:T(8,128)(2,1)S(1)}, u32[]{:S(2)}, u32[]{:S(2)}) collective-permute-start(bf16[384,1280]{1,0:T(8,128)(2,1)S(1)} %cut.10), channel_id=1, source_target_pairs={{0,8},{4,12},{8,0},{12,4},{16,24},{20,28},{24,16},{28,20},{1,9},{5... | collective-permute-start | bytes 2949128 | tf_op jit(solution)/shard_map/ppermute | solution.py:398
  138.8 13.7 %collective-permute-start.20 = (bf16[128,1280]{1,0:T(8,128)(2,1)S(1)}, bf16[128,1280]{1,0:T(8,128)(2,1)S(1)}, u32[]{:S(2)}, u32[]{:S(2)}) collective-permute-start(bf16[128,1280]{1,0:T(8,128)(2,1)S(1)} %get-tuple-element.68), channel_id=1, source_target_pairs={{0,1},{1,2},{2,3},{3,0},{4,5},{5,6},{6,7},{7,4},{8,9},{9,10},{10,1... | collective-permute-start | bytes 983048 | tf_op jit(solution)/shard_map/ppermute | solution.py:535
  142.5 17.0 %collective-permute-start.24 = (bf16[128,1280]{1,0:T(8,128)(2,1)S(1)}, bf16[128,1280]{1,0:T(8,128)(2,1)S(1)}, u32[]{:S(2)}, u32[]{:S(2)}) collective-permute-start(bf16[128,1280]{1,0:T(8,128)(2,1)S(1)} %get-tuple-element.72), channel_id=1, source_target_pairs={{0,1},{1,2},{2,3},{3,0},{4,5},{5,6},{6,7},{7,4},{8,9},{9,10},{10,1... | collective-permute-start | bytes 983048 | tf_op jit(solution)/shard_map/ppermute | solution.py:535
  145.4 21.2 %collective-permute-start.27 = (bf16[256,1280]{1,0:T(8,128)(2,1)S(1)}, bf16[256,1280]{1,0:T(8,128)(2,1)S(1)}, u32[]{:S(2)}, u32[]{:S(2)}) collective-permute-start(bf16[256,1280]{1,0:T(8,128)(2,1)S(1)} %cut.11), channel_id=1, source_target_pairs={{0,16},{4,20},{8,24},{12,28},{16,0},{20,4},{24,8},{28,12},{1,17},{... | collective-permute-start | bytes 1966088 | tf_op jit(solution)/shard_map/ppermute | solution.py:398
  152.6 14.0 %collective-permute-start.21 = (bf16[128,1280]{1,0:T(8,128)(2,1)S(1)}, bf16[128,1280]{1,0:T(8,128)(2,1)S(1)}, u32[]{:S(2)}, u32[]{:S(2)}) collective-permute-start(bf16[128,1280]{1,0:T(8,128)(2,1)S(1)} %add.16), channel_id=1, source_target_pairs={{0,1},{1,2},{2,3},{3,0},{4,5},{5,6},{6,7},{7,4},{8,9},{9,10},{10,1... | collective-permute-start | bytes 983048 | tf_op jit(solution)/shard_map/ppermute | solution.py:535
  159.6 13.6 %collective-permute-start.25 = (bf16[128,1280]{1,0:T(8,128)(2,1)S(1)}, bf16[128,1280]{1,0:T(8,128)(2,1)S(1)}, u32[]{:S(2)}, u32[]{:S(2)}) collective-permute-start(bf16[128,1280]{1,0:T(8,128)(2,1)S(1)} %add.17), channel_id=1, source_target_pairs={{0,1},{1,2},{2,3},{3,0},{4,5},{5,6},{6,7},{7,4},{8,9},{9,10},{10,1... | collective-permute-start | bytes 983048 | tf_op jit(solution)/shard_map/ppermute | solution.py:535
  177.1 30.5 %collective-permute-start.31 = (bf16[128,1280]{1,0:T(8,128)(2,1)S(1)}, bf16[128,1280]{1,0:T(8,128)(2,1)S(1)}, u32[]{:S(2)}, u32[]{:S(2)}) collective-permute-start(bf16[128,1280]{1,0:T(8,128)(2,1)S(1)} %add.19), channel_id=1, source_target_pairs={{0,1},{1,2},{2,3},{3,0},{4,5},{5,6},{6,7},{7,4},{8,9},{9,10},{10,1... | collective-permute-start | bytes 983048 | tf_op jit(solution)/shard_map/ppermute | solution.py:535
  179.2 17.2 %collective-permute-start.36 = (bf16[128,512]{1,0:T(8,128)(2,1)S(1)}, bf16[128,512]{1,0:T(8,128)(2,1)S(1)}, u32[]{:S(2)}, u32[]{:S(2)}) collective-permute-start(bf16[128,512]{1,0:T(8,128)(2,1)S(1)} %get-tuple-element.86), channel_id=1, source_target_pairs={{0,1},{1,2},{2,3},{3,0},{4,5},{5,6},{6,7},{7,4},{8,9},{9,10},{10,1... | collective-permute-start | bytes 393224 | tf_op jit(solution)/shard_map/ppermute | solution.py:535
  181.0 18.9 %collective-permute-start.33 = (bf16[128,640]{1,0:T(8,128)(2,1)S(1)}, bf16[128,640]{1,0:T(8,128)(2,1)S(1)}, u32[]{:S(2)}, u32[]{:S(2)}) collective-permute-start(bf16[128,640]{1,0:T(8,128)(2,1)S(1)} %add.21), channel_id=1, source_target_pairs={{0,1},{1,2},{2,3},{3,0},{4,5},{5,6},{6,7},{7,4},{8,9},{9,10},{10,1... | collective-permute-start | bytes 491528 | tf_op jit(solution)/shard_map/ppermute | solution.py:535
  186.6 21.0 %collective-permute-start.30 = (bf16[128,768]{1,0:T(8,128)(2,1)S(1)}, bf16[128,768]{1,0:T(8,128)(2,1)S(1)}, u32[]{:S(2)}, u32[]{:S(2)}) collective-permute-start(bf16[128,768]{1,0:T(8,128)(2,1)S(1)} %add.18), channel_id=1, source_target_pairs={{0,1},{1,2},{2,3},{3,0},{4,5},{5,6},{6,7},{7,4},{8,9},{9,10},{10,1... | collective-permute-start | bytes 589832 | tf_op jit(solution)/shard_map/ppermute | solution.py:535
  186.7 20.9 %collective-permute-start.32 = (bf16[128,640]{1,0:T(8,128)(2,1)S(1)}, bf16[128,640]{1,0:T(8,128)(2,1)S(1)}, u32[]{:S(2)}, u32[]{:S(2)}) collective-permute-start(bf16[128,640]{1,0:T(8,128)(2,1)S(1)} %add.20), channel_id=1, source_target_pairs={{0,1},{1,2},{2,3},{3,0},{4,5},{5,6},{6,7},{7,4},{8,9},{9,10},{10,1... | collective-permute-start | bytes 491528 | tf_op jit(solution)/shard_map/ppermute | solution.py:535
  196.4 21.2 %collective-permute-start.39 = (bf16[128,1280]{1,0:T(8,128)(2,1)S(1)}, bf16[128,1280]{1,0:T(8,128)(2,1)S(1)}, u32[]{:S(2)}, u32[]{:S(2)}) collective-permute-start(bf16[128,1280]{1,0:T(8,128)(2,1)S(1)} %add.25), channel_id=1, source_target_pairs={{0,1},{1,2},{2,3},{3,0},{4,5},{5,6},{6,7},{7,4},{8,9},{9,10},{10,1... | collective-permute-start | bytes 983048 | tf_op jit(solution)/shard_map/ppermute | solution.py:535
  199.9 17.6 %collective-permute-start.37 = (bf16[128,512]{1,0:T(8,128)(2,1)S(1)}, bf16[128,512]{1,0:T(8,128)(2,1)S(1)}, u32[]{:S(2)}, u32[]{:S(2)}) collective-permute-start(bf16[128,512]{1,0:T(8,128)(2,1)S(1)} %add.23), channel_id=1, source_target_pairs={{0,1},{1,2},{2,3},{3,0},{4,5},{5,6},{6,7},{7,4},{8,9},{9,10},{10,1... | collective-permute-start | bytes 393224 | tf_op jit(solution)/shard_map/ppermute | solution.py:535
  207.7 16.6 %collective-permute-start.34 = (bf16[128,768]{1,0:T(8,128)(2,1)S(1)}, bf16[128,768]{1,0:T(8,128)(2,1)S(1)}, u32[]{:S(2)}, u32[]{:S(2)}) collective-permute-start(bf16[128,768]{1,0:T(8,128)(2,1)S(1)} %add.22), channel_id=1, source_target_pairs={{0,1},{1,2},{2,3},{3,0},{4,5},{5,6},{6,7},{7,4},{8,9},{9,10},{10,1... | collective-permute-start | bytes 589832 | tf_op jit(solution)/shard_map/ppermute | solution.py:535
  (19 other events, 190.9 us)

commit v15 on v11

--- a/solution.py
+++ b/solution.py
@@ -524,7 +524,7 @@
         if level < 2:
             groups = [tuple((r, 0, core) for r in near) for core in (0, 1)]
         else:
-            groups = [((r, half, 0), (r, half, 1)) for r in near for half in (0, 1)]
+            groups = [tuple((r, half, core) for half in (0, 1) for core in (0, 1)) for r in near]
         terms = []
         for group in groups:
             weights = [(o_sibling if core else o_held)[r][half] for r, half, core in group]

time: 220 us -> 221 us (level)
    ppermute x18 -> x15, waiting for transfers between devices: 86 us -> 87.1 us  [body(): arrivals.append([lax.ppermute(total, 'sp', right) for total in totals])]
    pallas_call x6 -> x5, Pallas kernels: 8.27 us -> 8.09 us  [mix(): pl.pallas_call(functools.partial(mix_kernel, len(parts)), in_specs=[VMEM]...]
  transfers between devices with their start and end apart: 40 -> 37, of which waited for: 27 -> 27; matrix products, arithmetic and copies ran while one was open for 0% -> 0% of each run, Pallas kernels for 13% -> 12%
where the time goes in v15:
time: 221 us
  waiting for transfers between devices  165 us (75%)
  Pallas kernels  29.9 us (14%)
  starting transfers between devices  22.9 us (10%)
    ppermute x15, waiting for transfers between devices, body(): arrivals.append([lax.ppermute(total, 'sp', right) for total in totals])  87.1 us
    ppermute x18, waiting for transfers between devices, swapped(): return lax.ppermute(array, 'fsdp', [(i, i ^ mask) for i in range(n_f)])  48.7 us
    ppermute x1, waiting for transfers between devices, body(): behind = lax.ppermute(behind, 'sp', left)  26 us
    ppermute x18, starting transfers between devices, swapped(): return lax.ppermute(array, 'fsdp', [(i, i ^ mask) for i in range(n_f)])  11.1 us
    pallas_call x2, Pallas kernels, partial(): pl.pallas_call(functools.partial(partial_kernel, len(blocks), counts, wid...  8.88 us
    pallas_call x5, Pallas kernels, mix(): pl.pallas_call(functools.partial(mix_kernel, len(parts)), in_specs=[VMEM]...  8.09 us
    ppermute x1, starting transfers between devices, body(): behind = lax.ppermute(behind, 'sp', left)  5.1 us
  transfers between devices with their start and end apart: 37, of which 27 were waited for; matrix products, arithmetic and copies ran while one was open for 0% of the time, Pallas kernels for 12%

profile of v15, /device:TPU:0, one launch (start us, length us, event | category | flops | bytes accessed | tf_op | source)
XLA Modules:
  0.0 221.1 jit_solution(1403498686792099682)
XLA Ops:
  3.5 5.1 %collective-permute-start.1 = (bf16[128,5120]{1,0:T(8,128)(2,1)S(1)}, bf16[128,5120]{1,0:T(8,128)(2,1)S(1)}, u32[]{:S(2)}, u32[]{:S(2)}) collective-permute-start(bf16[128,5120]{1,0:T(8,128)(2,1)S(1)} %norm.1.refs_0_), channel_id=1, source_target_pairs={{0,3},{1,0},{2,1},{3,2},{4,7},{5,4},{6,5},{7,6},{8,11},{9,8},{10,9... | collective-permute-start | bytes 3932168 | tf_op jit(solution)/shard_map/ppermute | solution.py:479
  11.8 26.0 %collective-permute-done.1.ref.refs_2_ = bf16[128,5120]{1,0:T(8,128)(2,1)S(1)} collective-permute-done((bf16[128,5120]{1,0:T(8,128)(2,1)S(1)}, bf16[128,5120]{1,0:T(8,128)(2,1)S(1)}, u32[]{:S(2)}, u32[]{:S(2)}) %collective-permute-start.1) | collective-permute-done | bytes 1310752 | tf_op jit(solution)/shard_map/ppermute | solution.py:479
  37.9 22.3 %collective-permute-done.6.ref.refs_5_.refs_4_ = bf16[640,1792]{1,0:T(8,128)(2,1)S(1)} collective-permute-done((bf16[640,1792]{1,0:T(8,128)(2,1)S(1)}, bf16[640,1792]{1,0:T(8,128)(2,1)S(1)}, u32[]{:S(2)}, u32[]{:S(2)}) %collective-permute-start.6) | collective-permute-done | bytes 2293792 | tf_op jit(solution)/shard_map/ppermute | solution.py:398
  63.1 2.5 %collective-permute-done.ref.refs_1_ = bf16[128,5120]{1,0:T(8,128)(2,1)S(1)} collective-permute-done((bf16[128,5120]{1,0:T(8,128)(2,1)S(1)}, bf16[128,5120]{1,0:T(8,128)(2,1)S(1)}, u32[]{:S(2)}, u32[]{:S(2)}) %collective-permute-start) | collective-permute-done | bytes 1310752 | tf_op jit(solution)/shard_map/ppermute | solution.py:478
  67.2 3.5 %collective-permute-start.3 = (bf16[64,5120]{1,0:T(8,128)(2,1)S(1)}, bf16[64,5120]{1,0:T(8,128)(2,1)S(1)}, u32[]{:S(2)}, u32[]{:S(2)}) collective-permute-start(bf16[64,5120]{1,0:T(8,128)(2,1)S(1)} %cut.7), channel_id=1, source_target_pairs={{0,3},{1,0},{2,1},{3,2},{4,7},{5,4},{6,5},{7,6},{8,11},{9,8},{10,9... | collective-permute-start | bytes 1966088 | tf_op jit(solution)/shard_map/ppermute | solution.py:483
  70.8 6.6 %partial.2.refs_9_ = f32[384,1792]{1,0:T(8,128)S(1)} custom-call(bf16[128,5120]{1,0:T(8,128)(2,1)S(1)} %norm.1.refs_0_, bf16[128,5120]{1,0:T(8,128)(2,1)S(1)} %collective-permute-done.ref.refs_1_, bf16[128,5120]{1,0:T(8,128)(2,1)S(1)} %collective-permute-done.1.ref.refs_2_, bf16[640,1792]{1,0:T(8,128)(2,1)S(1)} %pack.1.refs_3_.refs_2_, ...), custom_call_target="tpu_custom_call" | custom-call | flops 5284823040 | tf_op jit(solution)/shard_map/partial/pallas_call | solution.py:141
  77.4 8.2 %collective-permute-done.7.refs_7_ = bf16[640,768]{1,0:T(8,128)(2,1)S(1)} collective-permute-done((bf16[640,768]{1,0:T(8,128)(2,1)S(1)}, bf16[640,768]{1,0:T(8,128)(2,1)S(1)}, u32[]{:S(2)}, u32[]{:S(2)}) %collective-permute-start.7) | collective-permute-done | bytes 983072 | tf_op jit(solution)/shard_map/ppermute | solution.py:398
  85.6 9.6 %collective-permute-done.5.refs_5_ = bf16[640,1024]{1,0:T(8,128)(2,1)S(1)} collective-permute-done((bf16[640,1024]{1,0:T(8,128)(2,1)S(1)}, bf16[640,1024]{1,0:T(8,128)(2,1)S(1)}, u32[]{:S(2)}, u32[]{:S(2)}) %collective-permute-start.5) | collective-permute-done | bytes 1310752 | tf_op jit(solution)/shard_map/ppermute | solution.py:398
  99.5 2.3 %partial.3.refs_10_ = f32[128,1792]{1,0:T(8,128)S(1)} custom-call(bf16[64,5120]{1,0:T(8,128)(2,1)S(1)} %collective-permute-done.2.refs_0_.refs_3_, bf16[64,5120]{1,0:T(8,128)(2,1)S(1)} %collective-permute-done.3.refs_1_.refs_4_, bf16[640,1792]{1,0:T(8,128)(2,1)S(1)} %pack.1.refs_3_.refs_2_, bf16[640,1792]{1,0:T(8,128)(2,1)S(1)} %collective-permute-done.8.refs_4_.refs_3_, ...), custom_call_target="tpu_custom_call" | custom-call | tf_op jit(solution)/shard_map/partial/pallas_call | solution.py:141
  102.1 3.7 %finish.1 = (bf16[512,1280]{1,0:T(8,128)(2,1)S(1)}, bf16[512,512]{1,0:T(8,128)(2,1)S(1)}) custom-call(s32[2]{0:T(128)S(1)} %pad_add_fusion.index_ref, bf16[128,5120]{1,0:T(8,128)(2,1)S(1)} %norm.1.refs_0_, bf16[128,5120]{1,0:T(8,128)(2,1)S(1)} %collective-permute-done.ref.refs_1_, bf16[128,5120]{1,0:T(8,128)(2,1)S(1)} %collective-permute-done.1.ref.refs_2_, ...), custom_call_target="tpu_custom_call" | custom-call | tf_op jit(solution)/shard_map/finish/pallas_call | solution.py:217
  105.8 4.0 %attend.1.heads_ref = bf16[512,1280]{1,0:T(8,128)(2,1)S(1)} custom-call(s32[2]{0:T(128)S(1)} %pad_add_fusion.index_ref, bf16[512,1280]{1,0:T(8,128)(2,1)S(1)} %get-tuple-element.53.q_ref, bf16[512,512]{1,0:T(8,128)(2,1)S(1)} %get-tuple-element.54.kv_ref), custom_call_target="tpu_custom_call" | custom-call | tf_op jit(solution)/shard_map/attend/pallas_call | solution.py:288
  111.0 1.7 collective-permute-start.17
  114.1 5.8 %collective-permute-done.17.a_ref = bf16[128,640]{1,0:T(8,128)(2,1)S(1)} collective-permute-done((bf16[128,640]{1,0:T(8,128)(2,1)S(1)}, bf16[128,640]{1,0:T(8,128)(2,1)S(1)}, u32[]{:S(2)}, u32[]{:S(2)}) %collective-permute-start.17) | collective-permute-done | bytes 163872 | tf_op jit(solution)/shard_map/ppermute | solution.py:535
  120.0 2.8 %collective-permute-done.13.a_ref = bf16[128,640]{1,0:T(8,128)(2,1)S(1)} collective-permute-done((bf16[128,640]{1,0:T(8,128)(2,1)S(1)}, bf16[128,640]{1,0:T(8,128)(2,1)S(1)}, u32[]{:S(2)}, u32[]{:S(2)}) %collective-permute-start.13) | collective-permute-done | bytes 163872 | tf_op jit(solution)/shard_map/ppermute | solution.py:535
  123.3 4.0 %collective-permute-done.18.a_ref = bf16[128,640]{1,0:T(8,128)(2,1)S(1)} collective-permute-done((bf16[128,640]{1,0:T(8,128)(2,1)S(1)}, bf16[128,640]{1,0:T(8,128)(2,1)S(1)}, u32[]{:S(2)}, u32[]{:S(2)}) %collective-permute-start.18) | collective-permute-done | bytes 163872 | tf_op jit(solution)/shard_map/ppermute | solution.py:535
  127.5 4.3 %collective-permute-done.14.a_ref = bf16[128,640]{1,0:T(8,128)(2,1)S(1)} collective-permute-done((bf16[128,640]{1,0:T(8,128)(2,1)S(1)}, bf16[128,640]{1,0:T(8,128)(2,1)S(1)}, u32[]{:S(2)}, u32[]{:S(2)}) %collective-permute-start.14) | collective-permute-done | bytes 163872 | tf_op jit(solution)/shard_map/ppermute | solution.py:535
  133.5 1.7 collective-permute-done.19.refs_1_
  135.2 3.8 %collective-permute-done.15.refs_0_ = bf16[128,640]{1,0:T(8,128)(2,1)S(1)} collective-permute-done((bf16[128,640]{1,0:T(8,128)(2,1)S(1)}, bf16[128,640]{1,0:T(8,128)(2,1)S(1)}, u32[]{:S(2)}, u32[]{:S(2)}) %collective-permute-start.15) | collective-permute-done | bytes 163872 | tf_op jit(solution)/shard_map/ppermute | solution.py:535
  140.3 1.9 mix.7
  142.5 2.3 %collective-permute-done.24.refs_0_ = bf16[640,1280]{1,0:T(8,128)(2,1)S(1)} collective-permute-done((bf16[640,1280]{1,0:T(8,128)(2,1)S(1)}, bf16[640,1280]{1,0:T(8,128)(2,1)S(1)}, u32[]{:S(2)}, u32[]{:S(2)}) %collective-permute-start.24) | collective-permute-done | bytes 1638432 | tf_op jit(solution)/shard_map/ppermute | solution.py:398
  144.8 1.9 mix.8
  147.0 7.7 %collective-permute-done.22.a_ref = bf16[128,1280]{1,0:T(8,128)(2,1)S(1)} collective-permute-done((bf16[128,1280]{1,0:T(8,128)(2,1)S(1)}, bf16[128,1280]{1,0:T(8,128)(2,1)S(1)}, u32[]{:S(2)}, u32[]{:S(2)}) %collective-permute-start.22) | collective-permute-done | bytes 327712 | tf_op jit(solution)/shard_map/ppermute | solution.py:535
  154.8 6.9 %collective-permute-done.26.a_ref = bf16[128,1280]{1,0:T(8,128)(2,1)S(1)} collective-permute-done((bf16[128,1280]{1,0:T(8,128)(2,1)S(1)}, bf16[128,1280]{1,0:T(8,128)(2,1)S(1)}, u32[]{:S(2)}, u32[]{:S(2)}) %collective-permute-start.26) | collective-permute-done | bytes 327712 | tf_op jit(solution)/shard_map/ppermute | solution.py:535
  161.8 6.9 %collective-permute-done.23.a_ref = bf16[128,1280]{1,0:T(8,128)(2,1)S(1)} collective-permute-done((bf16[128,1280]{1,0:T(8,128)(2,1)S(1)}, bf16[128,1280]{1,0:T(8,128)(2,1)S(1)}, u32[]{:S(2)}, u32[]{:S(2)}) %collective-permute-start.23) | collective-permute-done | bytes 327712 | tf_op jit(solution)/shard_map/ppermute | solution.py:535
  168.7 5.7 %collective-permute-done.27.a_ref = bf16[128,1280]{1,0:T(8,128)(2,1)S(1)} collective-permute-done((bf16[128,1280]{1,0:T(8,128)(2,1)S(1)}, bf16[128,1280]{1,0:T(8,128)(2,1)S(1)}, u32[]{:S(2)}, u32[]{:S(2)}) %collective-permute-start.27) | collective-permute-done | bytes 327712 | tf_op jit(solution)/shard_map/ppermute | solution.py:535
  175.0 3.0 %collective-permute-done.31.refs_3_ = bf16[256,1280]{1,0:T(8,128)(2,1)S(1)} collective-permute-done((bf16[256,1280]{1,0:T(8,128)(2,1)S(1)}, bf16[256,1280]{1,0:T(8,128)(2,1)S(1)}, u32[]{:S(2)}, u32[]{:S(2)}) %collective-permute-start.31) | collective-permute-done | bytes 655392 | tf_op jit(solution)/shard_map/ppermute | solution.py:398
  178.0 1.9 mix.9
  180.1 12.2 %collective-permute-done.32.a_ref = bf16[128,1280]{1,0:T(8,128)(2,1)S(1)} collective-permute-done((bf16[128,1280]{1,0:T(8,128)(2,1)S(1)}, bf16[128,1280]{1,0:T(8,128)(2,1)S(1)}, u32[]{:S(2)}, u32[]{:S(2)}) %collective-permute-start.32) | collective-permute-done | bytes 327712 | tf_op jit(solution)/shard_map/ppermute | solution.py:535
  192.6 6.7 %collective-permute-done.34.refs_2_ = bf16[128,1280]{1,0:T(8,128)(2,1)S(1)} collective-permute-done((bf16[128,1280]{1,0:T(8,128)(2,1)S(1)}, bf16[128,1280]{1,0:T(8,128)(2,1)S(1)}, u32[]{:S(2)}, u32[]{:S(2)}) %collective-permute-start.34) | collective-permute-done | bytes 327712 | tf_op jit(solution)/shard_map/ppermute | solution.py:535
  199.3 7.0 %collective-permute-done.33.a_ref = bf16[128,1280]{1,0:T(8,128)(2,1)S(1)} collective-permute-done((bf16[128,1280]{1,0:T(8,128)(2,1)S(1)}, bf16[128,1280]{1,0:T(8,128)(2,1)S(1)}, u32[]{:S(2)}, u32[]{:S(2)}) %collective-permute-start.33) | collective-permute-done | bytes 327712 | tf_op jit(solution)/shard_map/ppermute | solution.py:535
  206.5 6.9 %collective-permute-done.36.refs_3_ = bf16[128,1280]{1,0:T(8,128)(2,1)S(1)} collective-permute-done((bf16[128,1280]{1,0:T(8,128)(2,1)S(1)}, bf16[128,1280]{1,0:T(8,128)(2,1)S(1)}, u32[]{:S(2)}, u32[]{:S(2)}) %collective-permute-start.36) | collective-permute-done | bytes 327712 | tf_op jit(solution)/shard_map/ppermute | solution.py:535
  214.9 4.6 %collective-permute-done.35.refs_0_ = bf16[128,1280]{1,0:T(8,128)(2,1)S(1)} collective-permute-done((bf16[128,1280]{1,0:T(8,128)(2,1)S(1)}, bf16[128,1280]{1,0:T(8,128)(2,1)S(1)}, u32[]{:S(2)}, u32[]{:S(2)}) %collective-permute-start.35) | collective-permute-done | bytes 327712 | tf_op jit(solution)/shard_map/ppermute | solution.py:535
  (94 shorter events, 27.0 us)
Async XLA Ops:
  3.5 34.3 %collective-permute-start.1 = (bf16[128,5120]{1,0:T(8,128)(2,1)S(1)}, bf16[128,5120]{1,0:T(8,128)(2,1)S(1)}, u32[]{:S(2)}, u32[]{:S(2)}) collective-permute-start(bf16[128,5120]{1,0:T(8,128)(2,1)S(1)} %norm.1.refs_0_), channel_id=1, source_target_pairs={{0,3},{1,0},{2,1},{3,2},{4,7},{5,4},{6,5},{7,6},{8,11},{9,8},{10,9... | collective-permute-start | bytes 3932168 | tf_op jit(solution)/shard_map/ppermute | solution.py:479
  8.7 51.4 %collective-permute-start.6 = (bf16[640,1792]{1,0:T(8,128)(2,1)S(1)}, bf16[640,1792]{1,0:T(8,128)(2,1)S(1)}, u32[]{:S(2)}, u32[]{:S(2)}) collective-permute-start(bf16[640,1792]{1,0:T(8,128)(2,1)S(1)} %pack.1.refs_3_.refs_2_), channel_id=1, source_target_pairs={{0,8},{4,12},{8,0},{12,4},{16,24},{20,28},{24,16},{28,20},{1,9},{5... | collective-permute-start | bytes 6881288 | tf_op jit(solution)/shard_map/ppermute | solution.py:398
  10.3 51.0 %collective-permute-start.4 = (bf16[640,1792]{1,0:T(8,128)(2,1)S(1)}, bf16[640,1792]{1,0:T(8,128)(2,1)S(1)}, u32[]{:S(2)}, u32[]{:S(2)}) collective-permute-start(bf16[640,1792]{1,0:T(8,128)(2,1)S(1)} %pack.1.refs_3_.refs_2_), channel_id=1, source_target_pairs={{0,16},{4,20},{8,24},{12,28},{16,0},{20,4},{24,8},{28,12},{1,17},{... | collective-permute-start | bytes 6881288 | tf_op jit(solution)/shard_map/ppermute | solution.py:398
  11.8 53.8 %collective-permute-start = (bf16[128,5120]{1,0:T(8,128)(2,1)S(1)}, bf16[128,5120]{1,0:T(8,128)(2,1)S(1)}, u32[]{:S(2)}, u32[]{:S(2)}) collective-permute-start(bf16[128,5120]{1,0:T(8,128)(2,1)S(1)} %norm.1.refs_0_), channel_id=1, source_target_pairs={{0,1},{1,2},{2,3},{3,0},{4,5},{5,6},{6,7},{7,4},{8,9},{9,10},{10,1... | collective-permute-start | bytes 3932168 | tf_op jit(solution)/shard_map/ppermute | solution.py:478
  11.8 55.3 %collective-permute-start.8 = (bf16[640,1792]{1,0:T(8,128)(2,1)S(1)}, bf16[640,1792]{1,0:T(8,128)(2,1)S(1)}, u32[]{:S(2)}, u32[]{:S(2)}) collective-permute-start(bf16[640,1792]{1,0:T(8,128)(2,1)S(1)} %pack.1.refs_3_.refs_2_), channel_id=1, source_target_pairs={{0,4},{4,0},{8,12},{12,8},{16,20},{20,16},{24,28},{28,24},{1,5},{5... | collective-permute-start | bytes 6881288 | tf_op jit(solution)/shard_map/ppermute | solution.py:398
  60.1 10.6 %collective-permute-start.9 = (bf16[640,1792]{1,0:T(8,128)(2,1)S(1)}, bf16[640,1792]{1,0:T(8,128)(2,1)S(1)}, u32[]{:S(2)}, u32[]{:S(2)}) collective-permute-start(bf16[640,1792]{1,0:T(8,128)(2,1)S(1)} %collective-permute-done.6.ref.refs_5_.refs_4_), channel_id=1, source_target_pairs={{0,4},{4,0},{8,12},{12,8},{16,20},{20,16},{24,28},{28,24},{1,5},{5... | collective-permute-start | bytes 6881288 | tf_op jit(solution)/shard_map/ppermute | solution.py:398
  61.3 9.4 %collective-permute-start.10 = (bf16[640,1792]{1,0:T(8,128)(2,1)S(1)}, bf16[640,1792]{1,0:T(8,128)(2,1)S(1)}, u32[]{:S(2)}, u32[]{:S(2)}) collective-permute-start(bf16[640,1792]{1,0:T(8,128)(2,1)S(1)} %collective-permute-done.4.ref.refs_7_.refs_6_), channel_id=1, source_target_pairs={{0,4},{4,0},{8,12},{12,8},{16,20},{20,16},{24,28},{28,24},{1,5},{5... | collective-permute-start | bytes 6881288 | tf_op jit(solution)/shard_map/ppermute | solution.py:398
  61.4 24.2 %collective-permute-start.7 = (bf16[640,768]{1,0:T(8,128)(2,1)S(1)}, bf16[640,768]{1,0:T(8,128)(2,1)S(1)}, u32[]{:S(2)}, u32[]{:S(2)}) collective-permute-start(bf16[640,768]{1,0:T(8,128)(2,1)S(1)} %cut.9), channel_id=1, source_target_pairs={{0,16},{4,20},{8,24},{12,28},{16,0},{20,4},{24,8},{28,12},{1,17},{... | collective-permute-start | bytes 2949128 | tf_op jit(solution)/shard_map/ppermute | solution.py:398
  65.6 29.6 %collective-permute-start.5 = (bf16[640,1024]{1,0:T(8,128)(2,1)S(1)}, bf16[640,1024]{1,0:T(8,128)(2,1)S(1)}, u32[]{:S(2)}, u32[]{:S(2)}) collective-permute-start(bf16[640,1024]{1,0:T(8,128)(2,1)S(1)} %cut.8), channel_id=1, source_target_pairs={{0,8},{4,12},{8,0},{12,4},{16,24},{20,28},{24,16},{28,20},{1,9},{5... | collective-permute-start | bytes 3932168 | tf_op jit(solution)/shard_map/ppermute | solution.py:398
  67.2 29.6 %collective-permute-start.3 = (bf16[64,5120]{1,0:T(8,128)(2,1)S(1)}, bf16[64,5120]{1,0:T(8,128)(2,1)S(1)}, u32[]{:S(2)}, u32[]{:S(2)}) collective-permute-start(bf16[64,5120]{1,0:T(8,128)(2,1)S(1)} %cut.7), channel_id=1, source_target_pairs={{0,3},{1,0},{2,1},{3,2},{4,7},{5,4},{6,5},{7,6},{8,11},{9,8},{10,9... | collective-permute-start | bytes 1966088 | tf_op jit(solution)/shard_map/ppermute | solution.py:483
  70.7 28.8 %collective-permute-start.2 = (bf16[64,5120]{1,0:T(8,128)(2,1)S(1)}, bf16[64,5120]{1,0:T(8,128)(2,1)S(1)}, u32[]{:S(2)}, u32[]{:S(2)}) collective-permute-start(bf16[64,5120]{1,0:T(8,128)(2,1)S(1)} %cut.6), channel_id=1, source_target_pairs={{0,1},{1,2},{2,3},{3,0},{4,5},{5,6},{6,7},{7,4},{8,9},{9,10},{10,1... | collective-permute-start | bytes 1966088 | tf_op jit(solution)/shard_map/ppermute | solution.py:482
  70.7 39.1 %collective-permute-start.16 = (bf16[640,1280]{1,0:T(8,128)(2,1)S(1)}, bf16[640,1280]{1,0:T(8,128)(2,1)S(1)}, u32[]{:S(2)}, u32[]{:S(2)}) collective-permute-start(bf16[640,1280]{1,0:T(8,128)(2,1)S(1)} %copy-done.10), channel_id=1, source_target_pairs={{0,4},{4,0},{8,12},{12,8},{16,20},{20,16},{24,28},{28,24},{1,5},{5... | collective-permute-start | bytes 4915208 | tf_op jit(solution)/shard_map/ppermute | solution.py:398
  95.3 6.8 %collective-permute-start.11 = (bf16[640,1024]{1,0:T(8,128)(2,1)S(1)}, bf16[640,1024]{1,0:T(8,128)(2,1)S(1)}, u32[]{:S(2)}, u32[]{:S(2)}) collective-permute-start(bf16[640,1024]{1,0:T(8,128)(2,1)S(1)} %collective-permute-done.5.refs_5_), channel_id=1, source_target_pairs={{0,4},{4,0},{8,12},{12,8},{16,20},{20,16},{24,28},{28,24},{1,5},{5... | collective-permute-start | bytes 3932168 | tf_op jit(solution)/shard_map/ppermute | solution.py:398
  95.3 38.2 %collective-permute-start.21 = (bf16[640,1280]{1,0:T(8,128)(2,1)S(1)}, bf16[640,1280]{1,0:T(8,128)(2,1)S(1)}, u32[]{:S(2)}, u32[]{:S(2)}) collective-permute-start(bf16[640,1280]{1,0:T(8,128)(2,1)S(1)} %copy-done.10), channel_id=1, source_target_pairs={{0,16},{4,20},{8,24},{12,28},{16,0},{20,4},{24,8},{28,12},{1,17},{... | collective-permute-start | bytes 4915208 | tf_op jit(solution)/shard_map/ppermute | solution.py:398
  96.8 42.2 %collective-permute-start.20 = (bf16[640,1280]{1,0:T(8,128)(2,1)S(1)}, bf16[640,1280]{1,0:T(8,128)(2,1)S(1)}, u32[]{:S(2)}, u32[]{:S(2)}) collective-permute-start(bf16[640,1280]{1,0:T(8,128)(2,1)S(1)} %copy-done.10), channel_id=1, source_target_pairs={{0,8},{4,12},{8,0},{12,4},{16,24},{20,28},{24,16},{28,20},{1,9},{5... | collective-permute-start | bytes 4915208 | tf_op jit(solution)/shard_map/ppermute | solution.py:398
  111.0 8.9 %collective-permute-start.17 = (bf16[128,640]{1,0:T(8,128)(2,1)S(1)}, bf16[128,640]{1,0:T(8,128)(2,1)S(1)}, u32[]{:S(2)}, u32[]{:S(2)}) collective-permute-start(bf16[128,640]{1,0:T(8,128)(2,1)S(1)} %get-tuple-element.60), channel_id=1, source_target_pairs={{0,1},{1,2},{2,3},{3,0},{4,5},{5,6},{6,7},{7,4},{8,9},{9,10},{10,1... | collective-permute-start | bytes 491528 | tf_op jit(solution)/shard_map/ppermute | solution.py:535
  113.9 8.8 %collective-permute-start.13 = (bf16[128,640]{1,0:T(8,128)(2,1)S(1)}, bf16[128,640]{1,0:T(8,128)(2,1)S(1)}, u32[]{:S(2)}, u32[]{:S(2)}) collective-permute-start(bf16[128,640]{1,0:T(8,128)(2,1)S(1)} %get-tuple-element.56), channel_id=1, source_target_pairs={{0,1},{1,2},{2,3},{3,0},{4,5},{5,6},{6,7},{7,4},{8,9},{9,10},{10,1... | collective-permute-start | bytes 491528 | tf_op jit(solution)/shard_map/ppermute | solution.py:535
  119.9 7.5 %collective-permute-start.18 = (bf16[128,640]{1,0:T(8,128)(2,1)S(1)}, bf16[128,640]{1,0:T(8,128)(2,1)S(1)}, u32[]{:S(2)}, u32[]{:S(2)}) collective-permute-start(bf16[128,640]{1,0:T(8,128)(2,1)S(1)} %add.14), channel_id=1, source_target_pairs={{0,1},{1,2},{2,3},{3,0},{4,5},{5,6},{6,7},{7,4},{8,9},{9,10},{10,1... | collective-permute-start | bytes 491528 | tf_op jit(solution)/shard_map/ppermute | solution.py:535
  122.8 9.0 %collective-permute-start.14 = (bf16[128,640]{1,0:T(8,128)(2,1)S(1)}, bf16[128,640]{1,0:T(8,128)(2,1)S(1)}, u32[]{:S(2)}, u32[]{:S(2)}) collective-permute-start(bf16[128,640]{1,0:T(8,128)(2,1)S(1)} %add.12), channel_id=1, source_target_pairs={{0,1},{1,2},{2,3},{3,0},{4,5},{5,6},{6,7},{7,4},{8,9},{9,10},{10,1... | collective-permute-start | bytes 491528 | tf_op jit(solution)/shard_map/ppermute | solution.py:535
  127.4 7.7 %collective-permute-start.19 = (bf16[128,640]{1,0:T(8,128)(2,1)S(1)}, bf16[128,640]{1,0:T(8,128)(2,1)S(1)}, u32[]{:S(2)}, u32[]{:S(2)}) collective-permute-start(bf16[128,640]{1,0:T(8,128)(2,1)S(1)} %add.15), channel_id=1, source_target_pairs={{0,1},{1,2},{2,3},{3,0},{4,5},{5,6},{6,7},{7,4},{8,9},{9,10},{10,1... | collective-permute-start | bytes 491528 | tf_op jit(solution)/shard_map/ppermute | solution.py:535
  131.8 7.2 %collective-permute-start.15 = (bf16[128,640]{1,0:T(8,128)(2,1)S(1)}, bf16[128,640]{1,0:T(8,128)(2,1)S(1)}, u32[]{:S(2)}, u32[]{:S(2)}) collective-permute-start(bf16[128,640]{1,0:T(8,128)(2,1)S(1)} %add.13), channel_id=1, source_target_pairs={{0,1},{1,2},{2,3},{3,0},{4,5},{5,6},{6,7},{7,4},{8,9},{9,10},{10,1... | collective-permute-start | bytes 491528 | tf_op jit(solution)/shard_map/ppermute | solution.py:535
  139.6 29.2 %collective-permute-start.28 = (bf16[384,1280]{1,0:T(8,128)(2,1)S(1)}, bf16[384,1280]{1,0:T(8,128)(2,1)S(1)}, u32[]{:S(2)}, u32[]{:S(2)}) collective-permute-start(bf16[384,1280]{1,0:T(8,128)(2,1)S(1)} %cut.10), channel_id=1, source_target_pairs={{0,8},{4,12},{8,0},{12,4},{16,24},{20,28},{24,16},{28,20},{1,9},{5... | collective-permute-start | bytes 2949128 | tf_op jit(solution)/shard_map/ppermute | solution.py:398
  142.2 12.5 %collective-permute-start.22 = (bf16[128,1280]{1,0:T(8,128)(2,1)S(1)}, bf16[128,1280]{1,0:T(8,128)(2,1)S(1)}, u32[]{:S(2)}, u32[]{:S(2)}) collective-permute-start(bf16[128,1280]{1,0:T(8,128)(2,1)S(1)} %get-tuple-element.65), channel_id=1, source_target_pairs={{0,1},{1,2},{2,3},{3,0},{4,5},{5,6},{6,7},{7,4},{8,9},{9,10},{10,1... | collective-permute-start | bytes 983048 | tf_op jit(solution)/shard_map/ppermute | solution.py:535
  146.7 15.0 %collective-permute-start.26 = (bf16[128,1280]{1,0:T(8,128)(2,1)S(1)}, bf16[128,1280]{1,0:T(8,128)(2,1)S(1)}, u32[]{:S(2)}, u32[]{:S(2)}) collective-permute-start(bf16[128,1280]{1,0:T(8,128)(2,1)S(1)} %get-tuple-element.69), channel_id=1, source_target_pairs={{0,1},{1,2},{2,3},{3,0},{4,5},{5,6},{6,7},{7,4},{8,9},{9,10},{10,1... | collective-permute-start | bytes 983048 | tf_op jit(solution)/shard_map/ppermute | solution.py:535
  146.8 21.9 %collective-permute-start.29 = (bf16[256,1280]{1,0:T(8,128)(2,1)S(1)}, bf16[256,1280]{1,0:T(8,128)(2,1)S(1)}, u32[]{:S(2)}, u32[]{:S(2)}) collective-permute-start(bf16[256,1280]{1,0:T(8,128)(2,1)S(1)} %cut.11), channel_id=1, source_target_pairs={{0,16},{4,20},{8,24},{12,28},{16,0},{20,4},{24,8},{28,12},{1,17},{... | collective-permute-start | bytes 1966088 | tf_op jit(solution)/shard_map/ppermute | solution.py:398
  154.8 14.0 %collective-permute-start.23 = (bf16[128,1280]{1,0:T(8,128)(2,1)S(1)}, bf16[128,1280]{1,0:T(8,128)(2,1)S(1)}, u32[]{:S(2)}, u32[]{:S(2)}) collective-permute-start(bf16[128,1280]{1,0:T(8,128)(2,1)S(1)} %add.16), channel_id=1, source_target_pairs={{0,1},{1,2},{2,3},{3,0},{4,5},{5,6},{6,7},{7,4},{8,9},{9,10},{10,1... | collective-permute-start | bytes 983048 | tf_op jit(solution)/shard_map/ppermute | solution.py:535
  161.8 12.7 %collective-permute-start.27 = (bf16[128,1280]{1,0:T(8,128)(2,1)S(1)}, bf16[128,1280]{1,0:T(8,128)(2,1)S(1)}, u32[]{:S(2)}, u32[]{:S(2)}) collective-permute-start(bf16[128,1280]{1,0:T(8,128)(2,1)S(1)} %add.17), channel_id=1, source_target_pairs={{0,1},{1,2},{2,3},{3,0},{4,5},{5,6},{6,7},{7,4},{8,9},{9,10},{10,1... | collective-permute-start | bytes 983048 | tf_op jit(solution)/shard_map/ppermute | solution.py:535
  179.9 12.4 %collective-permute-start.32 = (bf16[128,1280]{1,0:T(8,128)(2,1)S(1)}, bf16[128,1280]{1,0:T(8,128)(2,1)S(1)}, u32[]{:S(2)}, u32[]{:S(2)}) collective-permute-start(bf16[128,1280]{1,0:T(8,128)(2,1)S(1)} %get-tuple-element.76), channel_id=1, source_target_pairs={{0,1},{1,2},{2,3},{3,0},{4,5},{5,6},{6,7},{7,4},{8,9},{9,10},{10,1... | collective-permute-start | bytes 983048 | tf_op jit(solution)/shard_map/ppermute | solution.py:535
  180.0 19.3 %collective-permute-start.34 = (bf16[128,1280]{1,0:T(8,128)(2,1)S(1)}, bf16[128,1280]{1,0:T(8,128)(2,1)S(1)}, u32[]{:S(2)}, u32[]{:S(2)}) collective-permute-start(bf16[128,1280]{1,0:T(8,128)(2,1)S(1)} %add.19), channel_id=1, source_target_pairs={{0,1},{1,2},{2,3},{3,0},{4,5},{5,6},{6,7},{7,4},{8,9},{9,10},{10,1... | collective-permute-start | bytes 983048 | tf_op jit(solution)/shard_map/ppermute | solution.py:535
  192.4 14.0 %collective-permute-start.33 = (bf16[128,1280]{1,0:T(8,128)(2,1)S(1)}, bf16[128,1280]{1,0:T(8,128)(2,1)S(1)}, u32[]{:S(2)}, u32[]{:S(2)}) collective-permute-start(bf16[128,1280]{1,0:T(8,128)(2,1)S(1)} %add.18), channel_id=1, source_target_pairs={{0,1},{1,2},{2,3},{3,0},{4,5},{5,6},{6,7},{7,4},{8,9},{9,10},{10,1... | collective-permute-start | bytes 983048 | tf_op jit(solution)/shard_map/ppermute | solution.py:535
  192.5 20.8 %collective-permute-start.36 = (bf16[128,1280]{1,0:T(8,128)(2,1)S(1)}, bf16[128,1280]{1,0:T(8,128)(2,1)S(1)}, u32[]{:S(2)}, u32[]{:S(2)}) collective-permute-start(bf16[128,1280]{1,0:T(8,128)(2,1)S(1)} %add.21), channel_id=1, source_target_pairs={{0,1},{1,2},{2,3},{3,0},{4,5},{5,6},{6,7},{7,4},{8,9},{9,10},{10,1... | collective-permute-start | bytes 983048 | tf_op jit(solution)/shard_map/ppermute | solution.py:535
  206.4 13.2 %collective-permute-start.35 = (bf16[128,1280]{1,0:T(8,128)(2,1)S(1)}, bf16[128,1280]{1,0:T(8,128)(2,1)S(1)}, u32[]{:S(2)}, u32[]{:S(2)}) collective-permute-start(bf16[128,1280]{1,0:T(8,128)(2,1)S(1)} %add.20), channel_id=1, source_target_pairs={{0,1},{1,2},{2,3},{3,0},{4,5},{5,6},{6,7},{7,4},{8,9},{9,10},{10,1... | collective-permute-start | bytes 983048 | tf_op jit(solution)/shard_map/ppermute | solution.py:535
  (16 other events, 173.3 us)
